TPU v7x, 32 devices: a whole 2x2x4 slice. The times are simulated.
32 devices in a mesh: gx: 8 (over z, x), gy: 4 (over y, core).
Axes of the slice: x: 2, y: 2, z: 4, core: 2. Of those that a mesh axis runs over, the one named last changes fastest.
Arguments:
- depth: float32 [1024, 2048], P('gx', 'gy'), may hold values from 0.3 to 1.2
- momentum_x: float32 [1024, 2048], P('gx', 'gy'), may hold values from -3 to 3
- momentum_y: float32 [1024, 2048], P('gx', 'gy'), may hold values from -3 to 3
- bed: float32 [1024, 2048], P('gx', 'gy'), may hold values from -1 to 1
- wet: int32 [1024, 2048], P('gx', 'gy'), may hold values 0 or 1
Outputs:
- new_depth: float32 [1024, 2048], P('gx', 'gy')
- velocity_x: float32 [1024, 2048], P('gx', 'gy')
- velocity_y: float32 [1024, 2048], P('gx', 'gy')
All inputs are finite; a program needn't handle non-finite values. No bound on the sum of `wet` on one device may be relied on, other than what follows from the above.
Results may differ from a plain program's by a relative error of at most 0.0013.
Values sent between devices are 32-bit elements; how exact they have to be, the bound alone decides.
No kernel may reach another device: no remote copies, remote signals or barrier semaphores. Data moves between devices by JAX's collectives and lax.ppermute only.
A program may use at most 64 MiB of HBM per device.

v0:
```python
import jax
import jax.numpy as jnp
from jax import lax
from jax.sharding import PartitionSpec as P

gravity = 9.81
ratio_x = 0.05
ratio_y = 0.05


def with_halo(block, sides, width):
    for axis, dim in sides:
        count = lax.axis_size(axis)
        forward = [(i, i + 1) for i in range(count - 1)]
        backward = [(target, source) for source, target in forward]
        low = lax.ppermute(
            lax.slice_in_dim(block, block.shape[dim] - width, None, axis=dim), axis, forward
        )
        high = lax.ppermute(lax.slice_in_dim(block, 0, width, axis=dim), axis, backward)
        block = jnp.concatenate([low, block, high], axis=dim)
    return block


def minmod(left, right):
    return 0.5 * (jnp.sign(left) + jnp.sign(right)) * jnp.minimum(jnp.abs(left), jnp.abs(right))


def window(values, start, stop, line_axis):
    return lax.slice_in_dim(values, start, stop, axis=line_axis)


def physical(height, normal, across):
    speed_n = normal / height
    fluxes = (normal, normal * speed_n + 0.5 * gravity * height * height, across * speed_n)
    return (fluxes, jnp.abs(speed_n) + jnp.sqrt(gravity * height))


def face_terms(depth, normal, across, wet_cells, line_axis):
    length = depth.shape[line_axis]
    states = (depth, normal, across)
    slopes = [
        minmod(
            window(field, 1, length - 1, line_axis) - window(field, 0, length - 2, line_axis),
            window(field, 2, length, line_axis) - window(field, 1, length - 1, line_axis),
        )
        for field in states
    ]
    lefts = [
        window(field, 1, length - 2, line_axis) + 0.5 * window(slope, 0, length - 3, line_axis)
        for field, slope in zip(states, slopes)
    ]
    rights = [
        window(field, 2, length - 1, line_axis) - 0.5 * window(slope, 1, length - 2, line_axis)
        for field, slope in zip(states, slopes)
    ]
    opened = window(wet_cells, 1, length - 2, line_axis) * window(
        wet_cells, 2, length - 1, line_axis
    )
    safe_left = jnp.where(opened > 0.5, lefts[0], 1.0)
    safe_right = jnp.where(opened > 0.5, rights[0], 1.0)
    flux_left, speed_left = physical(safe_left, lefts[1], lefts[2])
    flux_right, speed_right = physical(safe_right, rights[1], rights[2])
    fastest = jnp.maximum(speed_left, speed_right)
    result = []
    for flux_a, flux_b, state_a, state_b in zip(flux_left, flux_right, lefts, rights):
        face = opened * (0.5 * (flux_a + flux_b) - 0.5 * fastest * (state_b - state_a))
        count = face.shape[line_axis]
        result.append(window(face, 1, count, line_axis) - window(face, 0, count - 1, line_axis))
    return result


def predict(padded):
    along_x = padded[:, :, 2:-2]
    along_y = padded[:, 2:-2, :]
    center = padded[:, 2:-2, 2:-2]
    depth, flow_x, flow_y, wet_cells = (center[0], center[1], center[2], center[4])
    mass_x, normal_x, shear_x = face_terms(along_x[0], along_x[1], along_x[2], along_x[4], 0)
    mass_y, normal_y, shear_y = face_terms(along_y[0], along_y[2], along_y[1], along_y[4], 1)
    bed_x = 0.5 * (along_x[3, 3:-1] - along_x[3, 1:-3])
    bed_y = 0.5 * (along_y[3, :, 3:-1] - along_y[3, :, 1:-3])
    new_depth = depth - wet_cells * (ratio_x * mass_x + ratio_y * mass_y)
    push_x = wet_cells * (
        flow_x - ratio_x * normal_x - ratio_y * shear_y - ratio_x * gravity * depth * bed_x
    )
    push_y = wet_cells * (
        flow_y - ratio_x * shear_x - ratio_y * normal_y - ratio_y * gravity * depth * bed_y
    )
    return (new_depth, push_x, push_y)


def earlier(values, stride, line_axis, fill):
    which = line_axis % values.ndim
    widths = [(0, 0)] * values.ndim
    widths[which] = (stride, 0)
    padded = jnp.pad(values, widths, constant_values=fill)
    return lax.slice_in_dim(padded, 0, values.shape[which], axis=which)


def later(values, stride, line_axis, fill):
    which = line_axis % values.ndim
    widths = [(0, 0)] * values.ndim
    widths[which] = (0, stride)
    padded = jnp.pad(values, widths, constant_values=fill)
    return lax.slice_in_dim(padded, stride, stride + values.shape[which], axis=which)


def eliminate(rows, below, above):
    lower, diagonal, upper, right = rows
    left_factor = lower / below[1]
    right_factor = upper / above[1]
    return (
        -left_factor * below[0],
        diagonal - left_factor * below[2] - right_factor * above[0],
        -right_factor * above[2],
        right - left_factor * below[3] - right_factor * above[3],
    )


def reduce_lines(lower, diagonal, upper, right, line_axis):
    count = diagonal.shape[line_axis % diagonal.ndim]
    rows = (lower, diagonal, upper, right)
    stride = 1
    while stride < count:
        below = tuple(
            (
                earlier(member, stride, line_axis, fill)
                for member, fill in zip(rows, (0.0, 1.0, 0.0, 0.0))
            )
        )
        above = tuple(
            (
                later(member, stride, line_axis, fill)
                for member, fill in zip(rows, (0.0, 1.0, 0.0, 0.0))
            )
        )
        rows = lax.optimization_barrier(eliminate(rows, below, above))
        stride *= 2
    return rows[3] / rows[1]


def separator_rows(last_six, next_three):
    solved_y, solved_g, solved_e, sep_coef, sep_diag, sep_right = last_six
    first_y, first_g, first_e = next_three
    return (
        -sep_coef * solved_g,
        sep_diag - sep_coef * solved_e - sep_coef * first_g,
        -sep_coef * first_e,
        sep_right + sep_coef * solved_y + sep_coef * first_y,
    )


def local_spikes(coefficient, right, line_axis):
    which = line_axis % 2
    count = coefficient.shape[which]
    inner = lax.slice_in_dim(coefficient, 0, count - 1, axis=which)
    position = lax.broadcasted_iota(jnp.int32, inner.shape, which)
    zeros = jnp.zeros_like(inner)
    sources = jnp.stack(
        [
            lax.slice_in_dim(right, 0, count - 1, axis=which),
            jnp.where(position == 0, inner, zeros),
            jnp.where(position == count - 2, inner, zeros),
        ]
    )
    solved = reduce_lines(-inner, 1.0 + 2.0 * inner, -inner, sources, line_axis)
    first = lax.index_in_dim(solved, 0, which + 1, keepdims=False)
    final = lax.index_in_dim(solved, count - 2, which + 1, keepdims=False)
    sep_coef = lax.index_in_dim(coefficient, count - 1, which, keepdims=False)
    sep_right = lax.index_in_dim(right, count - 1, which, keepdims=False)
    last_six = jnp.concatenate([final, jnp.stack([sep_coef, 1.0 + 2.0 * sep_coef, sep_right])])
    return (solved, first, last_six)


def assemble(solved, own, previous, line_axis):
    which = line_axis % 2
    own_wide = jnp.expand_dims(own, which)
    prev_wide = jnp.expand_dims(previous, which)
    inner = solved[0] + solved[1] * prev_wide + solved[2] * own_wide
    return jnp.concatenate([inner, own_wide], axis=which)


def pick_rows(whole, index):
    first_all = whole[:3]
    rows = separator_rows(whole[3:], later(first_all, 1, -2, 0.0))
    solved = reduce_lines(rows[0], rows[1], rows[2], rows[3], -2)
    own = lax.dynamic_index_in_dim(solved, index, 0, keepdims=False)
    previous = lax.dynamic_index_in_dim(earlier(solved, 1, -2, 0.0), index, 0, keepdims=False)
    return (own, previous)


def interface_x(first, last_six):
    packed = jnp.concatenate([first, last_six])[:, None, :]
    whole = lax.all_gather(packed, "gx", axis=1, tiled=True)
    return pick_rows(whole, lax.axis_index("gx"))


def interface_y(first, last_six):
    packed = jnp.concatenate([first, last_six])[:, None, :]
    whole = lax.all_gather(packed, "gy", axis=1, tiled=True)
    return pick_rows(whole, lax.axis_index("gy"))


def on_device(depth, momentum_x, momentum_y, bed, wet):
    stacked = jnp.stack([depth, momentum_x, momentum_y, bed, wet.astype(jnp.float32)])
    padded = with_halo(stacked, (("gx", 1), ("gy", 2)), 2)
    new_depth, push_x, push_y = predict(padded)
    cells_x = depth.shape[0] * lax.axis_size("gx")
    cells_y = depth.shape[1] * lax.axis_size("gy")
    scale_x = (cells_x / 4.0) ** 2 / 3.0
    scale_y = (cells_y / 4.0) ** 2 / 3.0
    coef_x = scale_x * depth * depth
    coef_y = scale_y * depth * depth
    solved_x, first_x, last_x = local_spikes(coef_x, push_x, -2)
    own_x, prev_x = interface_x(first_x, last_x)
    flux_u = assemble(solved_x, own_x, prev_x, -2)
    solved_y, first_y, last_y = local_spikes(coef_y, push_y, -1)
    own_y, prev_y = interface_y(first_y, last_y)
    flux_v = assemble(solved_y, own_y, prev_y, -1)
    return (new_depth, flux_u / depth, flux_v / depth)


def solution(mesh):
    placed = (P("gx", "gy"), P("gx", "gy"), P("gx", "gy"), P("gx", "gy"), P("gx", "gy"))
    return jax.shard_map(
        on_device,
        mesh=mesh,
        in_specs=placed,
        out_specs=(P("gx", "gy"), P("gx", "gy"), P("gx", "gy")),
        check_vma=False,
    )
```

profile of v0, /device:TPU:0, one launch (start us, length us, event | category | flops | bytes accessed | tf_op | source)
XLA Modules:
  0.0 91.9 jit_solution(1714657368224538494)
XLA Ops:
  0.7 1.0 %bitcast_dynamic-update-slice_fusion.4 = f32[5,128,512]{2,1,0:T(8,128)S(1)} fusion(f32[128,512]{1,0:T(8,128)} %param.5), kind=kLoop, calls=%fused_computation.464 | loop fusion | bytes 524288
  1.7 1.0 %bitcast_dynamic-update-slice_fusion.3 = f32[5,128,512]{2,1,0:T(8,128)S(1)} fusion(f32[5,128,512]{2,1,0:T(8,128)S(1)} %bitcast_dynamic-update-slice_fusion.4, f32[128,512]{1,0:T(8,128)} %param.6), kind=kLoop, calls=%fused_computation.463 | loop fusion | bytes 524288
  2.7 1.0 %bitcast_dynamic-update-slice_fusion.2 = f32[5,128,512]{2,1,0:T(8,128)S(1)} fusion(f32[5,128,512]{2,1,0:T(8,128)S(1)} %bitcast_dynamic-update-slice_fusion.3, f32[128,512]{1,0:T(8,128)} %param.7), kind=kLoop, calls=%fused_computation.462 | loop fusion | bytes 524288
  3.7 4.8 %collective-permute-start = (f32[5,2,512]{2,1,0:T(2,128)S(1)}, f32[5,2,512]{2,1,0:T(2,128)S(1)}, u32[]{:S(2)}, u32[]{:S(2)}) collective-permute-start(f32[5,2,512]{2,1,0:T(2,128)S(1)} %get-tuple-element.250), channel_id=1, source_target_pairs={{0,4},{4,8},{8,12},{12,16},{16,20},{20,24},{24,28},{1,5},{5,9},{9,... | collective-permute-start | bytes 61448 | tf_op jit(solution)/shard_map/ppermute | solution.py:16
  8.6 1.3 %collective-permute-start.1 = (f32[5,2,512]{2,1,0:T(2,128)S(1)}, f32[5,2,512]{2,1,0:T(2,128)S(1)}, u32[]{:S(2)}, u32[]{:S(2)}) collective-permute-start(f32[5,2,512]{2,1,0:T(2,128)S(1)} %get-tuple-element.251), channel_id=1, source_target_pairs={{4,0},{8,4},{12,8},{16,12},{20,16},{24,20},{28,24},{5,1},{9,5},{13... | collective-permute-start | bytes 61448 | tf_op jit(solution)/shard_map/ppermute | solution.py:19
  9.9 0.6 iota_compare_fusion.2
  10.5 3.8 %collective-permute-done.1 = f32[5,2,512]{2,1,0:T(2,128)S(1)} collective-permute-done((f32[5,2,512]{2,1,0:T(2,128)S(1)}, f32[5,2,512]{2,1,0:T(2,128)S(1)}, u32[]{:S(2)}, u32[]{:S(2)}) %collective-permute-start.1) | collective-permute-done | bytes 20512 | tf_op jit(solution)/shard_map/ppermute | solution.py:19
  14.6 1.3 %collective-permute-start.2 = (f32[5,132,2]{2,1,0:T(8,128)S(1)}, f32[5,132,2]{2,1,0:T(8,128)S(1)}, u32[]{:S(2)}, u32[]{:S(2)}) collective-permute-start(f32[5,132,2]{2,1,0:T(8,128)S(1)} %get-tuple-element.248), channel_id=1, source_target_pairs={{0,1},{1,2},{2,3},{4,5},{5,6},{6,7},{8,9},{9,10},{10,11},{12,13},{... | collective-permute-start | bytes 15848 | tf_op jit(solution)/shard_map/ppermute | solution.py:16
  15.9 1.3 %collective-permute-start.3 = (f32[5,132,2]{2,1,0:T(8,128)S(1)}, f32[5,132,2]{2,1,0:T(8,128)S(1)}, u32[]{:S(2)}, u32[]{:S(2)}) collective-permute-start(f32[5,132,2]{2,1,0:T(8,128)S(1)} %get-tuple-element.249), channel_id=1, source_target_pairs={{1,0},{2,1},{3,2},{5,4},{6,5},{7,6},{9,8},{10,9},{11,10},{13,12},{... | collective-permute-start | bytes 15848 | tf_op jit(solution)/shard_map/ppermute | solution.py:19
  17.2 0.7 minimum_multiply_fusion.4
  18.0 0.6 subtract_multiply_fusion.2
  18.6 1.2 %fusion.73 = (f32[129,512]{1,0:T(8,128)}, f32[129,512]{1,0:T(8,128)S(1)}) fusion(f32[129,512]{1,0:T(8,128)S(1)} %get-tuple-element.205, f32[129,512]{1,0:T(8,128)S(1)} %get-tuple-element.201, f32[129,512]{1,0:T(8,128)S(1)} %get-tuple-element.202, f32[129,512]{1,0:T(8,128)S(1)} %get-tuple-element.204, f32[129,512]{1,0:T(8,128)S(1)} %get-tuple-element.203), kind=kLoop, calls=%fused_computation.230 | loop fusion | flops 2179584 | bytes 1849344 | tf_op jit(solution)/shard_map/mul | solution.py:66
  19.7 1.5 %collective-permute-done.3 = f32[5,132,2]{2,1,0:T(8,128)S(1)} collective-permute-done((f32[5,132,2]{2,1,0:T(8,128)S(1)}, f32[5,132,2]{2,1,0:T(8,128)S(1)}, u32[]{:S(2)}, u32[]{:S(2)}) %collective-permute-start.3) | collective-permute-done | bytes 5312 | tf_op jit(solution)/shard_map/ppermute | solution.py:19
  21.9 1.3 %minimum_multiply_fusion = (f32[128,514]{1,0:T(8,128)}, f32[128,514]{1,0:T(8,128)S(1)}) fusion(f32[128,516]{1,0:T(8,128)S(1)} %get-tuple-element.243, f32[128,516]{1,0:T(8,128)S(1)} %get-tuple-element.244), kind=kLoop, calls=%fused_computation.215 | loop fusion | flops 1315840 | bytes 2105344 | tf_op jit(solution)/shard_map/mul | solution.py:25
  23.4 0.8 fusion.60
  24.2 0.8 subtract_multiply_fusion.1
  25.3 1.1 %fusion.232 = (f32[128,512]{1,0:T(8,128)S(1)}, f32[128,512]{1,0:T(8,128)}, f32[128,512]{1,0:T(8,128)S(1)}) fusion(f32[5,132,2]{2,1,0:T(8,128)S(1)} %collective-permute-done.2, f32[5,2,512]{2,1,0:T(2,128)S(1)} %copy-done.12, f32[5,128,512]{2,1,0:T(8,128)S(1)} %bitcast_dynamic-update-slice_fusion, f32[5,2,512]{2,1,0:T(2,128)S(1)} %copy-done.10, ...), kind=kLoop, calls=%fused_computation.426 | loop fusion | flops 1769472 | bytes 5032256 | tf_op jit(solution)/shard_map/mul | solution.py:85
  26.4 0.7 slice_reduce_fusion.2
  27.4 0.5 multiply_add_fusion.3
  28.6 0.5 multiply_subtract_fusion
  30.8 0.5 fusion.26
  35.5 0.5 fusion.42
  36.7 0.9 copy-done
  37.9 1.3 %concatenate.52 = f32[9,128]{1,0:T(8,128)S(1)} concatenate(f32[3,128]{1,0:T(4,128)S(1)} %get-tuple-element.159, f32[3,128]{1,0:T(4,128)S(1)} %get-tuple-element.158, f32[1,128]{1,0:T(1,128)} %bitcast.167, f32[1,128]{1,0:T(1,128)} %multiply_add_fusion.3, f32[1,128]{1,0:T(1,128)} %bitcast.166), dimensions={0} | concatenate | bytes 9216 | tf_op jit(solution)/shard_map/concatenate | solution.py:198
  39.2 9.4 %all-gather.1 = f32[9,512]{1,0:T(8,128)S(1)} all-gather(f32[9,128]{1,0:T(8,128)S(1)} %concatenate.52), channel_id=3, replica_groups=mesh['gx'=8,'gy'=4] {'gy'}, dimensions={1}, use_global_device_ids=true | all-gather | bytes 23040 | tf_op jit(solution)/shard_map/all_gather | solution.py:199
  48.6 0.6 fusion.362
  49.2 2.8 %subtract_multiply_fusion = f32[128,513]{1,0:T(8,128)} fusion(f32[128,514]{1,0:T(8,128)} %get-tuple-element.296, f32[128,516]{1,0:T(8,128)S(1)} %get-tuple-element.243, f32[128,516]{1,0:T(8,128)S(1)} %maximum_bitcast_fusion.2, f32[128,514]{1,0:T(8,128)S(1)} %minimum_multiply_fusion.2, f32[128,516]{1,0:T(8,128)S(1)} %get-tuple-element.245, ...), kind=kLoop, calls=%fused_computation.214 | loop fusion | flops 2232576 | bytes 3939840 | tf_op jit(solution)/shard_map/mul | solution.py:66
  52.0 0.8 fusion.315
  53.1 1.2 %fusion.224 = f32[128,511]{1,0:T(8,128)S(1)} fusion(f32[3,128,511]{2,1,0:T(8,128)} %copy-done, f32[128]{0:T(128)S(1)} %get-tuple-element.294, f32[128]{0:T(128)S(1)} %fusion.321), kind=kLoop, calls=%fused_computation.414 | loop fusion | flops 261632 | bytes 1047552 | tf_op jit(solution)/shard_map/add | solution.py:178
  54.3 1.6 %maximum_divide_fusion.1 = (f32[128,512]{1,0:T(8,128)}, f32[128,512]{1,0:T(8,128)S(1)}, f32[128,512]{1,0:T(8,128)S(1)}) fusion(f32[128,512]{1,0:T(8,128)S(1)} %copy-done.1, f32[128,1]{1,0:T(8,128)S(1)} %copy.50, f32[128,511]{1,0:T(8,128)S(1)} %fusion.224, f32[5,128,512]{2,1,0:T(8,128)S(1)} %bitcast_dynamic-update-slice_fusion, f32[5,2,512]{2,1,0:T(2,128)} %copy-done.9, ...), kind=kLoop, calls=%fused_computation.459 | loop fusion | flops 1245184 | bytes 4235264 | tf_op jit(solution)/shard_map/div | solution.py:219
  59.3 31.2 %all-gather = f32[9,4096]{1,0:T(8,128)S(1)} all-gather(f32[9,512]{1,0:T(8,128)S(1)} %concatenate.48), channel_id=2, replica_groups=mesh['gx'=8,'gy'=4] {'gx'}, dimensions={1}, use_global_device_ids=true | all-gather | bytes 165888 | tf_op jit(solution)/shard_map/all_gather | solution.py:193
  91.1 0.7 maximum_divide_fusion
  (146 shorter events, 13.1 us)
Async XLA Ops:
  0.6 3.0 %copy-start.13 = (f32[128,512]{1,0:T(8,128)S(1)}, f32[128,512]{1,0:T(8,128)}, u32[]{:S(2)}) copy-start(f32[128,512]{1,0:T(8,128)} %param.8) | copy-start | bytes 786436
  0.6 3.0 %copy-start.2 = (s32[128,512]{1,0:T(8,128)S(1)}, s32[128,512]{1,0:T(8,128)}, u32[]{:S(2)}) copy-start(s32[128,512]{1,0:T(8,128)} %param.9) | copy-start | bytes 786436
  3.7 6.7 %collective-permute-start = (f32[5,2,512]{2,1,0:T(2,128)S(1)}, f32[5,2,512]{2,1,0:T(2,128)S(1)}, u32[]{:S(2)}, u32[]{:S(2)}) collective-permute-start(f32[5,2,512]{2,1,0:T(2,128)S(1)} %get-tuple-element.250), channel_id=1, source_target_pairs={{0,4},{4,8},{8,12},{12,16},{16,20},{20,24},{24,28},{1,5},{5,9},{9,... | collective-permute-start | bytes 61448 | tf_op jit(solution)/shard_map/ppermute | solution.py:16
  8.6 5.7 %collective-permute-start.1 = (f32[5,2,512]{2,1,0:T(2,128)S(1)}, f32[5,2,512]{2,1,0:T(2,128)S(1)}, u32[]{:S(2)}, u32[]{:S(2)}) collective-permute-start(f32[5,2,512]{2,1,0:T(2,128)S(1)} %get-tuple-element.251), channel_id=1, source_target_pairs={{4,0},{8,4},{12,8},{16,12},{20,16},{24,20},{28,24},{5,1},{9,5},{13... | collective-permute-start | bytes 61448 | tf_op jit(solution)/shard_map/ppermute | solution.py:19
  10.5 12.7 %copy-start.9 = (f32[5,2,512]{2,1,0:T(2,128)}, f32[5,2,512]{2,1,0:T(2,128)S(1)}, u32[]{:S(2)}) copy-start(f32[5,2,512]{2,1,0:T(2,128)S(1)} %collective-permute-done) | copy-start | bytes 61444
  14.3 9.0 %copy-start.11 = (f32[5,2,512]{2,1,0:T(2,128)}, f32[5,2,512]{2,1,0:T(2,128)S(1)}, u32[]{:S(2)}) copy-start(f32[5,2,512]{2,1,0:T(2,128)S(1)} %collective-permute-done.1) | copy-start | bytes 61444
  14.6 5.1 %collective-permute-start.2 = (f32[5,132,2]{2,1,0:T(8,128)S(1)}, f32[5,132,2]{2,1,0:T(8,128)S(1)}, u32[]{:S(2)}, u32[]{:S(2)}) collective-permute-start(f32[5,132,2]{2,1,0:T(8,128)S(1)} %get-tuple-element.248), channel_id=1, source_target_pairs={{0,1},{1,2},{2,3},{4,5},{5,6},{6,7},{8,9},{9,10},{10,11},{12,13},{... | collective-permute-start | bytes 15848 | tf_op jit(solution)/shard_map/ppermute | solution.py:16
  15.9 5.3 %collective-permute-start.3 = (f32[5,132,2]{2,1,0:T(8,128)S(1)}, f32[5,132,2]{2,1,0:T(8,128)S(1)}, u32[]{:S(2)}, u32[]{:S(2)}) collective-permute-start(f32[5,132,2]{2,1,0:T(8,128)S(1)} %get-tuple-element.249), channel_id=1, source_target_pairs={{1,0},{2,1},{3,2},{5,4},{6,5},{7,6},{9,8},{10,9},{11,10},{13,12},{... | collective-permute-start | bytes 15848 | tf_op jit(solution)/shard_map/ppermute | solution.py:19
  24.2 1.0 %copy-start.1 = (f32[128,512]{1,0:T(8,128)S(1)}, f32[128,512]{1,0:T(8,128)}, u32[]{:S(2)}) copy-start(f32[128,512]{1,0:T(8,128)} %param.5) | copy-start | bytes 786436
  24.2 1.0 %copy-start.3 = (s32[128,512]{1,0:T(8,128)S(1)}, s32[128,512]{1,0:T(8,128)}, u32[]{:S(2)}) copy-start(s32[128,512]{1,0:T(8,128)} %param.9) | copy-start | bytes 786436
  24.2 1.1 %copy-start.7 = (f32[128,512]{1,0:T(8,128)S(1)}, f32[128,512]{1,0:T(8,128)}, u32[]{:S(2)}) copy-start(f32[128,512]{1,0:T(8,128)} %param.7) | copy-start | bytes 786436
  24.2 1.1 %copy-start.10 = (f32[5,2,512]{2,1,0:T(2,128)S(1)}, f32[5,2,512]{2,1,0:T(2,128)}, u32[]{:S(2)}) copy-start(f32[5,2,512]{2,1,0:T(2,128)} %copy-done.9) | copy-start | bytes 61444
  24.2 1.1 %copy-start.12 = (f32[5,2,512]{2,1,0:T(2,128)S(1)}, f32[5,2,512]{2,1,0:T(2,128)}, u32[]{:S(2)}) copy-start(f32[5,2,512]{2,1,0:T(2,128)} %copy-done.11) | copy-start | bytes 61444
  27.3 1.1 %copy-start.14 = (f32[128]{0:T(128)}, f32[128]{0:T(128)S(1)}, u32[]{:S(2)}) copy-start(f32[128]{0:T(128)S(1)} %slice_reduce_fusion.3) | copy-start | bytes 1540
  36.7 0.9 copy-start
  52.0 2.3 %copy-start.4 = (s32[128,512]{1,0:T(8,128)S(1)}, s32[128,512]{1,0:T(8,128)}, u32[]{:S(2)}) copy-start(s32[128,512]{1,0:T(8,128)} %param.9) | copy-start | bytes 786436
  52.0 2.3 %copy-start.5 = (f32[129,512]{1,0:T(8,128)S(1)}, f32[129,512]{1,0:T(8,128)}, u32[]{:S(2)}) copy-start(f32[129,512]{1,0:T(8,128)} %get-tuple-element.246) | copy-start | bytes 792580
  52.0 2.3 %copy-start.6 = (f32[128,513]{1,0:T(8,128)S(1)}, f32[128,513]{1,0:T(8,128)}, u32[]{:S(2)}) copy-start(f32[128,513]{1,0:T(8,128)} %subtract_multiply_fusion) | copy-start | bytes 787972
  52.0 2.3 %copy-start.8 = (f32[128,512]{1,0:T(8,128)S(1)}, f32[128,512]{1,0:T(8,128)}, u32[]{:S(2)}) copy-start(f32[128,512]{1,0:T(8,128)} %param.6) | copy-start | bytes 786436
  54.3 1.8 %copy-start.15 = (pred[127]{0:T(512)(128)(4,1)S(1)}, pred[127]{0:T(512)(128)(4,1)}, u32[]{:S(2)}) copy-start(pred[127]{0:T(512)(128)(4,1)} %get-tuple-element.300) | copy-start | bytes 385
  54.3 1.8 %copy-start.16 = (pred[127]{0:T(512)(128)(4,1)S(1)}, pred[127]{0:T(512)(128)(4,1)}, u32[]{:S(2)}) copy-start(pred[127]{0:T(512)(128)(4,1)} %get-tuple-element.301) | copy-start | bytes 385
where the time goes:
time: 92.3 us; the launch traced here: 91.9 us
  blocking collectives  40.6 us (44%)
  other arithmetic  27.6 us (30%)
  starting transfers between devices  8.74 us (9%)
  local copies, waits for them, and re-layouts  8.04 us (9%)
  waiting for transfers between devices  5.29 us (6%)
  between operations  1.59 us (2%)
    all_gather x1, blocking collectives, interface_x(): whole = lax.all_gather(packed, 'gx', axis=1, tiled=True)  31.2 us
    all_gather x1, blocking collectives, interface_y(): whole = lax.all_gather(packed, 'gy', axis=1, tiled=True)  9.4 us
    ppermute x2, starting transfers between devices, with_halo(): lax.ppermute(lax.slice_in_dim(block, block.shape[dim] - width, None, axis...  6.16 us
    mul x5, other arithmetic, face_terms(): opened * (0.5 * (flux_a + flux_b) - 0.5 * fastest * (state_b - state_a))  6.07 us
    ppermute x2, waiting for transfers between devices, with_halo(): lax.ppermute(lax.slice_in_dim(block, 0, width, axis=dim), axis, backward)  5.28 us
    sub x21, other arithmetic, eliminate(): right - left_factor * below[3] - right_factor * above[3]  4.98 us
    unnamed x41, local copies, waits for them, and re-layouts  4.27 us
    sub x16, other arithmetic, eliminate(): diagonal - left_factor * below[2] - right_factor * above[0]  2.92 us
  transfers between devices with their start and end apart: 4, of which 2 were waited for; matrix products, arithmetic and copies ran while one was open for 3% of the time, Pallas kernels for 0%

commit v1 on v0

v1 whole, which is shorter than its diff:
```python
import functools

import jax
import jax.numpy as jnp
from jax import lax
from jax.experimental import pallas as pl
from jax.experimental.pallas import tpu as pltpu
from jax.sharding import PartitionSpec as P

gravity = 9.81
ratio = 0.05
LANES = 128
SUB = 8
VMEM = pl.BlockSpec(memory_space=pltpu.VMEM)
ANY = pl.BlockSpec(memory_space=pl.ANY)
PARAMS = pltpu.CompilerParams(vmem_limit_bytes=24 * 1024 * 1024)


def lane_index(shape):
    return lax.broadcasted_iota(jnp.int32, shape, len(shape) - 1)


def row_index(shape):
    return lax.broadcasted_iota(jnp.int32, shape, len(shape) - 2)


def pack_kernel(h, p, q, b, m, xa, xb, ya, yb, top, bottom, left, right, itop, ibottom, ileft, iright, sems):
    rows, cols = h.shape
    copies = []
    for f, src in enumerate((h, p, q, b, m)):
        floats = f < 4
        spots = (
            (src.at[pl.ds(0, SUB), :], top.at[f] if floats else itop),
            (src.at[pl.ds(rows - SUB, SUB), :], bottom.at[f] if floats else ibottom),
            (src.at[:, pl.ds(0, LANES)], left.at[f] if floats else ileft),
            (src.at[:, pl.ds(cols - LANES, LANES)], right.at[f] if floats else iright),
        )
        for g, (piece, target) in enumerate(spots):
            copy = pltpu.make_async_copy(piece, target, sems.at[4 * f + g])
            copy.start()
            copies.append(copy)
    for copy in copies:
        copy.wait()
    first_x = jnp.concatenate(
        [top[0, 0:2, :], top[1, 0:2, :], top[2, 0:2, :], top[3, 0:1, :], itop[0:1, :].astype(jnp.float32)]
    )
    last_x = jnp.concatenate(
        [
            bottom[0, SUB - 2 : SUB, :],
            bottom[1, SUB - 2 : SUB, :],
            bottom[2, SUB - 2 : SUB, :],
            bottom[3, SUB - 1 : SUB, :],
            ibottom[SUB - 1 : SUB, :].astype(jnp.float32),
        ]
    )
    even_x = lax.axis_index("gx") % 2 == 0
    xa[...] = jnp.where(even_x, last_x, first_x)
    xb[...] = jnp.where(even_x, first_x, last_x)
    lane = lane_index((rows, LANES))

    def columns(block, imask, shifts):
        fields = [block[0], block[1], block[2], block[3], imask[...].astype(jnp.float32)]
        moved = [pltpu.roll(v, s, 1) if s else v for v, s in zip(fields, shifts)]
        out = moved[0]
        for start, v in zip((2, 4, 6, 7), moved[1:]):
            out = jnp.where(lane >= start, v, out)
        return out.T[0:SUB, :]

    first_y = columns(left, ileft, (0, 2, 4, 6, 7))
    last_y = columns(right, iright, (2, 4, 6, 7, 8))
    even_y = lax.axis_index("gy") % 2 == 0
    ya[...] = jnp.where(even_y, last_y, first_y)
    yb[...] = jnp.where(even_y, first_y, last_y)


def pack(h, p, q, b, m):
    rows, cols = h.shape
    f32, i32 = jnp.float32, jnp.int32
    slab_x = jax.ShapeDtypeStruct((SUB, cols), f32)
    slab_y = jax.ShapeDtypeStruct((SUB, rows), f32)
    return pl.pallas_call(
        pack_kernel,
        out_shape=(slab_x, slab_x, slab_y, slab_y),
        in_specs=[ANY] * 5,
        out_specs=(VMEM,) * 4,
        scratch_shapes=[
            pltpu.VMEM((4, SUB, cols), f32),
            pltpu.VMEM((4, SUB, cols), f32),
            pltpu.VMEM((4, rows, LANES), f32),
            pltpu.VMEM((4, rows, LANES), f32),
            pltpu.VMEM((SUB, cols), i32),
            pltpu.VMEM((SUB, cols), i32),
            pltpu.VMEM((rows, LANES), i32),
            pltpu.VMEM((rows, LANES), i32),
            pltpu.SemaphoreType.DMA((20,)),
        ],
        compiler_params=PARAMS,
        name="pack",
    )(h, p, q, b, m)


def low_high(axis, a, b):
    index, count = lax.axis_index(axis), lax.axis_size(axis)
    even = index % 2 == 0
    low = jnp.where(index > 0, jnp.where(even, b, a), 0.0)
    high = jnp.where(index < count - 1, jnp.where(even, a, b), 0.0)
    return low, high


def half_slope(a, c):
    return 0.5 * (jnp.maximum(jnp.minimum(a, c), 0.0) + jnp.minimum(jnp.maximum(a, c), 0.0))


def face_flux(left, right, opened):
    is_open = opened > 0.5
    hl = jnp.where(is_open, left[0], 1.0)
    hr = jnp.where(is_open, right[0], 1.0)
    joint = 1.0 / (hl * hr)
    ul = left[1] * (hr * joint)
    ur = right[1] * (hl * joint)
    gl = gravity * hl
    gr = gravity * hr
    fastest = jnp.maximum(jnp.abs(ul) + gl * lax.rsqrt(gl), jnp.abs(ur) + gr * lax.rsqrt(gr))
    scale = (0.5 * ratio) * opened
    mass = (left[1] + right[1]) - fastest * (right[0] - left[0])
    push = 0.5 * (gl * hl + gr * hr) + left[1] * ul + right[1] * ur - fastest * (right[1] - left[1])
    shear = left[2] * ul + right[2] * ur - fastest * (right[2] - left[2])
    return scale * mass, scale * push, scale * shear


def merge(one, two):
    t1, gl1, gr1, sl1, sr1 = one
    t2, gl2, gr2, sl2, sr2 = two
    shunt = gr1 + gl2
    inverse = 1.0 / (t1 + t2 + shunt)
    w1, w2 = t1 * inverse, t2 * inverse
    source = sr1 - sl2
    merged = (w1 * t2, gl1 + w1 * shunt, gr2 + w2 * shunt, sl1 - w1 * source, sr2 + w2 * source)
    return merged, (w1, w2, source * inverse)


def march_segments(steps, d_at, r_at):
    zero = jnp.zeros_like(d_at(0))
    alpha, gamma, beta, delta, c, e = zero, zero, zero, zero, zero, zero
    for k in range(steps):
        d = d_at(k)
        alpha = alpha + gamma
        gamma = gamma + d * (1.0 + alpha)
        beta = beta + delta
        delta = delta + d * ((k + 1.0) + beta)
        c = c + e
        e = e + (d * c - r_at(k))
    t = 1.0 / (steps + beta)
    sl = t * c
    return t, t * alpha, t * delta, sl, (1.0 + delta) * sl - e


def tree(segments):
    count = segments[0].shape[0]
    levels = []
    stride = 1
    while stride < count:
        after = tuple(pltpu.roll(v, count - stride, 0) for v in segments)
        segments, weights = merge(segments, after)
        levels.append(weights)
        stride *= 2
    return segments, levels


def tile_writes(tiled, whole, sems):
    rows, cols = whole.shape
    return [
        pltpu.make_async_copy(
            tiled.at[pl.ds(tile * rows, rows), :], whole.at[:, pl.ds(tile * LANES, LANES)], sems.at[tile]
        )
        for tile in range(cols // LANES)
    ]


def flux_kernel(
    h_ref, p_ref, q_ref, b_ref, m_ref, xa, xb, ya, yb,
    nd_ref, invh_ref, rx_ref, dyt_ref, ryt_ref, segx_ref, levx_ref, segy_ref, levy_ref, endx_ref, endy_ref,
    hs, ps, qs, bs, ms, nds, edge, edge_t, dperm, rperm, sems, out_sems,
    *, inv_cx, inv_cy,
):
    rows, cols = h_ref.shape
    steps = rows // SUB
    tiles = cols // LANES
    copies = []
    for f, (src, target) in enumerate(zip((h_ref, p_ref, q_ref, b_ref, m_ref), (hs, ps, qs, bs, ms))):
        for tile in range(tiles):
            copies.append(
                pltpu.make_async_copy(
                    src.at[:, pl.ds(tile * LANES, LANES)],
                    target.at[pl.ds(tile * rows, rows), :],
                    sems.at[f * tiles + tile],
                )
            )
            copies[-1].start()
    wide = cols + LANES
    low_x, high_x = low_high("gx", xa[...], xb[...])
    low_y, high_y = low_high("gy", ya[...], yb[...])
    edge[...] = jnp.zeros_like(edge)
    edge[126:128, :] = low_y[0:2]
    edge[0:2, :] = high_y[0:2]
    edge[122:124, :] = low_y[2:4]
    edge[124:126, :] = high_y[2:4]
    edge[118:120, :] = low_y[4:6]
    edge[120:122, :] = high_y[4:6]
    edge[115:116, :] = low_y[6:7]
    edge[116:117, :] = high_y[6:7]
    edge[111:112, :] = low_y[7:8]
    edge[112:113, :] = high_y[7:8]
    edge_t[...] = edge[...].T
    for copy in copies:
        copy.wait()

    def at(ref, k):
        return jnp.concatenate(
            [ref[pl.ds(tile * rows + k, SUB, stride=steps), :] for tile in range(tiles)], axis=1
        )

    sub = row_index((SUB, cols))

    def before(value, row):
        return jnp.where(sub == 0, row, pltpu.roll(value, 1, 0))

    def after(value, row):
        return jnp.where(sub == SUB - 1, row, pltpu.roll(value, SUB - 1, 0))

    field = []
    for ref, first in ((hs, 0), (ps, 2), (qs, 4)):
        w = {k: at(ref, k) for k in range(steps)}
        w[-1] = before(w[steps - 1], low_x[first + 1 : first + 2])
        w[-2] = before(w[steps - 2], low_x[first : first + 1])
        w[steps] = after(w[0], high_x[first : first + 1])
        w[steps + 1] = after(w[1], high_x[first + 1 : first + 2])
        field.append(w)
    bed = {k: at(bs, k) for k in range(steps)}
    bed[-1] = before(bed[steps - 1], low_x[6:7])
    bed[steps] = after(bed[0], high_x[6:7])
    wet = {k: at(ms, k).astype(jnp.float32) for k in range(steps)}
    wet[-1] = before(wet[steps - 1], low_x[7:8])
    wet[steps] = after(wet[0], high_x[7:8])

    def back(v):
        return pltpu.roll(v, 1, 1)

    def ahead(v):
        return pltpu.roll(v, wide - 1, 1)

    def x_states(k):
        pair = [half_slope(w[k] - w[k - 1], w[k + 1] - w[k]) for w in field]
        return [w[k] + s for w, s in zip(field, pair)], [w[k] - s for w, s in zip(field, pair)]

    def x_face(left, right, k):
        return face_flux(left, right, wet[k] * wet[k + 1])

    left_state, _ = x_states(-1)
    face_before = None
    for k in range(-1, steps):
        left_next, right_state = x_states(k + 1)
        face = x_face(left_state, right_state, k)
        left_state = left_next
        if k >= 0:
            dfx = [a - c for a, c in zip(face, face_before)]
            h, p, q, m = field[0][k], field[1][k], field[2][k], wet[k]
            side = edge_t[pl.ds(k, SUB, stride=steps), :]
            sides = [pltpu.roll(side, s, 1) if s else side for s in (0, 4, 8, 12, 16)]
            hw, pw, qw, bw, mw = (
                jnp.concatenate([v, t], axis=1) for v, t in zip((h, p, q, bed[k], m), sides)
            )
            lefts, rights = [], []
            for w in (hw, qw, pw):
                slope = w - back(w)
                half = half_slope(slope, ahead(slope))
                lefts.append(w + half)
                rights.append(ahead(w - half))
            faces = face_flux(lefts, rights, mw * ahead(mw))
            dgy = [(f - back(f))[:, :cols] for f in faces]
            bed_y = (ahead(bw) - back(bw))[:, :cols]
            bed_x = bed[k + 1] - bed[k - 1]
            pull = (0.5 * ratio * gravity) * h
            depth = h - m * (dfx[0] + dgy[0])
            for tile in range(tiles):
                nds[pl.ds(tile * rows + k, SUB, stride=steps), :] = depth[:, tile * LANES : (tile + 1) * LANES]
            px = m * (p - dfx[1] - dgy[2] - pull * bed_x)
            py = m * (q - dfx[2] - dgy[1] - pull * bed_y)
            inverse = 1.0 / h
            square = inverse * inverse
            here = slice(k * SUB, (k + 1) * SUB)
            invh_ref[here, :] = inverse
            rx_ref[here, :] = px * (inv_cx * square)
            dy = inv_cy * square
            dperm[here, :] = dy
            rperm[here, :] = py * dy
        face_before = face
    writes = tile_writes(nds, nd_ref, out_sems)
    for write in writes:
        write.start()

    def dx_at(k):
        inverse = invh_ref[k * SUB : (k + 1) * SUB, :]
        return inv_cx * (inverse * inverse)

    def rx_at(k):
        return rx_ref[k * SUB : (k + 1) * SUB, :]

    seg_x = march_segments(steps, dx_at, rx_at)
    ends, levels = tree(seg_x)
    for i, v in enumerate(seg_x[:2] + (seg_x[3],)):
        segx_ref[i] = v
    for i, weights in enumerate(levels):
        for j, v in enumerate(weights):
            levx_ref[3 * i + j] = v
    for i, v in enumerate(ends):
        endx_ref[i : i + 1, :] = v[0:1, :]
    endx_ref[5:8, :] = jnp.zeros((3, cols), jnp.float32)

    for tile in range(tiles):
        span = slice(tile * LANES, (tile + 1) * LANES)
        dyt_ref[span, :] = dperm[:, span].T
        ryt_ref[span, :] = rperm[:, span].T

    def gathered(ref, k):
        return jnp.concatenate(
            [ref[pl.ds(tile * LANES + k, SUB, stride=LANES // SUB), :] for tile in range(cols // LANES)]
        )

    seg_y = march_segments(LANES // SUB, lambda k: gathered(dyt_ref, k), lambda k: gathered(ryt_ref, k))
    ends, levels = tree(seg_y)
    for i, v in enumerate(seg_y[:2] + (seg_y[3],)):
        segy_ref[i] = v
    for i, weights in enumerate(levels):
        for j, v in enumerate(weights):
            levy_ref[3 * i + j] = v
    for i, v in enumerate(ends):
        endy_ref[i : i + 1, :] = v[0:1, :]
    endy_ref[5:8, :] = jnp.zeros((3, rows), jnp.float32)
    for write in writes:
        write.wait()


def log2(count):
    return (count - 1).bit_length()


def fluxes(h, p, q, b, m, slabs, inv_cx, inv_cy):
    rows, cols = h.shape
    segs = cols // LANES * SUB
    shapes = [
        (rows, cols),
        (rows, cols),
        (rows, cols),
        (cols, rows),
        (cols, rows),
        (3, SUB, cols),
        (3 * log2(SUB), SUB, cols),
        (3, segs, rows),
        (3 * log2(segs), segs, rows),
        (SUB, cols),
        (SUB, rows),
    ]
    return pl.pallas_call(
        functools.partial(flux_kernel, inv_cx=inv_cx, inv_cy=inv_cy),
        out_shape=tuple(jax.ShapeDtypeStruct(s, jnp.float32) for s in shapes),
        in_specs=[ANY] * 5 + [VMEM] * 4,
        out_specs=(ANY,) + (VMEM,) * (len(shapes) - 1),
        scratch_shapes=[
            *[pltpu.VMEM((cols // LANES * rows, LANES), v.dtype) for v in (h, p, q, b, m, h)],
            pltpu.VMEM((LANES, rows), jnp.float32),
            pltpu.VMEM((rows, LANES), jnp.float32),
            pltpu.VMEM((rows, cols), jnp.float32),
            pltpu.VMEM((rows, cols), jnp.float32),
            pltpu.SemaphoreType.DMA((5 * (cols // LANES),)),
            pltpu.SemaphoreType.DMA((cols // LANES,)),
        ],
        compiler_params=PARAMS,
        name="fluxes",
    )(h, p, q, b, m, *slabs)


def ordered(axis, stage, mine, theirs):
    is_low = (lax.axis_index(axis) >> stage) % 2 == 0
    rows = range(5)
    one = tuple(jnp.where(is_low, mine[i : i + 1, :], theirs[i : i + 1, :]) for i in rows)
    two = tuple(jnp.where(is_low, theirs[i : i + 1, :], mine[i : i + 1, :]) for i in rows)
    return is_low, merge(one, two)


def merge_kernel(*refs, axes, stage):
    count = len(axes)
    for axis, mine, theirs, out in zip(axes, refs[:count], refs[count : 2 * count], refs[2 * count :]):
        _, (merged, _) = ordered(axis, stage, mine, theirs)
        for i, v in enumerate(merged):
            out[i : i + 1, :] = v
        out[5:8, :] = jnp.zeros((3, out.shape[1]), jnp.float32)


def merge_call(axes, stage, mine, theirs):
    count = len(axes)
    return pl.pallas_call(
        functools.partial(merge_kernel, axes=axes, stage=stage),
        out_shape=tuple(jax.ShapeDtypeStruct(v.shape, v.dtype) for v in mine),
        in_specs=[VMEM] * (2 * count),
        out_specs=(VMEM,) * count,
        compiler_params=PARAMS,
        name="merge",
    )(*mine, *theirs)


def line_ends(axis, pairs):
    steps = []
    merged = None
    for stage, (mine, theirs) in enumerate(pairs):
        is_low, (merged, weights) = ordered(axis, stage, mine, theirs)
        steps.append((is_low, weights))
    t, _, gr, _, sr = merged
    left = jnp.zeros_like(t)
    right = sr / (t + gr + 1.0)
    for is_low, (w1, w2, source) in reversed(steps):
        middle = w1 * left + w2 * right + source
        left = jnp.where(is_low, left, middle)
        right = jnp.where(is_low, middle, right)
    return left, right


def segment_ends(left, right, lev_ref):
    shape = lev_ref.shape[1:]
    count = shape[0]
    at = row_index(shape)
    left = jnp.broadcast_to(left, shape)
    right = jnp.broadcast_to(right, shape)
    for level in reversed(range(log2(count))):
        stride = 1 << level
        middle = lev_ref[3 * level] * left + lev_ref[3 * level + 1] * right + lev_ref[3 * level + 2]
        upper = (at >> level) % 2 == 1
        left, right = (
            jnp.where(upper, pltpu.roll(middle, stride, 0), left),
            jnp.where(upper, pltpu.roll(right, stride, 0), middle),
        )
    return left, right


def solve_kernel(*refs, stages_x, stages_y, inv_cx):
    (invh_ref, rx_ref, dyt_ref, ryt_ref, segx_ref, levx_ref, segy_ref, levy_ref), refs = refs[:8], refs[8:]
    pairs_x, refs = refs[: 2 * stages_x], refs[2 * stages_x :]
    pairs_y, refs = refs[: 2 * stages_y], refs[2 * stages_y :]
    vx_ref, vy_ref, v_t, vxs, vys, sems_x, sems_y = refs
    rows, cols = vx_ref.shape
    steps = rows // SUB
    tiles = cols // LANES
    left, right = line_ends("gx", list(zip(pairs_x[0::2], pairs_x[1::2])))
    left, right = segment_ends(left, right, levx_ref)
    value = left
    change = segx_ref[0] * (right - left) - segx_ref[1] * left - segx_ref[2]
    for k in range(steps):
        here = slice(k * SUB, (k + 1) * SUB)
        inverse = invh_ref[here, :]
        value = value + change
        change = change + ((inv_cx * (inverse * inverse)) * value - rx_ref[here, :])
        speed = value * inverse
        for tile in range(tiles):
            vxs[pl.ds(tile * rows + k, SUB, stride=steps), :] = speed[:, tile * LANES : (tile + 1) * LANES]
    writes = tile_writes(vxs, vx_ref, sems_x)
    for write in writes:
        write.start()

    left, right = line_ends("gy", list(zip(pairs_y[0::2], pairs_y[1::2])))
    left, right = segment_ends(left, right, levy_ref)
    value = left
    change = segy_ref[0] * (right - left) - segy_ref[1] * left - segy_ref[2]
    jump = LANES // SUB
    for k in range(jump):
        spots = [pl.ds(tile * LANES + k, SUB, stride=jump) for tile in range(cols // LANES)]
        d = jnp.concatenate([dyt_ref[s, :] for s in spots])
        r = jnp.concatenate([ryt_ref[s, :] for s in spots])
        value = value + change
        change = change + (d * value - r)
        for tile, s in enumerate(spots):
            v_t[s, :] = value[tile * SUB : (tile + 1) * SUB, :]
    for tile, write in enumerate(tile_writes(vys, vy_ref, sems_y)):
        span = slice(tile * LANES, (tile + 1) * LANES)
        block = v_t[span, :].T * invh_ref[:, span]
        for k in range(steps):
            vys[pl.ds(tile * rows + k, SUB, stride=steps), :] = block[k * SUB : (k + 1) * SUB, :]
        write.start()
        writes.append(write)
    for write in writes:
        write.wait()


def solve(pieces, pairs_x, pairs_y, shape, inv_cx):
    rows, cols = shape
    flat_x = [v for pair in pairs_x for v in pair]
    flat_y = [v for pair in pairs_y for v in pair]
    out = jax.ShapeDtypeStruct(shape, jnp.float32)
    return pl.pallas_call(
        functools.partial(solve_kernel, stages_x=len(pairs_x), stages_y=len(pairs_y), inv_cx=inv_cx),
        out_shape=(out, out),
        in_specs=[VMEM] * (len(pieces) + len(flat_x) + len(flat_y)),
        out_specs=(ANY, ANY),
        scratch_shapes=[
            pltpu.VMEM((cols, rows), jnp.float32),
            pltpu.VMEM((cols // LANES * rows, LANES), jnp.float32),
            pltpu.VMEM((cols // LANES * rows, LANES), jnp.float32),
            pltpu.SemaphoreType.DMA((cols // LANES,)),
            pltpu.SemaphoreType.DMA((cols // LANES,)),
        ],
        compiler_params=PARAMS,
        name="solve",
    )(*pieces, *flat_x, *flat_y)


def swap(value, axis, offset):
    count = lax.axis_size(axis)
    other = [((i - offset) ^ 1) + offset for i in range(count)]
    return lax.ppermute(value, axis, [(i, o if 0 <= o < count else i) for i, o in enumerate(other)])


def cross(value, axis, stage):
    return lax.ppermute(value, axis, [(i, i ^ (1 << stage)) for i in range(lax.axis_size(axis))])


def on_device(h, p, q, b, m):
    rows, cols = h.shape
    count_x, count_y = lax.axis_size("gx"), lax.axis_size("gy")
    inv_cx = 3.0 / (rows * count_x / 4.0) ** 2
    inv_cy = 3.0 / (cols * count_y / 4.0) ** 2
    xa, xb, ya, yb = pack(h, p, q, b, m)
    slabs = (swap(xa, "gx", 0), swap(xb, "gx", 1), swap(ya, "gy", 0), swap(yb, "gy", 1))
    new_depth, *pieces, end_x, end_y = fluxes(h, p, q, b, m, slabs, inv_cx, inv_cy)
    stages = {"gx": log2(count_x), "gy": log2(count_y)}
    mine = {"gx": end_x, "gy": end_y}
    pairs = {"gx": [], "gy": []}
    for stage in range(max(stages.values())):
        axes = [a for a in ("gx", "gy") if stage < stages[a]]
        theirs = {a: cross(mine[a], a, stage) for a in axes}
        for a in axes:
            pairs[a].append((mine[a], theirs[a]))
        more = [a for a in axes if stage + 1 < stages[a]]
        if more:
            merged = merge_call(more, stage, [mine[a] for a in more], [theirs[a] for a in more])
            mine.update(zip(more, merged))
    vx, vy = solve(pieces, pairs["gx"], pairs["gy"], (rows, cols), inv_cx)
    return new_depth, vx, vy


def solution(mesh):
    spec = P("gx", "gy")
    return jax.shard_map(
        on_device,
        mesh=mesh,
        in_specs=(spec,) * 5,
        out_specs=(spec,) * 3,
        check_vma=False,
    )
```

time: 92.3 us -> 42 us (0.46)
  blocking collectives: 40.6 us -> 0 us
  other arithmetic: 27.6 us -> 0 us
  Pallas kernels: 0 us -> 12 us
  starting transfers between devices: 8.74 us -> 19.2 us
  local copies, waits for them, and re-layouts: 8.04 us -> 4.74 us
    all_gather x2 -> x0, blocking collectives: 40.6 us -> none  [the longest x1 31.2 us: interface_x(): whole = lax.all_gather(packed, 'gx', axis=1, tiled=True)]
    mul x39 -> x0, other arithmetic: 12.9 us -> none  [the longest x5 6.07 us: face_terms(): opened * (0.5 * (flux_a + flux_b) - 0.5 * fastest * (state_b - state_a))]
    pallas_call x0 -> x5, Pallas kernels: none -> 12 us  [the longest x1 9.91 us: fluxes(): pl.pallas_call(functools.partial(flux_kernel, inv_cx=inv_cx, inv_cy=inv_c...]
    ppermute x4 -> x9, starting transfers between devices: 8.74 us -> 19.2 us  [the longest x5 14.8 us: cross(): lax.ppermute(value, axis, [(i, i ^ 1 << stage) for i in range(lax.axis_si...]
    sub x39 -> x0, other arithmetic: 8.71 us -> none  [the longest x21 4.98 us: eliminate(): right - left_factor * below[3] - right_factor * above[3]]
    div x6 -> x0, other arithmetic: 2.63 us -> none  [the longest x2 2.39 us: on_device(): return (new_depth, flux_u / depth, flux_v / depth)]
    add x6 -> x0, other arithmetic: 1.93 us -> none  [the longest x2 1.28 us: assemble(): inner = solved[0] + solved[1] * prev_wide + solved[2] * own_wide]
    slice x12 -> x0, local copies, waits for them, and re-layouts: 1.36 us -> none  [the longest x2 0.69 us: local_spikes(): sep_right = lax.index_in_dim(right, count - 1, which, keepdims=False)]
  transfers between devices with their start and end apart: 4 -> 9, of which waited for: 2 -> 4; matrix products, arithmetic and copies ran while one was open for 3% -> 0% of each run, Pallas kernels for 0% -> 0%
where the time goes in v1:
time: 42 us; the launch traced here: 41.7 us
  starting transfers between devices  19.2 us (46%)
  Pallas kernels  12 us (29%)
  waiting for transfers between devices  5.07 us (12%)
  local copies, waits for them, and re-layouts  4.74 us (11%)
  between operations  0.71 us (2%)
    ppermute x5, starting transfers between devices, cross(): lax.ppermute(value, axis, [(i, i ^ 1 << stage) for i in range(lax.axis_si...  14.8 us
    pallas_call x1, Pallas kernels, fluxes(): pl.pallas_call(functools.partial(flux_kernel, inv_cx=inv_cx, inv_cy=inv_c...  9.91 us
    unnamed x10, local copies, waits for them, and re-layouts  4.74 us
    ppermute x5, waiting for transfers between devices, cross(): lax.ppermute(value, axis, [(i, i ^ 1 << stage) for i in range(lax.axis_si...  4.57 us
    ppermute x4, starting transfers between devices, swap(): lax.ppermute(value, axis, [(i, o if 0 <= o < count else i) for i, o in en...  4.39 us
    pallas_call x1, Pallas kernels, solve(): pl.pallas_call(functools.partial(solve_kernel, stages_x=len(pairs_x), sta...  1.25 us
  transfers between devices with their start and end apart: 9, of which 4 were waited for; matrix products, arithmetic and copies ran while one was open for 0% of the time, Pallas kernels for 0%

profile of v1, /device:TPU:0, one launch (start us, length us, event | category | flops | bytes accessed | tf_op | source)
XLA Modules:
  0.0 41.7 jit_solution(898272342469973176)
XLA Ops:
  0.6 0.0 copy-start
  0.6 0.9 %copy-done = f32[128,512]{1,0:T(8,128)S(1)} copy-done((f32[128,512]{1,0:T(8,128)S(1)}, f32[128,512]{1,0:T(8,128)}, u32[]{:S(2)}) %copy-start) | copy-done | bytes 262168
  1.6 0.0 copy-start.1
  1.6 0.9 %copy-done.1 = f32[128,512]{1,0:T(8,128)S(1)} copy-done((f32[128,512]{1,0:T(8,128)S(1)}, f32[128,512]{1,0:T(8,128)}, u32[]{:S(2)}) %copy-start.1) | copy-done | bytes 262168
  2.5 0.0 copy-start.2
  2.5 0.9 %copy-done.2 = f32[128,512]{1,0:T(8,128)S(1)} copy-done((f32[128,512]{1,0:T(8,128)S(1)}, f32[128,512]{1,0:T(8,128)}, u32[]{:S(2)}) %copy-start.2) | copy-done | bytes 262168
  3.5 0.0 copy-start.3
  3.5 0.9 %copy-done.3 = f32[128,512]{1,0:T(8,128)S(1)} copy-done((f32[128,512]{1,0:T(8,128)S(1)}, f32[128,512]{1,0:T(8,128)}, u32[]{:S(2)}) %copy-start.3) | copy-done | bytes 262168
  4.4 0.0 copy-start.4
  4.4 0.9 %copy-done.4 = s32[128,512]{1,0:T(8,128)S(1)} copy-done((s32[128,512]{1,0:T(8,128)S(1)}, s32[128,512]{1,0:T(8,128)}, u32[]{:S(2)}) %copy-start.4) | copy-done | bytes 262168
  5.4 0.8 %pack.1 = (f32[8,512]{1,0:T(8,128)S(1)}, f32[8,512]{1,0:T(8,128)S(1)}, f32[8,128]{1,0:T(8,128)S(1)}, f32[8,128]{1,0:T(8,128)S(1)}) custom-call(f32[128,512]{1,0:T(8,128)S(1)} %copy-done, f32[128,512]{1,0:T(8,128)S(1)} %copy-done.1, f32[128,512]{1,0:T(8,128)S(1)} %copy-done.2, f32[128,512]{1,0:T(8,128)S(1)} %copy-done.3, s32[128,512]{1,0:T(8,128)S(1)} %copy-done.4), custom_call_target="tpu_custom_call" | custom-call | tf_op jit(solution)/shard_map/pack/pallas_call | solution.py:81
  6.2 3.0 %collective-permute-start = (f32[8,512]{1,0:T(8,128)S(1)}, f32[8,512]{1,0:T(8,128)S(1)}, u32[]{:S(2)}, u32[]{:S(2)}) collective-permute-start(f32[8,512]{1,0:T(8,128)S(1)} %get-tuple-element.22), channel_id=1, source_target_pairs={{0,4},{4,0},{8,12},{12,8},{16,20},{20,16},{24,28},{28,24},{1,5},{5... | collective-permute-start | bytes 49160 | tf_op jit(solution)/shard_map/ppermute | solution.py:518
  9.2 0.7 %collective-permute-start.1 = (f32[8,512]{1,0:T(8,128)S(1)}, f32[8,512]{1,0:T(8,128)S(1)}, u32[]{:S(2)}, u32[]{:S(2)}) collective-permute-start(f32[8,512]{1,0:T(8,128)S(1)} %get-tuple-element.23), channel_id=1, source_target_pairs={{0,0},{4,8},{8,4},{12,16},{16,12},{20,24},{24,20},{28,28},{1,1},{5... | collective-permute-start | bytes 49160 | tf_op jit(solution)/shard_map/ppermute | solution.py:518
  9.8 0.1 collective-permute-start.2
  9.9 0.7 %collective-permute-start.3 = (f32[8,128]{1,0:T(8,128)S(1)}, f32[8,128]{1,0:T(8,128)S(1)}, u32[]{:S(2)}, u32[]{:S(2)}) collective-permute-start(f32[8,128]{1,0:T(8,128)S(1)} %get-tuple-element.25), channel_id=1, source_target_pairs={{0,0},{1,2},{2,1},{3,3},{4,4},{5,6},{6,5},{7,7},{8,8},{9,10},{10,9... | collective-permute-start | bytes 12296 | tf_op jit(solution)/shard_map/ppermute | solution.py:518
  10.6 0.5 %collective-permute-done.2.ya = f32[8,128]{1,0:T(8,128)S(1)} collective-permute-done((f32[8,128]{1,0:T(8,128)S(1)}, f32[8,128]{1,0:T(8,128)S(1)}, u32[]{:S(2)}, u32[]{:S(2)}) %collective-permute-start.2) | collective-permute-done | bytes 4128 | tf_op jit(solution)/shard_map/ppermute | solution.py:518
  11.1 0.0 collective-permute-done.3.yb
  11.1 0.0 collective-permute-done.xa
  11.1 0.0 collective-permute-done.1.xb
  11.1 9.9 %fluxes.1 = (f32[128,512]{1,0:T(8,128)}, f32[128,512]{1,0:T(8,128)S(1)}, f32[128,512]{1,0:T(8,128)S(1)}, f32[512,128]{1,0:T(8,128)S(1)}, f32[512,128]{1,0:T(8,12...) custom-call(f32[128,512]{1,0:T(8,128)S(1)} %copy-done, ...), custom_call_target="tpu_custom_call" | custom-call | tf_op jit(solution)/shard_map/fluxes/pallas_call | solution.py:364
  21.0 4.8 %collective-permute-start.4 = (f32[8,512]{1,0:T(8,128)S(1)}, f32[8,512]{1,0:T(8,128)S(1)}, u32[]{:S(2)}, u32[]{:S(2)}) collective-permute-start(f32[8,512]{1,0:T(8,128)S(1)} %get-tuple-element.35.refs_0_.refs_8_), channel_id=1, source_target_pairs={{0,4},{4,0},{8,12},{12,8},{16,20},{20,16},{24,28},{28,24},{1,5},{5... | collective-permute-start | bytes 49160 | tf_op jit(solution)/shard_map/ppermute | solution.py:522
  25.8 3.5 %collective-permute-start.5 = (f32[8,128]{1,0:T(8,128)S(1)}, f32[8,128]{1,0:T(8,128)S(1)}, u32[]{:S(2)}, u32[]{:S(2)}) collective-permute-start(f32[8,128]{1,0:T(8,128)S(1)} %get-tuple-element.36.refs_1_.refs_14_), channel_id=1, source_target_pairs={{0,1},{1,0},{2,3},{3,2},{4,5},{5,4},{6,7},{7,6},{8,9},{9,8},{10,11... | collective-permute-start | bytes 12296 | tf_op jit(solution)/shard_map/ppermute | solution.py:522
  29.3 0.8 %collective-permute-done.5.refs_3_.refs_15_ = f32[8,128]{1,0:T(8,128)S(1)} collective-permute-done((f32[8,128]{1,0:T(8,128)S(1)}, f32[8,128]{1,0:T(8,128)S(1)}, u32[]{:S(2)}, u32[]{:S(2)}) %collective-permute-start.5) | collective-permute-done | bytes 4128 | tf_op jit(solution)/shard_map/ppermute | solution.py:522
  30.1 0.0 collective-permute-done.4.refs_2_.refs_9_
  30.2 1.6 %collective-permute-start.6 = (f32[8,512]{1,0:T(8,128)S(1)}, f32[8,512]{1,0:T(8,128)S(1)}, u32[]{:S(2)}, u32[]{:S(2)}) collective-permute-start(f32[8,512]{1,0:T(8,128)S(1)} %get-tuple-element.37.refs_0_.refs_10_), channel_id=1, source_target_pairs={{0,8},{4,12},{8,0},{12,4},{16,24},{20,28},{24,16},{28,20},{1,9},{5... | collective-permute-start | bytes 49160 | tf_op jit(solution)/shard_map/ppermute | solution.py:522
  31.8 2.2 %collective-permute-done.6.refs_1_.refs_11_ = f32[8,512]{1,0:T(8,128)S(1)} collective-permute-done((f32[8,512]{1,0:T(8,128)S(1)}, f32[8,512]{1,0:T(8,128)S(1)}, u32[]{:S(2)}, u32[]{:S(2)}) %collective-permute-start.6) | collective-permute-done | bytes 16416 | tf_op jit(solution)/shard_map/ppermute | solution.py:522
  34.0 2.7 %collective-permute-start.7 = (f32[8,512]{1,0:T(8,128)S(1)}, f32[8,512]{1,0:T(8,128)S(1)}, u32[]{:S(2)}, u32[]{:S(2)}) collective-permute-start(f32[8,512]{1,0:T(8,128)S(1)} %merge.3.refs_12_), channel_id=1, source_target_pairs={{0,16},{4,20},{8,24},{12,28},{16,0},{20,4},{24,8},{28,12},{1,17},{... | collective-permute-start | bytes 49160 | tf_op jit(solution)/shard_map/ppermute | solution.py:522
  36.6 2.2 %collective-permute-start.8 = (f32[8,128]{1,0:T(8,128)S(1)}, f32[8,128]{1,0:T(8,128)S(1)}, u32[]{:S(2)}, u32[]{:S(2)}) collective-permute-start(f32[8,128]{1,0:T(8,128)S(1)} %get-tuple-element.38.refs_16_), channel_id=1, source_target_pairs={{0,2},{1,3},{2,0},{3,1},{4,6},{5,7},{6,4},{7,5},{8,10},{9,11},{10,... | collective-permute-start | bytes 12296 | tf_op jit(solution)/shard_map/ppermute | solution.py:522
  38.9 1.6 %collective-permute-done.8.refs_17_ = f32[8,128]{1,0:T(8,128)S(1)} collective-permute-done((f32[8,128]{1,0:T(8,128)S(1)}, f32[8,128]{1,0:T(8,128)S(1)}, u32[]{:S(2)}, u32[]{:S(2)}) %collective-permute-start.8) | collective-permute-done | bytes 4128 | tf_op jit(solution)/shard_map/ppermute | solution.py:522
  40.4 0.0 collective-permute-done.7.refs_13_
  40.4 1.2 %solve.1 = (f32[128,512]{1,0:T(8,128)}, f32[128,512]{1,0:T(8,128)}) custom-call(f32[128,512]{1,0:T(8,128)S(1)} %get-tuple-element.27.refs_0_, f32[128,512]{1,0:T(8,128)S(1)} %get-tuple-element.28.refs_1_, f32[512,128]{1,0:T(8,128)S(1)} %get-tuple-element.29.refs_2_, f32[512,128]{1,0:T(8,128)S(1)} %get-tuple-element.30.refs_3_, ...), custom_call_target="tpu_custom_call" | custom-call | tf_op jit(solution)/shard_map/solve/pallas_call | solution.py:498
  (2 shorter events, 0.0 us)
Async XLA Ops:
  0.6 1.0 %copy-start = (f32[128,512]{1,0:T(8,128)S(1)}, f32[128,512]{1,0:T(8,128)}, u32[]{:S(2)}) copy-start(f32[128,512]{1,0:T(8,128)} %h_ref.1) | copy-start | bytes 786436
  1.6 0.9 %copy-start.1 = (f32[128,512]{1,0:T(8,128)S(1)}, f32[128,512]{1,0:T(8,128)}, u32[]{:S(2)}) copy-start(f32[128,512]{1,0:T(8,128)} %p_ref.1) | copy-start | bytes 786436
  2.5 0.9 %copy-start.2 = (f32[128,512]{1,0:T(8,128)S(1)}, f32[128,512]{1,0:T(8,128)}, u32[]{:S(2)}) copy-start(f32[128,512]{1,0:T(8,128)} %q_ref.1) | copy-start | bytes 786436
  3.5 0.9 %copy-start.3 = (f32[128,512]{1,0:T(8,128)S(1)}, f32[128,512]{1,0:T(8,128)}, u32[]{:S(2)}) copy-start(f32[128,512]{1,0:T(8,128)} %b_ref.1) | copy-start | bytes 786436
  4.4 0.9 %copy-start.4 = (s32[128,512]{1,0:T(8,128)S(1)}, s32[128,512]{1,0:T(8,128)}, u32[]{:S(2)}) copy-start(s32[128,512]{1,0:T(8,128)} %m_ref.1) | copy-start | bytes 786436
  6.2 4.9 %collective-permute-start = (f32[8,512]{1,0:T(8,128)S(1)}, f32[8,512]{1,0:T(8,128)S(1)}, u32[]{:S(2)}, u32[]{:S(2)}) collective-permute-start(f32[8,512]{1,0:T(8,128)S(1)} %get-tuple-element.22), channel_id=1, source_target_pairs={{0,4},{4,0},{8,12},{12,8},{16,20},{20,16},{24,28},{28,24},{1,5},{5... | collective-permute-start | bytes 49160 | tf_op jit(solution)/shard_map/ppermute | solution.py:518
  9.2 1.9 %collective-permute-start.1 = (f32[8,512]{1,0:T(8,128)S(1)}, f32[8,512]{1,0:T(8,128)S(1)}, u32[]{:S(2)}, u32[]{:S(2)}) collective-permute-start(f32[8,512]{1,0:T(8,128)S(1)} %get-tuple-element.23), channel_id=1, source_target_pairs={{0,0},{4,8},{8,4},{12,16},{16,12},{20,24},{24,20},{28,28},{1,1},{5... | collective-permute-start | bytes 49160 | tf_op jit(solution)/shard_map/ppermute | solution.py:518
  9.8 1.2 %collective-permute-start.2 = (f32[8,128]{1,0:T(8,128)S(1)}, f32[8,128]{1,0:T(8,128)S(1)}, u32[]{:S(2)}, u32[]{:S(2)}) collective-permute-start(f32[8,128]{1,0:T(8,128)S(1)} %get-tuple-element.24), channel_id=1, source_target_pairs={{0,1},{1,0},{2,3},{3,2},{4,5},{5,4},{6,7},{7,6},{8,9},{9,8},{10,11... | collective-permute-start | bytes 12296 | tf_op jit(solution)/shard_map/ppermute | solution.py:518
  9.9 1.2 %collective-permute-start.3 = (f32[8,128]{1,0:T(8,128)S(1)}, f32[8,128]{1,0:T(8,128)S(1)}, u32[]{:S(2)}, u32[]{:S(2)}) collective-permute-start(f32[8,128]{1,0:T(8,128)S(1)} %get-tuple-element.25), channel_id=1, source_target_pairs={{0,0},{1,2},{2,1},{3,3},{4,4},{5,6},{6,5},{7,7},{8,8},{9,10},{10,9... | collective-permute-start | bytes 12296 | tf_op jit(solution)/shard_map/ppermute | solution.py:518
  21.0 9.1 %collective-permute-start.4 = (f32[8,512]{1,0:T(8,128)S(1)}, f32[8,512]{1,0:T(8,128)S(1)}, u32[]{:S(2)}, u32[]{:S(2)}) collective-permute-start(f32[8,512]{1,0:T(8,128)S(1)} %get-tuple-element.35.refs_0_.refs_8_), channel_id=1, source_target_pairs={{0,4},{4,0},{8,12},{12,8},{16,20},{20,16},{24,28},{28,24},{1,5},{5... | collective-permute-start | bytes 49160 | tf_op jit(solution)/shard_map/ppermute | solution.py:522
  25.8 4.3 %collective-permute-start.5 = (f32[8,128]{1,0:T(8,128)S(1)}, f32[8,128]{1,0:T(8,128)S(1)}, u32[]{:S(2)}, u32[]{:S(2)}) collective-permute-start(f32[8,128]{1,0:T(8,128)S(1)} %get-tuple-element.36.refs_1_.refs_14_), channel_id=1, source_target_pairs={{0,1},{1,0},{2,3},{3,2},{4,5},{5,4},{6,7},{7,6},{8,9},{9,8},{10,11... | collective-permute-start | bytes 12296 | tf_op jit(solution)/shard_map/ppermute | solution.py:522
  30.2 3.8 %collective-permute-start.6 = (f32[8,512]{1,0:T(8,128)S(1)}, f32[8,512]{1,0:T(8,128)S(1)}, u32[]{:S(2)}, u32[]{:S(2)}) collective-permute-start(f32[8,512]{1,0:T(8,128)S(1)} %get-tuple-element.37.refs_0_.refs_10_), channel_id=1, source_target_pairs={{0,8},{4,12},{8,0},{12,4},{16,24},{20,28},{24,16},{28,20},{1,9},{5... | collective-permute-start | bytes 49160 | tf_op jit(solution)/shard_map/ppermute | solution.py:522
  34.0 6.4 %collective-permute-start.7 = (f32[8,512]{1,0:T(8,128)S(1)}, f32[8,512]{1,0:T(8,128)S(1)}, u32[]{:S(2)}, u32[]{:S(2)}) collective-permute-start(f32[8,512]{1,0:T(8,128)S(1)} %merge.3.refs_12_), channel_id=1, source_target_pairs={{0,16},{4,20},{8,24},{12,28},{16,0},{20,4},{24,8},{28,12},{1,17},{... | collective-permute-start | bytes 49160 | tf_op jit(solution)/shard_map/ppermute | solution.py:522
  36.6 3.8 %collective-permute-start.8 = (f32[8,128]{1,0:T(8,128)S(1)}, f32[8,128]{1,0:T(8,128)S(1)}, u32[]{:S(2)}, u32[]{:S(2)}) collective-permute-start(f32[8,128]{1,0:T(8,128)S(1)} %get-tuple-element.38.refs_16_), channel_id=1, source_target_pairs={{0,2},{1,3},{2,0},{3,1},{4,6},{5,7},{6,4},{7,5},{8,10},{9,11},{10,... | collective-permute-start | bytes 12296 | tf_op jit(solution)/shard_map/ppermute | solution.py:522

commit v2 on v1

--- a/solution.py
+++ b/solution.py
@@ -13,6 +13,7 @@
 SUB = 8
 VMEM = pl.BlockSpec(memory_space=pltpu.VMEM)
 ANY = pl.BlockSpec(memory_space=pl.ANY)
+HBM = pl.BlockSpec(memory_space=pltpu.HBM)
 PARAMS = pltpu.CompilerParams(vmem_limit_bytes=24 * 1024 * 1024)
 
 
@@ -24,7 +25,7 @@
     return lax.broadcasted_iota(jnp.int32, shape, len(shape) - 2)
 
 
-def pack_kernel(h, p, q, b, m, xa, xb, ya, yb, top, bottom, left, right, itop, ibottom, ileft, iright, sems):
+def pack_kernel(h, p, q, b, m, xa, ya, top, bottom, left, right, itop, ibottom, ileft, iright, sems):
     rows, cols = h.shape
     copies = []
     for f, src in enumerate((h, p, q, b, m)):
@@ -54,8 +55,8 @@
         ]
     )
     even_x = lax.axis_index("gx") % 2 == 0
-    xa[...] = jnp.where(even_x, last_x, first_x)
-    xb[...] = jnp.where(even_x, first_x, last_x)
+    xa[0] = jnp.where(even_x, last_x, first_x)
+    xa[1] = jnp.where(even_x, first_x, last_x)
     lane = lane_index((rows, LANES))
 
     def columns(block, imask, shifts):
@@ -69,20 +70,20 @@
     first_y = columns(left, ileft, (0, 2, 4, 6, 7))
     last_y = columns(right, iright, (2, 4, 6, 7, 8))
     even_y = lax.axis_index("gy") % 2 == 0
-    ya[...] = jnp.where(even_y, last_y, first_y)
-    yb[...] = jnp.where(even_y, first_y, last_y)
+    ya[0] = jnp.where(even_y, last_y, first_y)
+    ya[1] = jnp.where(even_y, first_y, last_y)
 
 
 def pack(h, p, q, b, m):
     rows, cols = h.shape
     f32, i32 = jnp.float32, jnp.int32
-    slab_x = jax.ShapeDtypeStruct((SUB, cols), f32)
-    slab_y = jax.ShapeDtypeStruct((SUB, rows), f32)
+    slab_x = jax.ShapeDtypeStruct((2, SUB, cols), f32)
+    slab_y = jax.ShapeDtypeStruct((2, SUB, rows), f32)
     return pl.pallas_call(
         pack_kernel,
-        out_shape=(slab_x, slab_x, slab_y, slab_y),
-        in_specs=[ANY] * 5,
-        out_specs=(VMEM,) * 4,
+        out_shape=(slab_x, slab_y),
+        in_specs=[HBM] * 5,
+        out_specs=(VMEM,) * 2,
         scratch_shapes=[
             pltpu.VMEM((4, SUB, cols), f32),
             pltpu.VMEM((4, SUB, cols), f32),
@@ -364,7 +365,7 @@
     return pl.pallas_call(
         functools.partial(flux_kernel, inv_cx=inv_cx, inv_cy=inv_cy),
         out_shape=tuple(jax.ShapeDtypeStruct(s, jnp.float32) for s in shapes),
-        in_specs=[ANY] * 5 + [VMEM] * 4,
+        in_specs=[HBM] * 5 + [VMEM] * 4,
         out_specs=(ANY,) + (VMEM,) * (len(shapes) - 1),
         scratch_shapes=[
             *[pltpu.VMEM((cols // LANES * rows, LANES), v.dtype) for v in (h, p, q, b, m, h)],
@@ -407,6 +408,36 @@
         compiler_params=PARAMS,
         name="merge",
     )(*mine, *theirs)
+
+
+def group_ends(group, left, right, place):
+    if len(group) == 1:
+        return left, right
+    levels = [group]
+    weights = []
+    while len(levels[-1]) > 1:
+        both = [merge(a, b) for a, b in zip(levels[-1][0::2], levels[-1][1::2])]
+        levels.append([v for v, _ in both])
+        weights.append([w for _, w in both])
+    t, _, gr, _, sr = levels[-1][0]
+    right = sr / (t + gr + 1.0)
+    for depth in reversed(range(len(weights))):
+        chosen = weights[depth][0]
+        for n, other in enumerate(weights[depth][1:], 1):
+            here = (place >> (depth + 1)) == n
+            chosen = tuple(jnp.where(here, b, a) for a, b in zip(chosen, other))
+        middle = chosen[0] * left + chosen[1] * right + chosen[2]
+        lower = (place >> depth) % 2 == 0
+        left, right = jnp.where(lower, left, middle), jnp.where(lower, middle, right)
+    return left, right
+
+
+def line_ends_x(mine, theirs, rest):
+    is_low, (merged, (w1, w2, source)) = ordered("gx", 0, mine, theirs)
+    group = [tuple(rest[n, i : i + 1, :] for i in range(5)) for n in range(rest.shape[0])]
+    left, right = group_ends(group, jnp.zeros_like(w1), None, lax.axis_index("gx") // 2)
+    middle = w1 * left + w2 * right + source
+    return jnp.where(is_low, left, middle), jnp.where(is_low, middle, right)
 
 
 def line_ends(axis, pairs):
@@ -442,15 +473,15 @@
     return left, right
 
 
-def solve_kernel(*refs, stages_x, stages_y, inv_cx):
+def solve_kernel(*refs, stages_y, inv_cx):
     (invh_ref, rx_ref, dyt_ref, ryt_ref, segx_ref, levx_ref, segy_ref, levy_ref), refs = refs[:8], refs[8:]
-    pairs_x, refs = refs[: 2 * stages_x], refs[2 * stages_x :]
+    pairs_x, refs = refs[:3], refs[3:]
     pairs_y, refs = refs[: 2 * stages_y], refs[2 * stages_y :]
     vx_ref, vy_ref, v_t, vxs, vys, sems_x, sems_y = refs
     rows, cols = vx_ref.shape
     steps = rows // SUB
     tiles = cols // LANES
-    left, right = line_ends("gx", list(zip(pairs_x[0::2], pairs_x[1::2])))
+    left, right = line_ends_x(*pairs_x)
     left, right = segment_ends(left, right, levx_ref)
     value = left
     change = segx_ref[0] * (right - left) - segx_ref[1] * left - segx_ref[2]
@@ -492,11 +523,11 @@
 
 def solve(pieces, pairs_x, pairs_y, shape, inv_cx):
     rows, cols = shape
-    flat_x = [v for pair in pairs_x for v in pair]
+    flat_x = list(pairs_x)
     flat_y = [v for pair in pairs_y for v in pair]
     out = jax.ShapeDtypeStruct(shape, jnp.float32)
     return pl.pallas_call(
-        functools.partial(solve_kernel, stages_x=len(pairs_x), stages_y=len(pairs_y), inv_cx=inv_cx),
+        functools.partial(solve_kernel, stages_y=len(pairs_y), inv_cx=inv_cx),
         out_shape=(out, out),
         in_specs=[VMEM] * (len(pieces) + len(flat_x) + len(flat_y)),
         out_specs=(ANY, ANY),
@@ -512,10 +543,17 @@
     )(*pieces, *flat_x, *flat_y)
 
 
-def swap(value, axis, offset):
+def hand_on(value, axis):
     count = lax.axis_size(axis)
-    other = [((i - offset) ^ 1) + offset for i in range(count)]
-    return lax.ppermute(value, axis, [(i, o if 0 <= o < count else i) for i, o in enumerate(other)])
+    far = [i + 2 if i % 2 == 0 else i - 2 for i in range(count)]
+    return lax.ppermute(value, axis, [(i, t if 0 <= t < count else i ^ 1) for i, t in enumerate(far)])
+
+
+def spread(value, axis):
+    count = lax.axis_size(axis)
+    groups = [list(range(parity, count, 2)) for parity in (0, 1)]
+    copies = jnp.broadcast_to(value[None], (count // 2, *value.shape))
+    return lax.all_to_all(copies, axis, 0, 0, axis_index_groups=groups)
 
 
 def cross(value, axis, stage):
@@ -527,22 +565,19 @@
     count_x, count_y = lax.axis_size("gx"), lax.axis_size("gy")
     inv_cx = 3.0 / (rows * count_x / 4.0) ** 2
     inv_cy = 3.0 / (cols * count_y / 4.0) ** 2
-    xa, xb, ya, yb = pack(h, p, q, b, m)
-    slabs = (swap(xa, "gx", 0), swap(xb, "gx", 1), swap(ya, "gy", 0), swap(yb, "gy", 1))
+    xa, ya = pack(h, p, q, b, m)
+    near_x, near_y = cross(xa, "gx", 0), cross(ya, "gy", 0)
+    slabs = (near_x[0], hand_on(near_x[1], "gx"), near_y[0], hand_on(near_y[1], "gy"))
     new_depth, *pieces, end_x, end_y = fluxes(h, p, q, b, m, slabs, inv_cx, inv_cy)
-    stages = {"gx": log2(count_x), "gy": log2(count_y)}
-    mine = {"gx": end_x, "gy": end_y}
-    pairs = {"gx": [], "gy": []}
-    for stage in range(max(stages.values())):
-        axes = [a for a in ("gx", "gy") if stage < stages[a]]
-        theirs = {a: cross(mine[a], a, stage) for a in axes}
-        for a in axes:
-            pairs[a].append((mine[a], theirs[a]))
-        more = [a for a in axes if stage + 1 < stages[a]]
-        if more:
-            merged = merge_call(more, stage, [mine[a] for a in more], [theirs[a] for a in more])
-            mine.update(zip(more, merged))
-    vx, vy = solve(pieces, pairs["gx"], pairs["gy"], (rows, cols), inv_cx)
+    their_x, their_y = cross(end_x, "gx", 0), cross(end_y, "gy", 0)
+    pairs_y = [(end_y, their_y)]
+    pair_x, pair_y = merge_call(("gx", "gy"), 0, [end_x, end_y], [their_x, their_y])
+    rest = spread(pair_x, "gx")
+    for stage in range(1, log2(count_y)):
+        if stage > 1:
+            (pair_y,) = merge_call(("gy",), stage - 1, [pairs_y[-1][0]], [pairs_y[-1][1]])
+        pairs_y.append((pair_y, cross(pair_y, "gy", stage)))
+    vx, vy = solve(pieces, (end_x, their_x, rest), pairs_y, (rows, cols), inv_cx)
     return new_depth, vx, vy
 
 

time: 42 us -> 42.6 us (1.014)
  starting transfers between devices: 19.2 us -> 14.6 us
  waiting for transfers between devices: 5.07 us -> 9.63 us
  local copies, waits for them, and re-layouts: 4.74 us -> 5.38 us
    ppermute x5, starting transfers between devices: 14.8 us -> 6.15 us  [cross(): lax.ppermute(value, axis, [(i, i ^ 1 << stage) for i in range(lax.axis_si...]
    all_to_all x0 -> x1, starting transfers between devices: none -> 4.79 us  [spread(): return lax.all_to_all(copies, axis, 0, 0, axis_index_groups=groups)]
    all_to_all x0 -> x1, waiting for transfers between devices: none -> 1.88 us  [spread(): return lax.all_to_all(copies, axis, 0, 0, axis_index_groups=groups)]
    ppermute x5, waiting for transfers between devices: 4.57 us -> 6.42 us  [cross(): lax.ppermute(value, axis, [(i, i ^ 1 << stage) for i in range(lax.axis_si...]
    ppermute x4 -> x2, waiting for transfers between devices: 0.49 us -> 1.33 us  [hand_on(): lax.ppermute(value, axis, [(i, t if 0 <= t < count else i ^ 1) for i, t i...]
    ppermute x4 -> x2, starting transfers between devices: 4.39 us -> 3.63 us  [hand_on(): lax.ppermute(value, axis, [(i, t if 0 <= t < count else i ^ 1) for i, t i...]
    broadcast_in_dim x0 -> x1, local copies, waits for them, and re-layouts: none -> 0.63 us  [spread(): copies = jnp.broadcast_to(value[None], (count // 2, *value.shape))]
  transfers between devices with their start and end apart: 9 -> 8, of which waited for: 4 -> 6; matrix products, arithmetic and copies ran while one was open for 0% -> 0% of each run, Pallas kernels for 0% -> 0%
where the time goes in v2:
time: 42.6 us; the launch traced here: 42.2 us
  starting transfers between devices  14.6 us (34%)
  Pallas kernels  11.9 us (28%)
  waiting for transfers between devices  9.63 us (23%)
  local copies, waits for them, and re-layouts  5.38 us (13%)
  between operations  0.68 us (2%)
    pallas_call x1, Pallas kernels, fluxes(): pl.pallas_call(functools.partial(flux_kernel, inv_cx=inv_cx, inv_cy=inv_c...  9.89 us
    ppermute x5, waiting for transfers between devices, cross(): lax.ppermute(value, axis, [(i, i ^ 1 << stage) for i in range(lax.axis_si...  6.42 us
    ppermute x5, starting transfers between devices, cross(): lax.ppermute(value, axis, [(i, i ^ 1 << stage) for i in range(lax.axis_si...  6.15 us
    all_to_all x1, starting transfers between devices, spread(): return lax.all_to_all(copies, axis, 0, 0, axis_index_groups=groups)  4.79 us
    unnamed x10, local copies, waits for them, and re-layouts  4.74 us
    ppermute x2, starting transfers between devices, hand_on(): lax.ppermute(value, axis, [(i, t if 0 <= t < count else i ^ 1) for i, t i...  3.63 us
    all_to_all x1, waiting for transfers between devices, spread(): return lax.all_to_all(copies, axis, 0, 0, axis_index_groups=groups)  1.88 us
    ppermute x2, waiting for transfers between devices, hand_on(): lax.ppermute(value, axis, [(i, t if 0 <= t < count else i ^ 1) for i, t i...  1.33 us
  transfers between devices with their start and end apart: 8, of which 6 were waited for; matrix products, arithmetic and copies ran while one was open for 0% of the time, Pallas kernels for 0%

profile of v2, /device:TPU:0, one launch (start us, length us, event | category | flops | bytes accessed | tf_op | source)
XLA Modules:
  0.0 42.2 jit_solution(9475504232005205459)
XLA Ops:
  0.6 0.0 copy-start
  0.6 0.9 %copy-done = f32[128,512]{1,0:T(8,128)S(1)} copy-done((f32[128,512]{1,0:T(8,128)S(1)}, f32[128,512]{1,0:T(8,128)}, u32[]{:S(2)}) %copy-start) | copy-done | bytes 262168
  1.6 0.0 copy-start.1
  1.6 0.9 %copy-done.1 = f32[128,512]{1,0:T(8,128)S(1)} copy-done((f32[128,512]{1,0:T(8,128)S(1)}, f32[128,512]{1,0:T(8,128)}, u32[]{:S(2)}) %copy-start.1) | copy-done | bytes 262168
  2.5 0.0 copy-start.2
  2.5 0.9 %copy-done.2 = f32[128,512]{1,0:T(8,128)S(1)} copy-done((f32[128,512]{1,0:T(8,128)S(1)}, f32[128,512]{1,0:T(8,128)}, u32[]{:S(2)}) %copy-start.2) | copy-done | bytes 262168
  3.5 0.0 copy-start.3
  3.5 0.9 %copy-done.3 = f32[128,512]{1,0:T(8,128)S(1)} copy-done((f32[128,512]{1,0:T(8,128)S(1)}, f32[128,512]{1,0:T(8,128)}, u32[]{:S(2)}) %copy-start.3) | copy-done | bytes 262168
  4.4 0.0 copy-start.4
  4.4 0.9 %copy-done.4 = s32[128,512]{1,0:T(8,128)S(1)} copy-done((s32[128,512]{1,0:T(8,128)S(1)}, s32[128,512]{1,0:T(8,128)}, u32[]{:S(2)}) %copy-start.4) | copy-done | bytes 262168
  5.4 0.8 %pack.1 = (f32[2,8,512]{2,1,0:T(8,128)S(1)}, f32[2,8,128]{2,1,0:T(8,128)S(1)}) custom-call(f32[128,512]{1,0:T(8,128)S(1)} %copy-done, f32[128,512]{1,0:T(8,128)S(1)} %copy-done.1, f32[128,512]{1,0:T(8,128)S(1)} %copy-done.2, f32[128,512]{1,0:T(8,128)S(1)} %copy-done.3, s32[128,512]{1,0:T(8,128)S(1)} %copy-done.4), custom_call_target="tpu_custom_call" | custom-call | tf_op jit(solution)/shard_map/pack/pallas_call | solution.py:82
  6.2 3.0 %collective-permute-start = (f32[2,8,512]{2,1,0:T(8,128)S(1)}, f32[2,8,512]{2,1,0:T(8,128)S(1)}, u32[]{:S(2)}, u32[]{:S(2)}) collective-permute-start(f32[2,8,512]{2,1,0:T(8,128)S(1)} %get-tuple-element.20), channel_id=1, source_target_pairs={{0,4},{4,0},{8,12},{12,8},{16,20},{20,16},{24,28},{28,24},{1,5},{5... | collective-permute-start | bytes 98312 | tf_op jit(solution)/shard_map/ppermute | solution.py:560
  9.2 0.0 collective-permute-start.2
  9.2 1.9 %collective-permute-done = f32[2,8,512]{2,1,0:T(8,128)S(1)} collective-permute-done((f32[2,8,512]{2,1,0:T(8,128)S(1)}, f32[2,8,512]{2,1,0:T(8,128)S(1)}, u32[]{:S(2)}, u32[]{:S(2)}) %collective-permute-start) | collective-permute-done | bytes 32800 | tf_op jit(solution)/shard_map/ppermute | solution.py:560
  11.1 2.1 %collective-permute-start.1 = (f32[8,512]{1,0:T(8,128)S(1)}, f32[8,512]{1,0:T(8,128)S(1)}, u32[]{:S(2)}, u32[]{:S(2)}) collective-permute-start(f32[8,512]{1,0:T(8,128)S(1)} %get-tuple-element.37), channel_id=1, source_target_pairs={{0,8},{4,0},{8,16},{12,4},{16,24},{20,12},{24,28},{28,20},{1,9},{5... | collective-permute-start | bytes 49160 | tf_op jit(solution)/shard_map/ppermute | solution.py:549
  13.2 0.0 collective-permute-done.2
  13.2 1.5 %collective-permute-start.3 = (f32[8,128]{1,0:T(8,128)S(1)}, f32[8,128]{1,0:T(8,128)S(1)}, u32[]{:S(2)}, u32[]{:S(2)}) collective-permute-start(f32[8,128]{1,0:T(8,128)S(1)} %get-tuple-element.39), channel_id=1, source_target_pairs={{0,2},{1,0},{2,3},{3,1},{4,6},{5,4},{6,7},{7,5},{8,10},{9,8},{10,1... | collective-permute-start | bytes 12296 | tf_op jit(solution)/shard_map/ppermute | solution.py:549
  14.7 1.3 %collective-permute-done.3.yb = f32[8,128]{1,0:T(8,128)S(1)} collective-permute-done((f32[8,128]{1,0:T(8,128)S(1)}, f32[8,128]{1,0:T(8,128)S(1)}, u32[]{:S(2)}, u32[]{:S(2)}) %collective-permute-start.3) | collective-permute-done | bytes 4128 | tf_op jit(solution)/shard_map/ppermute | solution.py:549
  16.0 0.0 collective-permute-done.1.xb
  16.0 9.9 %fluxes.1 = (f32[128,512]{1,0:T(8,128)}, f32[128,512]{1,0:T(8,128)S(1)}, f32[128,512]{1,0:T(8,128)S(1)}, f32[512,128]{1,0:T(8,128)S(1)}, f32[512,128]{1,0:T(8,12...) custom-call(f32[128,512]{1,0:T(8,128)S(1)} %copy-done, ...), custom_call_target="tpu_custom_call" | custom-call | tf_op jit(solution)/shard_map/fluxes/pallas_call | solution.py:365
  25.9 0.9 %collective-permute-start.4 = (f32[8,512]{1,0:T(8,128)S(1)}, f32[8,512]{1,0:T(8,128)S(1)}, u32[]{:S(2)}, u32[]{:S(2)}) collective-permute-start(f32[8,512]{1,0:T(8,128)S(1)} %get-tuple-element.31.refs_0_.refs_8_), channel_id=1, source_target_pairs={{0,4},{4,0},{8,12},{12,8},{16,20},{20,16},{24,28},{28,24},{1,5},{5... | collective-permute-start | bytes 49160 | tf_op jit(solution)/shard_map/ppermute | solution.py:560
  26.8 0.0 collective-permute-start.5
  26.8 1.2 %collective-permute-done.5.refs_3_.refs_12_ = f32[8,128]{1,0:T(8,128)S(1)} collective-permute-done((f32[8,128]{1,0:T(8,128)S(1)}, f32[8,128]{1,0:T(8,128)S(1)}, u32[]{:S(2)}, u32[]{:S(2)}) %collective-permute-start.5) | collective-permute-done | bytes 4128 | tf_op jit(solution)/shard_map/ppermute | solution.py:560
  28.0 1.8 %collective-permute-done.4.refs_2_.refs_9_ = f32[8,512]{1,0:T(8,128)S(1)} collective-permute-done((f32[8,512]{1,0:T(8,128)S(1)}, f32[8,512]{1,0:T(8,128)S(1)}, u32[]{:S(2)}, u32[]{:S(2)}) %collective-permute-start.4) | collective-permute-done | bytes 16416 | tf_op jit(solution)/shard_map/ppermute | solution.py:560
  29.8 0.6 %broadcast_in_dim.2 = f32[4,8,512]{2,1,0:T(8,128)} broadcast(f32[8,512]{1,0:T(8,128)S(1)} %get-tuple-element.33), dimensions={1,2} | broadcast | bytes 81920 | tf_op jit(solution)/shard_map/broadcast_in_dim | solution.py:555
  30.4 4.8 %all-to-all-start = ((f32[4,8,512]{2,1,0:T(8,128)}), f32[4,8,512]{2,1,0:T(8,128)S(1)}, u32[]{:S(2)}, u32[]{:S(2)}) async-start(f32[4,8,512]{2,1,0:T(8,128)} %broadcast_in_dim.2), calls=%async_computation | async-start | bytes 131072 | tf_op jit(solution)/shard_map/all_to_all | solution.py:556
  35.2 2.3 %collective-permute-start.6 = (f32[8,128]{1,0:T(8,128)S(1)}, f32[8,128]{1,0:T(8,128)S(1)}, u32[]{:S(2)}, u32[]{:S(2)}) collective-permute-start(f32[8,128]{1,0:T(8,128)S(1)} %get-tuple-element.34.refs_13_), channel_id=1, source_target_pairs={{0,2},{1,3},{2,0},{3,1},{4,6},{5,7},{6,4},{7,5},{8,10},{9,11},{10,... | collective-permute-start | bytes 12296 | tf_op jit(solution)/shard_map/ppermute | solution.py:560
  37.5 1.6 %collective-permute-done.6.refs_14_ = f32[8,128]{1,0:T(8,128)S(1)} collective-permute-done((f32[8,128]{1,0:T(8,128)S(1)}, f32[8,128]{1,0:T(8,128)S(1)}, u32[]{:S(2)}, u32[]{:S(2)}) %collective-permute-start.6) | collective-permute-done | bytes 4128 | tf_op jit(solution)/shard_map/ppermute | solution.py:560
  39.1 1.9 %all-to-all-done.refs_10_ = f32[4,8,512]{2,1,0:T(8,128)S(1)} async-done(((f32[4,8,512]{2,1,0:T(8,128)}), f32[4,8,512]{2,1,0:T(8,128)S(1)}, u32[]{:S(2)}, u32[]{:S(2)}) %all-to-all-start) | async-done | bytes 65568 | tf_op jit(solution)/shard_map/all_to_all | solution.py:556
  40.9 1.3 %solve.1 = (f32[128,512]{1,0:T(8,128)}, f32[128,512]{1,0:T(8,128)}) custom-call(f32[128,512]{1,0:T(8,128)S(1)} %get-tuple-element.23.refs_0_, f32[128,512]{1,0:T(8,128)S(1)} %get-tuple-element.24.refs_1_, f32[512,128]{1,0:T(8,128)S(1)} %get-tuple-element.25.refs_2_, f32[512,128]{1,0:T(8,128)S(1)} %get-tuple-element.26.refs_3_, ...), custom_call_target="tpu_custom_call" | custom-call | tf_op jit(solution)/shard_map/solve/pallas_call | solution.py:529
  (3 shorter events, 0.0 us)
Async XLA Ops:
  0.6 1.0 %copy-start = (f32[128,512]{1,0:T(8,128)S(1)}, f32[128,512]{1,0:T(8,128)}, u32[]{:S(2)}) copy-start(f32[128,512]{1,0:T(8,128)} %h_ref.1) | copy-start | bytes 786436
  1.6 0.9 %copy-start.1 = (f32[128,512]{1,0:T(8,128)S(1)}, f32[128,512]{1,0:T(8,128)}, u32[]{:S(2)}) copy-start(f32[128,512]{1,0:T(8,128)} %p_ref.1) | copy-start | bytes 786436
  2.5 0.9 %copy-start.2 = (f32[128,512]{1,0:T(8,128)S(1)}, f32[128,512]{1,0:T(8,128)}, u32[]{:S(2)}) copy-start(f32[128,512]{1,0:T(8,128)} %q_ref.1) | copy-start | bytes 786436
  3.5 0.9 %copy-start.3 = (f32[128,512]{1,0:T(8,128)S(1)}, f32[128,512]{1,0:T(8,128)}, u32[]{:S(2)}) copy-start(f32[128,512]{1,0:T(8,128)} %b_ref.1) | copy-start | bytes 786436
  4.4 0.9 %copy-start.4 = (s32[128,512]{1,0:T(8,128)S(1)}, s32[128,512]{1,0:T(8,128)}, u32[]{:S(2)}) copy-start(s32[128,512]{1,0:T(8,128)} %m_ref.1) | copy-start | bytes 786436
  6.2 4.9 %collective-permute-start = (f32[2,8,512]{2,1,0:T(8,128)S(1)}, f32[2,8,512]{2,1,0:T(8,128)S(1)}, u32[]{:S(2)}, u32[]{:S(2)}) collective-permute-start(f32[2,8,512]{2,1,0:T(8,128)S(1)} %get-tuple-element.20), channel_id=1, source_target_pairs={{0,4},{4,0},{8,12},{12,8},{16,20},{20,16},{24,28},{28,24},{1,5},{5... | collective-permute-start | bytes 98312 | tf_op jit(solution)/shard_map/ppermute | solution.py:560
  9.2 4.0 %collective-permute-start.2 = (f32[2,8,128]{2,1,0:T(8,128)S(1)}, f32[2,8,128]{2,1,0:T(8,128)S(1)}, u32[]{:S(2)}, u32[]{:S(2)}) collective-permute-start(f32[2,8,128]{2,1,0:T(8,128)S(1)} %get-tuple-element.21), channel_id=1, source_target_pairs={{0,1},{1,0},{2,3},{3,2},{4,5},{5,4},{6,7},{7,6},{8,9},{9,8},{10,11... | collective-permute-start | bytes 24584 | tf_op jit(solution)/shard_map/ppermute | solution.py:560
  11.1 5.0 %collective-permute-start.1 = (f32[8,512]{1,0:T(8,128)S(1)}, f32[8,512]{1,0:T(8,128)S(1)}, u32[]{:S(2)}, u32[]{:S(2)}) collective-permute-start(f32[8,512]{1,0:T(8,128)S(1)} %get-tuple-element.37), channel_id=1, source_target_pairs={{0,8},{4,0},{8,16},{12,4},{16,24},{20,12},{24,28},{28,20},{1,9},{5... | collective-permute-start | bytes 49160 | tf_op jit(solution)/shard_map/ppermute | solution.py:549
  13.2 2.8 %collective-permute-start.3 = (f32[8,128]{1,0:T(8,128)S(1)}, f32[8,128]{1,0:T(8,128)S(1)}, u32[]{:S(2)}, u32[]{:S(2)}) collective-permute-start(f32[8,128]{1,0:T(8,128)S(1)} %get-tuple-element.39), channel_id=1, source_target_pairs={{0,2},{1,0},{2,3},{3,1},{4,6},{5,4},{6,7},{7,5},{8,10},{9,8},{10,1... | collective-permute-start | bytes 12296 | tf_op jit(solution)/shard_map/ppermute | solution.py:549
  25.9 3.8 %collective-permute-start.4 = (f32[8,512]{1,0:T(8,128)S(1)}, f32[8,512]{1,0:T(8,128)S(1)}, u32[]{:S(2)}, u32[]{:S(2)}) collective-permute-start(f32[8,512]{1,0:T(8,128)S(1)} %get-tuple-element.31.refs_0_.refs_8_), channel_id=1, source_target_pairs={{0,4},{4,0},{8,12},{12,8},{16,20},{20,16},{24,28},{28,24},{1,5},{5... | collective-permute-start | bytes 49160 | tf_op jit(solution)/shard_map/ppermute | solution.py:560
  26.8 1.2 %collective-permute-start.5 = (f32[8,128]{1,0:T(8,128)S(1)}, f32[8,128]{1,0:T(8,128)S(1)}, u32[]{:S(2)}, u32[]{:S(2)}) collective-permute-start(f32[8,128]{1,0:T(8,128)S(1)} %get-tuple-element.32.refs_1_.refs_11_), channel_id=1, source_target_pairs={{0,1},{1,0},{2,3},{3,2},{4,5},{5,4},{6,7},{7,6},{8,9},{9,8},{10,11... | collective-permute-start | bytes 12296 | tf_op jit(solution)/shard_map/ppermute | solution.py:560
  30.4 10.5 %all-to-all-start = ((f32[4,8,512]{2,1,0:T(8,128)}), f32[4,8,512]{2,1,0:T(8,128)S(1)}, u32[]{:S(2)}, u32[]{:S(2)}) async-start(f32[4,8,512]{2,1,0:T(8,128)} %broadcast_in_dim.2), calls=%async_computation | async-start | bytes 131072 | tf_op jit(solution)/shard_map/all_to_all | solution.py:556
  35.2 3.9 %collective-permute-start.6 = (f32[8,128]{1,0:T(8,128)S(1)}, f32[8,128]{1,0:T(8,128)S(1)}, u32[]{:S(2)}, u32[]{:S(2)}) collective-permute-start(f32[8,128]{1,0:T(8,128)S(1)} %get-tuple-element.34.refs_13_), channel_id=1, source_target_pairs={{0,2},{1,3},{2,0},{3,1},{4,6},{5,7},{6,4},{7,5},{8,10},{9,11},{10,... | collective-permute-start | bytes 12296 | tf_op jit(solution)/shard_map/ppermute | solution.py:560

commit v3 on v1

v3 whole, which is shorter than its diff:
```python
import functools

import jax
import jax.numpy as jnp
from jax import lax
from jax.experimental import pallas as pl
from jax.experimental.pallas import tpu as pltpu
from jax.sharding import PartitionSpec as P

gravity = 9.81
ratio = 0.05
LANES = 128
SUB = 8
STEPS = LANES // SUB
F32 = jnp.float32
VMEM = pl.BlockSpec(memory_space=pltpu.VMEM)
HBM = pl.BlockSpec(memory_space=pltpu.HBM)
ANY = pl.BlockSpec(memory_space=pl.ANY)
PARAMS = pltpu.CompilerParams(vmem_limit_bytes=16 * 1024 * 1024)
WHOLE = pltpu.CompilerParams(vmem_limit_bytes=62 * 1024 * 1024)


def lane_index(shape):
    return lax.broadcasted_iota(jnp.int32, shape, len(shape) - 1)


def row_index(shape):
    return lax.broadcasted_iota(jnp.int32, shape, len(shape) - 2)


def at(tile, step):
    first = tile * LANES + step * SUB
    return slice(first, first + SUB)


def tile_span(tile):
    return slice(tile * LANES, (tile + 1) * LANES)


def spread_rows(tile, step):
    return pl.ds(tile * LANES + step, SUB, stride=STEPS)


def shape(*dims):
    return jax.ShapeDtypeStruct(dims, F32)


def pack_kernel(h, p, q, b, m, xa, ya, top, bottom, left, right, itop, ibottom, ileft, iright, sems):
    rows, cols = h.shape
    copies = []
    for f, src in enumerate((h, p, q, b, m)):
        floats = f < 4
        spots = (
            (src.at[pl.ds(0, SUB), :], top.at[f] if floats else itop),
            (src.at[pl.ds(rows - SUB, SUB), :], bottom.at[f] if floats else ibottom),
            (src.at[:, pl.ds(0, LANES)], left.at[f] if floats else ileft),
            (src.at[:, pl.ds(cols - LANES, LANES)], right.at[f] if floats else iright),
        )
        for g, (piece, target) in enumerate(spots):
            copy = pltpu.make_async_copy(piece, target, sems.at[4 * f + g])
            copy.start()
            copies.append(copy)
    for copy in copies:
        copy.wait()
    first_x = jnp.concatenate(
        [top[0, 0:2, :], top[1, 0:2, :], top[2, 0:2, :], top[3, 0:1, :], itop[0:1, :].astype(F32)]
    )
    last_x = jnp.concatenate(
        [
            bottom[0, SUB - 2 : SUB, :],
            bottom[1, SUB - 2 : SUB, :],
            bottom[2, SUB - 2 : SUB, :],
            bottom[3, SUB - 1 : SUB, :],
            ibottom[SUB - 1 : SUB, :].astype(F32),
        ]
    )
    even_x = lax.axis_index("gx") % 2 == 0
    xa[0] = jnp.where(even_x, last_x, first_x)
    xa[1] = jnp.where(even_x, first_x, last_x)
    lane = lane_index((rows, LANES))

    def columns(block, imask, shifts):
        def stacked(ref):
            return jnp.concatenate([ref[spread_rows(0, k), :] for k in range(STEPS)])

        fields = [stacked(block.at[f]) for f in range(4)] + [stacked(imask).astype(F32)]
        moved = [pltpu.roll(v, s, 1) if s else v for v, s in zip(fields, shifts)]
        out = moved[0]
        for start, v in zip((2, 4, 6, 7), moved[1:]):
            out = jnp.where(lane >= start, v, out)
        return out.T[0:SUB, :]

    first_y = columns(left, ileft, (0, 2, 4, 6, 7))
    last_y = columns(right, iright, (2, 4, 6, 7, 8))
    even_y = lax.axis_index("gy") % 2 == 0
    ya[0] = jnp.where(even_y, last_y, first_y)
    ya[1] = jnp.where(even_y, first_y, last_y)


def pack(h, p, q, b, m):
    rows, cols = h.shape
    i32 = jnp.int32
    return pl.pallas_call(
        pack_kernel,
        out_shape=(shape(2, SUB, cols), shape(2, SUB, rows)),
        in_specs=[HBM] * 5,
        out_specs=(VMEM,) * 2,
        scratch_shapes=[
            pltpu.VMEM((4, SUB, cols), F32),
            pltpu.VMEM((4, SUB, cols), F32),
            pltpu.VMEM((4, rows, LANES), F32),
            pltpu.VMEM((4, rows, LANES), F32),
            pltpu.VMEM((SUB, cols), i32),
            pltpu.VMEM((SUB, cols), i32),
            pltpu.VMEM((rows, LANES), i32),
            pltpu.VMEM((rows, LANES), i32),
            pltpu.SemaphoreType.DMA((20,)),
        ],
        compiler_params=WHOLE,
        name="pack",
    )(h, p, q, b, m)


def merge_coefficients(one, two):
    t1, gl1, gr1 = one
    t2, gl2, gr2 = two
    shunt = gr1 + gl2
    inverse = 1.0 / (t1 + t2 + shunt)
    w1, w2 = t1 * inverse, t2 * inverse
    return (w1 * t2, gl1 + w1 * shunt, gr2 + w2 * shunt), (w1, w2, inverse)


def merge_sources(one, two, weights):
    w1, w2, inverse = weights
    source = one[1] - two[0]
    return (one[0] - w1 * source, two[1] + w2 * source), source * inverse


def merge(one, two):
    coefficients, weights = merge_coefficients(one[:3], two[:3])
    sources, middle = merge_sources(one[3:], two[3:], weights)
    return coefficients + sources, weights[:2] + (middle,)


def log2(count):
    return (count - 1).bit_length()


def full(ref, step):
    return jnp.concatenate([ref[at(tile, step), :] for tile in range(ref.shape[0] // LANES)])


def march_depth(inv_ref, scale, out_t, out_w, levels):
    count = inv_ref.shape[0] // STEPS
    zero = jnp.zeros((count, LANES), F32)
    alpha, gamma, beta, delta = zero, zero, zero, zero
    for k in range(STEPS):
        inverse = full(inv_ref, k)
        d = scale * (inverse * inverse)
        alpha = alpha + gamma
        gamma = gamma + d * (1.0 + alpha)
        beta = beta + delta
        delta = delta + d * ((k + 1.0) + beta)
    t = 1.0 / (STEPS + beta)
    out_t[0] = t
    out_t[1] = t * alpha
    out_t[2] = 1.0 + delta
    coefficients = (t, t * alpha, t * delta)
    for level in range(levels):
        after = tuple(pltpu.roll(v, count - (1 << level), 0) for v in coefficients)
        coefficients, weights = merge_coefficients(coefficients, after)
        for j, v in enumerate(weights):
            out_w[3 * level + j] = v
    return coefficients


def prepare_kernel(
    h, p, q, b, m,
    hx, px, qx, bx, mx, ix, hy, py, qy, by, my, iy, tx, wx, ty, wy, endx, endy,
    hs, ps, qs, bs, ms, turned, sems,
    *, inv_cx, inv_cy,
):
    rows, cols = h.shape
    tiles = cols // LANES
    copies = []
    for f, (src, target) in enumerate(zip((h, p, q, b, m), (hs, ps, qs, bs, ms))):
        for tile in range(tiles):
            copies.append(
                pltpu.make_async_copy(
                    src.at[:, pl.ds(tile * LANES, LANES)],
                    target.at[pl.ds(tile * rows, rows), :],
                    sems.at[f * tiles + tile],
                )
            )
            copies[-1].start()
    for f, (src, xs, ys) in enumerate(
        ((hs, hx, hy), (ps, px, py), (qs, qx, qy), (bs, bx, by), (ms, mx, my))
    ):
        for tile in range(tiles):
            copies[f * tiles + tile].wait()
            for k in range(STEPS):
                xs[at(tile, k), :] = src[spread_rows(tile, k), :].astype(F32)
            turned[f % 2, tile_span(tile), :] = xs[tile_span(tile), :].T
            for k in range(STEPS):
                ys[at(tile, k), :] = turned[f % 2, spread_rows(tile, k), :]
        if f == 0:
            ix[...] = 1.0 / hx[...]
            iy[...] = 1.0 / hy[...]
            ends_x = march_depth(ix, inv_cx, tx, wx, log2(SUB))
            ends_y = march_depth(iy, inv_cy, ty, wy, log2(SUB * tiles))
            for i in range(3):
                for tile in range(tiles):
                    endx[i : i + 1, tile_span(tile)] = ends_x[i][tile * SUB : tile * SUB + 1, :]
                endy[i : i + 1, :] = ends_y[i][0:1, :]
            endx[3:8, :] = jnp.zeros((5, cols), F32)
            endy[3:8, :] = jnp.zeros((5, rows), F32)


def prepare(h, p, q, b, m, inv_cx, inv_cy):
    rows, cols = h.shape
    tiles = cols // LANES
    count = tiles * SUB
    stack = (tiles * LANES, LANES)
    shapes = [shape(*stack)] * 12 + [
        shape(3, count, LANES),
        shape(3 * log2(SUB), count, LANES),
        shape(3, count, LANES),
        shape(3 * log2(count), count, LANES),
        shape(SUB, cols),
        shape(SUB, rows),
    ]
    return pl.pallas_call(
        functools.partial(prepare_kernel, inv_cx=inv_cx, inv_cy=inv_cy),
        out_shape=tuple(shapes),
        in_specs=[HBM] * 5,
        out_specs=(VMEM,) * len(shapes),
        scratch_shapes=[
            *[pltpu.VMEM(stack, v.dtype) for v in (h, p, q, b, m)],
            pltpu.VMEM((2, *stack), F32),
            pltpu.SemaphoreType.DMA((5 * tiles,)),
        ],
        compiler_params=PARAMS,
        cost_estimate=pl.CostEstimate(flops=2_000_000, bytes_accessed=8_000_000, transcendentals=0),
        name="prepare",
    )(h, p, q, b, m)


def low_high(axis, near, far):
    index, count = lax.axis_index(axis), lax.axis_size(axis)
    even = index % 2 == 0
    low = jnp.where(index > 0, jnp.where(even, far, near), 0.0)
    high = jnp.where(index < count - 1, jnp.where(even, near, far), 0.0)
    return low, high


def half_slope(a, c):
    return 0.5 * (jnp.maximum(jnp.minimum(a, c), 0.0) + jnp.minimum(jnp.maximum(a, c), 0.0))


def face_flux(left, right, opened):
    is_open = opened > 0.5
    hl = jnp.where(is_open, left[0], 1.0)
    hr = jnp.where(is_open, right[0], 1.0)
    joint = 1.0 / (hl * hr)
    ul = left[1] * (hr * joint)
    ur = right[1] * (hl * joint)
    gl = gravity * hl
    gr = gravity * hr
    fastest = jnp.maximum(jnp.abs(ul) + gl * lax.rsqrt(gl), jnp.abs(ur) + gr * lax.rsqrt(gr))
    scale = (0.5 * ratio) * opened
    mass = (left[1] + right[1]) - fastest * (right[0] - left[0])
    push = 0.5 * (gl * hl + gr * hr) + left[1] * ul + right[1] * ur - fastest * (right[1] - left[1])
    shear = left[2] * ul + right[2] * ur - fastest * (right[2] - left[2])
    return scale * mass, scale * push, scale * shear


def extended(ref, tile, lows, highs):
    sub = row_index((SUB, LANES))
    out = {}
    for n, row in enumerate(lows, 1):
        value = ref[at(tile, STEPS - n), :]
        out[-n] = jnp.where(sub == 0, row, pltpu.roll(value, 1, 0))
    for n, row in enumerate(highs):
        value = ref[at(tile, n), :]
        out[STEPS + n] = jnp.where(sub == SUB - 1, row, pltpu.roll(value, SUB - 1, 0))
    return lambda k: out[k] if k in out else ref[at(tile, k), :]


def tile_fluxes(fields, bed, wet, store):
    def states(k):
        both = []
        for w in fields:
            here = w(k)
            both.append((here, half_slope(here - w(k - 1), w(k + 1) - here)))
        return [w + s for w, s in both], [w - s for w, s in both]

    left, _ = states(-1)
    before = None
    for k in range(-1, STEPS):
        left_next, right = states(k + 1)
        face = face_flux(left, right, wet(k) * wet(k + 1))
        left = left_next
        if k >= 0:
            store(k, [a - c for a, c in zip(face, before)], bed(k + 1) - bed(k - 1))
        before = face


def march_source(inv_ref, scale, r_ref, t_ref, w_ref, s_ref, levels):
    count = inv_ref.shape[0] // STEPS
    c = jnp.zeros((count, LANES), F32)
    e = c
    for k in range(STEPS):
        inverse = full(inv_ref, k)
        c = c + e
        e = e + (scale * (inverse * inverse) * c - full(r_ref, k))
    sl = t_ref[0] * c
    s_ref[0] = sl
    sources = (sl, t_ref[2] * sl - e)
    for level in range(levels):
        after = tuple(pltpu.roll(v, count - (1 << level), 0) for v in sources)
        sources, middle = merge_sources(sources, after, tuple(w_ref[3 * level + j] for j in range(3)))
        s_ref[1 + level] = middle
    return sources


def flux_kernel(
    near_x, far_x, near_y, far_y,
    hx, px, qx, bx, mx, ix, hy, py, qy, by, my, iy, tx, wx, ty, wy, coefx, coefy,
    depth, rx, ry, sx, sy, endx, endy,
    xpart, ypart, turned,
    *, inv_cx, inv_cy,
):
    tiles = hx.shape[0] // LANES
    low_x, high_x = low_high("gx", near_x[0], far_x[...])
    low_y, high_y = low_high("gy", near_y[0], far_y[...])

    for tile in range(tiles):
        span = tile_span(tile)

        def along_x(ref, row, layers):
            lows = [low_x[row + layers - 1 - n : row + layers - n, span] for n in range(layers)]
            highs = [high_x[row + n : row + n + 1, span] for n in range(layers)]
            return extended(ref, tile, lows, highs)

        def store_x(k, difference, bed):
            here = at(tile, k)
            for i in range(3):
                xpart[i, here, :] = difference[i]
            xpart[3, here, :] = bed

        tile_fluxes(
            [along_x(hx, 0, 2), along_x(px, 2, 2), along_x(qx, 4, 2)],
            along_x(bx, 6, 1), along_x(mx, 7, 1), store_x,
        )

        def along_y(ref, row, layers):
            lows, highs = [], []
            for n in range(layers):
                last = at(tile - 1, STEPS - 1 - n).stop - 1
                first = at(tile + 1, n).start
                lows.append(low_y[row + layers - 1 - n : row + layers - n, :] if tile == 0 else ref[last : last + 1, :])
                highs.append(high_y[row + n : row + n + 1, :] if tile == tiles - 1 else ref[first : first + 1, :])
            return extended(ref, tile, lows, highs)

        def store_y(k, difference, bed):
            here, natural = at(tile, k), spread_rows(tile, k)
            ypart[0, natural, :] = difference[0]
            ypart[1, here, :] = difference[1]
            ypart[2, natural, :] = difference[2]
            ypart[3, here, :] = bed

        tile_fluxes(
            [along_y(hy, 0, 2), along_y(qy, 4, 2), along_y(py, 2, 2)],
            along_y(by, 6, 1), along_y(my, 7, 1), store_y,
        )
        turned[span, :] = xpart[2, span, :].T
        from_y_mass = ypart[0, span, :].T
        from_y_shear = ypart[2, span, :].T
        h, m, inverse = hx[span, :], mx[span, :], ix[span, :]
        depth[span, :] = h - m * (xpart[0, span, :] + from_y_mass)
        push = px[span, :] - xpart[1, span, :] - from_y_shear - (0.5 * ratio * gravity) * h * xpart[3, span, :]
        rx[span, :] = (inv_cx * (inverse * inverse)) * m * push
        for k in range(STEPS):
            here = at(tile, k)
            inverse = iy[here, :]
            push = qy[here, :] - turned[spread_rows(tile, k), :] - ypart[1, here, :]
            push = push - (0.5 * ratio * gravity) * hy[here, :] * ypart[3, here, :]
            ry[here, :] = (inv_cy * (inverse * inverse)) * my[here, :] * push

    ends_x = march_source(ix, inv_cx, rx, tx, wx, sx, log2(SUB))
    ends_y = march_source(iy, inv_cy, ry, ty, wy, sy, log2(SUB * tiles))
    endx[...] = coefx[...]
    endy[...] = coefy[...]
    for i in range(2):
        for tile in range(tiles):
            endx[3 + i : 4 + i, tile_span(tile)] = ends_x[i][tile * SUB : tile * SUB + 1, :]
        endy[3 + i : 4 + i, :] = ends_y[i][0:1, :]


def fluxes(slabs, prepared, inv_cx, inv_cy):
    stack = prepared[0].shape
    count = stack[0] // STEPS
    shapes = (
        shape(*stack),
        shape(*stack),
        shape(*stack),
        shape(1 + log2(SUB), count, LANES),
        shape(1 + log2(count), count, LANES),
        shape(*prepared[-2].shape),
        shape(*prepared[-1].shape),
    )
    return pl.pallas_call(
        functools.partial(flux_kernel, inv_cx=inv_cx, inv_cy=inv_cy),
        out_shape=shapes,
        in_specs=[VMEM] * (len(slabs) + len(prepared)),
        out_specs=(VMEM,) * len(shapes),
        scratch_shapes=[
            pltpu.VMEM((4, *stack), F32),
            pltpu.VMEM((4, *stack), F32),
            pltpu.VMEM(stack, F32),
        ],
        compiler_params=PARAMS,
        name="fluxes",
    )(*slabs, *prepared)


def tile_write(tiled, whole, tile, sems):
    rows = whole.shape[0]
    return pltpu.make_async_copy(
        tiled.at[pl.ds(tile * rows, rows), :], whole.at[:, pl.ds(tile * LANES, LANES)], sems.at[tile]
    )


def write_scratch(cols):
    return [pltpu.VMEM((cols, LANES), F32), pltpu.SemaphoreType.DMA((cols // LANES,))]


def depth_kernel(depth, out, natural, sems):
    writes = []
    for tile in range(depth.shape[0] // LANES):
        for k in range(STEPS):
            natural[spread_rows(tile, k), :] = depth[at(tile, k), :]
        writes.append(tile_write(natural, out, tile, sems))
        writes[-1].start()
    for write in writes:
        write.wait()


def write_depth(depth, block):
    return pl.pallas_call(
        depth_kernel,
        out_shape=shape(*block),
        in_specs=[VMEM],
        out_specs=ANY,
        scratch_shapes=write_scratch(block[1]),
        compiler_params=PARAMS,
        cost_estimate=pl.CostEstimate(flops=100_000, bytes_accessed=2_000_000, transcendentals=0),
        name="write_depth",
    )(depth)


def ordered(axis, stage, mine, theirs):
    is_low = (lax.axis_index(axis) >> stage) % 2 == 0
    rows = range(5)
    one = tuple(jnp.where(is_low, mine[i : i + 1, :], theirs[i : i + 1, :]) for i in rows)
    two = tuple(jnp.where(is_low, theirs[i : i + 1, :], mine[i : i + 1, :]) for i in rows)
    return is_low, merge(one, two)


def merge_kernel(*refs, axes, stage):
    count = len(axes)
    for axis, mine, theirs, out in zip(axes, refs[:count], refs[count : 2 * count], refs[-count:]):
        _, (merged, _) = ordered(axis, stage, mine, theirs)
        for i, v in enumerate(merged):
            out[i : i + 1, :] = v
        out[5:8, :] = jnp.zeros((3, out.shape[1]), F32)


def merge_call(axes, stage, mine, theirs, also=()):
    count = len(axes)
    return pl.pallas_call(
        functools.partial(merge_kernel, axes=axes, stage=stage),
        out_shape=tuple(shape(*v.shape) for v in mine),
        in_specs=[VMEM] * (2 * count + len(also)),
        out_specs=(VMEM,) * count,
        compiler_params=PARAMS,
        name="merge",
    )(*mine, *theirs, *also)


def line_ends(axis, pairs):
    steps = []
    merged = None
    for stage, (mine, theirs) in enumerate(pairs):
        is_low, (merged, weights) = ordered(axis, stage, mine, theirs)
        steps.append((is_low, weights))
    t, _, gr, _, sr = merged
    left = jnp.zeros_like(t)
    right = sr / (t + gr + 1.0)
    for is_low, (w1, w2, source) in reversed(steps):
        middle = w1 * left + w2 * right + source
        left = jnp.where(is_low, left, middle)
        right = jnp.where(is_low, middle, right)
    return left, right


def segment_ends(left, right, w_ref, s_ref, levels):
    index = row_index(left.shape)
    for level in reversed(range(levels)):
        stride = 1 << level
        middle = w_ref[3 * level] * left + w_ref[3 * level + 1] * right + s_ref[1 + level]
        upper = (index >> level) % 2 == 1
        left, right = (
            jnp.where(upper, pltpu.roll(middle, stride, 0), left),
            jnp.where(upper, pltpu.roll(right, stride, 0), middle),
        )
    return left, right


def march_values(left, right, t_ref, s_ref, inv_ref, scale, r_ref, store):
    value = left
    change = t_ref[0] * (right - left) - t_ref[1] * left - s_ref[0]
    for k in range(STEPS):
        inverse = full(inv_ref, k)
        value = value + change
        change = change + (scale * (inverse * inverse) * value - full(r_ref, k))
        store(k, value * inverse)


def solve_x_kernel(inv_ref, r_ref, t_ref, w_ref, s_ref, *refs, scale):
    pairs, (out, natural, sems) = refs[:-3], refs[-3:]
    tiles = out.shape[1] // LANES
    ends = []
    for row in line_ends("gx", list(zip(pairs[0::2], pairs[1::2]))):
        ends.append(
            jnp.concatenate([jnp.broadcast_to(row[:, tile_span(t)], (SUB, LANES)) for t in range(tiles)])
        )
    left, right = segment_ends(*ends, w_ref, s_ref, log2(SUB))

    def store(k, speed):
        for tile in range(tiles):
            natural[spread_rows(tile, k), :] = speed[tile * SUB : (tile + 1) * SUB, :]

    march_values(left, right, t_ref, s_ref, inv_ref, scale, r_ref, store)
    writes = [tile_write(natural, out, tile, sems) for tile in range(tiles)]
    for write in writes:
        write.start()
    for write in writes:
        write.wait()


def solve_y_kernel(inv_ref, r_ref, t_ref, w_ref, s_ref, *refs, scale):
    pairs, (out, natural, sems, turned) = refs[:-4], refs[-4:]
    tiles = out.shape[1] // LANES
    ends = line_ends("gy", list(zip(pairs[0::2], pairs[1::2])))
    ends = [jnp.broadcast_to(row, (tiles * SUB, LANES)) for row in ends]
    left, right = segment_ends(*ends, w_ref, s_ref, log2(tiles * SUB))

    def store(k, speed):
        for tile in range(tiles):
            turned[spread_rows(tile, k), :] = speed[tile * SUB : (tile + 1) * SUB, :]

    march_values(left, right, t_ref, s_ref, inv_ref, scale, r_ref, store)
    writes = []
    for tile in range(tiles):
        block = turned[tile_span(tile), :].T
        for k in range(STEPS):
            natural[spread_rows(tile, k), :] = block[k * SUB : (k + 1) * SUB, :]
        writes.append(tile_write(natural, out, tile, sems))
        writes[-1].start()
    for write in writes:
        write.wait()


def solve(kernel, name, pieces, pairs, block, scale, extra=()):
    flat = [v for pair in pairs for v in pair]
    return pl.pallas_call(
        functools.partial(kernel, scale=scale),
        out_shape=shape(*block),
        in_specs=[VMEM] * (len(pieces) + len(flat)),
        out_specs=ANY,
        scratch_shapes=write_scratch(block[1]) + list(extra),
        compiler_params=PARAMS,
        cost_estimate=pl.CostEstimate(flops=1_000_000, bytes_accessed=4_000_000, transcendentals=0),
        name=name,
    )(*pieces, *flat)


def hand_on(value, axis):
    count = lax.axis_size(axis)
    far = [i + 2 if i % 2 == 0 else i - 2 for i in range(count)]
    return lax.ppermute(value, axis, [(i, t if 0 <= t < count else i ^ 1) for i, t in enumerate(far)])


def cross(value, axis, stage):
    return lax.ppermute(value, axis, [(i, i ^ (1 << stage)) for i in range(lax.axis_size(axis))])


def on_device(h, p, q, b, m):
    block = h.shape
    rows, cols = block
    count_x, count_y = lax.axis_size("gx"), lax.axis_size("gy")
    inv_cx = 3.0 / (rows * count_x / 4.0) ** 2
    inv_cy = 3.0 / (cols * count_y / 4.0) ** 2
    xa, ya = pack(h, p, q, b, m)
    near_x, near_y = cross(xa, "gx", 0), cross(ya, "gy", 0)
    slabs = (near_x, hand_on(near_x[1], "gx"), near_y, hand_on(near_y[1], "gy"))
    prepared = prepare(h, p, q, b, m, inv_cx, inv_cy)
    depth, rx, ry, sx, sy, end_x, end_y = fluxes(slabs, prepared, inv_cx, inv_cy)
    ix, iy = prepared[5], prepared[11]
    tx, wx, ty, wy = prepared[12:16]
    new_depth = write_depth(depth, block)
    stages = {"gx": log2(count_x), "gy": log2(count_y)}
    mine = {"gx": end_x, "gy": end_y}
    pairs = {"gx": [], "gy": []}
    for stage in range(max(stages.values())):
        axes = [a for a in ("gx", "gy") if stage < stages[a]]
        theirs = {a: cross(mine[a], a, stage) for a in axes}
        for a in axes:
            pairs[a].append((mine[a], theirs[a]))
        more = [a for a in axes if stage + 1 < stages[a]]
        if more:
            also = [theirs[a] for a in axes if a not in more]
            merged = merge_call(more, stage, [mine[a] for a in more], [theirs[a] for a in more], also)
            mine.update(zip(more, merged))
    turned = [pltpu.VMEM((cols, LANES), F32)]
    vy = solve(solve_y_kernel, "solve_y", (iy, ry, ty, wy, sy), pairs["gy"], block, inv_cy, turned)
    vx = solve(solve_x_kernel, "solve_x", (ix, rx, tx, wx, sx), pairs["gx"], block, inv_cx)
    return new_depth, vx, vy


def solution(mesh):
    spec = P("gx", "gy")
    return jax.shard_map(
        on_device,
        mesh=mesh,
        in_specs=(spec,) * 5,
        out_specs=(spec,) * 3,
        check_vma=False,
    )
```

time: 42 us -> 31.9 us (0.76)
  starting transfers between devices: 19.2 us -> 11.9 us
  local copies, waits for them, and re-layouts: 4.74 us -> 0.02 us
  waiting for transfers between devices: 5.07 us -> 8.94 us
  Pallas kernels: 12 us -> 10.2 us
    pallas_call x1, Pallas kernels: 9.91 us -> 2.05 us  [fluxes(): pl.pallas_call(functools.partial(flux_kernel, inv_cx=inv_cx, inv_cy=inv_c...]
    ppermute x5 -> x7, starting transfers between devices: 14.8 us -> 8.23 us  [cross(): lax.ppermute(value, axis, [(i, i ^ 1 << stage) for i in range(lax.axis_si...]
    pallas_call x2 -> x5, Pallas kernels: 2.03 us -> 8.06 us  [the longest x1 3.06 us: prepare(): pl.pallas_call(functools.partial(prepare_kernel, inv_cx=inv_cx, inv_cy=in...]
    unnamed x10, local copies, waits for them, and re-layouts: 4.74 us -> 0.02 us
    ppermute x5 -> x7, waiting for transfers between devices: 4.57 us -> 8.94 us  [cross(): lax.ppermute(value, axis, [(i, i ^ 1 << stage) for i in range(lax.axis_si...]
    ppermute x4 -> x2, starting transfers between devices: 4.39 us -> 3.63 us  [hand_on(): lax.ppermute(value, axis, [(i, t if 0 <= t < count else i ^ 1) for i, t i...]
    ppermute x4 -> x2, waiting for transfers between devices: 0.49 us -> 0.01 us  [hand_on(): lax.ppermute(value, axis, [(i, t if 0 <= t < count else i ^ 1) for i, t i...]
  transfers between devices with their start and end apart: 9 -> 9, of which waited for: 4 -> 5; matrix products, arithmetic and copies ran while one was open for 0% -> 0% of each run, Pallas kernels for 0% -> 15%
where the time goes in v3:
time: 31.9 us; the launch traced here: 31.7 us
  starting transfers between devices  11.9 us (37%)
  Pallas kernels  10.2 us (32%)
  waiting for transfers between devices  8.94 us (28%)
  between operations  0.76 us (2%)
    ppermute x7, waiting for transfers between devices, cross(): lax.ppermute(value, axis, [(i, i ^ 1 << stage) for i in range(lax.axis_si...  8.94 us
    ppermute x7, starting transfers between devices, cross(): lax.ppermute(value, axis, [(i, i ^ 1 << stage) for i in range(lax.axis_si...  8.23 us
    ppermute x2, starting transfers between devices, hand_on(): lax.ppermute(value, axis, [(i, t if 0 <= t < count else i ^ 1) for i, t i...  3.63 us
    pallas_call x1, Pallas kernels, prepare(): pl.pallas_call(functools.partial(prepare_kernel, inv_cx=inv_cx, inv_cy=in...  3.06 us
    pallas_call x1, Pallas kernels, pack(): pl.pallas_call(pack_kernel, out_shape=(shape(2, SUB, cols), shape(2, SUB,...  2.34 us
    pallas_call x1, Pallas kernels, fluxes(): pl.pallas_call(functools.partial(flux_kernel, inv_cx=inv_cx, inv_cy=inv_c...  2.05 us
    pallas_call x2, Pallas kernels, solve(): pl.pallas_call(functools.partial(kernel, scale=scale), out_shape=shape(*b...  1.92 us
    pallas_call x1, Pallas kernels, write_depth(): pl.pallas_call(depth_kernel, out_shape=shape(*block), in_specs=[VMEM], ou...  0.75 us
  transfers between devices with their start and end apart: 9, of which 5 were waited for; matrix products, arithmetic and copies ran while one was open for 0% of the time, Pallas kernels for 15%

profile of v3, /device:TPU:0, one launch (start us, length us, event | category | flops | bytes accessed | tf_op | source)
XLA Modules:
  0.0 31.7 jit_solution(632358959335238446)
XLA Ops:
  0.6 0.0 copy-start.4
  0.6 0.0 copy-start.3
  0.7 0.0 copy-start.2
  0.7 0.0 copy-start.1
  0.7 0.0 copy-start
  0.7 2.3 %pack.1 = (f32[2,8,512]{2,1,0:T(8,128)}, f32[2,8,128]{2,1,0:T(8,128)}) custom-call(f32[128,512]{1,0:T(8,128)} %h.3, f32[128,512]{1,0:T(8,128)} %p.3, f32[128,512]{1,0:T(8,128)} %q.3, f32[128,512]{1,0:T(8,128)} %b.3, s32[128,512]{1,0:T(8,128)} %m.3), custom_call_target="tpu_custom_call" | custom-call | tf_op jit(solution)/shard_map/pack/pallas_call | solution.py:103
  3.0 3.0 %collective-permute-start = (f32[2,8,512]{2,1,0:T(8,128)}, f32[2,8,512]{2,1,0:T(8,128)S(1)}, u32[]{:S(2)}, u32[]{:S(2)}) collective-permute-start(f32[2,8,512]{2,1,0:T(8,128)} %get-tuple-element.32), channel_id=1, source_target_pairs={{0,4},{4,0},{8,12},{12,8},{16,20},{20,16},{24,28},{28,24},{1,5},{5... | collective-permute-start | bytes 98312 | tf_op jit(solution)/shard_map/ppermute | solution.py:596
  6.0 0.0 collective-permute-start.2
  6.0 2.1 %collective-permute-done.near_x = f32[2,8,512]{2,1,0:T(8,128)S(1)} collective-permute-done((f32[2,8,512]{2,1,0:T(8,128)}, f32[2,8,512]{2,1,0:T(8,128)S(1)}, u32[]{:S(2)}, u32[]{:S(2)}) %collective-permute-start) | collective-permute-done | bytes 32800 | tf_op jit(solution)/shard_map/ppermute | solution.py:596
  8.1 2.1 %collective-permute-start.1 = (f32[8,512]{1,0:T(8,128)S(1)}, f32[8,512]{1,0:T(8,128)S(1)}, u32[]{:S(2)}, u32[]{:S(2)}) collective-permute-start(f32[8,512]{1,0:T(8,128)S(1)} %slice_bitcast_fusion), channel_id=1, source_target_pairs={{0,8},{4,0},{8,16},{12,4},{16,24},{20,12},{24,28},{28,20},{1,9},{5... | collective-permute-start | bytes 49160 | tf_op jit(solution)/shard_map/ppermute | solution.py:592
  10.2 0.0 collective-permute-done.2.near_y
  10.2 1.5 %collective-permute-start.3 = (f32[8,128]{1,0:T(8,128)S(1)}, f32[8,128]{1,0:T(8,128)S(1)}, u32[]{:S(2)}, u32[]{:S(2)}) collective-permute-start(f32[8,128]{1,0:T(8,128)S(1)} %slice_bitcast_fusion.1), channel_id=1, source_target_pairs={{0,2},{1,0},{2,3},{3,1},{4,6},{5,4},{6,7},{7,5},{8,10},{9,8},{10,1... | collective-permute-start | bytes 12296 | tf_op jit(solution)/shard_map/ppermute | solution.py:592
  11.8 0.0 copy-done.4
  11.8 0.0 copy-done.1
  11.8 0.0 copy-done
  11.8 3.1 %prepare.1 = (f32[512,128]{1,0:T(8,128)S(1)}, f32[512,128]{1,0:T(8,128)S(1)}, f32[512,128]{1,0:T(8,128)S(1)}, f32[512,128]{1,0:T(8,128)S(1)}, f32[512,128]{1,0:T...) custom-call(f32[128,512]{1,0:T(8,128)S(1)} %copy-done, ...), custom_call_target="tpu_custom_call" | custom-call | flops 2000000 | bytes 8000000 | tf_op jit(solution)/shard_map/prepare/pallas_call | solution.py:232
  14.9 0.0 collective-permute-done.3.far_y
  14.9 0.0 collective-permute-done.1.far_x
  14.9 2.1 %fluxes.1 = (f32[512,128]{1,0:T(8,128)S(1)}, f32[512,128]{1,0:T(8,128)S(1)}, f32[512,128]{1,0:T(8,128)S(1)}, f32[4,32,128]{2,1,0:T(8,128)S(1)}, f32[6,32,128]{2,...) custom-call(f32[2,8,512]{2,1,0:T(8,128)S(1)} %collective-permute-done.near_x, ...), custom_call_target="tpu_custom_call" | custom-call | tf_op jit(solution)/shard_map/fluxes/pallas_call | solution.py:412
  16.9 0.5 %collective-permute-start.4 = (f32[8,512]{1,0:T(8,128)S(1)}, f32[8,512]{1,0:T(8,128)S(1)}, u32[]{:S(2)}, u32[]{:S(2)}) collective-permute-start(f32[8,512]{1,0:T(8,128)S(1)} %get-tuple-element.55.refs_0_), channel_id=1, source_target_pairs={{0,4},{4,0},{8,12},{12,8},{16,20},{20,16},{24,28},{28,24},{1,5},{5... | collective-permute-start | bytes 49160 | tf_op jit(solution)/shard_map/ppermute | solution.py:596
  17.4 0.0 collective-permute-start.5
  17.5 1.2 %collective-permute-done.5.refs_3_.refs_1_ = f32[8,128]{1,0:T(8,128)S(1)} collective-permute-done((f32[8,128]{1,0:T(8,128)S(1)}, f32[8,128]{1,0:T(8,128)S(1)}, u32[]{:S(2)}, u32[]{:S(2)}) %collective-permute-start.5) | collective-permute-done | bytes 4128 | tf_op jit(solution)/shard_map/ppermute | solution.py:596
  18.6 2.1 %collective-permute-done.4.refs_2_.refs_1_ = f32[8,512]{1,0:T(8,128)S(1)} collective-permute-done((f32[8,512]{1,0:T(8,128)S(1)}, f32[8,512]{1,0:T(8,128)S(1)}, u32[]{:S(2)}, u32[]{:S(2)}) %collective-permute-start.4) | collective-permute-done | bytes 16416 | tf_op jit(solution)/shard_map/ppermute | solution.py:596
  20.8 1.6 %collective-permute-start.6 = (f32[8,512]{1,0:T(8,128)S(1)}, f32[8,512]{1,0:T(8,128)S(1)}, u32[]{:S(2)}, u32[]{:S(2)}) collective-permute-start(f32[8,512]{1,0:T(8,128)S(1)} %get-tuple-element.57.refs_0_.refs_2_), channel_id=1, source_target_pairs={{0,8},{4,12},{8,0},{12,4},{16,24},{20,28},{24,16},{28,20},{1,9},{5... | collective-permute-start | bytes 49160 | tf_op jit(solution)/shard_map/ppermute | solution.py:596
  22.4 0.5 %collective-permute-start.7 = (f32[8,128]{1,0:T(8,128)S(1)}, f32[8,128]{1,0:T(8,128)S(1)}, u32[]{:S(2)}, u32[]{:S(2)}) collective-permute-start(f32[8,128]{1,0:T(8,128)S(1)} %get-tuple-element.58.refs_2_), channel_id=1, source_target_pairs={{0,2},{1,3},{2,0},{3,1},{4,6},{5,7},{6,4},{7,5},{8,10},{9,11},{10,... | collective-permute-start | bytes 12296 | tf_op jit(solution)/shard_map/ppermute | solution.py:596
  22.9 3.1 %collective-permute-done.7.refs_2_.refs_3_ = f32[8,128]{1,0:T(8,128)S(1)} collective-permute-done((f32[8,128]{1,0:T(8,128)S(1)}, f32[8,128]{1,0:T(8,128)S(1)}, u32[]{:S(2)}, u32[]{:S(2)}) %collective-permute-start.7) | collective-permute-done | bytes 4128 | tf_op jit(solution)/shard_map/ppermute | solution.py:596
  26.0 0.0 collective-permute-done.6.refs_1_.refs_3_
  26.0 2.6 %collective-permute-start.8 = (f32[8,512]{1,0:T(8,128)S(1)}, f32[8,512]{1,0:T(8,128)S(1)}, u32[]{:S(2)}, u32[]{:S(2)}) collective-permute-start(f32[8,512]{1,0:T(8,128)S(1)} %merge.3.refs_4_), channel_id=1, source_target_pairs={{0,16},{4,20},{8,24},{12,28},{16,0},{20,4},{24,8},{28,12},{1,17},{... | collective-permute-start | bytes 49160 | tf_op jit(solution)/shard_map/ppermute | solution.py:596
  28.6 0.7 %write_depth.1 = f32[128,512]{1,0:T(8,128)} custom-call(f32[512,128]{1,0:T(8,128)S(1)} %get-tuple-element.52.depth), custom_call_target="tpu_custom_call" | custom-call | flops 100000 | bytes 2000000 | tf_op jit(solution)/shard_map/write_depth/pallas_call | solution.py:450
  29.4 1.0 %solve_y.1 = f32[128,512]{1,0:T(8,128)} custom-call(f32[512,128]{1,0:T(8,128)S(1)} %get-tuple-element.45.iy.inv_ref, f32[512,128]{1,0:T(8,128)S(1)} %get-tuple-element.59.r_ref, f32[3,32,128]{2,1,0:T(8,128)S(1)} %get-tuple-element.48.ty.t_ref, f32[15,32,128]{2,1,0:T(8,128)S(1)} %get-tuple-element.49.wy.w_ref, f32[6,32,128]{2,1,0:T(8,128)S(1)} %get-tuple-element.60.s_ref, ...), custom_call_target="tpu_custom_call" | custom-call | flops 1000000 | bytes 4000000 | tf_op jit(solution)/shard_map/solve_y/pallas_call | solution.py:577
  30.4 0.4 %collective-permute-done.8.refs_5_ = f32[8,512]{1,0:T(8,128)S(1)} collective-permute-done((f32[8,512]{1,0:T(8,128)S(1)}, f32[8,512]{1,0:T(8,128)S(1)}, u32[]{:S(2)}, u32[]{:S(2)}) %collective-permute-start.8) | collective-permute-done | bytes 16416 | tf_op jit(solution)/shard_map/ppermute | solution.py:596
  30.8 0.9 %solve_x.1 = f32[128,512]{1,0:T(8,128)} custom-call(f32[512,128]{1,0:T(8,128)S(1)} %get-tuple-element.39.ix.inv_ref, f32[512,128]{1,0:T(8,128)S(1)} %get-tuple-element.53.r_ref, f32[3,32,128]{2,1,0:T(8,128)S(1)} %get-tuple-element.46.tx.t_ref, f32[9,32,128]{2,1,0:T(8,128)S(1)} %get-tuple-element.47.wx.w_ref, f32[4,32,128]{2,1,0:T(8,128)S(1)} %get-tuple-element.54.s_ref, ...), custom_call_target="tpu_custom_call" | custom-call | flops 1000000 | bytes 4000000 | tf_op jit(solution)/shard_map/solve_x/pallas_call | solution.py:577
  (6 shorter events, 0.1 us)
Async XLA Ops:
  0.6 11.1 %copy-start.4 = (s32[128,512]{1,0:T(8,128)S(1)}, s32[128,512]{1,0:T(8,128)}, u32[]{:S(2)}) copy-start(s32[128,512]{1,0:T(8,128)} %m.3) | copy-start | bytes 786436
  0.6 11.1 %copy-start.3 = (f32[128,512]{1,0:T(8,128)S(1)}, f32[128,512]{1,0:T(8,128)}, u32[]{:S(2)}) copy-start(f32[128,512]{1,0:T(8,128)} %b.3) | copy-start | bytes 786436
  0.7 11.1 %copy-start.2 = (f32[128,512]{1,0:T(8,128)S(1)}, f32[128,512]{1,0:T(8,128)}, u32[]{:S(2)}) copy-start(f32[128,512]{1,0:T(8,128)} %q.3) | copy-start | bytes 786436
  0.7 11.1 %copy-start.1 = (f32[128,512]{1,0:T(8,128)S(1)}, f32[128,512]{1,0:T(8,128)}, u32[]{:S(2)}) copy-start(f32[128,512]{1,0:T(8,128)} %p.3) | copy-start | bytes 786436
  0.7 11.1 %copy-start = (f32[128,512]{1,0:T(8,128)S(1)}, f32[128,512]{1,0:T(8,128)}, u32[]{:S(2)}) copy-start(f32[128,512]{1,0:T(8,128)} %h.3) | copy-start | bytes 786436
  3.0 5.1 %collective-permute-start = (f32[2,8,512]{2,1,0:T(8,128)}, f32[2,8,512]{2,1,0:T(8,128)S(1)}, u32[]{:S(2)}, u32[]{:S(2)}) collective-permute-start(f32[2,8,512]{2,1,0:T(8,128)} %get-tuple-element.32), channel_id=1, source_target_pairs={{0,4},{4,0},{8,12},{12,8},{16,20},{20,16},{24,28},{28,24},{1,5},{5... | collective-permute-start | bytes 98312 | tf_op jit(solution)/shard_map/ppermute | solution.py:596
  6.0 4.2 %collective-permute-start.2 = (f32[2,8,128]{2,1,0:T(8,128)}, f32[2,8,128]{2,1,0:T(8,128)S(1)}, u32[]{:S(2)}, u32[]{:S(2)}) collective-permute-start(f32[2,8,128]{2,1,0:T(8,128)} %get-tuple-element.33), channel_id=1, source_target_pairs={{0,1},{1,0},{2,3},{3,2},{4,5},{5,4},{6,7},{7,6},{8,9},{9,8},{10,11... | collective-permute-start | bytes 24584 | tf_op jit(solution)/shard_map/ppermute | solution.py:596
  8.1 6.7 %collective-permute-start.1 = (f32[8,512]{1,0:T(8,128)S(1)}, f32[8,512]{1,0:T(8,128)S(1)}, u32[]{:S(2)}, u32[]{:S(2)}) collective-permute-start(f32[8,512]{1,0:T(8,128)S(1)} %slice_bitcast_fusion), channel_id=1, source_target_pairs={{0,8},{4,0},{8,16},{12,4},{16,24},{20,12},{24,28},{28,20},{1,9},{5... | collective-permute-start | bytes 49160 | tf_op jit(solution)/shard_map/ppermute | solution.py:592
  10.2 4.6 %collective-permute-start.3 = (f32[8,128]{1,0:T(8,128)S(1)}, f32[8,128]{1,0:T(8,128)S(1)}, u32[]{:S(2)}, u32[]{:S(2)}) collective-permute-start(f32[8,128]{1,0:T(8,128)S(1)} %slice_bitcast_fusion.1), channel_id=1, source_target_pairs={{0,2},{1,0},{2,3},{3,1},{4,6},{5,4},{6,7},{7,5},{8,10},{9,8},{10,1... | collective-permute-start | bytes 12296 | tf_op jit(solution)/shard_map/ppermute | solution.py:592
  16.9 3.8 %collective-permute-start.4 = (f32[8,512]{1,0:T(8,128)S(1)}, f32[8,512]{1,0:T(8,128)S(1)}, u32[]{:S(2)}, u32[]{:S(2)}) collective-permute-start(f32[8,512]{1,0:T(8,128)S(1)} %get-tuple-element.55.refs_0_), channel_id=1, source_target_pairs={{0,4},{4,0},{8,12},{12,8},{16,20},{20,16},{24,28},{28,24},{1,5},{5... | collective-permute-start | bytes 49160 | tf_op jit(solution)/shard_map/ppermute | solution.py:596
  17.4 1.2 %collective-permute-start.5 = (f32[8,128]{1,0:T(8,128)S(1)}, f32[8,128]{1,0:T(8,128)S(1)}, u32[]{:S(2)}, u32[]{:S(2)}) collective-permute-start(f32[8,128]{1,0:T(8,128)S(1)} %get-tuple-element.56.refs_1_.refs_0_), channel_id=1, source_target_pairs={{0,1},{1,0},{2,3},{3,2},{4,5},{5,4},{6,7},{7,6},{8,9},{9,8},{10,11... | collective-permute-start | bytes 12296 | tf_op jit(solution)/shard_map/ppermute | solution.py:596
  20.8 5.3 %collective-permute-start.6 = (f32[8,512]{1,0:T(8,128)S(1)}, f32[8,512]{1,0:T(8,128)S(1)}, u32[]{:S(2)}, u32[]{:S(2)}) collective-permute-start(f32[8,512]{1,0:T(8,128)S(1)} %get-tuple-element.57.refs_0_.refs_2_), channel_id=1, source_target_pairs={{0,8},{4,12},{8,0},{12,4},{16,24},{20,28},{24,16},{28,20},{1,9},{5... | collective-permute-start | bytes 49160 | tf_op jit(solution)/shard_map/ppermute | solution.py:596
  22.4 3.6 %collective-permute-start.7 = (f32[8,128]{1,0:T(8,128)S(1)}, f32[8,128]{1,0:T(8,128)S(1)}, u32[]{:S(2)}, u32[]{:S(2)}) collective-permute-start(f32[8,128]{1,0:T(8,128)S(1)} %get-tuple-element.58.refs_2_), channel_id=1, source_target_pairs={{0,2},{1,3},{2,0},{3,1},{4,6},{5,7},{6,4},{7,5},{8,10},{9,11},{10,... | collective-permute-start | bytes 12296 | tf_op jit(solution)/shard_map/ppermute | solution.py:596
  26.0 4.8 %collective-permute-start.8 = (f32[8,512]{1,0:T(8,128)S(1)}, f32[8,512]{1,0:T(8,128)S(1)}, u32[]{:S(2)}, u32[]{:S(2)}) collective-permute-start(f32[8,512]{1,0:T(8,128)S(1)} %merge.3.refs_4_), channel_id=1, source_target_pairs={{0,16},{4,20},{8,24},{12,28},{16,0},{20,4},{24,8},{28,12},{1,17},{... | collective-permute-start | bytes 49160 | tf_op jit(solution)/shard_map/ppermute | solution.py:596

commit v4 on v3

--- a/solution.py
+++ b/solution.py
@@ -47,20 +47,23 @@
 
 def pack_kernel(h, p, q, b, m, xa, ya, top, bottom, left, right, itop, ibottom, ileft, iright, sems):
     rows, cols = h.shape
-    copies = []
-    for f, src in enumerate((h, p, q, b, m)):
-        floats = f < 4
-        spots = (
-            (src.at[pl.ds(0, SUB), :], top.at[f] if floats else itop),
-            (src.at[pl.ds(rows - SUB, SUB), :], bottom.at[f] if floats else ibottom),
-            (src.at[:, pl.ds(0, LANES)], left.at[f] if floats else ileft),
-            (src.at[:, pl.ds(cols - LANES, LANES)], right.at[f] if floats else iright),
-        )
-        for g, (piece, target) in enumerate(spots):
-            copy = pltpu.make_async_copy(piece, target, sems.at[4 * f + g])
-            copy.start()
-            copies.append(copy)
-    for copy in copies:
+    sources = (h, p, q, b, m)
+
+    def load(places, piece, first):
+        copies = []
+        for f, (src, target) in enumerate(zip(sources, places)):
+            copies.append(pltpu.make_async_copy(src.at[piece], target, sems.at[first + f]))
+            copies[-1].start()
+        return copies
+
+    def places(floats, whole):
+        return [floats.at[f] for f in range(4)] + [whole]
+
+    edges_x = load(places(top, itop), (pl.ds(0, SUB), slice(None)), 0)
+    edges_x += load(places(bottom, ibottom), (pl.ds(rows - SUB, SUB), slice(None)), 5)
+    edges_y = load(places(left, ileft), (slice(None), pl.ds(0, LANES)), 10)
+    edges_y += load(places(right, iright), (slice(None), pl.ds(cols - LANES, LANES)), 15)
+    for copy in edges_x:
         copy.wait()
     first_x = jnp.concatenate(
         [top[0, 0:2, :], top[1, 0:2, :], top[2, 0:2, :], top[3, 0:1, :], itop[0:1, :].astype(F32)]
@@ -77,21 +80,20 @@
     even_x = lax.axis_index("gx") % 2 == 0
     xa[0] = jnp.where(even_x, last_x, first_x)
     xa[1] = jnp.where(even_x, first_x, last_x)
+    for copy in edges_y:
+        copy.wait()
     lane = lane_index((rows, LANES))
-
-    def columns(block, imask, shifts):
-        def stacked(ref):
-            return jnp.concatenate([ref[spread_rows(0, k), :] for k in range(STEPS)])
-
-        fields = [stacked(block.at[f]) for f in range(4)] + [stacked(imask).astype(F32)]
-        moved = [pltpu.roll(v, s, 1) if s else v for v, s in zip(fields, shifts)]
-        out = moved[0]
-        for start, v in zip((2, 4, 6, 7), moved[1:]):
-            out = jnp.where(lane >= start, v, out)
-        return out.T[0:SUB, :]
-
-    first_y = columns(left, ileft, (0, 2, 4, 6, 7))
-    last_y = columns(right, iright, (2, 4, 6, 7, 8))
+    out = jnp.zeros((rows, LANES), F32)
+    for block, mask, start, shifts in (
+        (left, ileft, 0, (0, 2, 4, 6, 7)),
+        (right, iright, SUB, (10, 12, 14, 15, 16)),
+    ):
+        fields = [block.at[f] for f in range(4)] + [mask]
+        for ref, to, shift in zip(fields, (0, 2, 4, 6, 7), shifts):
+            value = jnp.concatenate([ref[spread_rows(0, k), :] for k in range(STEPS)]).astype(F32)
+            out = jnp.where(lane >= start + to, pltpu.roll(value, shift, 1) if shift else value, out)
+    turned = out.T
+    first_y, last_y = turned[0:SUB, :], turned[SUB : 2 * SUB, :]
     even_y = lax.axis_index("gy") % 2 == 0
     ya[0] = jnp.where(even_y, last_y, first_y)
     ya[1] = jnp.where(even_y, first_y, last_y)
@@ -326,13 +328,13 @@
 def flux_kernel(
     near_x, far_x, near_y, far_y,
     hx, px, qx, bx, mx, ix, hy, py, qy, by, my, iy, tx, wx, ty, wy, coefx, coefy,
-    depth, rx, ry, sx, sy, endx, endy,
+    depth, rx, ry, sx, sy, endx, endy, tally,
     xpart, ypart, turned,
     *, inv_cx, inv_cy,
 ):
     tiles = hx.shape[0] // LANES
-    low_x, high_x = low_high("gx", near_x[0], far_x[...])
-    low_y, high_y = low_high("gy", near_y[0], far_y[...])
+    low_x, high_x = low_high("gx", near_x[0], far_x[0:SUB, :])
+    low_y, high_y = low_high("gy", near_y[0], far_y[0:SUB, :])
 
     for tile in range(tiles):
         span = tile_span(tile)
@@ -395,6 +397,8 @@
         for tile in range(tiles):
             endx[3 + i : 4 + i, tile_span(tile)] = ends_x[i][tile * SUB : tile * SUB + 1, :]
         endy[3 + i : 4 + i, :] = ends_y[i][0:1, :]
+    tally[...] = jnp.zeros_like(tally)
+    tally[0:SUB, :] = endy[...]
 
 
 def fluxes(slabs, prepared, inv_cx, inv_cy):
@@ -408,6 +412,7 @@
         shape(1 + log2(count), count, LANES),
         shape(*prepared[-2].shape),
         shape(*prepared[-1].shape),
+        shape(3 * SUB, prepared[-1].shape[1]),
     )
     return pl.pallas_call(
         functools.partial(flux_kernel, inv_cx=inv_cx, inv_cy=inv_cy),
@@ -459,42 +464,51 @@
     )(depth)
 
 
+def rows_of(ref):
+    return tuple(ref[i : i + 1, :] for i in range(5))
+
+
 def ordered(axis, stage, mine, theirs):
     is_low = (lax.axis_index(axis) >> stage) % 2 == 0
-    rows = range(5)
-    one = tuple(jnp.where(is_low, mine[i : i + 1, :], theirs[i : i + 1, :]) for i in rows)
-    two = tuple(jnp.where(is_low, theirs[i : i + 1, :], mine[i : i + 1, :]) for i in rows)
+    one = tuple(jnp.where(is_low, a, b) for a, b in zip(mine, theirs))
+    two = tuple(jnp.where(is_low, b, a) for a, b in zip(mine, theirs))
     return is_low, merge(one, two)
 
 
-def merge_kernel(*refs, axes, stage):
-    count = len(axes)
-    for axis, mine, theirs, out in zip(axes, refs[:count], refs[count : 2 * count], refs[-count:]):
-        _, (merged, _) = ordered(axis, stage, mine, theirs)
-        for i, v in enumerate(merged):
-            out[i : i + 1, :] = v
-        out[5:8, :] = jnp.zeros((3, out.shape[1]), F32)
-
-
-def merge_call(axes, stage, mine, theirs, also=()):
-    count = len(axes)
+def merge_kernel(mine, theirs, *refs, axis, stage):
+    out = refs[-1]
+    _, (merged, _) = ordered(axis, stage, rows_of(mine), rows_of(theirs))
+    for i, v in enumerate(merged):
+        out[i : i + 1, :] = v
+    out[5:8, :] = jnp.zeros((3, out.shape[1]), F32)
+
+
+def merge_call(axis, stage, mine, theirs, beside):
     return pl.pallas_call(
-        functools.partial(merge_kernel, axes=axes, stage=stage),
-        out_shape=tuple(shape(*v.shape) for v in mine),
-        in_specs=[VMEM] * (2 * count + len(also)),
-        out_specs=(VMEM,) * count,
+        functools.partial(merge_kernel, axis=axis, stage=stage),
+        out_shape=shape(*mine.shape),
+        in_specs=[VMEM] * (2 + len(beside)),
+        out_specs=VMEM,
         compiler_params=PARAMS,
         name="merge",
-    )(*mine, *theirs, *also)
-
-
-def line_ends(axis, pairs):
+    )(mine, theirs, *beside)
+
+
+def line_ends(axis, refs):
     steps = []
-    merged = None
-    for stage, (mine, theirs) in enumerate(pairs):
-        is_low, (merged, weights) = ordered(axis, stage, mine, theirs)
+    parts = [rows_of(ref) for ref in refs]
+    stage = 0
+    while len(parts) > 4:
+        is_low, (_, weights) = ordered(axis, stage, *parts[:2])
         steps.append((is_low, weights))
-    t, _, gr, _, sr = merged
+        parts = parts[2:]
+        stage += 1
+    is_low, (own, weights) = ordered(axis, stage, *parts[:2])
+    steps.append((is_low, weights))
+    _, (other, _) = ordered(axis, stage, *parts[2:])
+    is_low, (whole, weights) = ordered(axis, stage + 1, own, other)
+    steps.append((is_low, weights))
+    t, _, gr, _, sr = whole
     left = jnp.zeros_like(t)
     right = sr / (t + gr + 1.0)
     for is_low, (w1, w2, source) in reversed(steps):
@@ -528,10 +542,10 @@
 
 
 def solve_x_kernel(inv_ref, r_ref, t_ref, w_ref, s_ref, *refs, scale):
-    pairs, (out, natural, sems) = refs[:-3], refs[-3:]
+    parts, (out, natural, sems) = refs[:-3], refs[-3:]
     tiles = out.shape[1] // LANES
     ends = []
-    for row in line_ends("gx", list(zip(pairs[0::2], pairs[1::2]))):
+    for row in line_ends("gx", parts):
         ends.append(
             jnp.concatenate([jnp.broadcast_to(row[:, tile_span(t)], (SUB, LANES)) for t in range(tiles)])
         )
@@ -550,9 +564,9 @@
 
 
 def solve_y_kernel(inv_ref, r_ref, t_ref, w_ref, s_ref, *refs, scale):
-    pairs, (out, natural, sems, turned) = refs[:-4], refs[-4:]
+    parts, (out, natural, sems, turned) = refs[:-4], refs[-4:]
     tiles = out.shape[1] // LANES
-    ends = line_ends("gy", list(zip(pairs[0::2], pairs[1::2])))
+    ends = line_ends("gy", parts)
     ends = [jnp.broadcast_to(row, (tiles * SUB, LANES)) for row in ends]
     left, right = segment_ends(*ends, w_ref, s_ref, log2(tiles * SUB))
 
@@ -572,18 +586,17 @@
         write.wait()
 
 
-def solve(kernel, name, pieces, pairs, block, scale, extra=()):
-    flat = [v for pair in pairs for v in pair]
+def solve(kernel, name, pieces, parts, block, scale, extra=()):
     return pl.pallas_call(
         functools.partial(kernel, scale=scale),
         out_shape=shape(*block),
-        in_specs=[VMEM] * (len(pieces) + len(flat)),
+        in_specs=[VMEM] * (len(pieces) + len(parts)),
         out_specs=ANY,
         scratch_shapes=write_scratch(block[1]) + list(extra),
         compiler_params=PARAMS,
         cost_estimate=pl.CostEstimate(flops=1_000_000, bytes_accessed=4_000_000, transcendentals=0),
         name=name,
-    )(*pieces, *flat)
+    )(*pieces, *parts)
 
 
 def hand_on(value, axis):
@@ -592,40 +605,47 @@
     return lax.ppermute(value, axis, [(i, t if 0 <= t < count else i ^ 1) for i, t in enumerate(far)])
 
 
-def cross(value, axis, stage):
-    return lax.ppermute(value, axis, [(i, i ^ (1 << stage)) for i in range(lax.axis_size(axis))])
+def cross(value, axis, mask):
+    return lax.ppermute(value, axis, [(i, i ^ mask) for i in range(lax.axis_size(axis))])
+
+
+def parts_of_line(axis, mine, relay, beside=(), tall=None):
+    parts = []
+    last = log2(lax.axis_size(axis)) - 2
+    for stage in range(last):
+        theirs = cross(mine, axis, 1 << stage)
+        parts += [mine, theirs]
+        mine = merge_call(axis, stage, mine, theirs, beside)
+    if relay:
+        first = cross(mine, axis, 1 << last)
+        second = cross(mine if tall is None else tall, axis, 2 << last)
+        both = cross(second[0:SUB], axis, 1 << last)
+    else:
+        both = cross(mine, axis, 3 << last)
+        second = cross(mine, axis, 2 << last)
+        first = cross(mine, axis, 1 << last)
+    return parts + [mine, first, second, both]
 
 
 def on_device(h, p, q, b, m):
     block = h.shape
     rows, cols = block
-    count_x, count_y = lax.axis_size("gx"), lax.axis_size("gy")
-    inv_cx = 3.0 / (rows * count_x / 4.0) ** 2
-    inv_cy = 3.0 / (cols * count_y / 4.0) ** 2
+    inv_cx = 3.0 / (rows * lax.axis_size("gx") / 4.0) ** 2
+    inv_cy = 3.0 / (cols * lax.axis_size("gy") / 4.0) ** 2
     xa, ya = pack(h, p, q, b, m)
-    near_x, near_y = cross(xa, "gx", 0), cross(ya, "gy", 0)
-    slabs = (near_x, hand_on(near_x[1], "gx"), near_y, hand_on(near_y[1], "gy"))
+    near_x, near_y = cross(xa, "gx", 1), cross(ya, "gy", 1)
+    far_y = hand_on(jnp.pad(near_y[1], ((0, 5 * SUB), (0, 0))), "gy")
+    far_x = hand_on(near_x[1], "gx")
     prepared = prepare(h, p, q, b, m, inv_cx, inv_cy)
-    depth, rx, ry, sx, sy, end_x, end_y = fluxes(slabs, prepared, inv_cx, inv_cy)
+    depth, rx, ry, sx, sy, end_x, end_y, tall_y = fluxes((near_x, far_x, near_y, far_y), prepared, inv_cx, inv_cy)
     ix, iy = prepared[5], prepared[11]
     tx, wx, ty, wy = prepared[12:16]
     new_depth = write_depth(depth, block)
-    stages = {"gx": log2(count_x), "gy": log2(count_y)}
-    mine = {"gx": end_x, "gy": end_y}
-    pairs = {"gx": [], "gy": []}
-    for stage in range(max(stages.values())):
-        axes = [a for a in ("gx", "gy") if stage < stages[a]]
-        theirs = {a: cross(mine[a], a, stage) for a in axes}
-        for a in axes:
-            pairs[a].append((mine[a], theirs[a]))
-        more = [a for a in axes if stage + 1 < stages[a]]
-        if more:
-            also = [theirs[a] for a in axes if a not in more]
-            merged = merge_call(more, stage, [mine[a] for a in more], [theirs[a] for a in more], also)
-            mine.update(zip(more, merged))
+    parts_y = parts_of_line("gy", end_y, True, tall=tall_y if lax.axis_size("gy") == 4 else None)
+    parts_x = parts_of_line("gx", end_x, False, parts_y[1:2])
     turned = [pltpu.VMEM((cols, LANES), F32)]
-    vy = solve(solve_y_kernel, "solve_y", (iy, ry, ty, wy, sy), pairs["gy"], block, inv_cy, turned)
-    vx = solve(solve_x_kernel, "solve_x", (ix, rx, tx, wx, sx), pairs["gx"], block, inv_cx)
+    vy = solve(solve_y_kernel, "solve_y", (iy, ry, ty, wy, sy), parts_y, block, inv_cy, turned)
+    vx = solve(solve_x_kernel, "solve_x", (ix, rx, tx, wx, sx), parts_x, block, inv_cx)
     return new_depth, vx, vy
 
 

time: 31.9 us -> 28.6 us (0.90)
  waiting for transfers between devices: 8.94 us -> 4.33 us
  starting transfers between devices: 11.9 us -> 13.2 us
    ppermute x7 -> x9, waiting for transfers between devices: 8.94 us -> 4.32 us  [cross(): lax.ppermute(value, axis, [(i, i ^ mask) for i in range(lax.axis_size(axi...]
    ppermute x7 -> x9, starting transfers between devices: 8.23 us -> 9.65 us  [cross(): lax.ppermute(value, axis, [(i, i ^ mask) for i in range(lax.axis_size(axi...]
  transfers between devices with their start and end apart: 9 -> 11, of which waited for: 5 -> 4; matrix products, arithmetic and copies ran while one was open for 0% -> 0% of each run, Pallas kernels for 15% -> 17%
where the time goes in v4:
time: 28.6 us; the launch traced here: 28.5 us
  starting transfers between devices  13.2 us (46%)
  Pallas kernels  10.1 us (35%)
  waiting for transfers between devices  4.33 us (15%)
  between operations  0.76 us (3%)
    ppermute x9, starting transfers between devices, cross(): lax.ppermute(value, axis, [(i, i ^ mask) for i in range(lax.axis_size(axi...  9.65 us
    ppermute x9, waiting for transfers between devices, cross(): lax.ppermute(value, axis, [(i, i ^ mask) for i in range(lax.axis_size(axi...  4.32 us
    ppermute x2, starting transfers between devices, hand_on(): lax.ppermute(value, axis, [(i, t if 0 <= t < count else i ^ 1) for i, t i...  3.55 us
    pallas_call x1, Pallas kernels, prepare(): pl.pallas_call(functools.partial(prepare_kernel, inv_cx=inv_cx, inv_cy=in...  3.06 us
    pallas_call x1, Pallas kernels, pack(): pl.pallas_call(pack_kernel, out_shape=(shape(2, SUB, cols), shape(2, SUB,...  2.34 us
    pallas_call x1, Pallas kernels, fluxes(): pl.pallas_call(functools.partial(flux_kernel, inv_cx=inv_cx, inv_cy=inv_c...  2.05 us
    pallas_call x2, Pallas kernels, solve(): pl.pallas_call(functools.partial(kernel, scale=scale), out_shape=shape(*b...  1.93 us
    pallas_call x1, Pallas kernels, write_depth(): pl.pallas_call(depth_kernel, out_shape=shape(*block), in_specs=[VMEM], ou...  0.75 us
  transfers between devices with their start and end apart: 11, of which 4 were waited for; matrix products, arithmetic and copies ran while one was open for 0% of the time, Pallas kernels for 17%

profile of v4, /device:TPU:0, one launch (start us, length us, event | category | flops | bytes accessed | tf_op | source)
XLA Modules:
  0.0 28.5 jit_solution(3426839855021974148)
XLA Ops:
  0.6 0.0 copy-start.4
  0.6 0.0 copy-start.3
  0.7 0.0 copy-start.2
  0.7 2.3 %pack.1 = (f32[2,8,512]{2,1,0:T(8,128)}, f32[2,8,128]{2,1,0:T(8,128)}) custom-call(f32[128,512]{1,0:T(8,128)} %h.3, f32[128,512]{1,0:T(8,128)} %p.3, f32[128,512]{1,0:T(8,128)} %q.3, f32[128,512]{1,0:T(8,128)} %b.3, s32[128,512]{1,0:T(8,128)} %m.3), custom_call_target="tpu_custom_call" | custom-call | tf_op jit(solution)/shard_map/pack/pallas_call | solution.py:105
  3.0 0.5 %collective-permute-start.2 = (f32[2,8,128]{2,1,0:T(8,128)}, f32[2,8,128]{2,1,0:T(8,128)S(1)}, u32[]{:S(2)}, u32[]{:S(2)}) collective-permute-start(f32[2,8,128]{2,1,0:T(8,128)} %get-tuple-element.32), channel_id=1, source_target_pairs={{0,1},{1,0},{2,3},{3,2},{4,5},{5,4},{6,7},{7,6},{8,9},{9,8},{10,11... | collective-permute-start | bytes 24584 | tf_op jit(solution)/shard_map/ppermute | solution.py:609
  3.6 2.6 %collective-permute-start = (f32[2,8,512]{2,1,0:T(8,128)}, f32[2,8,512]{2,1,0:T(8,128)S(1)}, u32[]{:S(2)}, u32[]{:S(2)}) collective-permute-start(f32[2,8,512]{2,1,0:T(8,128)} %get-tuple-element.31), channel_id=1, source_target_pairs={{0,4},{4,0},{8,12},{12,8},{16,20},{20,16},{24,28},{28,24},{1,5},{5... | collective-permute-start | bytes 98312 | tf_op jit(solution)/shard_map/ppermute | solution.py:609
  6.1 0.0 collective-permute-done.2.near_y
  6.1 1.5 %collective-permute-start.3 = (f32[48,128]{1,0:T(8,128)S(1)}, f32[48,128]{1,0:T(8,128)S(1)}, u32[]{:S(2)}, u32[]{:S(2)}) collective-permute-start(f32[48,128]{1,0:T(8,128)S(1)} %pad.4), channel_id=1, source_target_pairs={{0,2},{1,0},{2,3},{3,1},{4,6},{5,4},{6,7},{7,5},{8,10},{9,8},{10,1... | collective-permute-start | bytes 73736 | tf_op jit(solution)/shard_map/ppermute | solution.py:605
  7.7 0.6 %collective-permute-done.near_x = f32[2,8,512]{2,1,0:T(8,128)S(1)} collective-permute-done((f32[2,8,512]{2,1,0:T(8,128)}, f32[2,8,512]{2,1,0:T(8,128)S(1)}, u32[]{:S(2)}, u32[]{:S(2)}) %collective-permute-start) | collective-permute-done | bytes 32800 | tf_op jit(solution)/shard_map/ppermute | solution.py:609
  8.3 2.0 %collective-permute-start.1 = (f32[8,512]{1,0:T(8,128)S(1)}, f32[8,512]{1,0:T(8,128)S(1)}, u32[]{:S(2)}, u32[]{:S(2)}) collective-permute-start(f32[8,512]{1,0:T(8,128)S(1)} %slice_bitcast_fusion), channel_id=1, source_target_pairs={{0,8},{4,0},{8,16},{12,4},{16,24},{20,12},{24,28},{28,20},{1,9},{5... | collective-permute-start | bytes 49160 | tf_op jit(solution)/shard_map/ppermute | solution.py:605
  10.3 0.0 copy-done.3
  10.4 3.1 %prepare.1 = (f32[512,128]{1,0:T(8,128)S(1)}, f32[512,128]{1,0:T(8,128)S(1)}, f32[512,128]{1,0:T(8,128)S(1)}, f32[512,128]{1,0:T(8,128)S(1)}, f32[512,128]{1,0:T...) custom-call(f32[128,512]{1,0:T(8,128)S(1)} %copy-done, ...), custom_call_target="tpu_custom_call" | custom-call | flops 2000000 | bytes 8000000 | tf_op jit(solution)/shard_map/prepare/pallas_call | solution.py:234
  13.4 0.0 collective-permute-done.3.far_y
  13.4 0.0 collective-permute-done.1.far_x
  13.4 2.0 %fluxes.1 = (f32[512,128]{1,0:T(8,128)S(1)}, f32[512,128]{1,0:T(8,128)S(1)}, f32[512,128]{1,0:T(8,128)S(1)}, f32[4,32,128]{2,1,0:T(8,128)S(1)}, f32[6,32,128]{2,...) custom-call(f32[2,8,512]{2,1,0:T(8,128)S(1)} %collective-permute-done.near_x, ...), custom_call_target="tpu_custom_call" | custom-call | tf_op jit(solution)/shard_map/fluxes/pallas_call | solution.py:417
  15.5 0.6 %collective-permute-start.4 = (f32[8,512]{1,0:T(8,128)S(1)}, f32[8,512]{1,0:T(8,128)S(1)}, u32[]{:S(2)}, u32[]{:S(2)}) collective-permute-start(f32[8,512]{1,0:T(8,128)S(1)} %get-tuple-element.54.mine.refs_0_), channel_id=1, source_target_pairs={{0,4},{4,0},{8,12},{12,8},{16,20},{20,16},{24,28},{28,24},{1,5},{5... | collective-permute-start | bytes 49160 | tf_op jit(solution)/shard_map/ppermute | solution.py:609
  16.1 0.0 collective-permute-start.5
  16.1 1.5 %collective-permute-start.9 = (f32[24,128]{1,0:T(8,128)S(1)}, f32[24,128]{1,0:T(8,128)S(1)}, u32[]{:S(2)}, u32[]{:S(2)}) collective-permute-start(f32[24,128]{1,0:T(8,128)S(1)} %get-tuple-element.58), channel_id=1, source_target_pairs={{0,2},{1,3},{2,0},{3,1},{4,6},{5,7},{6,4},{7,5},{8,10},{9,11},{10,... | collective-permute-start | bytes 36872 | tf_op jit(solution)/shard_map/ppermute | solution.py:609
  17.6 0.0 collective-permute-done.5.refs_0_.refs_1_
  17.6 1.7 %collective-permute-done.4.theirs.refs_1_ = f32[8,512]{1,0:T(8,128)S(1)} collective-permute-done((f32[8,512]{1,0:T(8,128)S(1)}, f32[8,512]{1,0:T(8,128)S(1)}, u32[]{:S(2)}, u32[]{:S(2)}) %collective-permute-start.4) | collective-permute-done | bytes 16416 | tf_op jit(solution)/shard_map/ppermute | solution.py:609
  19.3 3.6 %collective-permute-start.8 = (f32[8,512]{1,0:T(8,128)S(1)}, f32[8,512]{1,0:T(8,128)S(1)}, u32[]{:S(2)}, u32[]{:S(2)}) collective-permute-start(f32[8,512]{1,0:T(8,128)S(1)} %merge.1.refs_2_), channel_id=1, source_target_pairs={{0,24},{4,28},{8,16},{12,20},{16,8},{20,12},{24,0},{28,4},{1,25},{... | collective-permute-start | bytes 49160 | tf_op jit(solution)/shard_map/ppermute | solution.py:609
  22.9 0.0 collective-permute-start.7
  22.9 0.9 %collective-permute-start.6 = (f32[8,512]{1,0:T(8,128)S(1)}, f32[8,512]{1,0:T(8,128)S(1)}, u32[]{:S(2)}, u32[]{:S(2)}) collective-permute-start(f32[8,512]{1,0:T(8,128)S(1)} %merge.1.refs_2_), channel_id=1, source_target_pairs={{0,8},{4,12},{8,0},{12,4},{16,24},{20,28},{24,16},{28,20},{1,9},{5... | collective-permute-start | bytes 49160 | tf_op jit(solution)/shard_map/ppermute | solution.py:609
  23.8 0.0 collective-permute-done.9.refs_2_
  23.8 0.0 collective-permute-start.10
  23.8 0.7 %write_depth.1 = f32[128,512]{1,0:T(8,128)} custom-call(f32[512,128]{1,0:T(8,128)S(1)} %get-tuple-element.51.depth), custom_call_target="tpu_custom_call" | custom-call | flops 100000 | bytes 2000000 | tf_op jit(solution)/shard_map/write_depth/pallas_call | solution.py:455
  24.5 0.4 %collective-permute-done.10.refs_3_ = f32[8,128]{1,0:T(8,128)S(1)} collective-permute-done((f32[8,128]{1,0:T(8,128)S(1)}, f32[8,128]{1,0:T(8,128)S(1)}, u32[]{:S(2)}, u32[]{:S(2)}) %collective-permute-start.10) | collective-permute-done | bytes 4128 | tf_op jit(solution)/shard_map/ppermute | solution.py:609
  24.9 1.0 %solve_y.1 = f32[128,512]{1,0:T(8,128)} custom-call(f32[512,128]{1,0:T(8,128)S(1)} %get-tuple-element.44.iy.inv_ref, f32[512,128]{1,0:T(8,128)S(1)} %get-tuple-element.56.r_ref, f32[3,32,128]{2,1,0:T(8,128)S(1)} %get-tuple-element.47.ty.t_ref, f32[15,32,128]{2,1,0:T(8,128)S(1)} %get-tuple-element.48.wy.w_ref, f32[6,32,128]{2,1,0:T(8,128)S(1)} %get-tuple-element.57.s_ref, ...), custom_call_target="tpu_custom_call" | custom-call | flops 1000000 | bytes 4000000 | tf_op jit(solution)/shard_map/solve_y/pallas_call | solution.py:590
  25.9 0.0 collective-permute-done.8.refs_5_
  26.0 1.6 %collective-permute-done.7.refs_4_ = f32[8,512]{1,0:T(8,128)S(1)} collective-permute-done((f32[8,512]{1,0:T(8,128)S(1)}, f32[8,512]{1,0:T(8,128)S(1)}, u32[]{:S(2)}, u32[]{:S(2)}) %collective-permute-start.7) | collective-permute-done | bytes 16416 | tf_op jit(solution)/shard_map/ppermute | solution.py:609
  27.5 0.0 collective-permute-done.6.refs_3_
  27.5 0.9 %solve_x.1 = f32[128,512]{1,0:T(8,128)} custom-call(f32[512,128]{1,0:T(8,128)S(1)} %get-tuple-element.38.ix.inv_ref, f32[512,128]{1,0:T(8,128)S(1)} %get-tuple-element.52.r_ref, f32[3,32,128]{2,1,0:T(8,128)S(1)} %get-tuple-element.45.tx.t_ref, f32[9,32,128]{2,1,0:T(8,128)S(1)} %get-tuple-element.46.wx.w_ref, f32[4,32,128]{2,1,0:T(8,128)S(1)} %get-tuple-element.53.s_ref, ...), custom_call_target="tpu_custom_call" | custom-call | flops 1000000 | bytes 4000000 | tf_op jit(solution)/shard_map/solve_x/pallas_call | solution.py:590
  (11 shorter events, 0.0 us)
Async XLA Ops:
  0.6 9.7 %copy-start.4 = (s32[128,512]{1,0:T(8,128)S(1)}, s32[128,512]{1,0:T(8,128)}, u32[]{:S(2)}) copy-start(s32[128,512]{1,0:T(8,128)} %m.3) | copy-start | bytes 786436
  0.6 9.7 %copy-start.3 = (f32[128,512]{1,0:T(8,128)S(1)}, f32[128,512]{1,0:T(8,128)}, u32[]{:S(2)}) copy-start(f32[128,512]{1,0:T(8,128)} %b.3) | copy-start | bytes 786436
  0.7 9.7 %copy-start.2 = (f32[128,512]{1,0:T(8,128)S(1)}, f32[128,512]{1,0:T(8,128)}, u32[]{:S(2)}) copy-start(f32[128,512]{1,0:T(8,128)} %q.3) | copy-start | bytes 786436
  0.7 9.7 %copy-start.1 = (f32[128,512]{1,0:T(8,128)S(1)}, f32[128,512]{1,0:T(8,128)}, u32[]{:S(2)}) copy-start(f32[128,512]{1,0:T(8,128)} %p.3) | copy-start | bytes 786436
  0.7 9.7 %copy-start = (f32[128,512]{1,0:T(8,128)S(1)}, f32[128,512]{1,0:T(8,128)}, u32[]{:S(2)}) copy-start(f32[128,512]{1,0:T(8,128)} %h.3) | copy-start | bytes 786436
  3.0 3.1 %collective-permute-start.2 = (f32[2,8,128]{2,1,0:T(8,128)}, f32[2,8,128]{2,1,0:T(8,128)S(1)}, u32[]{:S(2)}, u32[]{:S(2)}) collective-permute-start(f32[2,8,128]{2,1,0:T(8,128)} %get-tuple-element.32), channel_id=1, source_target_pairs={{0,1},{1,0},{2,3},{3,2},{4,5},{5,4},{6,7},{7,6},{8,9},{9,8},{10,11... | collective-permute-start | bytes 24584 | tf_op jit(solution)/shard_map/ppermute | solution.py:609
  3.6 4.8 %collective-permute-start = (f32[2,8,512]{2,1,0:T(8,128)}, f32[2,8,512]{2,1,0:T(8,128)S(1)}, u32[]{:S(2)}, u32[]{:S(2)}) collective-permute-start(f32[2,8,512]{2,1,0:T(8,128)} %get-tuple-element.31), channel_id=1, source_target_pairs={{0,4},{4,0},{8,12},{12,8},{16,20},{20,16},{24,28},{28,24},{1,5},{5... | collective-permute-start | bytes 98312 | tf_op jit(solution)/shard_map/ppermute | solution.py:609
  6.1 7.3 %collective-permute-start.3 = (f32[48,128]{1,0:T(8,128)S(1)}, f32[48,128]{1,0:T(8,128)S(1)}, u32[]{:S(2)}, u32[]{:S(2)}) collective-permute-start(f32[48,128]{1,0:T(8,128)S(1)} %pad.4), channel_id=1, source_target_pairs={{0,2},{1,0},{2,3},{3,1},{4,6},{5,4},{6,7},{7,5},{8,10},{9,8},{10,1... | collective-permute-start | bytes 73736 | tf_op jit(solution)/shard_map/ppermute | solution.py:605
  8.3 5.1 %collective-permute-start.1 = (f32[8,512]{1,0:T(8,128)S(1)}, f32[8,512]{1,0:T(8,128)S(1)}, u32[]{:S(2)}, u32[]{:S(2)}) collective-permute-start(f32[8,512]{1,0:T(8,128)S(1)} %slice_bitcast_fusion), channel_id=1, source_target_pairs={{0,8},{4,0},{8,16},{12,4},{16,24},{20,12},{24,28},{28,20},{1,9},{5... | collective-permute-start | bytes 49160 | tf_op jit(solution)/shard_map/ppermute | solution.py:605
  15.5 3.8 %collective-permute-start.4 = (f32[8,512]{1,0:T(8,128)S(1)}, f32[8,512]{1,0:T(8,128)S(1)}, u32[]{:S(2)}, u32[]{:S(2)}) collective-permute-start(f32[8,512]{1,0:T(8,128)S(1)} %get-tuple-element.54.mine.refs_0_), channel_id=1, source_target_pairs={{0,4},{4,0},{8,12},{12,8},{16,20},{20,16},{24,28},{28,24},{1,5},{5... | collective-permute-start | bytes 49160 | tf_op jit(solution)/shard_map/ppermute | solution.py:609
  16.1 1.5 %collective-permute-start.5 = (f32[8,128]{1,0:T(8,128)S(1)}, f32[8,128]{1,0:T(8,128)S(1)}, u32[]{:S(2)}, u32[]{:S(2)}) collective-permute-start(f32[8,128]{1,0:T(8,128)S(1)} %get-tuple-element.55.refs_0_), channel_id=1, source_target_pairs={{0,1},{1,0},{2,3},{3,2},{4,5},{5,4},{6,7},{7,6},{8,9},{9,8},{10,11... | collective-permute-start | bytes 12296 | tf_op jit(solution)/shard_map/ppermute | solution.py:609
  16.1 7.7 %collective-permute-start.9 = (f32[24,128]{1,0:T(8,128)S(1)}, f32[24,128]{1,0:T(8,128)S(1)}, u32[]{:S(2)}, u32[]{:S(2)}) collective-permute-start(f32[24,128]{1,0:T(8,128)S(1)} %get-tuple-element.58), channel_id=1, source_target_pairs={{0,2},{1,3},{2,0},{3,1},{4,6},{5,7},{6,4},{7,5},{8,10},{9,11},{10,... | collective-permute-start | bytes 36872 | tf_op jit(solution)/shard_map/ppermute | solution.py:609
  19.3 6.6 %collective-permute-start.8 = (f32[8,512]{1,0:T(8,128)S(1)}, f32[8,512]{1,0:T(8,128)S(1)}, u32[]{:S(2)}, u32[]{:S(2)}) collective-permute-start(f32[8,512]{1,0:T(8,128)S(1)} %merge.1.refs_2_), channel_id=1, source_target_pairs={{0,24},{4,28},{8,16},{12,20},{16,8},{20,12},{24,0},{28,4},{1,25},{... | collective-permute-start | bytes 49160 | tf_op jit(solution)/shard_map/ppermute | solution.py:609
  22.9 4.6 %collective-permute-start.7 = (f32[8,512]{1,0:T(8,128)S(1)}, f32[8,512]{1,0:T(8,128)S(1)}, u32[]{:S(2)}, u32[]{:S(2)}) collective-permute-start(f32[8,512]{1,0:T(8,128)S(1)} %merge.1.refs_2_), channel_id=1, source_target_pairs={{0,16},{4,20},{8,24},{12,28},{16,0},{20,4},{24,8},{28,12},{1,17},{... | collective-permute-start | bytes 49160 | tf_op jit(solution)/shard_map/ppermute | solution.py:609
  22.9 4.6 %collective-permute-start.6 = (f32[8,512]{1,0:T(8,128)S(1)}, f32[8,512]{1,0:T(8,128)S(1)}, u32[]{:S(2)}, u32[]{:S(2)}) collective-permute-start(f32[8,512]{1,0:T(8,128)S(1)} %merge.1.refs_2_), channel_id=1, source_target_pairs={{0,8},{4,12},{8,0},{12,4},{16,24},{20,28},{24,16},{28,20},{1,9},{5... | collective-permute-start | bytes 49160 | tf_op jit(solution)/shard_map/ppermute | solution.py:609
  23.8 1.2 %collective-permute-start.10 = (f32[8,128]{1,0:T(8,128)S(1)}, f32[8,128]{1,0:T(8,128)S(1)}, u32[]{:S(2)}, u32[]{:S(2)}) collective-permute-start(f32[8,128]{1,0:T(8,128)S(1)} %slice.14), channel_id=1, source_target_pairs={{0,1},{1,0},{2,3},{3,2},{4,5},{5,4},{6,7},{7,6},{8,9},{9,8},{10,11... | collective-permute-start | bytes 12296 | tf_op jit(solution)/shard_map/ppermute | solution.py:609

commit v5 on v4

--- a/solution.py
+++ b/solution.py
@@ -17,7 +17,6 @@
 HBM = pl.BlockSpec(memory_space=pltpu.HBM)
 ANY = pl.BlockSpec(memory_space=pl.ANY)
 PARAMS = pltpu.CompilerParams(vmem_limit_bytes=16 * 1024 * 1024)
-WHOLE = pltpu.CompilerParams(vmem_limit_bytes=62 * 1024 * 1024)
 
 
 def lane_index(shape):
@@ -45,25 +44,30 @@
     return jax.ShapeDtypeStruct(dims, F32)
 
 
-def pack_kernel(h, p, q, b, m, xa, ya, top, bottom, left, right, itop, ibottom, ileft, iright, sems):
+def pack_kernel(h, p, q, b, m, xa, ya, hs, ps, qs, bs, ms, top, bottom, itop, ibottom, sems_x, sems):
     rows, cols = h.shape
+    tiles = cols // LANES
     sources = (h, p, q, b, m)
-
-    def load(places, piece, first):
-        copies = []
-        for f, (src, target) in enumerate(zip(sources, places)):
-            copies.append(pltpu.make_async_copy(src.at[piece], target, sems.at[first + f]))
-            copies[-1].start()
-        return copies
-
-    def places(floats, whole):
-        return [floats.at[f] for f in range(4)] + [whole]
-
-    edges_x = load(places(top, itop), (pl.ds(0, SUB), slice(None)), 0)
-    edges_x += load(places(bottom, ibottom), (pl.ds(rows - SUB, SUB), slice(None)), 5)
-    edges_y = load(places(left, ileft), (slice(None), pl.ds(0, LANES)), 10)
-    edges_y += load(places(right, iright), (slice(None), pl.ds(cols - LANES, LANES)), 15)
-    for copy in edges_x:
+    stacks = (hs, ps, qs, bs, ms)
+    edges = []
+    for f, src in enumerate(sources):
+        for side, (target, whole, row) in enumerate(((top, itop, 0), (bottom, ibottom, rows - SUB))):
+            copy = pltpu.make_async_copy(
+                src.at[pl.ds(row, SUB), :], target.at[f] if f < 4 else whole, sems_x.at[2 * f + side]
+            )
+            copy.start()
+            edges.append(copy)
+    loads = {}
+    for tile in [0, tiles - 1] + list(range(1, tiles - 1)):
+        for f, (src, target) in enumerate(zip(sources, stacks)):
+            copy = pltpu.make_async_copy(
+                src.at[:, pl.ds(tile * LANES, LANES)],
+                target.at[pl.ds(tile * rows, rows), :],
+                sems.at[f * tiles + tile],
+            )
+            copy.start()
+            loads[tile, f] = copy
+    for copy in edges:
         copy.wait()
     first_x = jnp.concatenate(
         [top[0, 0:2, :], top[1, 0:2, :], top[2, 0:2, :], top[3, 0:1, :], itop[0:1, :].astype(F32)]
@@ -80,47 +84,58 @@
     even_x = lax.axis_index("gx") % 2 == 0
     xa[0] = jnp.where(even_x, last_x, first_x)
     xa[1] = jnp.where(even_x, first_x, last_x)
-    for copy in edges_y:
-        copy.wait()
     lane = lane_index((rows, LANES))
     out = jnp.zeros((rows, LANES), F32)
-    for block, mask, start, shifts in (
-        (left, ileft, 0, (0, 2, 4, 6, 7)),
-        (right, iright, SUB, (10, 12, 14, 15, 16)),
-    ):
-        fields = [block.at[f] for f in range(4)] + [mask]
-        for ref, to, shift in zip(fields, (0, 2, 4, 6, 7), shifts):
-            value = jnp.concatenate([ref[spread_rows(0, k), :] for k in range(STEPS)]).astype(F32)
+    for tile, start, shifts in ((0, 0, (0, 2, 4, 6, 7)), (tiles - 1, SUB, (10, 12, 14, 15, 16))):
+        for f, (ref, to, shift) in enumerate(zip(stacks, (0, 2, 4, 6, 7), shifts)):
+            loads[tile, f].wait()
+            value = jnp.concatenate([ref[spread_rows(tile, k), :] for k in range(STEPS)]).astype(F32)
             out = jnp.where(lane >= start + to, pltpu.roll(value, shift, 1) if shift else value, out)
     turned = out.T
     first_y, last_y = turned[0:SUB, :], turned[SUB : 2 * SUB, :]
     even_y = lax.axis_index("gy") % 2 == 0
     ya[0] = jnp.where(even_y, last_y, first_y)
     ya[1] = jnp.where(even_y, first_y, last_y)
-
-
-def pack(h, p, q, b, m):
-    rows, cols = h.shape
-    i32 = jnp.int32
+    for tile in range(1, tiles - 1):
+        for f in range(len(sources)):
+            loads[tile, f].wait()
+
+
+def pack(*fields):
+    rows, cols = fields[0].shape
+    tiles = cols // LANES
+    stacks = [jax.ShapeDtypeStruct((tiles * rows, LANES), v.dtype) for v in fields]
     return pl.pallas_call(
         pack_kernel,
-        out_shape=(shape(2, SUB, cols), shape(2, SUB, rows)),
+        out_shape=(shape(2, SUB, cols), shape(2, SUB, rows), *stacks),
         in_specs=[HBM] * 5,
-        out_specs=(VMEM,) * 2,
+        out_specs=(VMEM,) * 7,
         scratch_shapes=[
             pltpu.VMEM((4, SUB, cols), F32),
             pltpu.VMEM((4, SUB, cols), F32),
-            pltpu.VMEM((4, rows, LANES), F32),
-            pltpu.VMEM((4, rows, LANES), F32),
-            pltpu.VMEM((SUB, cols), i32),
-            pltpu.VMEM((SUB, cols), i32),
-            pltpu.VMEM((rows, LANES), i32),
-            pltpu.VMEM((rows, LANES), i32),
-            pltpu.SemaphoreType.DMA((20,)),
+            pltpu.VMEM((SUB, cols), jnp.int32),
+            pltpu.VMEM((SUB, cols), jnp.int32),
+            pltpu.SemaphoreType.DMA((10,)),
+            pltpu.SemaphoreType.DMA((5 * tiles,)),
         ],
-        compiler_params=WHOLE,
+        compiler_params=PARAMS,
         name="pack",
-    )(h, p, q, b, m)
+    )(*[pltpu.with_memory_space_constraint(v, pltpu.HBM) for v in fields])
+
+
+def tie_kernel(both, _, out):
+    out[...] = both[1]
+
+
+def second_of(both, after):
+    return pl.pallas_call(
+        tie_kernel,
+        out_shape=shape(*both.shape[1:]),
+        in_specs=[VMEM, VMEM],
+        out_specs=VMEM,
+        compiler_params=PARAMS,
+        name="second_of",
+    )(both, after)
 
 
 def merge_coefficients(one, two):
@@ -176,75 +191,71 @@
     return coefficients
 
 
-def prepare_kernel(
-    h, p, q, b, m,
-    hx, px, qx, bx, mx, ix, hy, py, qy, by, my, iy, tx, wx, ty, wy, endx, endy,
-    hs, ps, qs, bs, ms, turned, sems,
-    *, inv_cx, inv_cy,
-):
-    rows, cols = h.shape
-    tiles = cols // LANES
-    copies = []
-    for f, (src, target) in enumerate(zip((h, p, q, b, m), (hs, ps, qs, bs, ms))):
+def lay_out(src, xs, ys, turned):
+    for tile in range(src.shape[0] // LANES):
+        for k in range(STEPS):
+            xs[at(tile, k), :] = src[spread_rows(tile, k), :].astype(F32)
+        turned[tile_span(tile), :] = xs[tile_span(tile), :].T
+        for k in range(STEPS):
+            ys[at(tile, k), :] = turned[spread_rows(tile, k), :]
+
+
+def prepare_depth_kernel(hs, hx, hy, ix, iy, tx, wx, ty, wy, endx, endy, turned, *, inv_cx, inv_cy):
+    tiles = hs.shape[0] // LANES
+    lay_out(hs, hx, hy, turned)
+    ix[...] = 1.0 / hx[...]
+    iy[...] = 1.0 / hy[...]
+    ends_x = march_depth(ix, inv_cx, tx, wx, log2(SUB))
+    ends_y = march_depth(iy, inv_cy, ty, wy, log2(SUB * tiles))
+    for i in range(3):
         for tile in range(tiles):
-            copies.append(
-                pltpu.make_async_copy(
-                    src.at[:, pl.ds(tile * LANES, LANES)],
-                    target.at[pl.ds(tile * rows, rows), :],
-                    sems.at[f * tiles + tile],
-                )
-            )
-            copies[-1].start()
-    for f, (src, xs, ys) in enumerate(
-        ((hs, hx, hy), (ps, px, py), (qs, qx, qy), (bs, bx, by), (ms, mx, my))
-    ):
-        for tile in range(tiles):
-            copies[f * tiles + tile].wait()
-            for k in range(STEPS):
-                xs[at(tile, k), :] = src[spread_rows(tile, k), :].astype(F32)
-            turned[f % 2, tile_span(tile), :] = xs[tile_span(tile), :].T
-            for k in range(STEPS):
-                ys[at(tile, k), :] = turned[f % 2, spread_rows(tile, k), :]
-        if f == 0:
-            ix[...] = 1.0 / hx[...]
-            iy[...] = 1.0 / hy[...]
-            ends_x = march_depth(ix, inv_cx, tx, wx, log2(SUB))
-            ends_y = march_depth(iy, inv_cy, ty, wy, log2(SUB * tiles))
-            for i in range(3):
-                for tile in range(tiles):
-                    endx[i : i + 1, tile_span(tile)] = ends_x[i][tile * SUB : tile * SUB + 1, :]
-                endy[i : i + 1, :] = ends_y[i][0:1, :]
-            endx[3:8, :] = jnp.zeros((5, cols), F32)
-            endy[3:8, :] = jnp.zeros((5, rows), F32)
-
-
-def prepare(h, p, q, b, m, inv_cx, inv_cy):
-    rows, cols = h.shape
-    tiles = cols // LANES
-    count = tiles * SUB
-    stack = (tiles * LANES, LANES)
-    shapes = [shape(*stack)] * 12 + [
+            endx[i : i + 1, tile_span(tile)] = ends_x[i][tile * SUB : tile * SUB + 1, :]
+        endy[i : i + 1, :] = ends_y[i][0:1, :]
+    endx[3:8, :] = jnp.zeros((5, endx.shape[1]), F32)
+    endy[3:8, :] = jnp.zeros((5, endy.shape[1]), F32)
+
+
+def prepare_depth(hs, inv_cx, inv_cy):
+    stack = hs.shape
+    count = stack[0] // STEPS
+    shapes = [shape(*stack)] * 4 + [
         shape(3, count, LANES),
         shape(3 * log2(SUB), count, LANES),
         shape(3, count, LANES),
         shape(3 * log2(count), count, LANES),
-        shape(SUB, cols),
-        shape(SUB, rows),
+        shape(SUB, stack[0]),
+        shape(SUB, LANES),
     ]
     return pl.pallas_call(
-        functools.partial(prepare_kernel, inv_cx=inv_cx, inv_cy=inv_cy),
+        functools.partial(prepare_depth_kernel, inv_cx=inv_cx, inv_cy=inv_cy),
         out_shape=tuple(shapes),
-        in_specs=[HBM] * 5,
+        in_specs=[VMEM],
         out_specs=(VMEM,) * len(shapes),
-        scratch_shapes=[
-            *[pltpu.VMEM(stack, v.dtype) for v in (h, p, q, b, m)],
-            pltpu.VMEM((2, *stack), F32),
-            pltpu.SemaphoreType.DMA((5 * tiles,)),
-        ],
-        compiler_params=PARAMS,
-        cost_estimate=pl.CostEstimate(flops=2_000_000, bytes_accessed=8_000_000, transcendentals=0),
-        name="prepare",
-    )(h, p, q, b, m)
+        scratch_shapes=[pltpu.VMEM(stack, F32)],
+        compiler_params=PARAMS,
+        cost_estimate=pl.CostEstimate(flops=2_000_000, bytes_accessed=4_000_000, transcendentals=0),
+        name="prepare_depth",
+    )(hs)
+
+
+def prepare_rest_kernel(*refs):
+    sources, outs, turned = refs[:4], refs[4:12], refs[12]
+    for f, src in enumerate(sources):
+        lay_out(src, outs[2 * f], outs[2 * f + 1], turned.at[f % 2])
+
+
+def prepare_rest(*sources):
+    stack = sources[0].shape
+    return pl.pallas_call(
+        prepare_rest_kernel,
+        out_shape=(shape(*stack),) * 8,
+        in_specs=[VMEM] * 4,
+        out_specs=(VMEM,) * 8,
+        scratch_shapes=[pltpu.VMEM((2, *stack), F32)],
+        compiler_params=PARAMS,
+        cost_estimate=pl.CostEstimate(flops=2_000_000, bytes_accessed=6_000_000, transcendentals=0),
+        name="prepare_rest",
+    )(*sources)
 
 
 def low_high(axis, near, far):
@@ -325,68 +336,77 @@
     return sources
 
 
-def flux_kernel(
-    near_x, far_x, near_y, far_y,
-    hx, px, qx, bx, mx, ix, hy, py, qy, by, my, iy, tx, wx, ty, wy, coefx, coefy,
-    depth, rx, ry, sx, sy, endx, endy, tally,
-    xpart, ypart, turned,
-    *, inv_cx, inv_cy,
-):
-    tiles = hx.shape[0] // LANES
-    low_x, high_x = low_high("gx", near_x[0], far_x[0:SUB, :])
-    low_y, high_y = low_high("gy", near_y[0], far_y[0:SUB, :])
-
+def flux_y_kernel(near, far, hy, py, qy, by, my, mass, shear, normal, across, along):
+    tiles = hy.shape[0] // LANES
+    low, high = low_high("gy", near[0], far[0:SUB, :])
     for tile in range(tiles):
-        span = tile_span(tile)
-
-        def along_x(ref, row, layers):
-            lows = [low_x[row + layers - 1 - n : row + layers - n, span] for n in range(layers)]
-            highs = [high_x[row + n : row + n + 1, span] for n in range(layers)]
-            return extended(ref, tile, lows, highs)
-
-        def store_x(k, difference, bed):
-            here = at(tile, k)
-            for i in range(3):
-                xpart[i, here, :] = difference[i]
-            xpart[3, here, :] = bed
-
-        tile_fluxes(
-            [along_x(hx, 0, 2), along_x(px, 2, 2), along_x(qx, 4, 2)],
-            along_x(bx, 6, 1), along_x(mx, 7, 1), store_x,
-        )
-
-        def along_y(ref, row, layers):
+
+        def extend(ref, row, layers):
             lows, highs = [], []
             for n in range(layers):
                 last = at(tile - 1, STEPS - 1 - n).stop - 1
                 first = at(tile + 1, n).start
-                lows.append(low_y[row + layers - 1 - n : row + layers - n, :] if tile == 0 else ref[last : last + 1, :])
-                highs.append(high_y[row + n : row + n + 1, :] if tile == tiles - 1 else ref[first : first + 1, :])
+                lows.append(low[row + layers - 1 - n : row + layers - n, :] if tile == 0 else ref[last : last + 1, :])
+                highs.append(high[row + n : row + n + 1, :] if tile == tiles - 1 else ref[first : first + 1, :])
             return extended(ref, tile, lows, highs)
 
-        def store_y(k, difference, bed):
+        def store(k, difference, bed):
             here, natural = at(tile, k), spread_rows(tile, k)
-            ypart[0, natural, :] = difference[0]
-            ypart[1, here, :] = difference[1]
-            ypart[2, natural, :] = difference[2]
-            ypart[3, here, :] = bed
-
-        tile_fluxes(
-            [along_y(hy, 0, 2), along_y(qy, 4, 2), along_y(py, 2, 2)],
-            along_y(by, 6, 1), along_y(my, 7, 1), store_y,
-        )
-        turned[span, :] = xpart[2, span, :].T
-        from_y_mass = ypart[0, span, :].T
-        from_y_shear = ypart[2, span, :].T
-        h, m, inverse = hx[span, :], mx[span, :], ix[span, :]
-        depth[span, :] = h - m * (xpart[0, span, :] + from_y_mass)
-        push = px[span, :] - xpart[1, span, :] - from_y_shear - (0.5 * ratio * gravity) * h * xpart[3, span, :]
-        rx[span, :] = (inv_cx * (inverse * inverse)) * m * push
+            across[natural, :] = difference[0]
+            along[natural, :] = difference[2]
+            pull = (0.5 * ratio * gravity) * hy[here, :]
+            normal[here, :] = qy[here, :] - difference[1] - pull * bed
+
+        tile_fluxes([extend(hy, 0, 2), extend(qy, 4, 2), extend(py, 2, 2)], extend(by, 6, 1), extend(my, 7, 1), store)
+        span = tile_span(tile)
+        mass[span, :] = across[span, :].T
+        shear[span, :] = along[span, :].T
+
+
+def fluxes_y(*arrays):
+    stack = arrays[2].shape
+    return pl.pallas_call(
+        flux_y_kernel,
+        out_shape=(shape(*stack),) * 3,
+        in_specs=[VMEM] * len(arrays),
+        out_specs=(VMEM,) * 3,
+        scratch_shapes=[pltpu.VMEM(stack, F32)] * 2,
+        compiler_params=PARAMS,
+        cost_estimate=pl.CostEstimate(flops=4_000_000, bytes_accessed=4_000_000, transcendentals=0),
+        name="fluxes_y",
+    )(*arrays)
+
+
+def flux_x_kernel(
+    near, far, hx, px, qx, bx, mx, ix, iy, my, mass_y, shear_y, normal_y, tx, wx, ty, wy, coefx, coefy,
+    depth, rx, ry, sx, sy, endx, endy, tally,
+    across, turned,
+    *, inv_cx, inv_cy,
+):
+    tiles = hx.shape[0] // LANES
+    low, high = low_high("gx", near[0], far[...])
+    for tile in range(tiles):
+        span = tile_span(tile)
+
+        def extend(ref, row, layers):
+            lows = [low[row + layers - 1 - n : row + layers - n, span] for n in range(layers)]
+            highs = [high[row + n : row + n + 1, span] for n in range(layers)]
+            return extended(ref, tile, lows, highs)
+
+        def store(k, difference, bed):
+            here = at(tile, k)
+            h, m, inverse = hx[here, :], mx[here, :], ix[here, :]
+            depth[here, :] = h - m * (difference[0] + mass_y[here, :])
+            push = px[here, :] - difference[1] - shear_y[here, :] - (0.5 * ratio * gravity) * h * bed
+            rx[here, :] = (inv_cx * (inverse * inverse)) * m * push
+            across[here, :] = difference[2]
+
+        tile_fluxes([extend(hx, 0, 2), extend(px, 2, 2), extend(qx, 4, 2)], extend(bx, 6, 1), extend(mx, 7, 1), store)
+        turned[span, :] = across[span, :].T
         for k in range(STEPS):
             here = at(tile, k)
             inverse = iy[here, :]
-            push = qy[here, :] - turned[spread_rows(tile, k), :] - ypart[1, here, :]
-            push = push - (0.5 * ratio * gravity) * hy[here, :] * ypart[3, here, :]
+            push = normal_y[here, :] - turned[spread_rows(tile, k), :]
             ry[here, :] = (inv_cy * (inverse * inverse)) * my[here, :] * push
 
     ends_x = march_source(ix, inv_cx, rx, tx, wx, sx, log2(SUB))
@@ -401,8 +421,8 @@
     tally[0:SUB, :] = endy[...]
 
 
-def fluxes(slabs, prepared, inv_cx, inv_cy):
-    stack = prepared[0].shape
+def fluxes_x(*arrays, inv_cx, inv_cy):
+    stack = arrays[2].shape
     count = stack[0] // STEPS
     shapes = (
         shape(*stack),
@@ -410,23 +430,19 @@
         shape(*stack),
         shape(1 + log2(SUB), count, LANES),
         shape(1 + log2(count), count, LANES),
-        shape(*prepared[-2].shape),
-        shape(*prepared[-1].shape),
-        shape(3 * SUB, prepared[-1].shape[1]),
+        shape(*arrays[-2].shape),
+        shape(*arrays[-1].shape),
+        shape(3 * SUB, arrays[-1].shape[1]),
     )
     return pl.pallas_call(
-        functools.partial(flux_kernel, inv_cx=inv_cx, inv_cy=inv_cy),
+        functools.partial(flux_x_kernel, inv_cx=inv_cx, inv_cy=inv_cy),
         out_shape=shapes,
-        in_specs=[VMEM] * (len(slabs) + len(prepared)),
+        in_specs=[VMEM] * len(arrays),
         out_specs=(VMEM,) * len(shapes),
-        scratch_shapes=[
-            pltpu.VMEM((4, *stack), F32),
-            pltpu.VMEM((4, *stack), F32),
-            pltpu.VMEM(stack, F32),
-        ],
-        compiler_params=PARAMS,
-        name="fluxes",
-    )(*slabs, *prepared)
+        scratch_shapes=[pltpu.VMEM(stack, F32)] * 2,
+        compiler_params=PARAMS,
+        name="fluxes_x",
+    )(*arrays)
 
 
 def tile_write(tiled, whole, tile, sems):
@@ -621,9 +637,7 @@
         second = cross(mine if tall is None else tall, axis, 2 << last)
         both = cross(second[0:SUB], axis, 1 << last)
     else:
-        both = cross(mine, axis, 3 << last)
-        second = cross(mine, axis, 2 << last)
-        first = cross(mine, axis, 1 << last)
+        first, second, both = (cross(mine, axis, n << last) for n in (1, 2, 3))
     return parts + [mine, first, second, both]
 
 
@@ -632,14 +646,17 @@
     rows, cols = block
     inv_cx = 3.0 / (rows * lax.axis_size("gx") / 4.0) ** 2
     inv_cy = 3.0 / (cols * lax.axis_size("gy") / 4.0) ** 2
-    xa, ya = pack(h, p, q, b, m)
+    xa, ya, hs, ps, qs, bs, ms = pack(h, p, q, b, m)
     near_x, near_y = cross(xa, "gx", 1), cross(ya, "gy", 1)
     far_y = hand_on(jnp.pad(near_y[1], ((0, 5 * SUB), (0, 0))), "gy")
-    far_x = hand_on(near_x[1], "gx")
-    prepared = prepare(h, p, q, b, m, inv_cx, inv_cy)
-    depth, rx, ry, sx, sy, end_x, end_y, tall_y = fluxes((near_x, far_x, near_y, far_y), prepared, inv_cx, inv_cy)
-    ix, iy = prepared[5], prepared[11]
-    tx, wx, ty, wy = prepared[12:16]
+    hx, hy, ix, iy, tx, wx, ty, wy, coef_x, coef_y = prepare_depth(hs, inv_cx, inv_cy)
+    far_x = hand_on(second_of(near_x, coef_x), "gx")
+    px, py, qx, qy, bx, by, mx, my = prepare_rest(ps, qs, bs, ms)
+    mass_y, shear_y, normal_y = fluxes_y(near_y, far_y, hy, py, qy, by, my)
+    depth, rx, ry, sx, sy, end_x, end_y, tall_y = fluxes_x(
+        near_x, far_x, hx, px, qx, bx, mx, ix, iy, my, mass_y, shear_y, normal_y,
+        tx, wx, ty, wy, coef_x, coef_y, inv_cx=inv_cx, inv_cy=inv_cy,
+    )
     new_depth = write_depth(depth, block)
     parts_y = parts_of_line("gy", end_y, True, tall=tall_y if lax.axis_size("gy") == 4 else None)
     parts_x = parts_of_line("gx", end_x, False, parts_y[1:2])

time: 28.6 us -> 28.3 us (0.990)
  Pallas kernels: 10.1 us -> 8.42 us
  starting transfers between devices: 13.2 us -> 14.8 us
    pallas_call x2 -> x5, Pallas kernels: 5.1 us -> 3.3 us  [the longest x1 1.25 us: fluxes_x(): pl.pallas_call(functools.partial(flux_x_kernel, inv_cx=inv_cx, inv_cy=inv...]
    ppermute x9, starting transfers between devices: 9.65 us -> 11.3 us  [cross(): lax.ppermute(value, axis, [(i, i ^ mask) for i in range(lax.axis_size(axi...]
    ppermute x9, waiting for transfers between devices: 4.32 us -> 4.02 us  [cross(): lax.ppermute(value, axis, [(i, i ^ mask) for i in range(lax.axis_size(axi...]
  transfers between devices with their start and end apart: 11 -> 11, of which waited for: 4 -> 4; matrix products, arithmetic and copies ran while one was open for 0% -> 0% of each run, Pallas kernels for 17% -> 14%
where the time goes in v5:
time: 28.3 us; the launch traced here: 28.1 us
  starting transfers between devices  14.8 us (52%)
  Pallas kernels  8.42 us (30%)
  waiting for transfers between devices  4.09 us (14%)
  between operations  0.72 us (3%)
    ppermute x9, starting transfers between devices, cross(): lax.ppermute(value, axis, [(i, i ^ mask) for i in range(lax.axis_size(axi...  11.3 us
    ppermute x9, waiting for transfers between devices, cross(): lax.ppermute(value, axis, [(i, i ^ mask) for i in range(lax.axis_size(axi...  4.02 us
    ppermute x2, starting transfers between devices, hand_on(): lax.ppermute(value, axis, [(i, t if 0 <= t < count else i ^ 1) for i, t i...  3.55 us
    pallas_call x1, Pallas kernels, pack(): pl.pallas_call(pack_kernel, out_shape=(shape(2, SUB, cols), shape(2, SUB,...  2.43 us
    pallas_call x2, Pallas kernels, solve(): pl.pallas_call(functools.partial(kernel, scale=scale), out_shape=shape(*b...  1.93 us
    pallas_call x1, Pallas kernels, fluxes_x(): pl.pallas_call(functools.partial(flux_x_kernel, inv_cx=inv_cx, inv_cy=inv...  1.25 us
    pallas_call x1, Pallas kernels, fluxes_y(): pl.pallas_call(flux_y_kernel, out_shape=(shape(*stack),) * 3, in_specs=[V...  0.98 us
    pallas_call x1, Pallas kernels, write_depth(): pl.pallas_call(depth_kernel, out_shape=shape(*block), in_specs=[VMEM], ou...  0.75 us
  transfers between devices with their start and end apart: 11, of which 4 were waited for; matrix products, arithmetic and copies ran while one was open for 0% of the time, Pallas kernels for 14%

profile of v5, /device:TPU:0, one launch (start us, length us, event | category | flops | bytes accessed | tf_op | source)
XLA Modules:
  0.0 28.1 jit_solution(16313749300928794992)
XLA Ops:
  0.6 2.4 %pack.1 = (f32[2,8,512]{2,1,0:T(8,128)S(1)}, f32[2,8,128]{2,1,0:T(8,128)S(1)}, f32[512,128]{1,0:T(8,128)S(1)}, f32[512,128]{1,0:T(8,128)S(1)}, f32[512,128]{1,0:...) custom-call(f32[128,512]{1,0:T(8,128)} %h.1, f32[128,512]{1,0:T(8,128)} %p.1, f32[128,512]{1,0:T(8,128)} %q.1, ...), custom_call_target="tpu_custom_call" | custom-call | tf_op jit(solution)/shard_map/pack/pallas_call | solution.py:108
  3.1 0.5 %collective-permute-start.2 = (f32[2,8,128]{2,1,0:T(8,128)S(1)}, f32[2,8,128]{2,1,0:T(8,128)S(1)}, u32[]{:S(2)}, u32[]{:S(2)}) collective-permute-start(f32[2,8,128]{2,1,0:T(8,128)S(1)} %get-tuple-element.54), channel_id=1, source_target_pairs={{0,1},{1,0},{2,3},{3,2},{4,5},{5,4},{6,7},{7,6},{8,9},{9,8},{10,11... | collective-permute-start | bytes 24584 | tf_op jit(solution)/shard_map/ppermute | solution.py:625
  3.6 2.6 %collective-permute-start = (f32[2,8,512]{2,1,0:T(8,128)S(1)}, f32[2,8,512]{2,1,0:T(8,128)S(1)}, u32[]{:S(2)}, u32[]{:S(2)}) collective-permute-start(f32[2,8,512]{2,1,0:T(8,128)S(1)} %get-tuple-element.39), channel_id=1, source_target_pairs={{0,4},{4,0},{8,12},{12,8},{16,20},{20,16},{24,28},{28,24},{1,5},{5... | collective-permute-start | bytes 98312 | tf_op jit(solution)/shard_map/ppermute | solution.py:625
  6.2 0.0 collective-permute-done.2.near
  6.2 1.5 %collective-permute-start.3 = (f32[48,128]{1,0:T(8,128)S(1)}, f32[48,128]{1,0:T(8,128)S(1)}, u32[]{:S(2)}, u32[]{:S(2)}) collective-permute-start(f32[48,128]{1,0:T(8,128)S(1)} %pad.4), channel_id=1, source_target_pairs={{0,2},{1,0},{2,3},{3,1},{4,6},{5,4},{6,7},{7,5},{8,10},{9,8},{10,1... | collective-permute-start | bytes 73736 | tf_op jit(solution)/shard_map/ppermute | solution.py:621
  7.7 0.4 %prepare_depth.1 = (f32[512,128]{1,0:T(8,128)S(1)}, f32[512,128]{1,0:T(8,128)S(1)}, f32[512,128]{1,0:T(8,128)S(1)}, f32[512,128]{1,0:T(8,128)S(1)}, f32[3,32,128...) custom-call(f32[512,128]{1,0:T(8,128)S(1)} %get-tuple-element.40.hs), custom_call_target="tpu_custom_call" | custom-call | flops 2000000 | bytes 4000000 | tf_op jit(solution)/shard_map/prepare_depth/pallas_call | solution.py:229
  8.1 0.0 collective-permute-done.both.near
  8.1 2.0 %collective-permute-start.1 = (f32[8,512]{1,0:T(8,128)S(1)}, f32[8,512]{1,0:T(8,128)S(1)}, u32[]{:S(2)}, u32[]{:S(2)}) collective-permute-start(f32[8,512]{1,0:T(8,128)S(1)} %second_of.1), channel_id=1, source_target_pairs={{0,8},{4,0},{8,16},{12,4},{16,24},{20,12},{24,28},{28,20},{1,9},{5... | collective-permute-start | bytes 49160 | tf_op jit(solution)/shard_map/ppermute | solution.py:621
  10.2 0.7 %prepare_rest.1 = (f32[512,128]{1,0:T(8,128)S(1)}, f32[512,128]{1,0:T(8,128)S(1)}, f32[512,128]{1,0:T(8,128)S(1)}, f32[512,128]{1,0:T(8,128)S(1)}, f32[512,128]{...) custom-call(f32[512,128]{1,0:T(8,128)S(1)} %get-tuple-element.43.refs_0_, ...), custom_call_target="tpu_custom_call" | custom-call | flops 2000000 | bytes 6000000 | tf_op jit(solution)/shard_map/prepare_rest/pallas_call | solution.py:249
  10.8 0.0 collective-permute-done.3.far
  10.8 1.0 %fluxes_y.1 = (f32[512,128]{1,0:T(8,128)S(1)}, f32[512,128]{1,0:T(8,128)S(1)}, f32[512,128]{1,0:T(8,128)S(1)}) custom-call(f32[2,8,128]{2,1,0:T(8,128)S(1)} %collective-permute-done.2.near, f32[48,128]{1,0:T(8,128)S(1)} %collective-permute-done.3.far, f32[512,128]{1,0:T(8,128)S(1)} %get-tuple-element.55.hy, f32[512,128]{1,0:T(8,128)S(1)} %get-tuple-element.56.py, ...), custom_call_target="tpu_custom_call" | custom-call | flops 4000000 | bytes 4000000 | tf_op jit(solution)/shard_map/fluxes_y/pallas_call | solution.py:368
  11.8 0.1 collective-permute-done.1.far
  11.9 1.2 %fluxes_x.1 = (f32[512,128]{1,0:T(8,128)S(1)}, f32[512,128]{1,0:T(8,128)S(1)}, f32[512,128]{1,0:T(8,128)S(1)}, f32[4,32,128]{2,1,0:T(8,128)S(1)}, f32[6,32,128]{...) custom-call(f32[2,8,512]{2,1,0:T(8,128)S(1)} %collective-permute-done.both.near, ...), custom_call_target="tpu_custom_call" | custom-call | tf_op jit(solution)/shard_map/fluxes_x/pallas_call | solution.py:437
  13.2 2.0 %collective-permute-start.4 = (f32[8,512]{1,0:T(8,128)S(1)}, f32[8,512]{1,0:T(8,128)S(1)}, u32[]{:S(2)}, u32[]{:S(2)}) collective-permute-start(f32[8,512]{1,0:T(8,128)S(1)} %get-tuple-element.70.mine.refs_0_), channel_id=1, source_target_pairs={{0,4},{4,0},{8,12},{12,8},{16,20},{20,16},{24,28},{28,24},{1,5},{5... | collective-permute-start | bytes 49160 | tf_op jit(solution)/shard_map/ppermute | solution.py:625
  15.1 0.0 collective-permute-start.5
  15.1 1.5 %collective-permute-start.9 = (f32[24,128]{1,0:T(8,128)S(1)}, f32[24,128]{1,0:T(8,128)S(1)}, u32[]{:S(2)}, u32[]{:S(2)}) collective-permute-start(f32[24,128]{1,0:T(8,128)S(1)} %get-tuple-element.74), channel_id=1, source_target_pairs={{0,2},{1,3},{2,0},{3,1},{4,6},{5,7},{6,4},{7,5},{8,10},{9,11},{10,... | collective-permute-start | bytes 36872 | tf_op jit(solution)/shard_map/ppermute | solution.py:625
  16.6 0.0 collective-permute-done.5.refs_0_.refs_1_
  16.6 0.3 %collective-permute-done.4.theirs.refs_1_ = f32[8,512]{1,0:T(8,128)S(1)} collective-permute-done((f32[8,512]{1,0:T(8,128)S(1)}, f32[8,512]{1,0:T(8,128)S(1)}, u32[]{:S(2)}, u32[]{:S(2)}) %collective-permute-start.4) | collective-permute-done | bytes 16416 | tf_op jit(solution)/shard_map/ppermute | solution.py:625
  17.0 2.1 %collective-permute-start.6 = (f32[8,512]{1,0:T(8,128)S(1)}, f32[8,512]{1,0:T(8,128)S(1)}, u32[]{:S(2)}, u32[]{:S(2)}) collective-permute-start(f32[8,512]{1,0:T(8,128)S(1)} %merge.1.refs_2_), channel_id=1, source_target_pairs={{0,8},{4,12},{8,0},{12,4},{16,24},{20,28},{24,16},{28,20},{1,9},{5... | collective-permute-start | bytes 49160 | tf_op jit(solution)/shard_map/ppermute | solution.py:625
  19.0 2.6 %collective-permute-start.7 = (f32[8,512]{1,0:T(8,128)S(1)}, f32[8,512]{1,0:T(8,128)S(1)}, u32[]{:S(2)}, u32[]{:S(2)}) collective-permute-start(f32[8,512]{1,0:T(8,128)S(1)} %merge.1.refs_2_), channel_id=1, source_target_pairs={{0,16},{4,20},{8,24},{12,28},{16,0},{20,4},{24,8},{28,12},{1,17},{... | collective-permute-start | bytes 49160 | tf_op jit(solution)/shard_map/ppermute | solution.py:625
  21.6 0.0 collective-permute-start.8
  21.6 0.0 collective-permute-done.9.refs_2_
  21.6 0.1 collective-permute-start.10
  21.7 0.7 %write_depth.1 = f32[128,512]{1,0:T(8,128)} custom-call(f32[512,128]{1,0:T(8,128)S(1)} %get-tuple-element.67.depth), custom_call_target="tpu_custom_call" | custom-call | flops 100000 | bytes 2000000 | tf_op jit(solution)/shard_map/write_depth/pallas_call | solution.py:471
  22.5 0.4 %collective-permute-done.10.refs_3_ = f32[8,128]{1,0:T(8,128)S(1)} collective-permute-done((f32[8,128]{1,0:T(8,128)S(1)}, f32[8,128]{1,0:T(8,128)S(1)}, u32[]{:S(2)}, u32[]{:S(2)}) %collective-permute-start.10) | collective-permute-done | bytes 4128 | tf_op jit(solution)/shard_map/ppermute | solution.py:625
  22.9 1.0 %solve_y.1 = f32[128,512]{1,0:T(8,128)} custom-call(f32[512,128]{1,0:T(8,128)S(1)} %get-tuple-element.52.iy.inv_ref, f32[512,128]{1,0:T(8,128)S(1)} %get-tuple-element.72.r_ref, f32[3,32,128]{2,1,0:T(8,128)S(1)} %get-tuple-element.64.ty.t_ref, f32[15,32,128]{2,1,0:T(8,128)S(1)} %get-tuple-element.65.wy.w_ref, f32[6,32,128]{2,1,0:T(8,128)S(1)} %get-tuple-element.73.s_ref, ...), custom_call_target="tpu_custom_call" | custom-call | flops 1000000 | bytes 4000000 | tf_op jit(solution)/shard_map/solve_y/pallas_call | solution.py:606
  23.9 0.0 collective-permute-done.6.refs_3_
  23.9 0.0 collective-permute-done.7.refs_4_
  23.9 3.3 %collective-permute-done.8.refs_5_ = f32[8,512]{1,0:T(8,128)S(1)} collective-permute-done((f32[8,512]{1,0:T(8,128)S(1)}, f32[8,512]{1,0:T(8,128)S(1)}, u32[]{:S(2)}, u32[]{:S(2)}) %collective-permute-start.8) | collective-permute-done | bytes 16416 | tf_op jit(solution)/shard_map/ppermute | solution.py:625
  27.2 0.9 %solve_x.1 = f32[128,512]{1,0:T(8,128)} custom-call(f32[512,128]{1,0:T(8,128)S(1)} %get-tuple-element.51.ix.inv_ref, f32[512,128]{1,0:T(8,128)S(1)} %get-tuple-element.68.r_ref, f32[3,32,128]{2,1,0:T(8,128)S(1)} %get-tuple-element.62.tx.t_ref, f32[9,32,128]{2,1,0:T(8,128)S(1)} %get-tuple-element.63.wx.w_ref, f32[4,32,128]{2,1,0:T(8,128)S(1)} %get-tuple-element.69.s_ref, ...), custom_call_target="tpu_custom_call" | custom-call | flops 1000000 | bytes 4000000 | tf_op jit(solution)/shard_map/solve_x/pallas_call | solution.py:606
  (5 shorter events, 0.0 us)
Async XLA Ops:
  3.1 3.1 %collective-permute-start.2 = (f32[2,8,128]{2,1,0:T(8,128)S(1)}, f32[2,8,128]{2,1,0:T(8,128)S(1)}, u32[]{:S(2)}, u32[]{:S(2)}) collective-permute-start(f32[2,8,128]{2,1,0:T(8,128)S(1)} %get-tuple-element.54), channel_id=1, source_target_pairs={{0,1},{1,0},{2,3},{3,2},{4,5},{5,4},{6,7},{7,6},{8,9},{9,8},{10,11... | collective-permute-start | bytes 24584 | tf_op jit(solution)/shard_map/ppermute | solution.py:625
  3.6 4.5 %collective-permute-start = (f32[2,8,512]{2,1,0:T(8,128)S(1)}, f32[2,8,512]{2,1,0:T(8,128)S(1)}, u32[]{:S(2)}, u32[]{:S(2)}) collective-permute-start(f32[2,8,512]{2,1,0:T(8,128)S(1)} %get-tuple-element.39), channel_id=1, source_target_pairs={{0,4},{4,0},{8,12},{12,8},{16,20},{20,16},{24,28},{28,24},{1,5},{5... | collective-permute-start | bytes 98312 | tf_op jit(solution)/shard_map/ppermute | solution.py:625
  6.2 4.7 %collective-permute-start.3 = (f32[48,128]{1,0:T(8,128)S(1)}, f32[48,128]{1,0:T(8,128)S(1)}, u32[]{:S(2)}, u32[]{:S(2)}) collective-permute-start(f32[48,128]{1,0:T(8,128)S(1)} %pad.4), channel_id=1, source_target_pairs={{0,2},{1,0},{2,3},{3,1},{4,6},{5,4},{6,7},{7,5},{8,10},{9,8},{10,1... | collective-permute-start | bytes 73736 | tf_op jit(solution)/shard_map/ppermute | solution.py:621
  8.1 3.8 %collective-permute-start.1 = (f32[8,512]{1,0:T(8,128)S(1)}, f32[8,512]{1,0:T(8,128)S(1)}, u32[]{:S(2)}, u32[]{:S(2)}) collective-permute-start(f32[8,512]{1,0:T(8,128)S(1)} %second_of.1), channel_id=1, source_target_pairs={{0,8},{4,0},{8,16},{12,4},{16,24},{20,12},{24,28},{28,20},{1,9},{5... | collective-permute-start | bytes 49160 | tf_op jit(solution)/shard_map/ppermute | solution.py:621
  13.2 3.8 %collective-permute-start.4 = (f32[8,512]{1,0:T(8,128)S(1)}, f32[8,512]{1,0:T(8,128)S(1)}, u32[]{:S(2)}, u32[]{:S(2)}) collective-permute-start(f32[8,512]{1,0:T(8,128)S(1)} %get-tuple-element.70.mine.refs_0_), channel_id=1, source_target_pairs={{0,4},{4,0},{8,12},{12,8},{16,20},{20,16},{24,28},{28,24},{1,5},{5... | collective-permute-start | bytes 49160 | tf_op jit(solution)/shard_map/ppermute | solution.py:625
  15.1 1.5 %collective-permute-start.5 = (f32[8,128]{1,0:T(8,128)S(1)}, f32[8,128]{1,0:T(8,128)S(1)}, u32[]{:S(2)}, u32[]{:S(2)}) collective-permute-start(f32[8,128]{1,0:T(8,128)S(1)} %get-tuple-element.71.refs_0_), channel_id=1, source_target_pairs={{0,1},{1,0},{2,3},{3,2},{4,5},{5,4},{6,7},{7,6},{8,9},{9,8},{10,11... | collective-permute-start | bytes 12296 | tf_op jit(solution)/shard_map/ppermute | solution.py:625
  15.1 6.5 %collective-permute-start.9 = (f32[24,128]{1,0:T(8,128)S(1)}, f32[24,128]{1,0:T(8,128)S(1)}, u32[]{:S(2)}, u32[]{:S(2)}) collective-permute-start(f32[24,128]{1,0:T(8,128)S(1)} %get-tuple-element.74), channel_id=1, source_target_pairs={{0,2},{1,3},{2,0},{3,1},{4,6},{5,7},{6,4},{7,5},{8,10},{9,11},{10,... | collective-permute-start | bytes 36872 | tf_op jit(solution)/shard_map/ppermute | solution.py:625
  17.0 6.9 %collective-permute-start.6 = (f32[8,512]{1,0:T(8,128)S(1)}, f32[8,512]{1,0:T(8,128)S(1)}, u32[]{:S(2)}, u32[]{:S(2)}) collective-permute-start(f32[8,512]{1,0:T(8,128)S(1)} %merge.1.refs_2_), channel_id=1, source_target_pairs={{0,8},{4,12},{8,0},{12,4},{16,24},{20,28},{24,16},{28,20},{1,9},{5... | collective-permute-start | bytes 49160 | tf_op jit(solution)/shard_map/ppermute | solution.py:625
  19.0 4.9 %collective-permute-start.7 = (f32[8,512]{1,0:T(8,128)S(1)}, f32[8,512]{1,0:T(8,128)S(1)}, u32[]{:S(2)}, u32[]{:S(2)}) collective-permute-start(f32[8,512]{1,0:T(8,128)S(1)} %merge.1.refs_2_), channel_id=1, source_target_pairs={{0,16},{4,20},{8,24},{12,28},{16,0},{20,4},{24,8},{28,12},{1,17},{... | collective-permute-start | bytes 49160 | tf_op jit(solution)/shard_map/ppermute | solution.py:625
  21.6 5.5 %collective-permute-start.8 = (f32[8,512]{1,0:T(8,128)S(1)}, f32[8,512]{1,0:T(8,128)S(1)}, u32[]{:S(2)}, u32[]{:S(2)}) collective-permute-start(f32[8,512]{1,0:T(8,128)S(1)} %merge.1.refs_2_), channel_id=1, source_target_pairs={{0,24},{4,28},{8,16},{12,20},{16,8},{20,12},{24,0},{28,4},{1,25},{... | collective-permute-start | bytes 49160 | tf_op jit(solution)/shard_map/ppermute | solution.py:625
  21.6 1.2 %collective-permute-start.10 = (f32[8,128]{1,0:T(8,128)S(1)}, f32[8,128]{1,0:T(8,128)S(1)}, u32[]{:S(2)}, u32[]{:S(2)}) collective-permute-start(f32[8,128]{1,0:T(8,128)S(1)} %slice.9), channel_id=1, source_target_pairs={{0,1},{1,0},{2,3},{3,2},{4,5},{5,4},{6,7},{7,6},{8,9},{9,8},{10,11... | collective-permute-start | bytes 12296 | tf_op jit(solution)/shard_map/ppermute | solution.py:625

commit v6 on v5

--- a/solution.py
+++ b/solution.py
@@ -561,7 +561,7 @@
     parts, (out, natural, sems) = refs[:-3], refs[-3:]
     tiles = out.shape[1] // LANES
     ends = []
-    for row in line_ends("gx", parts):
+    for row in line_ends("gx", parts[:-3] + parts[:-4:-1]):
         ends.append(
             jnp.concatenate([jnp.broadcast_to(row[:, tile_span(t)], (SUB, LANES)) for t in range(tiles)])
         )
@@ -638,7 +638,7 @@
         both = cross(second[0:SUB], axis, 1 << last)
     else:
         first, second, both = (cross(mine, axis, n << last) for n in (1, 2, 3))
-    return parts + [mine, first, second, both]
+    return parts + [mine] + ([first, second, both] if relay else [both, second, first])
 
 
 def on_device(h, p, q, b, m):

time: 28.3 us -> 26.8 us (0.947)
  waiting for transfers between devices: 4.09 us -> 2.64 us
    ppermute x9, waiting for transfers between devices: 4.02 us -> 2.57 us  [cross(): lax.ppermute(value, axis, [(i, i ^ mask) for i in range(lax.axis_size(axi...]
where the time goes in v6:
time: 26.8 us; the launch traced here: 26.6 us
  starting transfers between devices  14.8 us (55%)
  Pallas kernels  8.42 us (31%)
  waiting for transfers between devices  2.64 us (10%)
  between operations  0.71 us (3%)
    ppermute x9, starting transfers between devices, cross(): lax.ppermute(value, axis, [(i, i ^ mask) for i in range(lax.axis_size(axi...  11.3 us
    ppermute x2, starting transfers between devices, hand_on(): lax.ppermute(value, axis, [(i, t if 0 <= t < count else i ^ 1) for i, t i...  3.55 us
    ppermute x9, waiting for transfers between devices, cross(): lax.ppermute(value, axis, [(i, i ^ mask) for i in range(lax.axis_size(axi...  2.57 us
    pallas_call x1, Pallas kernels, pack(): pl.pallas_call(pack_kernel, out_shape=(shape(2, SUB, cols), shape(2, SUB,...  2.43 us
    pallas_call x2, Pallas kernels, solve(): pl.pallas_call(functools.partial(kernel, scale=scale), out_shape=shape(*b...  1.93 us
    pallas_call x1, Pallas kernels, fluxes_x(): pl.pallas_call(functools.partial(flux_x_kernel, inv_cx=inv_cx, inv_cy=inv...  1.25 us
    pallas_call x1, Pallas kernels, fluxes_y(): pl.pallas_call(flux_y_kernel, out_shape=(shape(*stack),) * 3, in_specs=[V...  0.98 us
    pallas_call x1, Pallas kernels, write_depth(): pl.pallas_call(depth_kernel, out_shape=shape(*block), in_specs=[VMEM], ou...  0.75 us
  transfers between devices with their start and end apart: 11, of which 4 were waited for; matrix products, arithmetic and copies ran while one was open for 0% of the time, Pallas kernels for 14%

profile of v6, /device:TPU:0, one launch (start us, length us, event | category | flops | bytes accessed | tf_op | source)
XLA Modules:
  0.0 26.6 jit_solution(3643179724053224235)
XLA Ops:
  0.6 2.4 %pack.1 = (f32[2,8,512]{2,1,0:T(8,128)S(1)}, f32[2,8,128]{2,1,0:T(8,128)S(1)}, f32[512,128]{1,0:T(8,128)S(1)}, f32[512,128]{1,0:T(8,128)S(1)}, f32[512,128]{1,0:...) custom-call(f32[128,512]{1,0:T(8,128)} %h.1, f32[128,512]{1,0:T(8,128)} %p.1, f32[128,512]{1,0:T(8,128)} %q.1, ...), custom_call_target="tpu_custom_call" | custom-call | tf_op jit(solution)/shard_map/pack/pallas_call | solution.py:108
  3.1 0.5 %collective-permute-start.2 = (f32[2,8,128]{2,1,0:T(8,128)S(1)}, f32[2,8,128]{2,1,0:T(8,128)S(1)}, u32[]{:S(2)}, u32[]{:S(2)}) collective-permute-start(f32[2,8,128]{2,1,0:T(8,128)S(1)} %get-tuple-element.54), channel_id=1, source_target_pairs={{0,1},{1,0},{2,3},{3,2},{4,5},{5,4},{6,7},{7,6},{8,9},{9,8},{10,11... | collective-permute-start | bytes 24584 | tf_op jit(solution)/shard_map/ppermute | solution.py:625
  3.6 2.6 %collective-permute-start = (f32[2,8,512]{2,1,0:T(8,128)S(1)}, f32[2,8,512]{2,1,0:T(8,128)S(1)}, u32[]{:S(2)}, u32[]{:S(2)}) collective-permute-start(f32[2,8,512]{2,1,0:T(8,128)S(1)} %get-tuple-element.39), channel_id=1, source_target_pairs={{0,4},{4,0},{8,12},{12,8},{16,20},{20,16},{24,28},{28,24},{1,5},{5... | collective-permute-start | bytes 98312 | tf_op jit(solution)/shard_map/ppermute | solution.py:625
  6.2 0.0 collective-permute-done.2.near
  6.2 1.5 %collective-permute-start.3 = (f32[48,128]{1,0:T(8,128)S(1)}, f32[48,128]{1,0:T(8,128)S(1)}, u32[]{:S(2)}, u32[]{:S(2)}) collective-permute-start(f32[48,128]{1,0:T(8,128)S(1)} %pad.4), channel_id=1, source_target_pairs={{0,2},{1,0},{2,3},{3,1},{4,6},{5,4},{6,7},{7,5},{8,10},{9,8},{10,1... | collective-permute-start | bytes 73736 | tf_op jit(solution)/shard_map/ppermute | solution.py:621
  7.7 0.4 %prepare_depth.1 = (f32[512,128]{1,0:T(8,128)S(1)}, f32[512,128]{1,0:T(8,128)S(1)}, f32[512,128]{1,0:T(8,128)S(1)}, f32[512,128]{1,0:T(8,128)S(1)}, f32[3,32,128...) custom-call(f32[512,128]{1,0:T(8,128)S(1)} %get-tuple-element.40.hs), custom_call_target="tpu_custom_call" | custom-call | flops 2000000 | bytes 4000000 | tf_op jit(solution)/shard_map/prepare_depth/pallas_call | solution.py:229
  8.1 0.0 collective-permute-done.both.near
  8.1 2.0 %collective-permute-start.1 = (f32[8,512]{1,0:T(8,128)S(1)}, f32[8,512]{1,0:T(8,128)S(1)}, u32[]{:S(2)}, u32[]{:S(2)}) collective-permute-start(f32[8,512]{1,0:T(8,128)S(1)} %second_of.1), channel_id=1, source_target_pairs={{0,8},{4,0},{8,16},{12,4},{16,24},{20,12},{24,28},{28,20},{1,9},{5... | collective-permute-start | bytes 49160 | tf_op jit(solution)/shard_map/ppermute | solution.py:621
  10.2 0.7 %prepare_rest.1 = (f32[512,128]{1,0:T(8,128)S(1)}, f32[512,128]{1,0:T(8,128)S(1)}, f32[512,128]{1,0:T(8,128)S(1)}, f32[512,128]{1,0:T(8,128)S(1)}, f32[512,128]{...) custom-call(f32[512,128]{1,0:T(8,128)S(1)} %get-tuple-element.43.refs_0_, ...), custom_call_target="tpu_custom_call" | custom-call | flops 2000000 | bytes 6000000 | tf_op jit(solution)/shard_map/prepare_rest/pallas_call | solution.py:249
  10.8 0.0 collective-permute-done.3.far
  10.8 1.0 %fluxes_y.1 = (f32[512,128]{1,0:T(8,128)S(1)}, f32[512,128]{1,0:T(8,128)S(1)}, f32[512,128]{1,0:T(8,128)S(1)}) custom-call(f32[2,8,128]{2,1,0:T(8,128)S(1)} %collective-permute-done.2.near, f32[48,128]{1,0:T(8,128)S(1)} %collective-permute-done.3.far, f32[512,128]{1,0:T(8,128)S(1)} %get-tuple-element.55.hy, f32[512,128]{1,0:T(8,128)S(1)} %get-tuple-element.56.py, ...), custom_call_target="tpu_custom_call" | custom-call | flops 4000000 | bytes 4000000 | tf_op jit(solution)/shard_map/fluxes_y/pallas_call | solution.py:368
  11.8 0.1 collective-permute-done.1.far
  11.9 1.2 %fluxes_x.1 = (f32[512,128]{1,0:T(8,128)S(1)}, f32[512,128]{1,0:T(8,128)S(1)}, f32[512,128]{1,0:T(8,128)S(1)}, f32[4,32,128]{2,1,0:T(8,128)S(1)}, f32[6,32,128]{...) custom-call(f32[2,8,512]{2,1,0:T(8,128)S(1)} %collective-permute-done.both.near, ...), custom_call_target="tpu_custom_call" | custom-call | tf_op jit(solution)/shard_map/fluxes_x/pallas_call | solution.py:437
  13.2 2.0 %collective-permute-start.4 = (f32[8,512]{1,0:T(8,128)S(1)}, f32[8,512]{1,0:T(8,128)S(1)}, u32[]{:S(2)}, u32[]{:S(2)}) collective-permute-start(f32[8,512]{1,0:T(8,128)S(1)} %get-tuple-element.70.mine.refs_0_), channel_id=1, source_target_pairs={{0,4},{4,0},{8,12},{12,8},{16,20},{20,16},{24,28},{28,24},{1,5},{5... | collective-permute-start | bytes 49160 | tf_op jit(solution)/shard_map/ppermute | solution.py:625
  15.1 0.0 collective-permute-start.5
  15.1 1.5 %collective-permute-start.9 = (f32[24,128]{1,0:T(8,128)S(1)}, f32[24,128]{1,0:T(8,128)S(1)}, u32[]{:S(2)}, u32[]{:S(2)}) collective-permute-start(f32[24,128]{1,0:T(8,128)S(1)} %get-tuple-element.74), channel_id=1, source_target_pairs={{0,2},{1,3},{2,0},{3,1},{4,6},{5,7},{6,4},{7,5},{8,10},{9,11},{10,... | collective-permute-start | bytes 36872 | tf_op jit(solution)/shard_map/ppermute | solution.py:625
  16.6 0.0 collective-permute-done.5.refs_0_.refs_1_
  16.6 0.3 %collective-permute-done.4.theirs.refs_1_ = f32[8,512]{1,0:T(8,128)S(1)} collective-permute-done((f32[8,512]{1,0:T(8,128)S(1)}, f32[8,512]{1,0:T(8,128)S(1)}, u32[]{:S(2)}, u32[]{:S(2)}) %collective-permute-start.4) | collective-permute-done | bytes 16416 | tf_op jit(solution)/shard_map/ppermute | solution.py:625
  17.0 4.1 %collective-permute-start.6 = (f32[8,512]{1,0:T(8,128)S(1)}, f32[8,512]{1,0:T(8,128)S(1)}, u32[]{:S(2)}, u32[]{:S(2)}) collective-permute-start(f32[8,512]{1,0:T(8,128)S(1)} %merge.1.refs_2_), channel_id=1, source_target_pairs={{0,24},{4,28},{8,16},{12,20},{16,8},{20,12},{24,0},{28,4},{1,25},{... | collective-permute-start | bytes 49160 | tf_op jit(solution)/shard_map/ppermute | solution.py:625
  21.1 0.0 collective-permute-start.7
  21.1 0.6 %collective-permute-start.8 = (f32[8,512]{1,0:T(8,128)S(1)}, f32[8,512]{1,0:T(8,128)S(1)}, u32[]{:S(2)}, u32[]{:S(2)}) collective-permute-start(f32[8,512]{1,0:T(8,128)S(1)} %merge.1.refs_2_), channel_id=1, source_target_pairs={{0,8},{4,12},{8,0},{12,4},{16,24},{20,28},{24,16},{28,20},{1,9},{5... | collective-permute-start | bytes 49160 | tf_op jit(solution)/shard_map/ppermute | solution.py:625
  21.7 0.0 collective-permute-done.9.refs_2_
  21.7 0.0 collective-permute-start.10
  21.7 0.7 %write_depth.1 = f32[128,512]{1,0:T(8,128)} custom-call(f32[512,128]{1,0:T(8,128)S(1)} %get-tuple-element.67.depth), custom_call_target="tpu_custom_call" | custom-call | flops 100000 | bytes 2000000 | tf_op jit(solution)/shard_map/write_depth/pallas_call | solution.py:471
  22.5 0.4 %collective-permute-done.10.refs_3_ = f32[8,128]{1,0:T(8,128)S(1)} collective-permute-done((f32[8,128]{1,0:T(8,128)S(1)}, f32[8,128]{1,0:T(8,128)S(1)}, u32[]{:S(2)}, u32[]{:S(2)}) %collective-permute-start.10) | collective-permute-done | bytes 4128 | tf_op jit(solution)/shard_map/ppermute | solution.py:625
  22.9 1.0 %solve_y.1 = f32[128,512]{1,0:T(8,128)} custom-call(f32[512,128]{1,0:T(8,128)S(1)} %get-tuple-element.52.iy.inv_ref, f32[512,128]{1,0:T(8,128)S(1)} %get-tuple-element.72.r_ref, f32[3,32,128]{2,1,0:T(8,128)S(1)} %get-tuple-element.64.ty.t_ref, f32[15,32,128]{2,1,0:T(8,128)S(1)} %get-tuple-element.65.wy.w_ref, f32[6,32,128]{2,1,0:T(8,128)S(1)} %get-tuple-element.73.s_ref, ...), custom_call_target="tpu_custom_call" | custom-call | flops 1000000 | bytes 4000000 | tf_op jit(solution)/shard_map/solve_y/pallas_call | solution.py:606
  23.9 0.0 collective-permute-done.6.refs_3_
  23.9 1.8 %collective-permute-done.7.refs_4_ = f32[8,512]{1,0:T(8,128)S(1)} collective-permute-done((f32[8,512]{1,0:T(8,128)S(1)}, f32[8,512]{1,0:T(8,128)S(1)}, u32[]{:S(2)}, u32[]{:S(2)}) %collective-permute-start.7) | collective-permute-done | bytes 16416 | tf_op jit(solution)/shard_map/ppermute | solution.py:625
  25.7 0.0 collective-permute-done.8.refs_5_
  25.7 0.9 %solve_x.1 = f32[128,512]{1,0:T(8,128)} custom-call(f32[512,128]{1,0:T(8,128)S(1)} %get-tuple-element.51.ix.inv_ref, f32[512,128]{1,0:T(8,128)S(1)} %get-tuple-element.68.r_ref, f32[3,32,128]{2,1,0:T(8,128)S(1)} %get-tuple-element.62.tx.t_ref, f32[9,32,128]{2,1,0:T(8,128)S(1)} %get-tuple-element.63.wx.w_ref, f32[4,32,128]{2,1,0:T(8,128)S(1)} %get-tuple-element.69.s_ref, ...), custom_call_target="tpu_custom_call" | custom-call | flops 1000000 | bytes 4000000 | tf_op jit(solution)/shard_map/solve_x/pallas_call | solution.py:606
  (5 shorter events, 0.0 us)
Async XLA Ops:
  3.1 3.1 %collective-permute-start.2 = (f32[2,8,128]{2,1,0:T(8,128)S(1)}, f32[2,8,128]{2,1,0:T(8,128)S(1)}, u32[]{:S(2)}, u32[]{:S(2)}) collective-permute-start(f32[2,8,128]{2,1,0:T(8,128)S(1)} %get-tuple-element.54), channel_id=1, source_target_pairs={{0,1},{1,0},{2,3},{3,2},{4,5},{5,4},{6,7},{7,6},{8,9},{9,8},{10,11... | collective-permute-start | bytes 24584 | tf_op jit(solution)/shard_map/ppermute | solution.py:625
  3.6 4.5 %collective-permute-start = (f32[2,8,512]{2,1,0:T(8,128)S(1)}, f32[2,8,512]{2,1,0:T(8,128)S(1)}, u32[]{:S(2)}, u32[]{:S(2)}) collective-permute-start(f32[2,8,512]{2,1,0:T(8,128)S(1)} %get-tuple-element.39), channel_id=1, source_target_pairs={{0,4},{4,0},{8,12},{12,8},{16,20},{20,16},{24,28},{28,24},{1,5},{5... | collective-permute-start | bytes 98312 | tf_op jit(solution)/shard_map/ppermute | solution.py:625
  6.2 4.7 %collective-permute-start.3 = (f32[48,128]{1,0:T(8,128)S(1)}, f32[48,128]{1,0:T(8,128)S(1)}, u32[]{:S(2)}, u32[]{:S(2)}) collective-permute-start(f32[48,128]{1,0:T(8,128)S(1)} %pad.4), channel_id=1, source_target_pairs={{0,2},{1,0},{2,3},{3,1},{4,6},{5,4},{6,7},{7,5},{8,10},{9,8},{10,1... | collective-permute-start | bytes 73736 | tf_op jit(solution)/shard_map/ppermute | solution.py:621
  8.1 3.8 %collective-permute-start.1 = (f32[8,512]{1,0:T(8,128)S(1)}, f32[8,512]{1,0:T(8,128)S(1)}, u32[]{:S(2)}, u32[]{:S(2)}) collective-permute-start(f32[8,512]{1,0:T(8,128)S(1)} %second_of.1), channel_id=1, source_target_pairs={{0,8},{4,0},{8,16},{12,4},{16,24},{20,12},{24,28},{28,20},{1,9},{5... | collective-permute-start | bytes 49160 | tf_op jit(solution)/shard_map/ppermute | solution.py:621
  13.2 3.8 %collective-permute-start.4 = (f32[8,512]{1,0:T(8,128)S(1)}, f32[8,512]{1,0:T(8,128)S(1)}, u32[]{:S(2)}, u32[]{:S(2)}) collective-permute-start(f32[8,512]{1,0:T(8,128)S(1)} %get-tuple-element.70.mine.refs_0_), channel_id=1, source_target_pairs={{0,4},{4,0},{8,12},{12,8},{16,20},{20,16},{24,28},{28,24},{1,5},{5... | collective-permute-start | bytes 49160 | tf_op jit(solution)/shard_map/ppermute | solution.py:625
  15.1 1.5 %collective-permute-start.5 = (f32[8,128]{1,0:T(8,128)S(1)}, f32[8,128]{1,0:T(8,128)S(1)}, u32[]{:S(2)}, u32[]{:S(2)}) collective-permute-start(f32[8,128]{1,0:T(8,128)S(1)} %get-tuple-element.71.refs_0_), channel_id=1, source_target_pairs={{0,1},{1,0},{2,3},{3,2},{4,5},{5,4},{6,7},{7,6},{8,9},{9,8},{10,11... | collective-permute-start | bytes 12296 | tf_op jit(solution)/shard_map/ppermute | solution.py:625
  15.1 6.6 %collective-permute-start.9 = (f32[24,128]{1,0:T(8,128)S(1)}, f32[24,128]{1,0:T(8,128)S(1)}, u32[]{:S(2)}, u32[]{:S(2)}) collective-permute-start(f32[24,128]{1,0:T(8,128)S(1)} %get-tuple-element.74), channel_id=1, source_target_pairs={{0,2},{1,3},{2,0},{3,1},{4,6},{5,7},{6,4},{7,5},{8,10},{9,11},{10,... | collective-permute-start | bytes 36872 | tf_op jit(solution)/shard_map/ppermute | solution.py:625
  17.0 6.9 %collective-permute-start.6 = (f32[8,512]{1,0:T(8,128)S(1)}, f32[8,512]{1,0:T(8,128)S(1)}, u32[]{:S(2)}, u32[]{:S(2)}) collective-permute-start(f32[8,512]{1,0:T(8,128)S(1)} %merge.1.refs_2_), channel_id=1, source_target_pairs={{0,24},{4,28},{8,16},{12,20},{16,8},{20,12},{24,0},{28,4},{1,25},{... | collective-permute-start | bytes 49160 | tf_op jit(solution)/shard_map/ppermute | solution.py:625
  21.1 4.6 %collective-permute-start.7 = (f32[8,512]{1,0:T(8,128)S(1)}, f32[8,512]{1,0:T(8,128)S(1)}, u32[]{:S(2)}, u32[]{:S(2)}) collective-permute-start(f32[8,512]{1,0:T(8,128)S(1)} %merge.1.refs_2_), channel_id=1, source_target_pairs={{0,16},{4,20},{8,24},{12,28},{16,0},{20,4},{24,8},{28,12},{1,17},{... | collective-permute-start | bytes 49160 | tf_op jit(solution)/shard_map/ppermute | solution.py:625
  21.1 4.6 %collective-permute-start.8 = (f32[8,512]{1,0:T(8,128)S(1)}, f32[8,512]{1,0:T(8,128)S(1)}, u32[]{:S(2)}, u32[]{:S(2)}) collective-permute-start(f32[8,512]{1,0:T(8,128)S(1)} %merge.1.refs_2_), channel_id=1, source_target_pairs={{0,8},{4,12},{8,0},{12,4},{16,24},{20,28},{24,16},{28,20},{1,9},{5... | collective-permute-start | bytes 49160 | tf_op jit(solution)/shard_map/ppermute | solution.py:625
  21.7 1.2 %collective-permute-start.10 = (f32[8,128]{1,0:T(8,128)S(1)}, f32[8,128]{1,0:T(8,128)S(1)}, u32[]{:S(2)}, u32[]{:S(2)}) collective-permute-start(f32[8,128]{1,0:T(8,128)S(1)} %slice.9), channel_id=1, source_target_pairs={{0,1},{1,0},{2,3},{3,2},{4,5},{5,4},{6,7},{7,6},{8,9},{9,8},{10,11... | collective-permute-start | bytes 12296 | tf_op jit(solution)/shard_map/ppermute | solution.py:625

commit v7 on v5

--- a/solution.py
+++ b/solution.py
@@ -58,15 +58,13 @@
             copy.start()
             edges.append(copy)
     loads = {}
-    for tile in [0, tiles - 1] + list(range(1, tiles - 1)):
+    for place, tile in enumerate((0, tiles - 1)):
         for f, (src, target) in enumerate(zip(sources, stacks)):
             copy = pltpu.make_async_copy(
-                src.at[:, pl.ds(tile * LANES, LANES)],
-                target.at[pl.ds(tile * rows, rows), :],
-                sems.at[f * tiles + tile],
+                src.at[:, pl.ds(tile * LANES, LANES)], target.at[pl.ds(place * rows, rows), :], sems.at[2 * f + place]
             )
             copy.start()
-            loads[tile, f] = copy
+            loads[place, f] = copy
     for copy in edges:
         copy.wait()
     first_x = jnp.concatenate(
@@ -86,25 +84,21 @@
     xa[1] = jnp.where(even_x, first_x, last_x)
     lane = lane_index((rows, LANES))
     out = jnp.zeros((rows, LANES), F32)
-    for tile, start, shifts in ((0, 0, (0, 2, 4, 6, 7)), (tiles - 1, SUB, (10, 12, 14, 15, 16))):
+    for place, start, shifts in ((0, 0, (0, 2, 4, 6, 7)), (1, SUB, (10, 12, 14, 15, 16))):
         for f, (ref, to, shift) in enumerate(zip(stacks, (0, 2, 4, 6, 7), shifts)):
-            loads[tile, f].wait()
-            value = jnp.concatenate([ref[spread_rows(tile, k), :] for k in range(STEPS)]).astype(F32)
+            loads[place, f].wait()
+            value = jnp.concatenate([ref[spread_rows(place, k), :] for k in range(STEPS)]).astype(F32)
             out = jnp.where(lane >= start + to, pltpu.roll(value, shift, 1) if shift else value, out)
     turned = out.T
     first_y, last_y = turned[0:SUB, :], turned[SUB : 2 * SUB, :]
     even_y = lax.axis_index("gy") % 2 == 0
     ya[0] = jnp.where(even_y, last_y, first_y)
     ya[1] = jnp.where(even_y, first_y, last_y)
-    for tile in range(1, tiles - 1):
-        for f in range(len(sources)):
-            loads[tile, f].wait()
 
 
 def pack(*fields):
     rows, cols = fields[0].shape
-    tiles = cols // LANES
-    stacks = [jax.ShapeDtypeStruct((tiles * rows, LANES), v.dtype) for v in fields]
+    stacks = [jax.ShapeDtypeStruct((2 * rows, LANES), v.dtype) for v in fields]
     return pl.pallas_call(
         pack_kernel,
         out_shape=(shape(2, SUB, cols), shape(2, SUB, rows), *stacks),
@@ -116,10 +110,43 @@
             pltpu.VMEM((SUB, cols), jnp.int32),
             pltpu.VMEM((SUB, cols), jnp.int32),
             pltpu.SemaphoreType.DMA((10,)),
-            pltpu.SemaphoreType.DMA((5 * tiles,)),
+            pltpu.SemaphoreType.DMA((10,)),
         ],
         compiler_params=PARAMS,
         name="pack",
+    )(*[pltpu.with_memory_space_constraint(v, pltpu.HBM) for v in fields])
+
+
+def load_kernel(*refs):
+    sources, targets, sems = refs[:5], refs[5:10], refs[10]
+    rows, cols = sources[0].shape
+    copies = []
+    for f, (src, target) in enumerate(zip(sources, targets)):
+        for tile in range(1, cols // LANES - 1):
+            copies.append(
+                pltpu.make_async_copy(
+                    src.at[:, pl.ds(tile * LANES, LANES)],
+                    target.at[pl.ds((tile - 1) * rows, rows), :],
+                    sems.at[f * (cols // LANES) + tile],
+                )
+            )
+            copies[-1].start()
+    for copy in copies:
+        copy.wait()
+
+
+def load_middle(*fields):
+    rows, cols = fields[0].shape
+    tiles = cols // LANES
+    return pl.pallas_call(
+        load_kernel,
+        out_shape=tuple(jax.ShapeDtypeStruct(((tiles - 2) * rows, LANES), v.dtype) for v in fields),
+        in_specs=[HBM] * 5,
+        out_specs=(VMEM,) * 5,
+        scratch_shapes=[pltpu.SemaphoreType.DMA((5 * tiles,))],
+        compiler_params=PARAMS,
+        cost_estimate=pl.CostEstimate(flops=0, bytes_accessed=1_300_000, transcendentals=0),
+        name="load_middle",
     )(*[pltpu.with_memory_space_constraint(v, pltpu.HBM) for v in fields])
 
 
@@ -191,18 +218,20 @@
     return coefficients
 
 
-def lay_out(src, xs, ys, turned):
-    for tile in range(src.shape[0] // LANES):
+def lay_out(outer, middle, xs, ys, turned):
+    tiles = xs.shape[0] // LANES
+    for tile in range(tiles):
+        src, place = (middle, tile - 1) if 0 < tile < tiles - 1 else (outer, min(tile, 1))
         for k in range(STEPS):
-            xs[at(tile, k), :] = src[spread_rows(tile, k), :].astype(F32)
+            xs[at(tile, k), :] = src[spread_rows(place, k), :].astype(F32)
         turned[tile_span(tile), :] = xs[tile_span(tile), :].T
         for k in range(STEPS):
             ys[at(tile, k), :] = turned[spread_rows(tile, k), :]
 
 
-def prepare_depth_kernel(hs, hx, hy, ix, iy, tx, wx, ty, wy, endx, endy, turned, *, inv_cx, inv_cy):
-    tiles = hs.shape[0] // LANES
-    lay_out(hs, hx, hy, turned)
+def prepare_depth_kernel(outer, middle, hx, hy, ix, iy, tx, wx, ty, wy, endx, endy, turned, *, inv_cx, inv_cy):
+    tiles = hx.shape[0] // LANES
+    lay_out(outer, middle, hx, hy, turned)
     ix[...] = 1.0 / hx[...]
     iy[...] = 1.0 / hy[...]
     ends_x = march_depth(ix, inv_cx, tx, wx, log2(SUB))
@@ -215,8 +244,8 @@
     endy[3:8, :] = jnp.zeros((5, endy.shape[1]), F32)
 
 
-def prepare_depth(hs, inv_cx, inv_cy):
-    stack = hs.shape
+def prepare_depth(outer, middle, inv_cx, inv_cy):
+    stack = (outer.shape[0] + middle.shape[0], LANES)
     count = stack[0] // STEPS
     shapes = [shape(*stack)] * 4 + [
         shape(3, count, LANES),
@@ -229,33 +258,33 @@
     return pl.pallas_call(
         functools.partial(prepare_depth_kernel, inv_cx=inv_cx, inv_cy=inv_cy),
         out_shape=tuple(shapes),
-        in_specs=[VMEM],
+        in_specs=[VMEM] * 2,
         out_specs=(VMEM,) * len(shapes),
         scratch_shapes=[pltpu.VMEM(stack, F32)],
         compiler_params=PARAMS,
         cost_estimate=pl.CostEstimate(flops=2_000_000, bytes_accessed=4_000_000, transcendentals=0),
         name="prepare_depth",
-    )(hs)
+    )(outer, middle)
 
 
 def prepare_rest_kernel(*refs):
-    sources, outs, turned = refs[:4], refs[4:12], refs[12]
-    for f, src in enumerate(sources):
-        lay_out(src, outs[2 * f], outs[2 * f + 1], turned.at[f % 2])
-
-
-def prepare_rest(*sources):
-    stack = sources[0].shape
+    outer, middle, outs, turned = refs[:4], refs[4:8], refs[8:16], refs[16]
+    for f in range(4):
+        lay_out(outer[f], middle[f], outs[2 * f], outs[2 * f + 1], turned.at[f % 2])
+
+
+def prepare_rest(outer, middle):
+    stack = (outer[0].shape[0] + middle[0].shape[0], LANES)
     return pl.pallas_call(
         prepare_rest_kernel,
         out_shape=(shape(*stack),) * 8,
-        in_specs=[VMEM] * 4,
+        in_specs=[VMEM] * 8,
         out_specs=(VMEM,) * 8,
         scratch_shapes=[pltpu.VMEM((2, *stack), F32)],
         compiler_params=PARAMS,
         cost_estimate=pl.CostEstimate(flops=2_000_000, bytes_accessed=6_000_000, transcendentals=0),
         name="prepare_rest",
-    )(*sources)
+    )(*outer, *middle)
 
 
 def low_high(axis, near, far):
@@ -299,7 +328,7 @@
     return lambda k: out[k] if k in out else ref[at(tile, k), :]
 
 
-def tile_fluxes(fields, bed, wet, store):
+def tile_fluxes(fields, bed, wet, store, start=0, stop=STEPS):
     def states(k):
         both = []
         for w in fields:
@@ -307,13 +336,13 @@
             both.append((here, half_slope(here - w(k - 1), w(k + 1) - here)))
         return [w + s for w, s in both], [w - s for w, s in both]
 
-    left, _ = states(-1)
+    left, _ = states(start - 1)
     before = None
-    for k in range(-1, STEPS):
+    for k in range(start - 1, stop):
         left_next, right = states(k + 1)
         face = face_flux(left, right, wet(k) * wet(k + 1))
         left = left_next
-        if k >= 0:
+        if k >= start:
             store(k, [a - c for a, c in zip(face, before)], bed(k + 1) - bed(k - 1))
         before = face
 
@@ -377,22 +406,11 @@
     )(*arrays)
 
 
-def flux_x_kernel(
-    near, far, hx, px, qx, bx, mx, ix, iy, my, mass_y, shear_y, normal_y, tx, wx, ty, wy, coefx, coefy,
-    depth, rx, ry, sx, sy, endx, endy, tally,
-    across, turned,
-    *, inv_cx, inv_cy,
-):
-    tiles = hx.shape[0] // LANES
-    low, high = low_high("gx", near[0], far[...])
-    for tile in range(tiles):
-        span = tile_span(tile)
-
-        def extend(ref, row, layers):
-            lows = [low[row + layers - 1 - n : row + layers - n, span] for n in range(layers)]
-            highs = [high[row + n : row + n + 1, span] for n in range(layers)]
-            return extended(ref, tile, lows, highs)
-
+INNER = (2, STEPS - 2)
+
+
+def x_store(hx, px, mx, ix, mass_y, shear_y, depth, rx, across, inv_cx):
+    def of_tile(tile):
         def store(k, difference, bed):
             here = at(tile, k)
             h, m, inverse = hx[here, :], mx[here, :], ix[here, :]
@@ -401,7 +419,58 @@
             rx[here, :] = (inv_cx * (inverse * inverse)) * m * push
             across[here, :] = difference[2]
 
-        tile_fluxes([extend(hx, 0, 2), extend(px, 2, 2), extend(qx, 4, 2)], extend(bx, 6, 1), extend(mx, 7, 1), store)
+        return store
+
+    return of_tile
+
+
+def flux_x_inner_kernel(hx, px, qx, bx, mx, ix, mass_y, shear_y, depth, rx, across, *, inv_cx):
+    store = x_store(hx, px, mx, ix, mass_y, shear_y, depth, rx, across, inv_cx)
+    for tile in range(hx.shape[0] // LANES):
+        fields, bed, wet = ([extended(v, tile, (), ()) for v in (hx, px, qx)], *(extended(v, tile, (), ()) for v in (bx, mx)))
+        tile_fluxes(fields, bed, wet, store(tile), *INNER)
+        for k in (*range(INNER[0]), *range(INNER[1], STEPS)):
+            for ref in (depth, rx, across):
+                ref[at(tile, k), :] = jnp.zeros((SUB, LANES), F32)
+
+
+def fluxes_x_inner(*arrays, inv_cx):
+    stack = arrays[0].shape
+    return pl.pallas_call(
+        functools.partial(flux_x_inner_kernel, inv_cx=inv_cx),
+        out_shape=(shape(*stack),) * 3,
+        in_specs=[VMEM] * len(arrays),
+        out_specs=(VMEM,) * 3,
+        compiler_params=PARAMS,
+        cost_estimate=pl.CostEstimate(flops=4_000_000, bytes_accessed=4_000_000, transcendentals=0),
+        name="fluxes_x_inner",
+    )(*arrays)
+
+
+def flux_x_kernel(
+    near, far, hx, px, qx, bx, mx, ix, iy, my, mass_y, shear_y, normal_y, depth_in, rx_in, across_in,
+    tx, wx, ty, wy, coefx, coefy,
+    depth, rx, ry, sx, sy, endx, endy, tally,
+    across, turned,
+    *, inv_cx, inv_cy,
+):
+    tiles = hx.shape[0] // LANES
+    low, high = low_high("gx", near[0], far[...])
+    store = x_store(hx, px, mx, ix, mass_y, shear_y, depth, rx, across, inv_cx)
+    for tile in range(tiles):
+        span = tile_span(tile)
+
+        def extend(ref, row, layers):
+            lows = [low[row + layers - 1 - n : row + layers - n, span] for n in range(layers)]
+            highs = [high[row + n : row + n + 1, span] for n in range(layers)]
+            return extended(ref, tile, lows, highs)
+
+        fields, bed, wet = [extend(hx, 0, 2), extend(px, 2, 2), extend(qx, 4, 2)], extend(bx, 6, 1), extend(mx, 7, 1)
+        tile_fluxes(fields, bed, wet, store(tile), 0, INNER[0])
+        tile_fluxes(fields, bed, wet, store(tile), INNER[1], STEPS)
+        inner = slice(at(tile, INNER[0]).start, at(tile, INNER[1]).start)
+        for done, ref in ((depth_in, depth), (rx_in, rx), (across_in, across)):
+            ref[inner, :] = done[inner, :]
         turned[span, :] = across[span, :].T
         for k in range(STEPS):
             here = at(tile, k)
@@ -646,15 +715,17 @@
     rows, cols = block
     inv_cx = 3.0 / (rows * lax.axis_size("gx") / 4.0) ** 2
     inv_cy = 3.0 / (cols * lax.axis_size("gy") / 4.0) ** 2
-    xa, ya, hs, ps, qs, bs, ms = pack(h, p, q, b, m)
+    xa, ya, *outer = pack(h, p, q, b, m)
+    middle = load_middle(h, p, q, b, m)
     near_x, near_y = cross(xa, "gx", 1), cross(ya, "gy", 1)
     far_y = hand_on(jnp.pad(near_y[1], ((0, 5 * SUB), (0, 0))), "gy")
-    hx, hy, ix, iy, tx, wx, ty, wy, coef_x, coef_y = prepare_depth(hs, inv_cx, inv_cy)
+    hx, hy, ix, iy, tx, wx, ty, wy, coef_x, coef_y = prepare_depth(outer[0], middle[0], inv_cx, inv_cy)
     far_x = hand_on(second_of(near_x, coef_x), "gx")
-    px, py, qx, qy, bx, by, mx, my = prepare_rest(ps, qs, bs, ms)
+    px, py, qx, qy, bx, by, mx, my = prepare_rest(outer[1:], middle[1:])
     mass_y, shear_y, normal_y = fluxes_y(near_y, far_y, hy, py, qy, by, my)
+    inner = fluxes_x_inner(hx, px, qx, bx, mx, ix, mass_y, shear_y, inv_cx=inv_cx)
     depth, rx, ry, sx, sy, end_x, end_y, tall_y = fluxes_x(
-        near_x, far_x, hx, px, qx, bx, mx, ix, iy, my, mass_y, shear_y, normal_y,
+        near_x, far_x, hx, px, qx, bx, mx, ix, iy, my, mass_y, shear_y, normal_y, *inner,
         tx, wx, ty, wy, coef_x, coef_y, inv_cx=inv_cx, inv_cy=inv_cy,
     )
     new_depth = write_depth(depth, block)

time: 28.3 us -> 26.9 us (0.951)
  starting transfers between devices: 14.8 us -> 12.7 us
  Pallas kernels: 8.42 us -> 9.55 us
  waiting for transfers between devices: 4.09 us -> 3.7 us
    pallas_call x0 -> x2, Pallas kernels: none -> 1.96 us  [the longest x1 1.3 us: load_middle(): pl.pallas_call(load_kernel, out_shape=tuple((jax.ShapeDtypeStruct(((tiles...]
    ppermute x9, starting transfers between devices: 11.3 us -> 9.51 us  [cross(): lax.ppermute(value, axis, [(i, i ^ mask) for i in range(lax.axis_size(axi...]
    pallas_call x1, Pallas kernels: 1.25 us -> 0.68 us  [fluxes_x(): pl.pallas_call(functools.partial(flux_x_kernel, inv_cx=inv_cx, inv_cy=inv...]
    ppermute x2, starting transfers between devices: 3.55 us -> 3.16 us  [hand_on(): lax.ppermute(value, axis, [(i, t if 0 <= t < count else i ^ 1) for i, t i...]
    ppermute x9, waiting for transfers between devices: 4.02 us -> 3.7 us  [cross(): lax.ppermute(value, axis, [(i, i ^ mask) for i in range(lax.axis_size(axi...]
  transfers between devices with their start and end apart: 11 -> 11, of which waited for: 4 -> 4; matrix products, arithmetic and copies ran while one was open for 0% -> 0% of each run, Pallas kernels for 14% -> 22%
where the time goes in v7:
time: 26.9 us; the launch traced here: 26.7 us
  starting transfers between devices  12.7 us (47%)
  Pallas kernels  9.55 us (36%)
  waiting for transfers between devices  3.7 us (14%)
  between operations  0.74 us (3%)
    ppermute x9, starting transfers between devices, cross(): lax.ppermute(value, axis, [(i, i ^ mask) for i in range(lax.axis_size(axi...  9.51 us
    ppermute x9, waiting for transfers between devices, cross(): lax.ppermute(value, axis, [(i, i ^ mask) for i in range(lax.axis_size(axi...  3.7 us
    ppermute x2, starting transfers between devices, hand_on(): lax.ppermute(value, axis, [(i, t if 0 <= t < count else i ^ 1) for i, t i...  3.16 us
    pallas_call x1, Pallas kernels, pack(): pl.pallas_call(pack_kernel, out_shape=(shape(2, SUB, cols), shape(2, SUB,...  2.15 us
    pallas_call x2, Pallas kernels, solve(): pl.pallas_call(functools.partial(kernel, scale=scale), out_shape=shape(*b...  1.93 us
    pallas_call x1, Pallas kernels, load_middle(): pl.pallas_call(load_kernel, out_shape=tuple((jax.ShapeDtypeStruct(((tiles...  1.3 us
    pallas_call x1, Pallas kernels, fluxes_y(): pl.pallas_call(flux_y_kernel, out_shape=(shape(*stack),) * 3, in_specs=[V...  0.98 us
    pallas_call x1, Pallas kernels, write_depth(): pl.pallas_call(depth_kernel, out_shape=shape(*block), in_specs=[VMEM], ou...  0.75 us
  transfers between devices with their start and end apart: 11, of which 4 were waited for; matrix products, arithmetic and copies ran while one was open for 0% of the time, Pallas kernels for 22%

profile of v7, /device:TPU:0, one launch (start us, length us, event | category | flops | bytes accessed | tf_op | source)
XLA Modules:
  0.0 26.7 jit_solution(18407874955889720307)
XLA Ops:
  0.6 2.2 %pack.1 = (f32[2,8,512]{2,1,0:T(8,128)S(1)}, f32[2,8,128]{2,1,0:T(8,128)S(1)}, f32[256,128]{1,0:T(8,128)S(1)}, f32[256,128]{1,0:T(8,128)S(1)}, f32[256,128]{1,0:...) custom-call(f32[128,512]{1,0:T(8,128)} %refs_0_.1, f32[128,512]{1,0:T(8,128)} %refs_1_.1, ...), custom_call_target="tpu_custom_call" | custom-call | tf_op jit(solution)/shard_map/pack/pallas_call | solution.py:102
  2.8 0.5 %collective-permute-start.2 = (f32[2,8,128]{2,1,0:T(8,128)S(1)}, f32[2,8,128]{2,1,0:T(8,128)S(1)}, u32[]{:S(2)}, u32[]{:S(2)}) collective-permute-start(f32[2,8,128]{2,1,0:T(8,128)S(1)} %get-tuple-element.67), channel_id=1, source_target_pairs={{0,1},{1,0},{2,3},{3,2},{4,5},{5,4},{6,7},{7,6},{8,9},{9,8},{10,11... | collective-permute-start | bytes 24584 | tf_op jit(solution)/shard_map/ppermute | solution.py:694
  3.3 2.6 %collective-permute-start = (f32[2,8,512]{2,1,0:T(8,128)S(1)}, f32[2,8,512]{2,1,0:T(8,128)S(1)}, u32[]{:S(2)}, u32[]{:S(2)}) collective-permute-start(f32[2,8,512]{2,1,0:T(8,128)S(1)} %get-tuple-element.47), channel_id=1, source_target_pairs={{0,4},{4,0},{8,12},{12,8},{16,20},{20,16},{24,28},{28,24},{1,5},{5... | collective-permute-start | bytes 98312 | tf_op jit(solution)/shard_map/ppermute | solution.py:694
  5.9 0.0 collective-permute-done.2.near
  5.9 1.5 %collective-permute-start.3 = (f32[48,128]{1,0:T(8,128)S(1)}, f32[48,128]{1,0:T(8,128)S(1)}, u32[]{:S(2)}, u32[]{:S(2)}) collective-permute-start(f32[48,128]{1,0:T(8,128)S(1)} %pad.4), channel_id=1, source_target_pairs={{0,2},{1,0},{2,3},{3,1},{4,6},{5,4},{6,7},{7,5},{8,10},{9,8},{10,1... | collective-permute-start | bytes 73736 | tf_op jit(solution)/shard_map/ppermute | solution.py:690
  7.4 1.3 %load_middle.1 = (f32[256,128]{1,0:T(8,128)S(1)}, f32[256,128]{1,0:T(8,128)S(1)}, f32[256,128]{1,0:T(8,128)S(1)}, f32[256,128]{1,0:T(8,128)S(1)}, s32[256,128]{1,0:T(8,128)S(1)}) custom-call(f32[128,512]{1,0:T(8,128)} %refs_0_.1, f32[128,512]{1,0:T(8,128)} %refs_1_.1, f32[128,512]{1,0:T(8,128)} %refs_2_.1, f32[128,512]{1,0:T(8,128)} %refs_3_.1, ...), custom_call_target="tpu_custom_call" | custom-call | bytes 1300000 | tf_op jit(solution)/shard_map/load_middle/pallas_call | solution.py:141
  8.7 0.4 %prepare_depth.1 = (f32[512,128]{1,0:T(8,128)S(1)}, f32[512,128]{1,0:T(8,128)S(1)}, f32[512,128]{1,0:T(8,128)S(1)}, f32[512,128]{1,0:T(8,128)S(1)}, f32[3,32,128...) custom-call(f32[256,128]{1,0:T(8,128)S(1)} %get-tuple-element.48.out, ...), custom_call_target="tpu_custom_call" | custom-call | flops 2000000 | bytes 4000000 | tf_op jit(solution)/shard_map/prepare_depth/pallas_call | solution.py:258
  9.1 0.0 collective-permute-done.both.near
  9.1 1.6 %collective-permute-start.1 = (f32[8,512]{1,0:T(8,128)S(1)}, f32[8,512]{1,0:T(8,128)S(1)}, u32[]{:S(2)}, u32[]{:S(2)}) collective-permute-start(f32[8,512]{1,0:T(8,128)S(1)} %second_of.1), channel_id=1, source_target_pairs={{0,8},{4,0},{8,16},{12,4},{16,24},{20,12},{24,28},{28,20},{1,9},{5... | collective-permute-start | bytes 49160 | tf_op jit(solution)/shard_map/ppermute | solution.py:690
  10.8 0.7 %prepare_rest.1 = (f32[512,128]{1,0:T(8,128)S(1)}, f32[512,128]{1,0:T(8,128)S(1)}, f32[512,128]{1,0:T(8,128)S(1)}, f32[512,128]{1,0:T(8,128)S(1)}, f32[512,128]{...) custom-call(f32[256,128]{1,0:T(8,128)S(1)} %get-tuple-element.52.refs_0_, ...), custom_call_target="tpu_custom_call" | custom-call | flops 2000000 | bytes 6000000 | tf_op jit(solution)/shard_map/prepare_rest/pallas_call | solution.py:278
  11.5 0.0 collective-permute-done.3.far
  11.5 1.0 %fluxes_y.1 = (f32[512,128]{1,0:T(8,128)S(1)}, f32[512,128]{1,0:T(8,128)S(1)}, f32[512,128]{1,0:T(8,128)S(1)}) custom-call(f32[2,8,128]{2,1,0:T(8,128)S(1)} %collective-permute-done.2.near, f32[48,128]{1,0:T(8,128)S(1)} %collective-permute-done.3.far, f32[512,128]{1,0:T(8,128)S(1)} %get-tuple-element.68.hy, f32[512,128]{1,0:T(8,128)S(1)} %get-tuple-element.69.py, ...), custom_call_target="tpu_custom_call" | custom-call | flops 4000000 | bytes 4000000 | tf_op jit(solution)/shard_map/fluxes_y/pallas_call | solution.py:397
  12.5 0.7 %fluxes_x_inner.1 = (f32[512,128]{1,0:T(8,128)S(1)}, f32[512,128]{1,0:T(8,128)S(1)}, f32[512,128]{1,0:T(8,128)S(1)}) custom-call(f32[512,128]{1,0:T(8,128)S(1)} %get-tuple-element.51.hx, f32[512,128]{1,0:T(8,128)S(1)} %get-tuple-element.60.px, f32[512,128]{1,0:T(8,128)S(1)} %get-tuple-element.61.qx, f32[512,128]{1,0:T(8,128)S(1)} %get-tuple-element.62.bx, ...), custom_call_target="tpu_custom_call" | custom-call | flops 4000000 | bytes 4000000 | tf_op jit(solution)/shard_map/fluxes_x_inner/pallas_call | solution.py:439
  13.1 0.0 collective-permute-done.1.far
  13.1 0.7 %fluxes_x.1 = (f32[512,128]{1,0:T(8,128)S(1)}, f32[512,128]{1,0:T(8,128)S(1)}, f32[512,128]{1,0:T(8,128)S(1)}, f32[4,32,128]{2,1,0:T(8,128)S(1)}, f32[6,32,128]{...) custom-call(f32[2,8,512]{2,1,0:T(8,128)S(1)} %collective-permute-done.both.near, ...), custom_call_target="tpu_custom_call" | custom-call | tf_op jit(solution)/shard_map/fluxes_x/pallas_call | solution.py:506
  13.8 0.9 %collective-permute-start.4 = (f32[8,512]{1,0:T(8,128)S(1)}, f32[8,512]{1,0:T(8,128)S(1)}, u32[]{:S(2)}, u32[]{:S(2)}) collective-permute-start(f32[8,512]{1,0:T(8,128)S(1)} %get-tuple-element.86.mine.refs_0_), channel_id=1, source_target_pairs={{0,4},{4,0},{8,12},{12,8},{16,20},{20,16},{24,28},{28,24},{1,5},{5... | collective-permute-start | bytes 49160 | tf_op jit(solution)/shard_map/ppermute | solution.py:694
  14.7 0.0 collective-permute-start.5
  14.7 1.0 %collective-permute-start.9 = (f32[24,128]{1,0:T(8,128)S(1)}, f32[24,128]{1,0:T(8,128)S(1)}, u32[]{:S(2)}, u32[]{:S(2)}) collective-permute-start(f32[24,128]{1,0:T(8,128)S(1)} %get-tuple-element.90), channel_id=1, source_target_pairs={{0,2},{1,3},{2,0},{3,1},{4,6},{5,7},{6,4},{7,5},{8,10},{9,11},{10,... | collective-permute-start | bytes 36872 | tf_op jit(solution)/shard_map/ppermute | solution.py:694
  15.8 0.1 collective-permute-done.5.refs_0_.refs_1_
  15.9 1.7 %collective-permute-done.4.theirs.refs_1_ = f32[8,512]{1,0:T(8,128)S(1)} collective-permute-done((f32[8,512]{1,0:T(8,128)S(1)}, f32[8,512]{1,0:T(8,128)S(1)}, u32[]{:S(2)}, u32[]{:S(2)}) %collective-permute-start.4) | collective-permute-done | bytes 16416 | tf_op jit(solution)/shard_map/ppermute | solution.py:694
  17.6 3.5 %collective-permute-start.8 = (f32[8,512]{1,0:T(8,128)S(1)}, f32[8,512]{1,0:T(8,128)S(1)}, u32[]{:S(2)}, u32[]{:S(2)}) collective-permute-start(f32[8,512]{1,0:T(8,128)S(1)} %merge.1.refs_2_), channel_id=1, source_target_pairs={{0,24},{4,28},{8,16},{12,20},{16,8},{20,12},{24,0},{28,4},{1,25},{... | collective-permute-start | bytes 49160 | tf_op jit(solution)/shard_map/ppermute | solution.py:694
  21.1 0.0 collective-permute-start.7
  21.1 1.0 %collective-permute-start.6 = (f32[8,512]{1,0:T(8,128)S(1)}, f32[8,512]{1,0:T(8,128)S(1)}, u32[]{:S(2)}, u32[]{:S(2)}) collective-permute-start(f32[8,512]{1,0:T(8,128)S(1)} %merge.1.refs_2_), channel_id=1, source_target_pairs={{0,8},{4,12},{8,0},{12,4},{16,24},{20,28},{24,16},{28,20},{1,9},{5... | collective-permute-start | bytes 49160 | tf_op jit(solution)/shard_map/ppermute | solution.py:694
  22.1 0.0 collective-permute-done.9.refs_2_
  22.1 0.0 collective-permute-start.10
  22.1 0.7 %write_depth.1 = f32[128,512]{1,0:T(8,128)} custom-call(f32[512,128]{1,0:T(8,128)S(1)} %get-tuple-element.83.depth), custom_call_target="tpu_custom_call" | custom-call | flops 100000 | bytes 2000000 | tf_op jit(solution)/shard_map/write_depth/pallas_call | solution.py:540
  22.9 0.4 %collective-permute-done.10.refs_3_ = f32[8,128]{1,0:T(8,128)S(1)} collective-permute-done((f32[8,128]{1,0:T(8,128)S(1)}, f32[8,128]{1,0:T(8,128)S(1)}, u32[]{:S(2)}, u32[]{:S(2)}) %collective-permute-start.10) | collective-permute-done | bytes 4128 | tf_op jit(solution)/shard_map/ppermute | solution.py:694
  23.3 1.0 %solve_y.1 = f32[128,512]{1,0:T(8,128)} custom-call(f32[512,128]{1,0:T(8,128)S(1)} %get-tuple-element.65.iy.inv_ref, f32[512,128]{1,0:T(8,128)S(1)} %get-tuple-element.88.r_ref, f32[3,32,128]{2,1,0:T(8,128)S(1)} %get-tuple-element.80.ty.t_ref, f32[15,32,128]{2,1,0:T(8,128)S(1)} %get-tuple-element.81.wy.w_ref, f32[6,32,128]{2,1,0:T(8,128)S(1)} %get-tuple-element.89.s_ref, ...), custom_call_target="tpu_custom_call" | custom-call | flops 1000000 | bytes 4000000 | tf_op jit(solution)/shard_map/solve_y/pallas_call | solution.py:675
  24.3 0.0 collective-permute-done.8.refs_5_
  24.3 1.4 %collective-permute-done.7.refs_4_ = f32[8,512]{1,0:T(8,128)S(1)} collective-permute-done((f32[8,512]{1,0:T(8,128)S(1)}, f32[8,512]{1,0:T(8,128)S(1)}, u32[]{:S(2)}, u32[]{:S(2)}) %collective-permute-start.7) | collective-permute-done | bytes 16416 | tf_op jit(solution)/shard_map/ppermute | solution.py:694
  25.7 0.0 collective-permute-done.6.refs_3_
  25.7 0.9 %solve_x.1 = f32[128,512]{1,0:T(8,128)} custom-call(f32[512,128]{1,0:T(8,128)S(1)} %get-tuple-element.64.ix.inv_ref, f32[512,128]{1,0:T(8,128)S(1)} %get-tuple-element.84.r_ref, f32[3,32,128]{2,1,0:T(8,128)S(1)} %get-tuple-element.78.tx.t_ref, f32[9,32,128]{2,1,0:T(8,128)S(1)} %get-tuple-element.79.wx.w_ref, f32[4,32,128]{2,1,0:T(8,128)S(1)} %get-tuple-element.85.s_ref, ...), custom_call_target="tpu_custom_call" | custom-call | flops 1000000 | bytes 4000000 | tf_op jit(solution)/shard_map/solve_x/pallas_call | solution.py:675
  (5 shorter events, 0.0 us)
Async XLA Ops:
  2.8 3.1 %collective-permute-start.2 = (f32[2,8,128]{2,1,0:T(8,128)S(1)}, f32[2,8,128]{2,1,0:T(8,128)S(1)}, u32[]{:S(2)}, u32[]{:S(2)}) collective-permute-start(f32[2,8,128]{2,1,0:T(8,128)S(1)} %get-tuple-element.67), channel_id=1, source_target_pairs={{0,1},{1,0},{2,3},{3,2},{4,5},{5,4},{6,7},{7,6},{8,9},{9,8},{10,11... | collective-permute-start | bytes 24584 | tf_op jit(solution)/shard_map/ppermute | solution.py:694
  3.3 5.8 %collective-permute-start = (f32[2,8,512]{2,1,0:T(8,128)S(1)}, f32[2,8,512]{2,1,0:T(8,128)S(1)}, u32[]{:S(2)}, u32[]{:S(2)}) collective-permute-start(f32[2,8,512]{2,1,0:T(8,128)S(1)} %get-tuple-element.47), channel_id=1, source_target_pairs={{0,4},{4,0},{8,12},{12,8},{16,20},{20,16},{24,28},{28,24},{1,5},{5... | collective-permute-start | bytes 98312 | tf_op jit(solution)/shard_map/ppermute | solution.py:694
  5.9 5.6 %collective-permute-start.3 = (f32[48,128]{1,0:T(8,128)S(1)}, f32[48,128]{1,0:T(8,128)S(1)}, u32[]{:S(2)}, u32[]{:S(2)}) collective-permute-start(f32[48,128]{1,0:T(8,128)S(1)} %pad.4), channel_id=1, source_target_pairs={{0,2},{1,0},{2,3},{3,1},{4,6},{5,4},{6,7},{7,5},{8,10},{9,8},{10,1... | collective-permute-start | bytes 73736 | tf_op jit(solution)/shard_map/ppermute | solution.py:690
  9.1 4.0 %collective-permute-start.1 = (f32[8,512]{1,0:T(8,128)S(1)}, f32[8,512]{1,0:T(8,128)S(1)}, u32[]{:S(2)}, u32[]{:S(2)}) collective-permute-start(f32[8,512]{1,0:T(8,128)S(1)} %second_of.1), channel_id=1, source_target_pairs={{0,8},{4,0},{8,16},{12,4},{16,24},{20,12},{24,28},{28,20},{1,9},{5... | collective-permute-start | bytes 49160 | tf_op jit(solution)/shard_map/ppermute | solution.py:690
  13.8 3.8 %collective-permute-start.4 = (f32[8,512]{1,0:T(8,128)S(1)}, f32[8,512]{1,0:T(8,128)S(1)}, u32[]{:S(2)}, u32[]{:S(2)}) collective-permute-start(f32[8,512]{1,0:T(8,128)S(1)} %get-tuple-element.86.mine.refs_0_), channel_id=1, source_target_pairs={{0,4},{4,0},{8,12},{12,8},{16,20},{20,16},{24,28},{28,24},{1,5},{5... | collective-permute-start | bytes 49160 | tf_op jit(solution)/shard_map/ppermute | solution.py:694
  14.7 1.2 %collective-permute-start.5 = (f32[8,128]{1,0:T(8,128)S(1)}, f32[8,128]{1,0:T(8,128)S(1)}, u32[]{:S(2)}, u32[]{:S(2)}) collective-permute-start(f32[8,128]{1,0:T(8,128)S(1)} %get-tuple-element.87.refs_0_), channel_id=1, source_target_pairs={{0,1},{1,0},{2,3},{3,2},{4,5},{5,4},{6,7},{7,6},{8,9},{9,8},{10,11... | collective-permute-start | bytes 12296 | tf_op jit(solution)/shard_map/ppermute | solution.py:694
  14.7 7.3 %collective-permute-start.9 = (f32[24,128]{1,0:T(8,128)S(1)}, f32[24,128]{1,0:T(8,128)S(1)}, u32[]{:S(2)}, u32[]{:S(2)}) collective-permute-start(f32[24,128]{1,0:T(8,128)S(1)} %get-tuple-element.90), channel_id=1, source_target_pairs={{0,2},{1,3},{2,0},{3,1},{4,6},{5,7},{6,4},{7,5},{8,10},{9,11},{10,... | collective-permute-start | bytes 36872 | tf_op jit(solution)/shard_map/ppermute | solution.py:694
  17.6 6.6 %collective-permute-start.8 = (f32[8,512]{1,0:T(8,128)S(1)}, f32[8,512]{1,0:T(8,128)S(1)}, u32[]{:S(2)}, u32[]{:S(2)}) collective-permute-start(f32[8,512]{1,0:T(8,128)S(1)} %merge.1.refs_2_), channel_id=1, source_target_pairs={{0,24},{4,28},{8,16},{12,20},{16,8},{20,12},{24,0},{28,4},{1,25},{... | collective-permute-start | bytes 49160 | tf_op jit(solution)/shard_map/ppermute | solution.py:694
  21.1 4.6 %collective-permute-start.7 = (f32[8,512]{1,0:T(8,128)S(1)}, f32[8,512]{1,0:T(8,128)S(1)}, u32[]{:S(2)}, u32[]{:S(2)}) collective-permute-start(f32[8,512]{1,0:T(8,128)S(1)} %merge.1.refs_2_), channel_id=1, source_target_pairs={{0,16},{4,20},{8,24},{12,28},{16,0},{20,4},{24,8},{28,12},{1,17},{... | collective-permute-start | bytes 49160 | tf_op jit(solution)/shard_map/ppermute | solution.py:694
  21.1 4.6 %collective-permute-start.6 = (f32[8,512]{1,0:T(8,128)S(1)}, f32[8,512]{1,0:T(8,128)S(1)}, u32[]{:S(2)}, u32[]{:S(2)}) collective-permute-start(f32[8,512]{1,0:T(8,128)S(1)} %merge.1.refs_2_), channel_id=1, source_target_pairs={{0,8},{4,12},{8,0},{12,4},{16,24},{20,28},{24,16},{28,20},{1,9},{5... | collective-permute-start | bytes 49160 | tf_op jit(solution)/shard_map/ppermute | solution.py:694
  22.1 1.2 %collective-permute-start.10 = (f32[8,128]{1,0:T(8,128)S(1)}, f32[8,128]{1,0:T(8,128)S(1)}, u32[]{:S(2)}, u32[]{:S(2)}) collective-permute-start(f32[8,128]{1,0:T(8,128)S(1)} %slice.9), channel_id=1, source_target_pairs={{0,1},{1,0},{2,3},{3,2},{4,5},{5,4},{6,7},{7,6},{8,9},{9,8},{10,11... | collective-permute-start | bytes 12296 | tf_op jit(solution)/shard_map/ppermute | solution.py:694

commit v8 on v7

--- a/solution.py
+++ b/solution.py
@@ -44,33 +44,22 @@
     return jax.ShapeDtypeStruct(dims, F32)
 
 
-def pack_kernel(h, p, q, b, m, xa, ya, hs, ps, qs, bs, ms, top, bottom, itop, ibottom, sems_x, sems):
-    rows, cols = h.shape
-    tiles = cols // LANES
-    sources = (h, p, q, b, m)
-    stacks = (hs, ps, qs, bs, ms)
-    edges = []
-    for f, src in enumerate(sources):
+def pack_x_kernel(h, p, q, b, m, slabs, top, bottom, itop, ibottom, sems):
+    rows = h.shape[0]
+    copies = []
+    for f, src in enumerate((h, p, q, b, m)):
         for side, (target, whole, row) in enumerate(((top, itop, 0), (bottom, ibottom, rows - SUB))):
             copy = pltpu.make_async_copy(
-                src.at[pl.ds(row, SUB), :], target.at[f] if f < 4 else whole, sems_x.at[2 * f + side]
+                src.at[pl.ds(row, SUB), :], target.at[f] if f < 4 else whole, sems.at[2 * f + side]
             )
             copy.start()
-            edges.append(copy)
-    loads = {}
-    for place, tile in enumerate((0, tiles - 1)):
-        for f, (src, target) in enumerate(zip(sources, stacks)):
-            copy = pltpu.make_async_copy(
-                src.at[:, pl.ds(tile * LANES, LANES)], target.at[pl.ds(place * rows, rows), :], sems.at[2 * f + place]
-            )
-            copy.start()
-            loads[place, f] = copy
-    for copy in edges:
+            copies.append(copy)
+    for copy in copies:
         copy.wait()
-    first_x = jnp.concatenate(
+    first = jnp.concatenate(
         [top[0, 0:2, :], top[1, 0:2, :], top[2, 0:2, :], top[3, 0:1, :], itop[0:1, :].astype(F32)]
     )
-    last_x = jnp.concatenate(
+    last = jnp.concatenate(
         [
             bottom[0, SUB - 2 : SUB, :],
             bottom[1, SUB - 2 : SUB, :],
@@ -79,75 +68,59 @@
             ibottom[SUB - 1 : SUB, :].astype(F32),
         ]
     )
-    even_x = lax.axis_index("gx") % 2 == 0
-    xa[0] = jnp.where(even_x, last_x, first_x)
-    xa[1] = jnp.where(even_x, first_x, last_x)
-    lane = lane_index((rows, LANES))
-    out = jnp.zeros((rows, LANES), F32)
-    for place, start, shifts in ((0, 0, (0, 2, 4, 6, 7)), (1, SUB, (10, 12, 14, 15, 16))):
-        for f, (ref, to, shift) in enumerate(zip(stacks, (0, 2, 4, 6, 7), shifts)):
-            loads[place, f].wait()
-            value = jnp.concatenate([ref[spread_rows(place, k), :] for k in range(STEPS)]).astype(F32)
-            out = jnp.where(lane >= start + to, pltpu.roll(value, shift, 1) if shift else value, out)
-    turned = out.T
-    first_y, last_y = turned[0:SUB, :], turned[SUB : 2 * SUB, :]
-    even_y = lax.axis_index("gy") % 2 == 0
-    ya[0] = jnp.where(even_y, last_y, first_y)
-    ya[1] = jnp.where(even_y, first_y, last_y)
-
-
-def pack(*fields):
-    rows, cols = fields[0].shape
-    stacks = [jax.ShapeDtypeStruct((2 * rows, LANES), v.dtype) for v in fields]
-    return pl.pallas_call(
-        pack_kernel,
-        out_shape=(shape(2, SUB, cols), shape(2, SUB, rows), *stacks),
+    even = lax.axis_index("gx") % 2 == 0
+    slabs[0] = jnp.where(even, last, first)
+    slabs[1] = jnp.where(even, first, last)
+
+
+def pack_x(*fields):
+    cols = fields[0].shape[1]
+    return pl.pallas_call(
+        pack_x_kernel,
+        out_shape=shape(2, SUB, cols),
         in_specs=[HBM] * 5,
-        out_specs=(VMEM,) * 7,
+        out_specs=VMEM,
         scratch_shapes=[
             pltpu.VMEM((4, SUB, cols), F32),
             pltpu.VMEM((4, SUB, cols), F32),
             pltpu.VMEM((SUB, cols), jnp.int32),
             pltpu.VMEM((SUB, cols), jnp.int32),
             pltpu.SemaphoreType.DMA((10,)),
-            pltpu.SemaphoreType.DMA((10,)),
         ],
         compiler_params=PARAMS,
-        name="pack",
+        name="pack_x",
     )(*[pltpu.with_memory_space_constraint(v, pltpu.HBM) for v in fields])
 
 
-def load_kernel(*refs):
-    sources, targets, sems = refs[:5], refs[5:10], refs[10]
-    rows, cols = sources[0].shape
-    copies = []
-    for f, (src, target) in enumerate(zip(sources, targets)):
-        for tile in range(1, cols // LANES - 1):
-            copies.append(
-                pltpu.make_async_copy(
-                    src.at[:, pl.ds(tile * LANES, LANES)],
-                    target.at[pl.ds((tile - 1) * rows, rows), :],
-                    sems.at[f * (cols // LANES) + tile],
-                )
-            )
-            copies[-1].start()
-    for copy in copies:
-        copy.wait()
-
-
-def load_middle(*fields):
-    rows, cols = fields[0].shape
-    tiles = cols // LANES
-    return pl.pallas_call(
-        load_kernel,
-        out_shape=tuple(jax.ShapeDtypeStruct(((tiles - 2) * rows, LANES), v.dtype) for v in fields),
-        in_specs=[HBM] * 5,
-        out_specs=(VMEM,) * 5,
-        scratch_shapes=[pltpu.SemaphoreType.DMA((5 * tiles,))],
-        compiler_params=PARAMS,
-        cost_estimate=pl.CostEstimate(flops=0, bytes_accessed=1_300_000, transcendentals=0),
-        name="load_middle",
-    )(*[pltpu.with_memory_space_constraint(v, pltpu.HBM) for v in fields])
+def pack_y_kernel(h, p, q, b, m, _, slabs, natural):
+    rows, cols = h.shape
+    lane = lane_index((rows, LANES))
+    out = None
+    for f, src in enumerate((h, p, q, b, m)):
+        both = jnp.where(lane < LANES // 2, src[:, 0:LANES], src[:, cols - LANES : cols]).astype(F32)
+        moved = pltpu.roll(both, 4 * f + 2, 1)
+        out = moved if out is None else jnp.where(lane >= 4 * f, moved, out)
+    natural[...] = out
+    turned = jnp.concatenate([natural[spread_rows(0, k), :] for k in range(STEPS)]).T
+    last = jnp.concatenate([turned[0:2], turned[4:6], turned[8:10], turned[13:14], turned[17:18]])
+    first = jnp.concatenate([turned[2:4], turned[6:8], turned[10:12], turned[14:15], turned[18:19]])
+    even = lax.axis_index("gy") % 2 == 0
+    slabs[0] = jnp.where(even, last, first)
+    slabs[1] = jnp.where(even, first, last)
+
+
+def pack_y(*fields, after):
+    rows = fields[0].shape[0]
+    return pl.pallas_call(
+        pack_y_kernel,
+        out_shape=shape(2, SUB, rows),
+        in_specs=[VMEM] * 6,
+        out_specs=VMEM,
+        scratch_shapes=[pltpu.VMEM((rows, LANES), F32)],
+        compiler_params=PARAMS,
+        cost_estimate=pl.CostEstimate(flops=500_000, bytes_accessed=1_000_000, transcendentals=0),
+        name="pack_y",
+    )(*fields, after)
 
 
 def tie_kernel(both, _, out):
@@ -218,20 +191,19 @@
     return coefficients
 
 
-def lay_out(outer, middle, xs, ys, turned):
-    tiles = xs.shape[0] // LANES
-    for tile in range(tiles):
-        src, place = (middle, tile - 1) if 0 < tile < tiles - 1 else (outer, min(tile, 1))
+def lay_out(src, xs, ys, natural, turned):
+    for tile in range(xs.shape[0] // LANES):
+        natural[tile_span(tile), :] = src[:, tile_span(tile)].astype(F32)
         for k in range(STEPS):
-            xs[at(tile, k), :] = src[spread_rows(place, k), :].astype(F32)
+            xs[at(tile, k), :] = natural[spread_rows(tile, k), :]
         turned[tile_span(tile), :] = xs[tile_span(tile), :].T
         for k in range(STEPS):
             ys[at(tile, k), :] = turned[spread_rows(tile, k), :]
 
 
-def prepare_depth_kernel(outer, middle, hx, hy, ix, iy, tx, wx, ty, wy, endx, endy, turned, *, inv_cx, inv_cy):
+def prepare_depth_kernel(h, hx, hy, ix, iy, tx, wx, ty, wy, endx, endy, natural, turned, *, inv_cx, inv_cy):
     tiles = hx.shape[0] // LANES
-    lay_out(outer, middle, hx, hy, turned)
+    lay_out(h, hx, hy, natural, turned)
     ix[...] = 1.0 / hx[...]
     iy[...] = 1.0 / hy[...]
     ends_x = march_depth(ix, inv_cx, tx, wx, log2(SUB))
@@ -244,8 +216,8 @@
     endy[3:8, :] = jnp.zeros((5, endy.shape[1]), F32)
 
 
-def prepare_depth(outer, middle, inv_cx, inv_cy):
-    stack = (outer.shape[0] + middle.shape[0], LANES)
+def prepare_depth(h, inv_cx, inv_cy):
+    stack = (h.shape[1], LANES)
     count = stack[0] // STEPS
     shapes = [shape(*stack)] * 4 + [
         shape(3, count, LANES),
@@ -258,33 +230,33 @@
     return pl.pallas_call(
         functools.partial(prepare_depth_kernel, inv_cx=inv_cx, inv_cy=inv_cy),
         out_shape=tuple(shapes),
-        in_specs=[VMEM] * 2,
+        in_specs=[VMEM],
         out_specs=(VMEM,) * len(shapes),
-        scratch_shapes=[pltpu.VMEM(stack, F32)],
+        scratch_shapes=[pltpu.VMEM(stack, F32)] * 2,
         compiler_params=PARAMS,
         cost_estimate=pl.CostEstimate(flops=2_000_000, bytes_accessed=4_000_000, transcendentals=0),
         name="prepare_depth",
-    )(outer, middle)
+    )(h)
 
 
 def prepare_rest_kernel(*refs):
-    outer, middle, outs, turned = refs[:4], refs[4:8], refs[8:16], refs[16]
-    for f in range(4):
-        lay_out(outer[f], middle[f], outs[2 * f], outs[2 * f + 1], turned.at[f % 2])
-
-
-def prepare_rest(outer, middle):
-    stack = (outer[0].shape[0] + middle[0].shape[0], LANES)
+    fields, outs, natural, turned = refs[:4], refs[4:12], refs[12], refs[13]
+    for f, src in enumerate(fields):
+        lay_out(src, outs[2 * f], outs[2 * f + 1], natural.at[f % 2], turned.at[f % 2])
+
+
+def prepare_rest(*fields):
+    stack = (fields[0].shape[1], LANES)
     return pl.pallas_call(
         prepare_rest_kernel,
         out_shape=(shape(*stack),) * 8,
-        in_specs=[VMEM] * 8,
+        in_specs=[VMEM] * 4,
         out_specs=(VMEM,) * 8,
-        scratch_shapes=[pltpu.VMEM((2, *stack), F32)],
+        scratch_shapes=[pltpu.VMEM((2, *stack), F32)] * 2,
         compiler_params=PARAMS,
         cost_estimate=pl.CostEstimate(flops=2_000_000, bytes_accessed=6_000_000, transcendentals=0),
         name="prepare_rest",
-    )(*outer, *middle)
+    )(*fields)
 
 
 def low_high(axis, near, far):
@@ -409,14 +381,13 @@
 INNER = (2, STEPS - 2)
 
 
-def x_store(hx, px, mx, ix, mass_y, shear_y, depth, rx, across, inv_cx):
+def x_store(hx, px, mx, depth, push, across):
     def of_tile(tile):
         def store(k, difference, bed):
             here = at(tile, k)
-            h, m, inverse = hx[here, :], mx[here, :], ix[here, :]
-            depth[here, :] = h - m * (difference[0] + mass_y[here, :])
-            push = px[here, :] - difference[1] - shear_y[here, :] - (0.5 * ratio * gravity) * h * bed
-            rx[here, :] = (inv_cx * (inverse * inverse)) * m * push
+            h = hx[here, :]
+            depth[here, :] = h - mx[here, :] * difference[0]
+            push[here, :] = px[here, :] - difference[1] - (0.5 * ratio * gravity) * h * bed
             across[here, :] = difference[2]
 
         return store
@@ -424,20 +395,20 @@
     return of_tile
 
 
-def flux_x_inner_kernel(hx, px, qx, bx, mx, ix, mass_y, shear_y, depth, rx, across, *, inv_cx):
-    store = x_store(hx, px, mx, ix, mass_y, shear_y, depth, rx, across, inv_cx)
+def flux_x_inner_kernel(hx, px, qx, bx, mx, depth, push, across):
+    store = x_store(hx, px, mx, depth, push, across)
     for tile in range(hx.shape[0] // LANES):
-        fields, bed, wet = ([extended(v, tile, (), ()) for v in (hx, px, qx)], *(extended(v, tile, (), ()) for v in (bx, mx)))
-        tile_fluxes(fields, bed, wet, store(tile), *INNER)
+        fields = [extended(v, tile, (), ()) for v in (hx, px, qx, bx, mx)]
+        tile_fluxes(fields[:3], fields[3], fields[4], store(tile), *INNER)
         for k in (*range(INNER[0]), *range(INNER[1], STEPS)):
-            for ref in (depth, rx, across):
+            for ref in (depth, push, across):
                 ref[at(tile, k), :] = jnp.zeros((SUB, LANES), F32)
 
 
-def fluxes_x_inner(*arrays, inv_cx):
+def fluxes_x_inner(*arrays):
     stack = arrays[0].shape
     return pl.pallas_call(
-        functools.partial(flux_x_inner_kernel, inv_cx=inv_cx),
+        flux_x_inner_kernel,
         out_shape=(shape(*stack),) * 3,
         in_specs=[VMEM] * len(arrays),
         out_specs=(VMEM,) * 3,
@@ -448,15 +419,15 @@
 
 
 def flux_x_kernel(
-    near, far, hx, px, qx, bx, mx, ix, iy, my, mass_y, shear_y, normal_y, depth_in, rx_in, across_in,
+    near, far, hx, px, qx, bx, mx, ix, iy, my, mass_y, shear_y, normal_y, depth_in, push_in, across_in,
     tx, wx, ty, wy, coefx, coefy,
     depth, rx, ry, sx, sy, endx, endy, tally,
-    across, turned,
+    outer_depth, push, across, turned,
     *, inv_cx, inv_cy,
 ):
     tiles = hx.shape[0] // LANES
     low, high = low_high("gx", near[0], far[...])
-    store = x_store(hx, px, mx, ix, mass_y, shear_y, depth, rx, across, inv_cx)
+    store = x_store(hx, px, mx, outer_depth, push, across)
     for tile in range(tiles):
         span = tile_span(tile)
 
@@ -469,14 +440,17 @@
         tile_fluxes(fields, bed, wet, store(tile), 0, INNER[0])
         tile_fluxes(fields, bed, wet, store(tile), INNER[1], STEPS)
         inner = slice(at(tile, INNER[0]).start, at(tile, INNER[1]).start)
-        for done, ref in ((depth_in, depth), (rx_in, rx), (across_in, across)):
+        for done, ref in ((depth_in, outer_depth), (push_in, push), (across_in, across)):
             ref[inner, :] = done[inner, :]
         turned[span, :] = across[span, :].T
+        m, inverse = mx[span, :], ix[span, :]
+        depth[span, :] = outer_depth[span, :] - m * mass_y[span, :]
+        rx[span, :] = (inv_cx * (inverse * inverse)) * m * (push[span, :] - shear_y[span, :])
         for k in range(STEPS):
             here = at(tile, k)
             inverse = iy[here, :]
-            push = normal_y[here, :] - turned[spread_rows(tile, k), :]
-            ry[here, :] = (inv_cy * (inverse * inverse)) * my[here, :] * push
+            total = normal_y[here, :] - turned[spread_rows(tile, k), :]
+            ry[here, :] = (inv_cy * (inverse * inverse)) * my[here, :] * total
 
     ends_x = march_source(ix, inv_cx, rx, tx, wx, sx, log2(SUB))
     ends_y = march_source(iy, inv_cy, ry, ty, wy, sy, log2(SUB * tiles))
@@ -508,7 +482,7 @@
         out_shape=shapes,
         in_specs=[VMEM] * len(arrays),
         out_specs=(VMEM,) * len(shapes),
-        scratch_shapes=[pltpu.VMEM(stack, F32)] * 2,
+        scratch_shapes=[pltpu.VMEM(stack, F32)] * 4,
         compiler_params=PARAMS,
         name="fluxes_x",
     )(*arrays)
@@ -715,15 +689,15 @@
     rows, cols = block
     inv_cx = 3.0 / (rows * lax.axis_size("gx") / 4.0) ** 2
     inv_cy = 3.0 / (cols * lax.axis_size("gy") / 4.0) ** 2
-    xa, ya, *outer = pack(h, p, q, b, m)
-    middle = load_middle(h, p, q, b, m)
-    near_x, near_y = cross(xa, "gx", 1), cross(ya, "gy", 1)
+    slabs_x = pack_x(h, p, q, b, m)
+    near_x = cross(slabs_x, "gx", 1)
+    near_y = cross(pack_y(h, p, q, b, m, after=slabs_x), "gy", 1)
     far_y = hand_on(jnp.pad(near_y[1], ((0, 5 * SUB), (0, 0))), "gy")
-    hx, hy, ix, iy, tx, wx, ty, wy, coef_x, coef_y = prepare_depth(outer[0], middle[0], inv_cx, inv_cy)
-    far_x = hand_on(second_of(near_x, coef_x), "gx")
-    px, py, qx, qy, bx, by, mx, my = prepare_rest(outer[1:], middle[1:])
+    far_x = hand_on(near_x[1], "gx")
+    hx, hy, ix, iy, tx, wx, ty, wy, coef_x, coef_y = prepare_depth(h, inv_cx, inv_cy)
+    px, py, qx, qy, bx, by, mx, my = prepare_rest(p, q, b, m)
+    inner = fluxes_x_inner(hx, px, qx, bx, mx)
     mass_y, shear_y, normal_y = fluxes_y(near_y, far_y, hy, py, qy, by, my)
-    inner = fluxes_x_inner(hx, px, qx, bx, mx, ix, mass_y, shear_y, inv_cx=inv_cx)
     depth, rx, ry, sx, sy, end_x, end_y, tall_y = fluxes_x(
         near_x, far_x, hx, px, qx, bx, mx, ix, iy, my, mass_y, shear_y, normal_y, *inner,
         tx, wx, ty, wy, coef_x, coef_y, inv_cx=inv_cx, inv_cy=inv_cy,

time: 26.9 us -> 25.9 us (0.963)
  Pallas kernels: 9.55 us -> 7.39 us
  starting transfers between devices: 12.7 us -> 13.5 us
  local copies, waits for them, and re-layouts: 0.01 us -> 0.32 us
    pallas_call x4 -> x3, Pallas kernels: 4.11 us -> 1.81 us  [the longest x1 0.99 us: pack_x(): pl.pallas_call(pack_x_kernel, out_shape=shape(2, SUB, cols), in_specs=[HB...]
    ppermute x9, starting transfers between devices: 9.51 us -> 9.92 us  [cross(): lax.ppermute(value, axis, [(i, i ^ mask) for i in range(lax.axis_size(axi...]
    ppermute x2, starting transfers between devices: 3.16 us -> 3.55 us  [hand_on(): lax.ppermute(value, axis, [(i, t if 0 <= t < count else i ^ 1) for i, t i...]
    unnamed x0 -> x10, local copies, waits for them, and re-layouts: none -> 0.3 us
  transfers between devices with their start and end apart: 11 -> 11, of which waited for: 4 -> 4; matrix products, arithmetic and copies ran while one was open for 0% -> 0% of each run, Pallas kernels for 22% -> 18%
where the time goes in v8:
time: 25.9 us; the launch traced here: 25.8 us
  starting transfers between devices  13.5 us (52%)
  Pallas kernels  7.39 us (29%)
  waiting for transfers between devices  3.82 us (15%)
  between operations  0.77 us (3%)
  local copies, waits for them, and re-layouts  0.32 us (1%)
    ppermute x9, starting transfers between devices, cross(): lax.ppermute(value, axis, [(i, i ^ mask) for i in range(lax.axis_size(axi...  9.92 us
    ppermute x9, waiting for transfers between devices, cross(): lax.ppermute(value, axis, [(i, i ^ mask) for i in range(lax.axis_size(axi...  3.82 us
    ppermute x2, starting transfers between devices, hand_on(): lax.ppermute(value, axis, [(i, t if 0 <= t < count else i ^ 1) for i, t i...  3.55 us
    pallas_call x2, Pallas kernels, solve(): pl.pallas_call(functools.partial(kernel, scale=scale), out_shape=shape(*b...  1.93 us
    pallas_call x1, Pallas kernels, pack_x(): pl.pallas_call(pack_x_kernel, out_shape=shape(2, SUB, cols), in_specs=[HB...  0.99 us
    pallas_call x1, Pallas kernels, fluxes_y(): pl.pallas_call(flux_y_kernel, out_shape=(shape(*stack),) * 3, in_specs=[V...  0.98 us
    pallas_call x1, Pallas kernels, prepare_rest(): pl.pallas_call(prepare_rest_kernel, out_shape=(shape(*stack),) * 8, in_sp...  0.76 us
    pallas_call x1, Pallas kernels, write_depth(): pl.pallas_call(depth_kernel, out_shape=shape(*block), in_specs=[VMEM], ou...  0.75 us
  transfers between devices with their start and end apart: 11, of which 4 were waited for; matrix products, arithmetic and copies ran while one was open for 0% of the time, Pallas kernels for 18%

profile of v8, /device:TPU:0, one launch (start us, length us, event | category | flops | bytes accessed | tf_op | source)
XLA Modules:
  0.0 25.8 jit_solution(6676679345048970494)
XLA Ops:
  0.7 1.0 %pack_x.1._ = f32[2,8,512]{2,1,0:T(8,128)S(1)} custom-call(f32[128,512]{1,0:T(8,128)} %h.5, f32[128,512]{1,0:T(8,128)} %p.3, f32[128,512]{1,0:T(8,128)} %q.3, f32[128,512]{1,0:T(8,128)} %b.3, s32[128,512]{1,0:T(8,128)} %m.3), custom_call_target="tpu_custom_call" | custom-call | tf_op jit(solution)/shard_map/pack_x/pallas_call | solution.py:78
  1.7 0.1 copy-done.3
  1.7 0.1 copy-done.2
  1.8 0.1 copy-done.1
  1.9 0.1 copy-done
  2.0 0.2 pack_y.1
  2.2 0.5 %collective-permute-start.2 = (f32[2,8,128]{2,1,0:T(8,128)S(1)}, f32[2,8,128]{2,1,0:T(8,128)S(1)}, u32[]{:S(2)}, u32[]{:S(2)}) collective-permute-start(f32[2,8,128]{2,1,0:T(8,128)S(1)} %pack_y.1), channel_id=1, source_target_pairs={{0,1},{1,0},{2,3},{3,2},{4,5},{5,4},{6,7},{7,6},{8,9},{9,8},{10,11... | collective-permute-start | bytes 24584 | tf_op jit(solution)/shard_map/ppermute | solution.py:668
  2.7 2.6 %collective-permute-start = (f32[2,8,512]{2,1,0:T(8,128)S(1)}, f32[2,8,512]{2,1,0:T(8,128)S(1)}, u32[]{:S(2)}, u32[]{:S(2)}) collective-permute-start(f32[2,8,512]{2,1,0:T(8,128)S(1)} %pack_x.1._), channel_id=1, source_target_pairs={{0,4},{4,0},{8,12},{12,8},{16,20},{20,16},{24,28},{28,24},{1,5},{5... | collective-permute-start | bytes 98312 | tf_op jit(solution)/shard_map/ppermute | solution.py:668
  5.3 0.0 collective-permute-done.2.near
  5.3 1.5 %collective-permute-start.3 = (f32[48,128]{1,0:T(8,128)S(1)}, f32[48,128]{1,0:T(8,128)S(1)}, u32[]{:S(2)}, u32[]{:S(2)}) collective-permute-start(f32[48,128]{1,0:T(8,128)S(1)} %pad.4), channel_id=1, source_target_pairs={{0,2},{1,0},{2,3},{3,1},{4,6},{5,4},{6,7},{7,5},{8,10},{9,8},{10,1... | collective-permute-start | bytes 73736 | tf_op jit(solution)/shard_map/ppermute | solution.py:664
  6.8 0.4 %collective-permute-done.near = f32[2,8,512]{2,1,0:T(8,128)S(1)} collective-permute-done((f32[2,8,512]{2,1,0:T(8,128)S(1)}, f32[2,8,512]{2,1,0:T(8,128)S(1)}, u32[]{:S(2)}, u32[]{:S(2)}) %collective-permute-start) | collective-permute-done | bytes 32800 | tf_op jit(solution)/shard_map/ppermute | solution.py:668
  7.2 2.0 %collective-permute-start.1 = (f32[8,512]{1,0:T(8,128)S(1)}, f32[8,512]{1,0:T(8,128)S(1)}, u32[]{:S(2)}, u32[]{:S(2)}) collective-permute-start(f32[8,512]{1,0:T(8,128)S(1)} %slice_bitcast_fusion), channel_id=1, source_target_pairs={{0,8},{4,0},{8,16},{12,4},{16,24},{20,12},{24,28},{28,20},{1,9},{5... | collective-permute-start | bytes 49160 | tf_op jit(solution)/shard_map/ppermute | solution.py:664
  9.3 0.4 %prepare_depth.1 = (f32[512,128]{1,0:T(8,128)S(1)}, f32[512,128]{1,0:T(8,128)S(1)}, f32[512,128]{1,0:T(8,128)S(1)}, f32[512,128]{1,0:T(8,128)S(1)}, f32[3,32,128...) custom-call(f32[128,512]{1,0:T(8,128)S(1)} %copy-done), custom_call_target="tpu_custom_call" | custom-call | flops 2000000 | bytes 4000000 | tf_op jit(solution)/shard_map/prepare_depth/pallas_call | solution.py:230
  9.7 0.8 %prepare_rest.1 = (f32[512,128]{1,0:T(8,128)S(1)}, f32[512,128]{1,0:T(8,128)S(1)}, f32[512,128]{1,0:T(8,128)S(1)}, f32[512,128]{1,0:T(8,128)S(1)}, f32[512,128]{...) custom-call(f32[128,512]{1,0:T(8,128)S(1)} %copy-done.1, ...), custom_call_target="tpu_custom_call" | custom-call | flops 2000000 | bytes 6000000 | tf_op jit(solution)/shard_map/prepare_rest/pallas_call | solution.py:250
  10.4 0.6 %fluxes_x_inner.1 = (f32[512,128]{1,0:T(8,128)S(1)}, f32[512,128]{1,0:T(8,128)S(1)}, f32[512,128]{1,0:T(8,128)S(1)}) custom-call(f32[512,128]{1,0:T(8,128)S(1)} %get-tuple-element.35.hx, f32[512,128]{1,0:T(8,128)S(1)} %get-tuple-element.36.px, f32[512,128]{1,0:T(8,128)S(1)} %get-tuple-element.37.qx, f32[512,128]{1,0:T(8,128)S(1)} %get-tuple-element.38.bx, ...), custom_call_target="tpu_custom_call" | custom-call | flops 4000000 | bytes 4000000 | tf_op jit(solution)/shard_map/fluxes_x_inner/pallas_call | solution.py:410
  11.1 0.0 collective-permute-done.3.far
  11.1 1.0 %fluxes_y.1 = (f32[512,128]{1,0:T(8,128)S(1)}, f32[512,128]{1,0:T(8,128)S(1)}, f32[512,128]{1,0:T(8,128)S(1)}) custom-call(f32[2,8,128]{2,1,0:T(8,128)S(1)} %collective-permute-done.2.near, f32[48,128]{1,0:T(8,128)S(1)} %collective-permute-done.3.far, f32[512,128]{1,0:T(8,128)S(1)} %get-tuple-element.43.hy, f32[512,128]{1,0:T(8,128)S(1)} %get-tuple-element.44.py, ...), custom_call_target="tpu_custom_call" | custom-call | flops 4000000 | bytes 4000000 | tf_op jit(solution)/shard_map/fluxes_y/pallas_call | solution.py:369
  12.1 0.0 collective-permute-done.1.far
  12.1 0.7 %fluxes_x.1 = (f32[512,128]{1,0:T(8,128)S(1)}, f32[512,128]{1,0:T(8,128)S(1)}, f32[512,128]{1,0:T(8,128)S(1)}, f32[4,32,128]{2,1,0:T(8,128)S(1)}, f32[6,32,128]{...) custom-call(f32[2,8,512]{2,1,0:T(8,128)S(1)} %collective-permute-done.near, ...), custom_call_target="tpu_custom_call" | custom-call | tf_op jit(solution)/shard_map/fluxes_x/pallas_call | solution.py:480
  12.8 0.9 %collective-permute-start.4 = (f32[8,512]{1,0:T(8,128)S(1)}, f32[8,512]{1,0:T(8,128)S(1)}, u32[]{:S(2)}, u32[]{:S(2)}) collective-permute-start(f32[8,512]{1,0:T(8,128)S(1)} %get-tuple-element.62.mine.refs_0_), channel_id=1, source_target_pairs={{0,4},{4,0},{8,12},{12,8},{16,20},{20,16},{24,28},{28,24},{1,5},{5... | collective-permute-start | bytes 49160 | tf_op jit(solution)/shard_map/ppermute | solution.py:668
  13.7 1.5 %collective-permute-start.9 = (f32[24,128]{1,0:T(8,128)S(1)}, f32[24,128]{1,0:T(8,128)S(1)}, u32[]{:S(2)}, u32[]{:S(2)}) collective-permute-start(f32[24,128]{1,0:T(8,128)S(1)} %get-tuple-element.66), channel_id=1, source_target_pairs={{0,2},{1,3},{2,0},{3,1},{4,6},{5,7},{6,4},{7,5},{8,10},{9,11},{10,... | collective-permute-start | bytes 36872 | tf_op jit(solution)/shard_map/ppermute | solution.py:668
  15.2 1.4 %collective-permute-done.4.theirs.refs_1_ = f32[8,512]{1,0:T(8,128)S(1)} collective-permute-done((f32[8,512]{1,0:T(8,128)S(1)}, f32[8,512]{1,0:T(8,128)S(1)}, u32[]{:S(2)}, u32[]{:S(2)}) %collective-permute-start.4) | collective-permute-done | bytes 16416 | tf_op jit(solution)/shard_map/ppermute | solution.py:668
  16.6 3.6 %collective-permute-start.8 = (f32[8,512]{1,0:T(8,128)S(1)}, f32[8,512]{1,0:T(8,128)S(1)}, u32[]{:S(2)}, u32[]{:S(2)}) collective-permute-start(f32[8,512]{1,0:T(8,128)S(1)} %merge.1.refs_2_), channel_id=1, source_target_pairs={{0,24},{4,28},{8,16},{12,20},{16,8},{20,12},{24,0},{28,4},{1,25},{... | collective-permute-start | bytes 49160 | tf_op jit(solution)/shard_map/ppermute | solution.py:668
  20.2 0.9 %collective-permute-start.6 = (f32[8,512]{1,0:T(8,128)S(1)}, f32[8,512]{1,0:T(8,128)S(1)}, u32[]{:S(2)}, u32[]{:S(2)}) collective-permute-start(f32[8,512]{1,0:T(8,128)S(1)} %merge.1.refs_2_), channel_id=1, source_target_pairs={{0,8},{4,12},{8,0},{12,4},{16,24},{20,28},{24,16},{28,20},{1,9},{5... | collective-permute-start | bytes 49160 | tf_op jit(solution)/shard_map/ppermute | solution.py:668
  21.1 0.0 collective-permute-done.9.refs_2_
  21.1 0.0 collective-permute-start.10
  21.1 0.7 %write_depth.1 = f32[128,512]{1,0:T(8,128)} custom-call(f32[512,128]{1,0:T(8,128)S(1)} %get-tuple-element.59.depth), custom_call_target="tpu_custom_call" | custom-call | flops 100000 | bytes 2000000 | tf_op jit(solution)/shard_map/write_depth/pallas_call | solution.py:514
  21.8 0.4 %collective-permute-done.10.refs_3_ = f32[8,128]{1,0:T(8,128)S(1)} collective-permute-done((f32[8,128]{1,0:T(8,128)S(1)}, f32[8,128]{1,0:T(8,128)S(1)}, u32[]{:S(2)}, u32[]{:S(2)}) %collective-permute-start.10) | collective-permute-done | bytes 4128 | tf_op jit(solution)/shard_map/ppermute | solution.py:668
  22.2 1.0 %solve_y.1 = f32[128,512]{1,0:T(8,128)} custom-call(f32[512,128]{1,0:T(8,128)S(1)} %get-tuple-element.41.iy.inv_ref, f32[512,128]{1,0:T(8,128)S(1)} %get-tuple-element.64.r_ref, f32[3,32,128]{2,1,0:T(8,128)S(1)} %get-tuple-element.55.ty.t_ref, f32[15,32,128]{2,1,0:T(8,128)S(1)} %get-tuple-element.56.wy.w_ref, f32[6,32,128]{2,1,0:T(8,128)S(1)} %get-tuple-element.65.s_ref, ...), custom_call_target="tpu_custom_call" | custom-call | flops 1000000 | bytes 4000000 | tf_op jit(solution)/shard_map/solve_y/pallas_call | solution.py:649
  23.3 0.0 collective-permute-done.8.refs_5_
  23.3 1.6 %collective-permute-done.7.refs_4_ = f32[8,512]{1,0:T(8,128)S(1)} collective-permute-done((f32[8,512]{1,0:T(8,128)S(1)}, f32[8,512]{1,0:T(8,128)S(1)}, u32[]{:S(2)}, u32[]{:S(2)}) %collective-permute-start.7) | collective-permute-done | bytes 16416 | tf_op jit(solution)/shard_map/ppermute | solution.py:668
  24.8 0.9 %solve_x.1 = f32[128,512]{1,0:T(8,128)} custom-call(f32[512,128]{1,0:T(8,128)S(1)} %get-tuple-element.40.ix.inv_ref, f32[512,128]{1,0:T(8,128)S(1)} %get-tuple-element.60.r_ref, f32[3,32,128]{2,1,0:T(8,128)S(1)} %get-tuple-element.53.tx.t_ref, f32[9,32,128]{2,1,0:T(8,128)S(1)} %get-tuple-element.54.wx.w_ref, f32[4,32,128]{2,1,0:T(8,128)S(1)} %get-tuple-element.61.s_ref, ...), custom_call_target="tpu_custom_call" | custom-call | flops 1000000 | bytes 4000000 | tf_op jit(solution)/shard_map/solve_x/pallas_call | solution.py:649
  (15 shorter events, 0.0 us)
Async XLA Ops:
  0.6 1.1 %copy-start.4 = (s32[128,512]{1,0:T(8,128)S(1)}, s32[128,512]{1,0:T(8,128)}, u32[]{:S(2)}) copy-start(s32[128,512]{1,0:T(8,128)} %m.3) | copy-start | bytes 786436
  0.6 1.1 %copy-start.3 = (f32[128,512]{1,0:T(8,128)S(1)}, f32[128,512]{1,0:T(8,128)}, u32[]{:S(2)}) copy-start(f32[128,512]{1,0:T(8,128)} %b.3) | copy-start | bytes 786436
  0.7 1.2 %copy-start.2 = (f32[128,512]{1,0:T(8,128)S(1)}, f32[128,512]{1,0:T(8,128)}, u32[]{:S(2)}) copy-start(f32[128,512]{1,0:T(8,128)} %q.3) | copy-start | bytes 786436
  0.7 1.2 %copy-start.1 = (f32[128,512]{1,0:T(8,128)S(1)}, f32[128,512]{1,0:T(8,128)}, u32[]{:S(2)}) copy-start(f32[128,512]{1,0:T(8,128)} %p.3) | copy-start | bytes 786436
  0.7 1.3 %copy-start = (f32[128,512]{1,0:T(8,128)S(1)}, f32[128,512]{1,0:T(8,128)}, u32[]{:S(2)}) copy-start(f32[128,512]{1,0:T(8,128)} %h.5) | copy-start | bytes 786436
  2.2 3.1 %collective-permute-start.2 = (f32[2,8,128]{2,1,0:T(8,128)S(1)}, f32[2,8,128]{2,1,0:T(8,128)S(1)}, u32[]{:S(2)}, u32[]{:S(2)}) collective-permute-start(f32[2,8,128]{2,1,0:T(8,128)S(1)} %pack_y.1), channel_id=1, source_target_pairs={{0,1},{1,0},{2,3},{3,2},{4,5},{5,4},{6,7},{7,6},{8,9},{9,8},{10,11... | collective-permute-start | bytes 24584 | tf_op jit(solution)/shard_map/ppermute | solution.py:668
  2.7 4.5 %collective-permute-start = (f32[2,8,512]{2,1,0:T(8,128)S(1)}, f32[2,8,512]{2,1,0:T(8,128)S(1)}, u32[]{:S(2)}, u32[]{:S(2)}) collective-permute-start(f32[2,8,512]{2,1,0:T(8,128)S(1)} %pack_x.1._), channel_id=1, source_target_pairs={{0,4},{4,0},{8,12},{12,8},{16,20},{20,16},{24,28},{28,24},{1,5},{5... | collective-permute-start | bytes 98312 | tf_op jit(solution)/shard_map/ppermute | solution.py:668
  5.3 5.8 %collective-permute-start.3 = (f32[48,128]{1,0:T(8,128)S(1)}, f32[48,128]{1,0:T(8,128)S(1)}, u32[]{:S(2)}, u32[]{:S(2)}) collective-permute-start(f32[48,128]{1,0:T(8,128)S(1)} %pad.4), channel_id=1, source_target_pairs={{0,2},{1,0},{2,3},{3,1},{4,6},{5,4},{6,7},{7,5},{8,10},{9,8},{10,1... | collective-permute-start | bytes 73736 | tf_op jit(solution)/shard_map/ppermute | solution.py:664
  7.2 4.8 %collective-permute-start.1 = (f32[8,512]{1,0:T(8,128)S(1)}, f32[8,512]{1,0:T(8,128)S(1)}, u32[]{:S(2)}, u32[]{:S(2)}) collective-permute-start(f32[8,512]{1,0:T(8,128)S(1)} %slice_bitcast_fusion), channel_id=1, source_target_pairs={{0,8},{4,0},{8,16},{12,4},{16,24},{20,12},{24,28},{28,20},{1,9},{5... | collective-permute-start | bytes 49160 | tf_op jit(solution)/shard_map/ppermute | solution.py:664
  12.8 3.8 %collective-permute-start.4 = (f32[8,512]{1,0:T(8,128)S(1)}, f32[8,512]{1,0:T(8,128)S(1)}, u32[]{:S(2)}, u32[]{:S(2)}) collective-permute-start(f32[8,512]{1,0:T(8,128)S(1)} %get-tuple-element.62.mine.refs_0_), channel_id=1, source_target_pairs={{0,4},{4,0},{8,12},{12,8},{16,20},{20,16},{24,28},{28,24},{1,5},{5... | collective-permute-start | bytes 49160 | tf_op jit(solution)/shard_map/ppermute | solution.py:668
  13.7 1.5 %collective-permute-start.5 = (f32[8,128]{1,0:T(8,128)S(1)}, f32[8,128]{1,0:T(8,128)S(1)}, u32[]{:S(2)}, u32[]{:S(2)}) collective-permute-start(f32[8,128]{1,0:T(8,128)S(1)} %get-tuple-element.63.refs_0_), channel_id=1, source_target_pairs={{0,1},{1,0},{2,3},{3,2},{4,5},{5,4},{6,7},{7,6},{8,9},{9,8},{10,11... | collective-permute-start | bytes 12296 | tf_op jit(solution)/shard_map/ppermute | solution.py:668
  13.7 7.4 %collective-permute-start.9 = (f32[24,128]{1,0:T(8,128)S(1)}, f32[24,128]{1,0:T(8,128)S(1)}, u32[]{:S(2)}, u32[]{:S(2)}) collective-permute-start(f32[24,128]{1,0:T(8,128)S(1)} %get-tuple-element.66), channel_id=1, source_target_pairs={{0,2},{1,3},{2,0},{3,1},{4,6},{5,7},{6,4},{7,5},{8,10},{9,11},{10,... | collective-permute-start | bytes 36872 | tf_op jit(solution)/shard_map/ppermute | solution.py:668
  16.6 6.6 %collective-permute-start.8 = (f32[8,512]{1,0:T(8,128)S(1)}, f32[8,512]{1,0:T(8,128)S(1)}, u32[]{:S(2)}, u32[]{:S(2)}) collective-permute-start(f32[8,512]{1,0:T(8,128)S(1)} %merge.1.refs_2_), channel_id=1, source_target_pairs={{0,24},{4,28},{8,16},{12,20},{16,8},{20,12},{24,0},{28,4},{1,25},{... | collective-permute-start | bytes 49160 | tf_op jit(solution)/shard_map/ppermute | solution.py:668
  20.2 4.6 %collective-permute-start.7 = (f32[8,512]{1,0:T(8,128)S(1)}, f32[8,512]{1,0:T(8,128)S(1)}, u32[]{:S(2)}, u32[]{:S(2)}) collective-permute-start(f32[8,512]{1,0:T(8,128)S(1)} %merge.1.refs_2_), channel_id=1, source_target_pairs={{0,16},{4,20},{8,24},{12,28},{16,0},{20,4},{24,8},{28,12},{1,17},{... | collective-permute-start | bytes 49160 | tf_op jit(solution)/shard_map/ppermute | solution.py:668
  20.2 4.6 %collective-permute-start.6 = (f32[8,512]{1,0:T(8,128)S(1)}, f32[8,512]{1,0:T(8,128)S(1)}, u32[]{:S(2)}, u32[]{:S(2)}) collective-permute-start(f32[8,512]{1,0:T(8,128)S(1)} %merge.1.refs_2_), channel_id=1, source_target_pairs={{0,8},{4,12},{8,0},{12,4},{16,24},{20,28},{24,16},{28,20},{1,9},{5... | collective-permute-start | bytes 49160 | tf_op jit(solution)/shard_map/ppermute | solution.py:668
  21.1 1.2 %collective-permute-start.10 = (f32[8,128]{1,0:T(8,128)S(1)}, f32[8,128]{1,0:T(8,128)S(1)}, u32[]{:S(2)}, u32[]{:S(2)}) collective-permute-start(f32[8,128]{1,0:T(8,128)S(1)} %slice.14), channel_id=1, source_target_pairs={{0,1},{1,0},{2,3},{3,2},{4,5},{5,4},{6,7},{7,6},{8,9},{9,8},{10,11... | collective-permute-start | bytes 12296 | tf_op jit(solution)/shard_map/ppermute | solution.py:668

commit v9 on v8

--- a/solution.py
+++ b/solution.py
@@ -419,15 +419,14 @@
 
 
 def flux_x_kernel(
-    near, far, hx, px, qx, bx, mx, ix, iy, my, mass_y, shear_y, normal_y, depth_in, push_in, across_in,
-    tx, wx, ty, wy, coefx, coefy,
-    depth, rx, ry, sx, sy, endx, endy, tally,
-    outer_depth, push, across, turned,
-    *, inv_cx, inv_cy,
+    near, far, hx, px, qx, bx, mx, ix, shear_y, push_in, tx, wx, coef,
+    depth, across, rx, sx, ends,
+    push,
+    *, inv_cx,
 ):
     tiles = hx.shape[0] // LANES
     low, high = low_high("gx", near[0], far[...])
-    store = x_store(hx, px, mx, outer_depth, push, across)
+    store = x_store(hx, px, mx, depth, push, across)
     for tile in range(tiles):
         span = tile_span(tile)
 
@@ -439,32 +438,19 @@
         fields, bed, wet = [extend(hx, 0, 2), extend(px, 2, 2), extend(qx, 4, 2)], extend(bx, 6, 1), extend(mx, 7, 1)
         tile_fluxes(fields, bed, wet, store(tile), 0, INNER[0])
         tile_fluxes(fields, bed, wet, store(tile), INNER[1], STEPS)
-        inner = slice(at(tile, INNER[0]).start, at(tile, INNER[1]).start)
-        for done, ref in ((depth_in, outer_depth), (push_in, push), (across_in, across)):
-            ref[inner, :] = done[inner, :]
-        turned[span, :] = across[span, :].T
-        m, inverse = mx[span, :], ix[span, :]
-        depth[span, :] = outer_depth[span, :] - m * mass_y[span, :]
-        rx[span, :] = (inv_cx * (inverse * inverse)) * m * (push[span, :] - shear_y[span, :])
         for k in range(STEPS):
             here = at(tile, k)
-            inverse = iy[here, :]
-            total = normal_y[here, :] - turned[spread_rows(tile, k), :]
-            ry[here, :] = (inv_cy * (inverse * inverse)) * my[here, :] * total
-
-    ends_x = march_source(ix, inv_cx, rx, tx, wx, sx, log2(SUB))
-    ends_y = march_source(iy, inv_cy, ry, ty, wy, sy, log2(SUB * tiles))
-    endx[...] = coefx[...]
-    endy[...] = coefy[...]
+            inverse = ix[here, :]
+            total = (push_in if INNER[0] <= k < INNER[1] else push)[here, :] - shear_y[here, :]
+            rx[here, :] = (inv_cx * (inverse * inverse)) * mx[here, :] * total
+    sources = march_source(ix, inv_cx, rx, tx, wx, sx, log2(SUB))
+    ends[...] = coef[...]
     for i in range(2):
         for tile in range(tiles):
-            endx[3 + i : 4 + i, tile_span(tile)] = ends_x[i][tile * SUB : tile * SUB + 1, :]
-        endy[3 + i : 4 + i, :] = ends_y[i][0:1, :]
-    tally[...] = jnp.zeros_like(tally)
-    tally[0:SUB, :] = endy[...]
-
-
-def fluxes_x(*arrays, inv_cx, inv_cy):
+            ends[3 + i : 4 + i, tile_span(tile)] = sources[i][tile * SUB : tile * SUB + 1, :]
+
+
+def fluxes_x(*arrays, inv_cx):
     stack = arrays[2].shape
     count = stack[0] // STEPS
     shapes = (
@@ -472,19 +458,66 @@
         shape(*stack),
         shape(*stack),
         shape(1 + log2(SUB), count, LANES),
+        shape(*arrays[-1].shape),
+    )
+    return pl.pallas_call(
+        functools.partial(flux_x_kernel, inv_cx=inv_cx),
+        out_shape=shapes,
+        in_specs=[VMEM] * len(arrays),
+        out_specs=(VMEM,) * len(shapes),
+        scratch_shapes=[pltpu.VMEM(stack, F32)],
+        compiler_params=PARAMS,
+        name="fluxes_x",
+    )(*arrays)
+
+
+def join_y_kernel(
+    depth_inner, across_inner, depth_outer, across_outer, mass_y, mx, normal_y, iy, my, ty, wy, coef,
+    depth, ry, sy, ends, tall,
+    across, turned,
+    *, inv_cy,
+):
+    tiles = mx.shape[0] // LANES
+    for tile in range(tiles):
+        span = tile_span(tile)
+        for k in range(STEPS):
+            here = at(tile, k)
+            inner = INNER[0] <= k < INNER[1]
+            across[here, :] = (across_inner if inner else across_outer)[here, :]
+            depth[here, :] = (depth_inner if inner else depth_outer)[here, :] - mx[here, :] * mass_y[here, :]
+        turned[span, :] = across[span, :].T
+        for k in range(STEPS):
+            here = at(tile, k)
+            inverse = iy[here, :]
+            total = normal_y[here, :] - turned[spread_rows(tile, k), :]
+            ry[here, :] = (inv_cy * (inverse * inverse)) * my[here, :] * total
+    sources = march_source(iy, inv_cy, ry, ty, wy, sy, log2(SUB * tiles))
+    ends[...] = coef[...]
+    for i in range(2):
+        ends[3 + i : 4 + i, :] = sources[i][0:1, :]
+    tall[...] = jnp.zeros_like(tall)
+    tall[0:SUB, :] = ends[...]
+
+
+def join_y(*arrays, inv_cy):
+    stack = arrays[0].shape
+    count = stack[0] // STEPS
+    shapes = (
+        shape(*stack),
+        shape(*stack),
         shape(1 + log2(count), count, LANES),
-        shape(*arrays[-2].shape),
         shape(*arrays[-1].shape),
         shape(3 * SUB, arrays[-1].shape[1]),
     )
     return pl.pallas_call(
-        functools.partial(flux_x_kernel, inv_cx=inv_cx, inv_cy=inv_cy),
+        functools.partial(join_y_kernel, inv_cy=inv_cy),
         out_shape=shapes,
         in_specs=[VMEM] * len(arrays),
         out_specs=(VMEM,) * len(shapes),
-        scratch_shapes=[pltpu.VMEM(stack, F32)] * 4,
-        compiler_params=PARAMS,
-        name="fluxes_x",
+        scratch_shapes=[pltpu.VMEM(stack, F32)] * 2,
+        compiler_params=PARAMS,
+        cost_estimate=pl.CostEstimate(flops=2_000_000, bytes_accessed=2_000_000, transcendentals=0),
+        name="join_y",
     )(*arrays)
 
 
@@ -693,14 +726,16 @@
     near_x = cross(slabs_x, "gx", 1)
     near_y = cross(pack_y(h, p, q, b, m, after=slabs_x), "gy", 1)
     far_y = hand_on(jnp.pad(near_y[1], ((0, 5 * SUB), (0, 0))), "gy")
-    far_x = hand_on(near_x[1], "gx")
     hx, hy, ix, iy, tx, wx, ty, wy, coef_x, coef_y = prepare_depth(h, inv_cx, inv_cy)
+    far_x = hand_on(second_of(near_x, coef_x), "gx")
     px, py, qx, qy, bx, by, mx, my = prepare_rest(p, q, b, m)
-    inner = fluxes_x_inner(hx, px, qx, bx, mx)
+    depth_inner, push_inner, across_inner = fluxes_x_inner(hx, px, qx, bx, mx)
     mass_y, shear_y, normal_y = fluxes_y(near_y, far_y, hy, py, qy, by, my)
-    depth, rx, ry, sx, sy, end_x, end_y, tall_y = fluxes_x(
-        near_x, far_x, hx, px, qx, bx, mx, ix, iy, my, mass_y, shear_y, normal_y, *inner,
-        tx, wx, ty, wy, coef_x, coef_y, inv_cx=inv_cx, inv_cy=inv_cy,
+    depth_outer, across_outer, rx, sx, end_x = fluxes_x(
+        near_x, far_x, hx, px, qx, bx, mx, ix, shear_y, push_inner, tx, wx, coef_x, inv_cx=inv_cx
+    )
+    depth, ry, sy, end_y, tall_y = join_y(
+        depth_inner, across_inner, depth_outer, across_outer, mass_y, mx, normal_y, iy, my, ty, wy, coef_y, inv_cy=inv_cy
     )
     new_depth = write_depth(depth, block)
     parts_y = parts_of_line("gy", end_y, True, tall=tall_y if lax.axis_size("gy") == 4 else None)

time: 25.9 us -> 25.3 us (0.977)
  waiting for transfers between devices: 3.82 us -> 2.52 us
  starting transfers between devices: 13.5 us -> 14 us
    ppermute x9, waiting for transfers between devices: 3.82 us -> 2.52 us  [cross(): lax.ppermute(value, axis, [(i, i ^ mask) for i in range(lax.axis_size(axi...]
    ppermute x9, starting transfers between devices: 9.92 us -> 10.4 us  [cross(): lax.ppermute(value, axis, [(i, i ^ mask) for i in range(lax.axis_size(axi...]
    pallas_call x1 -> x3, Pallas kernels: 0.73 us -> 0.82 us  [the longest x1 0.47 us: fluxes_x(): pl.pallas_call(functools.partial(flux_x_kernel, inv_cx=inv_cx), out_shape...]
  transfers between devices with their start and end apart: 11 -> 11, of which waited for: 4 -> 3; matrix products, arithmetic and copies ran while one was open for 0% -> 0% of each run, Pallas kernels for 18% -> 20%
where the time goes in v9:
time: 25.3 us; the launch traced here: 25.1 us
  starting transfers between devices  14 us (55%)
  Pallas kernels  7.53 us (30%)
  waiting for transfers between devices  2.52 us (10%)
  between operations  0.79 us (3%)
  local copies, waits for them, and re-layouts  0.31 us (1%)
    ppermute x9, starting transfers between devices, cross(): lax.ppermute(value, axis, [(i, i ^ mask) for i in range(lax.axis_size(axi...  10.4 us
    ppermute x2, starting transfers between devices, hand_on(): lax.ppermute(value, axis, [(i, t if 0 <= t < count else i ^ 1) for i, t i...  3.54 us
    ppermute x9, waiting for transfers between devices, cross(): lax.ppermute(value, axis, [(i, i ^ mask) for i in range(lax.axis_size(axi...  2.52 us
    pallas_call x2, Pallas kernels, solve(): pl.pallas_call(functools.partial(kernel, scale=scale), out_shape=shape(*b...  1.93 us
    pallas_call x1, Pallas kernels, pack_x(): pl.pallas_call(pack_x_kernel, out_shape=shape(2, SUB, cols), in_specs=[HB...  0.99 us
    pallas_call x1, Pallas kernels, fluxes_y(): pl.pallas_call(flux_y_kernel, out_shape=(shape(*stack),) * 3, in_specs=[V...  0.98 us
    pallas_call x1, Pallas kernels, prepare_rest(): pl.pallas_call(prepare_rest_kernel, out_shape=(shape(*stack),) * 8, in_sp...  0.81 us
    pallas_call x1, Pallas kernels, write_depth(): pl.pallas_call(depth_kernel, out_shape=shape(*block), in_specs=[VMEM], ou...  0.75 us
  transfers between devices with their start and end apart: 11, of which 3 were waited for; matrix products, arithmetic and copies ran while one was open for 0% of the time, Pallas kernels for 20%

profile of v9, /device:TPU:0, one launch (start us, length us, event | category | flops | bytes accessed | tf_op | source)
XLA Modules:
  0.0 25.1 jit_solution(4402007658549698693)
XLA Ops:
  0.7 1.0 %pack_x.1._ = f32[2,8,512]{2,1,0:T(8,128)S(1)} custom-call(f32[128,512]{1,0:T(8,128)} %h.5, f32[128,512]{1,0:T(8,128)} %p.3, f32[128,512]{1,0:T(8,128)} %q.3, f32[128,512]{1,0:T(8,128)} %b.3, s32[128,512]{1,0:T(8,128)} %m.3), custom_call_target="tpu_custom_call" | custom-call | tf_op jit(solution)/shard_map/pack_x/pallas_call | solution.py:78
  1.7 0.1 copy-done.3
  1.7 0.1 copy-done.2
  1.8 0.1 copy-done.1
  1.9 0.1 copy-done
  2.0 0.2 pack_y.1
  2.2 0.5 %collective-permute-start.2 = (f32[2,8,128]{2,1,0:T(8,128)S(1)}, f32[2,8,128]{2,1,0:T(8,128)S(1)}, u32[]{:S(2)}, u32[]{:S(2)}) collective-permute-start(f32[2,8,128]{2,1,0:T(8,128)S(1)} %pack_y.1), channel_id=1, source_target_pairs={{0,1},{1,0},{2,3},{3,2},{4,5},{5,4},{6,7},{7,6},{8,9},{9,8},{10,11... | collective-permute-start | bytes 24584 | tf_op jit(solution)/shard_map/ppermute | solution.py:701
  2.7 2.6 %collective-permute-start = (f32[2,8,512]{2,1,0:T(8,128)S(1)}, f32[2,8,512]{2,1,0:T(8,128)S(1)}, u32[]{:S(2)}, u32[]{:S(2)}) collective-permute-start(f32[2,8,512]{2,1,0:T(8,128)S(1)} %pack_x.1._), channel_id=1, source_target_pairs={{0,4},{4,0},{8,12},{12,8},{16,20},{20,16},{24,28},{28,24},{1,5},{5... | collective-permute-start | bytes 98312 | tf_op jit(solution)/shard_map/ppermute | solution.py:701
  5.3 0.0 collective-permute-done.2.near
  5.3 1.5 %collective-permute-start.3 = (f32[48,128]{1,0:T(8,128)S(1)}, f32[48,128]{1,0:T(8,128)S(1)}, u32[]{:S(2)}, u32[]{:S(2)}) collective-permute-start(f32[48,128]{1,0:T(8,128)S(1)} %pad.4), channel_id=1, source_target_pairs={{0,2},{1,0},{2,3},{3,1},{4,6},{5,4},{6,7},{7,5},{8,10},{9,8},{10,1... | collective-permute-start | bytes 73736 | tf_op jit(solution)/shard_map/ppermute | solution.py:697
  6.8 0.4 %prepare_depth.1 = (f32[512,128]{1,0:T(8,128)S(1)}, f32[512,128]{1,0:T(8,128)S(1)}, f32[512,128]{1,0:T(8,128)S(1)}, f32[512,128]{1,0:T(8,128)S(1)}, f32[3,32,128...) custom-call(f32[128,512]{1,0:T(8,128)S(1)} %copy-done), custom_call_target="tpu_custom_call" | custom-call | flops 2000000 | bytes 4000000 | tf_op jit(solution)/shard_map/prepare_depth/pallas_call | solution.py:230
  7.2 0.0 collective-permute-done.both.near
  7.2 2.0 %collective-permute-start.1 = (f32[8,512]{1,0:T(8,128)S(1)}, f32[8,512]{1,0:T(8,128)S(1)}, u32[]{:S(2)}, u32[]{:S(2)}) collective-permute-start(f32[8,512]{1,0:T(8,128)S(1)} %second_of.1), channel_id=1, source_target_pairs={{0,8},{4,0},{8,16},{12,4},{16,24},{20,12},{24,28},{28,20},{1,9},{5... | collective-permute-start | bytes 49160 | tf_op jit(solution)/shard_map/ppermute | solution.py:697
  9.3 0.8 %prepare_rest.1 = (f32[512,128]{1,0:T(8,128)S(1)}, f32[512,128]{1,0:T(8,128)S(1)}, f32[512,128]{1,0:T(8,128)S(1)}, f32[512,128]{1,0:T(8,128)S(1)}, f32[512,128]{...) custom-call(f32[128,512]{1,0:T(8,128)S(1)} %copy-done.1, ...), custom_call_target="tpu_custom_call" | custom-call | flops 2000000 | bytes 6000000 | tf_op jit(solution)/shard_map/prepare_rest/pallas_call | solution.py:250
  10.1 0.6 %fluxes_x_inner.1 = (f32[512,128]{1,0:T(8,128)S(1)}, f32[512,128]{1,0:T(8,128)S(1)}, f32[512,128]{1,0:T(8,128)S(1)}) custom-call(f32[512,128]{1,0:T(8,128)S(1)} %get-tuple-element.37.hx, f32[512,128]{1,0:T(8,128)S(1)} %get-tuple-element.38.px, f32[512,128]{1,0:T(8,128)S(1)} %get-tuple-element.39.qx, f32[512,128]{1,0:T(8,128)S(1)} %get-tuple-element.40.bx, ...), custom_call_target="tpu_custom_call" | custom-call | flops 4000000 | bytes 4000000 | tf_op jit(solution)/shard_map/fluxes_x_inner/pallas_call | solution.py:410
  10.7 0.0 collective-permute-done.3.far
  10.7 1.0 %fluxes_y.1 = (f32[512,128]{1,0:T(8,128)S(1)}, f32[512,128]{1,0:T(8,128)S(1)}, f32[512,128]{1,0:T(8,128)S(1)}) custom-call(f32[2,8,128]{2,1,0:T(8,128)S(1)} %collective-permute-done.2.near, f32[48,128]{1,0:T(8,128)S(1)} %collective-permute-done.3.far, f32[512,128]{1,0:T(8,128)S(1)} %get-tuple-element.46.hy, f32[512,128]{1,0:T(8,128)S(1)} %get-tuple-element.47.py, ...), custom_call_target="tpu_custom_call" | custom-call | flops 4000000 | bytes 4000000 | tf_op jit(solution)/shard_map/fluxes_y/pallas_call | solution.py:369
  11.7 0.5 %fluxes_x.1 = (f32[512,128]{1,0:T(8,128)S(1)}, f32[512,128]{1,0:T(8,128)S(1)}, f32[512,128]{1,0:T(8,128)S(1)}, f32[4,32,128]{2,1,0:T(8,128)S(1)}, f32[8,512]{1,0:T(8,128)S(1)}) custom-call(f32[2,8,512]{2,1,0:T(8,128)S(1)} %collective-permute-done.both.near, f32[8,512]{1,0:T(8,128)S(1)} %collective-permute-done.1.far, f32[512,128]{1,0:T(8,128)S(1)} %get-tuple-element.37.hx, ...), custom_call_target="tpu_custom_call" | custom-call | tf_op jit(solution)/shard_map/fluxes_x/pallas_call | solution.py:463
  12.2 1.3 %collective-permute-start.4 = (f32[8,512]{1,0:T(8,128)S(1)}, f32[8,512]{1,0:T(8,128)S(1)}, u32[]{:S(2)}, u32[]{:S(2)}) collective-permute-start(f32[8,512]{1,0:T(8,128)S(1)} %get-tuple-element.66.mine.refs_0_), channel_id=1, source_target_pairs={{0,4},{4,0},{8,12},{12,8},{16,20},{20,16},{24,28},{28,24},{1,5},{5... | collective-permute-start | bytes 49160 | tf_op jit(solution)/shard_map/ppermute | solution.py:701
  13.4 0.3 %join_y.1 = (f32[512,128]{1,0:T(8,128)S(1)}, f32[512,128]{1,0:T(8,128)S(1)}, f32[6,32,128]{2,1,0:T(8,128)S(1)}, f32[8,128]{1,0:T(8,128)S(1)}, f32[24,128]{1,0:T(8,128)S(1)}) custom-call(f32[512,128]{1,0:T(8,128)S(1)} %get-tuple-element.42.depth_inner, f32[512,128]{1,0:T(8,128)S(1)} %get-tuple-element.43.across_inner, ...), custom_call_target="tpu_custom_call" | custom-call | flops 2000000 | bytes 2000000 | tf_op jit(solution)/shard_map/join_y/pallas_call | solution.py:512
  13.8 0.1 collective-permute-start.5
  13.9 1.6 %collective-permute-start.9 = (f32[24,128]{1,0:T(8,128)S(1)}, f32[24,128]{1,0:T(8,128)S(1)}, u32[]{:S(2)}, u32[]{:S(2)}) collective-permute-start(f32[24,128]{1,0:T(8,128)S(1)} %get-tuple-element.70), channel_id=1, source_target_pairs={{0,2},{1,3},{2,0},{3,1},{4,6},{5,7},{6,4},{7,5},{8,10},{9,11},{10,... | collective-permute-start | bytes 36872 | tf_op jit(solution)/shard_map/ppermute | solution.py:701
  15.5 0.5 %collective-permute-done.4.theirs.refs_1_ = f32[8,512]{1,0:T(8,128)S(1)} collective-permute-done((f32[8,512]{1,0:T(8,128)S(1)}, f32[8,512]{1,0:T(8,128)S(1)}, u32[]{:S(2)}, u32[]{:S(2)}) %collective-permute-start.4) | collective-permute-done | bytes 16416 | tf_op jit(solution)/shard_map/ppermute | solution.py:701
  16.0 3.6 %collective-permute-start.8 = (f32[8,512]{1,0:T(8,128)S(1)}, f32[8,512]{1,0:T(8,128)S(1)}, u32[]{:S(2)}, u32[]{:S(2)}) collective-permute-start(f32[8,512]{1,0:T(8,128)S(1)} %merge.1.refs_2_), channel_id=1, source_target_pairs={{0,24},{4,28},{8,16},{12,20},{16,8},{20,12},{24,0},{28,4},{1,25},{... | collective-permute-start | bytes 49160 | tf_op jit(solution)/shard_map/ppermute | solution.py:701
  19.6 0.0 collective-permute-start.7
  19.6 0.9 %collective-permute-start.6 = (f32[8,512]{1,0:T(8,128)S(1)}, f32[8,512]{1,0:T(8,128)S(1)}, u32[]{:S(2)}, u32[]{:S(2)}) collective-permute-start(f32[8,512]{1,0:T(8,128)S(1)} %merge.1.refs_2_), channel_id=1, source_target_pairs={{0,8},{4,12},{8,0},{12,4},{16,24},{20,28},{24,16},{28,20},{1,9},{5... | collective-permute-start | bytes 49160 | tf_op jit(solution)/shard_map/ppermute | solution.py:701
  20.4 0.0 collective-permute-done.9.refs_2_
  20.5 0.7 %write_depth.1 = f32[128,512]{1,0:T(8,128)} custom-call(f32[512,128]{1,0:T(8,128)S(1)} %get-tuple-element.63.depth), custom_call_target="tpu_custom_call" | custom-call | flops 100000 | bytes 2000000 | tf_op jit(solution)/shard_map/write_depth/pallas_call | solution.py:547
  21.2 0.4 %collective-permute-done.10.refs_3_ = f32[8,128]{1,0:T(8,128)S(1)} collective-permute-done((f32[8,128]{1,0:T(8,128)S(1)}, f32[8,128]{1,0:T(8,128)S(1)}, u32[]{:S(2)}, u32[]{:S(2)}) %collective-permute-start.10) | collective-permute-done | bytes 4128 | tf_op jit(solution)/shard_map/ppermute | solution.py:701
  21.6 1.0 %solve_y.1 = f32[128,512]{1,0:T(8,128)} custom-call(f32[512,128]{1,0:T(8,128)S(1)} %get-tuple-element.59.iy.inv_ref, f32[512,128]{1,0:T(8,128)S(1)} %get-tuple-element.68.r_ref, f32[3,32,128]{2,1,0:T(8,128)S(1)} %get-tuple-element.60.ty.t_ref, f32[15,32,128]{2,1,0:T(8,128)S(1)} %get-tuple-element.61.wy.w_ref, f32[6,32,128]{2,1,0:T(8,128)S(1)} %get-tuple-element.69.s_ref, ...), custom_call_target="tpu_custom_call" | custom-call | flops 1000000 | bytes 4000000 | tf_op jit(solution)/shard_map/solve_y/pallas_call | solution.py:682
  22.6 1.6 %collective-permute-done.7.refs_4_ = f32[8,512]{1,0:T(8,128)S(1)} collective-permute-done((f32[8,512]{1,0:T(8,128)S(1)}, f32[8,512]{1,0:T(8,128)S(1)}, u32[]{:S(2)}, u32[]{:S(2)}) %collective-permute-start.7) | collective-permute-done | bytes 16416 | tf_op jit(solution)/shard_map/ppermute | solution.py:701
  24.2 0.9 %solve_x.1 = f32[128,512]{1,0:T(8,128)} custom-call(f32[512,128]{1,0:T(8,128)S(1)} %get-tuple-element.45.ix.inv_ref, f32[512,128]{1,0:T(8,128)S(1)} %get-tuple-element.64.r_ref, f32[3,32,128]{2,1,0:T(8,128)S(1)} %get-tuple-element.53.tx.t_ref, f32[9,32,128]{2,1,0:T(8,128)S(1)} %get-tuple-element.54.wx.w_ref, f32[4,32,128]{2,1,0:T(8,128)S(1)} %get-tuple-element.65.s_ref, ...), custom_call_target="tpu_custom_call" | custom-call | flops 1000000 | bytes 4000000 | tf_op jit(solution)/shard_map/solve_x/pallas_call | solution.py:682
  (16 shorter events, 0.1 us)
Async XLA Ops:
  0.6 1.1 %copy-start.4 = (s32[128,512]{1,0:T(8,128)S(1)}, s32[128,512]{1,0:T(8,128)}, u32[]{:S(2)}) copy-start(s32[128,512]{1,0:T(8,128)} %m.3) | copy-start | bytes 786436
  0.6 1.1 %copy-start.3 = (f32[128,512]{1,0:T(8,128)S(1)}, f32[128,512]{1,0:T(8,128)}, u32[]{:S(2)}) copy-start(f32[128,512]{1,0:T(8,128)} %b.3) | copy-start | bytes 786436
  0.7 1.2 %copy-start.2 = (f32[128,512]{1,0:T(8,128)S(1)}, f32[128,512]{1,0:T(8,128)}, u32[]{:S(2)}) copy-start(f32[128,512]{1,0:T(8,128)} %q.3) | copy-start | bytes 786436
  0.7 1.2 %copy-start.1 = (f32[128,512]{1,0:T(8,128)S(1)}, f32[128,512]{1,0:T(8,128)}, u32[]{:S(2)}) copy-start(f32[128,512]{1,0:T(8,128)} %p.3) | copy-start | bytes 786436
  0.7 1.3 %copy-start = (f32[128,512]{1,0:T(8,128)S(1)}, f32[128,512]{1,0:T(8,128)}, u32[]{:S(2)}) copy-start(f32[128,512]{1,0:T(8,128)} %h.5) | copy-start | bytes 786436
  2.2 3.1 %collective-permute-start.2 = (f32[2,8,128]{2,1,0:T(8,128)S(1)}, f32[2,8,128]{2,1,0:T(8,128)S(1)}, u32[]{:S(2)}, u32[]{:S(2)}) collective-permute-start(f32[2,8,128]{2,1,0:T(8,128)S(1)} %pack_y.1), channel_id=1, source_target_pairs={{0,1},{1,0},{2,3},{3,2},{4,5},{5,4},{6,7},{7,6},{8,9},{9,8},{10,11... | collective-permute-start | bytes 24584 | tf_op jit(solution)/shard_map/ppermute | solution.py:701
  2.7 4.5 %collective-permute-start = (f32[2,8,512]{2,1,0:T(8,128)S(1)}, f32[2,8,512]{2,1,0:T(8,128)S(1)}, u32[]{:S(2)}, u32[]{:S(2)}) collective-permute-start(f32[2,8,512]{2,1,0:T(8,128)S(1)} %pack_x.1._), channel_id=1, source_target_pairs={{0,4},{4,0},{8,12},{12,8},{16,20},{20,16},{24,28},{28,24},{1,5},{5... | collective-permute-start | bytes 98312 | tf_op jit(solution)/shard_map/ppermute | solution.py:701
  5.3 5.4 %collective-permute-start.3 = (f32[48,128]{1,0:T(8,128)S(1)}, f32[48,128]{1,0:T(8,128)S(1)}, u32[]{:S(2)}, u32[]{:S(2)}) collective-permute-start(f32[48,128]{1,0:T(8,128)S(1)} %pad.4), channel_id=1, source_target_pairs={{0,2},{1,0},{2,3},{3,1},{4,6},{5,4},{6,7},{7,5},{8,10},{9,8},{10,1... | collective-permute-start | bytes 73736 | tf_op jit(solution)/shard_map/ppermute | solution.py:697
  7.2 4.4 %collective-permute-start.1 = (f32[8,512]{1,0:T(8,128)S(1)}, f32[8,512]{1,0:T(8,128)S(1)}, u32[]{:S(2)}, u32[]{:S(2)}) collective-permute-start(f32[8,512]{1,0:T(8,128)S(1)} %second_of.1), channel_id=1, source_target_pairs={{0,8},{4,0},{8,16},{12,4},{16,24},{20,12},{24,28},{28,20},{1,9},{5... | collective-permute-start | bytes 49160 | tf_op jit(solution)/shard_map/ppermute | solution.py:697
  12.2 3.8 %collective-permute-start.4 = (f32[8,512]{1,0:T(8,128)S(1)}, f32[8,512]{1,0:T(8,128)S(1)}, u32[]{:S(2)}, u32[]{:S(2)}) collective-permute-start(f32[8,512]{1,0:T(8,128)S(1)} %get-tuple-element.66.mine.refs_0_), channel_id=1, source_target_pairs={{0,4},{4,0},{8,12},{12,8},{16,20},{20,16},{24,28},{28,24},{1,5},{5... | collective-permute-start | bytes 49160 | tf_op jit(solution)/shard_map/ppermute | solution.py:701
  13.8 1.7 %collective-permute-start.5 = (f32[8,128]{1,0:T(8,128)S(1)}, f32[8,128]{1,0:T(8,128)S(1)}, u32[]{:S(2)}, u32[]{:S(2)}) collective-permute-start(f32[8,128]{1,0:T(8,128)S(1)} %get-tuple-element.67.refs_0_), channel_id=1, source_target_pairs={{0,1},{1,0},{2,3},{3,2},{4,5},{5,4},{6,7},{7,6},{8,9},{9,8},{10,11... | collective-permute-start | bytes 12296 | tf_op jit(solution)/shard_map/ppermute | solution.py:701
  13.9 6.6 %collective-permute-start.9 = (f32[24,128]{1,0:T(8,128)S(1)}, f32[24,128]{1,0:T(8,128)S(1)}, u32[]{:S(2)}, u32[]{:S(2)}) collective-permute-start(f32[24,128]{1,0:T(8,128)S(1)} %get-tuple-element.70), channel_id=1, source_target_pairs={{0,2},{1,3},{2,0},{3,1},{4,6},{5,7},{6,4},{7,5},{8,10},{9,11},{10,... | collective-permute-start | bytes 36872 | tf_op jit(solution)/shard_map/ppermute | solution.py:701
  16.0 6.6 %collective-permute-start.8 = (f32[8,512]{1,0:T(8,128)S(1)}, f32[8,512]{1,0:T(8,128)S(1)}, u32[]{:S(2)}, u32[]{:S(2)}) collective-permute-start(f32[8,512]{1,0:T(8,128)S(1)} %merge.1.refs_2_), channel_id=1, source_target_pairs={{0,24},{4,28},{8,16},{12,20},{16,8},{20,12},{24,0},{28,4},{1,25},{... | collective-permute-start | bytes 49160 | tf_op jit(solution)/shard_map/ppermute | solution.py:701
  19.6 4.6 %collective-permute-start.7 = (f32[8,512]{1,0:T(8,128)S(1)}, f32[8,512]{1,0:T(8,128)S(1)}, u32[]{:S(2)}, u32[]{:S(2)}) collective-permute-start(f32[8,512]{1,0:T(8,128)S(1)} %merge.1.refs_2_), channel_id=1, source_target_pairs={{0,16},{4,20},{8,24},{12,28},{16,0},{20,4},{24,8},{28,12},{1,17},{... | collective-permute-start | bytes 49160 | tf_op jit(solution)/shard_map/ppermute | solution.py:701
  19.6 4.6 %collective-permute-start.6 = (f32[8,512]{1,0:T(8,128)S(1)}, f32[8,512]{1,0:T(8,128)S(1)}, u32[]{:S(2)}, u32[]{:S(2)}) collective-permute-start(f32[8,512]{1,0:T(8,128)S(1)} %merge.1.refs_2_), channel_id=1, source_target_pairs={{0,8},{4,12},{8,0},{12,4},{16,24},{20,28},{24,16},{28,20},{1,9},{5... | collective-permute-start | bytes 49160 | tf_op jit(solution)/shard_map/ppermute | solution.py:701
  20.5 1.2 %collective-permute-start.10 = (f32[8,128]{1,0:T(8,128)S(1)}, f32[8,128]{1,0:T(8,128)S(1)}, u32[]{:S(2)}, u32[]{:S(2)}) collective-permute-start(f32[8,128]{1,0:T(8,128)S(1)} %slice.9), channel_id=1, source_target_pairs={{0,1},{1,0},{2,3},{3,2},{4,5},{5,4},{6,7},{7,6},{8,9},{9,8},{10,11... | collective-permute-start | bytes 12296 | tf_op jit(solution)/shard_map/ppermute | solution.py:701

commit v10 on v9

--- a/solution.py
+++ b/solution.py
@@ -201,7 +201,9 @@
             ys[at(tile, k), :] = turned[spread_rows(tile, k), :]
 
 
-def prepare_depth_kernel(h, hx, hy, ix, iy, tx, wx, ty, wy, endx, endy, natural, turned, *, inv_cx, inv_cy):
+def prepare_depth_kernel(
+    h, hx, hy, ix, iy, tx, wx, ty, wy, endx, endy, from_left, from_right, natural, turned, *, inv_cx, inv_cy
+):
     tiles = hx.shape[0] // LANES
     lay_out(h, hx, hy, natural, turned)
     ix[...] = 1.0 / hx[...]
@@ -210,10 +212,19 @@
     ends_y = march_depth(iy, inv_cy, ty, wy, log2(SUB * tiles))
     for i in range(3):
         for tile in range(tiles):
-            endx[i : i + 1, tile_span(tile)] = ends_x[i][tile * SUB : tile * SUB + 1, :]
-        endy[i : i + 1, :] = ends_y[i][0:1, :]
-    endx[3:8, :] = jnp.zeros((5, endx.shape[1]), F32)
-    endy[3:8, :] = jnp.zeros((5, endy.shape[1]), F32)
+            first = (i * tiles + tile) * LANES
+            endx[0:1, first : first + LANES] = ends_x[i][tile * SUB : tile * SUB + 1, :]
+        endy[0:1, i * LANES : (i + 1) * LANES] = ends_y[i][0:1, :]
+    one = jnp.ones((tiles * SUB, LANES), F32)
+    zero = jnp.zeros_like(one)
+    for out, left, right in ((from_left, one, zero), (from_right, zero, one)):
+
+        def store(k, speed):
+            for tile in range(tiles):
+                out[at(tile, k), :] = speed[tile * SUB : (tile + 1) * SUB, :]
+
+        left, right = segment_ends(left, right, wx, None, log2(SUB))
+        march_values(left, right, tx, None, ix, inv_cx, None, store)
 
 
 def prepare_depth(h, inv_cx, inv_cy):
@@ -224,8 +235,10 @@
         shape(3 * log2(SUB), count, LANES),
         shape(3, count, LANES),
         shape(3 * log2(count), count, LANES),
-        shape(SUB, stack[0]),
-        shape(SUB, LANES),
+        shape(1, 3 * stack[0]),
+        shape(1, 3 * LANES),
+        shape(*stack),
+        shape(*stack),
     ]
     return pl.pallas_call(
         functools.partial(prepare_depth_kernel, inv_cx=inv_cx, inv_cy=inv_cy),
@@ -379,6 +392,7 @@
 
 
 INNER = (2, STEPS - 2)
+TALL = 16
 
 
 def x_store(hx, px, mx, depth, push, across):
@@ -444,10 +458,12 @@
             total = (push_in if INNER[0] <= k < INNER[1] else push)[here, :] - shear_y[here, :]
             rx[here, :] = (inv_cx * (inverse * inverse)) * mx[here, :] * total
     sources = march_source(ix, inv_cx, rx, tx, wx, sx, log2(SUB))
-    ends[...] = coef[...]
+    count = tiles * LANES
+    ends[0:1, 0 : 3 * count] = coef[...]
     for i in range(2):
         for tile in range(tiles):
-            ends[3 + i : 4 + i, tile_span(tile)] = sources[i][tile * SUB : tile * SUB + 1, :]
+            first = (3 + i) * count + tile * LANES
+            ends[0:1, first : first + LANES] = sources[i][tile * SUB : tile * SUB + 1, :]
 
 
 def fluxes_x(*arrays, inv_cx):
@@ -458,7 +474,7 @@
         shape(*stack),
         shape(*stack),
         shape(1 + log2(SUB), count, LANES),
-        shape(*arrays[-1].shape),
+        shape(1, 5 * stack[0]),
     )
     return pl.pallas_call(
         functools.partial(flux_x_kernel, inv_cx=inv_cx),
@@ -492,11 +508,11 @@
             total = normal_y[here, :] - turned[spread_rows(tile, k), :]
             ry[here, :] = (inv_cy * (inverse * inverse)) * my[here, :] * total
     sources = march_source(iy, inv_cy, ry, ty, wy, sy, log2(SUB * tiles))
-    ends[...] = coef[...]
+    ends[0:1, 0 : 3 * LANES] = coef[...]
     for i in range(2):
-        ends[3 + i : 4 + i, :] = sources[i][0:1, :]
+        ends[0:1, (3 + i) * LANES : (4 + i) * LANES] = sources[i][0:1, :]
     tall[...] = jnp.zeros_like(tall)
-    tall[0:SUB, :] = ends[...]
+    tall[0:1, 0 : 5 * LANES] = ends[...]
 
 
 def join_y(*arrays, inv_cy):
@@ -506,8 +522,8 @@
         shape(*stack),
         shape(*stack),
         shape(1 + log2(count), count, LANES),
-        shape(*arrays[-1].shape),
-        shape(3 * SUB, arrays[-1].shape[1]),
+        shape(1, 5 * LANES),
+        shape(1, TALL * LANES),
     )
     return pl.pallas_call(
         functools.partial(join_y_kernel, inv_cy=inv_cy),
@@ -556,8 +572,8 @@
     )(depth)
 
 
-def rows_of(ref):
-    return tuple(ref[i : i + 1, :] for i in range(5))
+def rows_of(ref, count):
+    return tuple(ref[0:1, i * count : (i + 1) * count] for i in range(5))
 
 
 def ordered(axis, stage, mine, theirs):
@@ -569,10 +585,10 @@
 
 def merge_kernel(mine, theirs, *refs, axis, stage):
     out = refs[-1]
-    _, (merged, _) = ordered(axis, stage, rows_of(mine), rows_of(theirs))
+    count = mine.shape[1] // 5
+    _, (merged, _) = ordered(axis, stage, rows_of(mine, count), rows_of(theirs, count))
     for i, v in enumerate(merged):
-        out[i : i + 1, :] = v
-    out[5:8, :] = jnp.zeros((3, out.shape[1]), F32)
+        out[0:1, i * v.shape[1] : (i + 1) * v.shape[1]] = v
 
 
 def merge_call(axis, stage, mine, theirs, beside):
@@ -588,7 +604,7 @@
 
 def line_ends(axis, refs):
     steps = []
-    parts = [rows_of(ref) for ref in refs]
+    parts = [rows_of(ref, refs[0].shape[1] // 5) for ref in refs]
     stage = 0
     while len(parts) > 4:
         is_low, (_, weights) = ordered(axis, stage, *parts[:2])
@@ -614,7 +630,9 @@
     index = row_index(left.shape)
     for level in reversed(range(levels)):
         stride = 1 << level
-        middle = w_ref[3 * level] * left + w_ref[3 * level + 1] * right + s_ref[1 + level]
+        middle = w_ref[3 * level] * left + w_ref[3 * level + 1] * right
+        if s_ref is not None:
+            middle = middle + s_ref[1 + level]
         upper = (index >> level) % 2 == 1
         left, right = (
             jnp.where(upper, pltpu.roll(middle, stride, 0), left),
@@ -625,32 +643,54 @@
 
 def march_values(left, right, t_ref, s_ref, inv_ref, scale, r_ref, store):
     value = left
-    change = t_ref[0] * (right - left) - t_ref[1] * left - s_ref[0]
+    change = t_ref[0] * (right - left) - t_ref[1] * left
+    if s_ref is not None:
+        change = change - s_ref[0]
     for k in range(STEPS):
         inverse = full(inv_ref, k)
         value = value + change
-        change = change + (scale * (inverse * inverse) * value - full(r_ref, k))
+        push = scale * (inverse * inverse) * value
+        change = change + (push if r_ref is None else push - full(r_ref, k))
         store(k, value * inverse)
 
 
-def solve_x_kernel(inv_ref, r_ref, t_ref, w_ref, s_ref, *refs, scale):
-    parts, (out, natural, sems) = refs[:-3], refs[-3:]
-    tiles = out.shape[1] // LANES
-    ends = []
-    for row in line_ends("gx", parts):
-        ends.append(
-            jnp.concatenate([jnp.broadcast_to(row[:, tile_span(t)], (SUB, LANES)) for t in range(tiles)])
-        )
-    left, right = segment_ends(*ends, w_ref, s_ref, log2(SUB))
+def rest_x_kernel(inv_ref, r_ref, t_ref, w_ref, s_ref, out, *, scale):
+    tiles = out.shape[0] // LANES
+    zero = jnp.zeros((tiles * SUB, LANES), F32)
 
     def store(k, speed):
         for tile in range(tiles):
-            natural[spread_rows(tile, k), :] = speed[tile * SUB : (tile + 1) * SUB, :]
-
+            out[at(tile, k), :] = speed[tile * SUB : (tile + 1) * SUB, :]
+
+    left, right = segment_ends(zero, zero, w_ref, s_ref, log2(SUB))
     march_values(left, right, t_ref, s_ref, inv_ref, scale, r_ref, store)
-    writes = [tile_write(natural, out, tile, sems) for tile in range(tiles)]
-    for write in writes:
-        write.start()
+
+
+def rest_x(*pieces, scale):
+    return pl.pallas_call(
+        functools.partial(rest_x_kernel, scale=scale),
+        out_shape=shape(*pieces[0].shape),
+        in_specs=[VMEM] * len(pieces),
+        out_specs=VMEM,
+        compiler_params=PARAMS,
+        cost_estimate=pl.CostEstimate(flops=1_000_000, bytes_accessed=2_000_000, transcendentals=0),
+        name="rest_x",
+    )(*pieces)
+
+
+def solve_x_kernel(from_left, from_right, rest, *refs):
+    parts, (out, natural, sems) = refs[:-3], refs[-3:]
+    left, right = line_ends("gx", parts)
+    writes = []
+    for tile in range(out.shape[1] // LANES):
+        span = tile_span(tile)
+        for k in range(STEPS):
+            here = at(tile, k)
+            natural[spread_rows(tile, k), :] = (
+                from_left[here, :] * left[:, span] + from_right[here, :] * right[:, span] + rest[here, :]
+            )
+        writes.append(tile_write(natural, out, tile, sems))
+        writes[-1].start()
     for write in writes:
         write.wait()
 
@@ -678,9 +718,9 @@
         write.wait()
 
 
-def solve(kernel, name, pieces, parts, block, scale, extra=()):
-    return pl.pallas_call(
-        functools.partial(kernel, scale=scale),
+def solve(kernel, name, pieces, parts, block, extra=()):
+    return pl.pallas_call(
+        kernel,
         out_shape=shape(*block),
         in_specs=[VMEM] * (len(pieces) + len(parts)),
         out_specs=ANY,
@@ -711,7 +751,7 @@
     if relay:
         first = cross(mine, axis, 1 << last)
         second = cross(mine if tall is None else tall, axis, 2 << last)
-        both = cross(second[0:SUB], axis, 1 << last)
+        both = cross(second[:, 0 : mine.shape[1]], axis, 1 << last)
     else:
         first, second, both = (cross(mine, axis, n << last) for n in (1, 2, 3))
     return parts + [mine, first, second, both]
@@ -726,7 +766,7 @@
     near_x = cross(slabs_x, "gx", 1)
     near_y = cross(pack_y(h, p, q, b, m, after=slabs_x), "gy", 1)
     far_y = hand_on(jnp.pad(near_y[1], ((0, 5 * SUB), (0, 0))), "gy")
-    hx, hy, ix, iy, tx, wx, ty, wy, coef_x, coef_y = prepare_depth(h, inv_cx, inv_cy)
+    hx, hy, ix, iy, tx, wx, ty, wy, coef_x, coef_y, left_x, right_x = prepare_depth(h, inv_cx, inv_cy)
     far_x = hand_on(second_of(near_x, coef_x), "gx")
     px, py, qx, qy, bx, by, mx, my = prepare_rest(p, q, b, m)
     depth_inner, push_inner, across_inner = fluxes_x_inner(hx, px, qx, bx, mx)
@@ -741,8 +781,10 @@
     parts_y = parts_of_line("gy", end_y, True, tall=tall_y if lax.axis_size("gy") == 4 else None)
     parts_x = parts_of_line("gx", end_x, False, parts_y[1:2])
     turned = [pltpu.VMEM((cols, LANES), F32)]
-    vy = solve(solve_y_kernel, "solve_y", (iy, ry, ty, wy, sy), parts_y, block, inv_cy, turned)
-    vx = solve(solve_x_kernel, "solve_x", (ix, rx, tx, wx, sx), parts_x, block, inv_cx)
+    solve_y_scaled = functools.partial(solve_y_kernel, scale=inv_cy)
+    vy = solve(solve_y_scaled, "solve_y", (iy, ry, ty, wy, sy), parts_y, block, turned)
+    own_x = rest_x(ix, rx, tx, wx, sx, scale=inv_cx)
+    vx = solve(solve_x_kernel, "solve_x", (left_x, right_x, own_x), parts_x, block)
     return new_depth, vx, vy
 
 

time: 25.3 us -> 25 us (0.988)
  waiting for transfers between devices: 2.52 us -> 2.22 us
    ppermute x9, waiting for transfers between devices: 2.52 us -> 2.21 us  [cross(): lax.ppermute(value, axis, [(i, i ^ mask) for i in range(lax.axis_size(axi...]
    pallas_call x2 -> x3, Pallas kernels: 1.93 us -> 1.95 us  [the longest x2 1.83 us: solve(): pl.pallas_call(kernel, out_shape=shape(*block), in_specs=[VMEM] * (len(pi...]
where the time goes in v10:
time: 25 us; the launch traced here: 24.8 us
  starting transfers between devices  13.9 us (56%)
  Pallas kernels  7.56 us (30%)
  waiting for transfers between devices  2.22 us (9%)
  between operations  0.81 us (3%)
  local copies, waits for them, and re-layouts  0.31 us (1%)
    ppermute x9, starting transfers between devices, cross(): lax.ppermute(value, axis, [(i, i ^ mask) for i in range(lax.axis_size(axi...  10.5 us
    ppermute x2, starting transfers between devices, hand_on(): lax.ppermute(value, axis, [(i, t if 0 <= t < count else i ^ 1) for i, t i...  3.42 us
    ppermute x9, waiting for transfers between devices, cross(): lax.ppermute(value, axis, [(i, i ^ mask) for i in range(lax.axis_size(axi...  2.21 us
    pallas_call x2, Pallas kernels, solve(): pl.pallas_call(kernel, out_shape=shape(*block), in_specs=[VMEM] * (len(pi...  1.83 us
    pallas_call x1, Pallas kernels, pack_x(): pl.pallas_call(pack_x_kernel, out_shape=shape(2, SUB, cols), in_specs=[HB...  0.99 us
    pallas_call x1, Pallas kernels, fluxes_y(): pl.pallas_call(flux_y_kernel, out_shape=(shape(*stack),) * 3, in_specs=[V...  0.97 us
    pallas_call x1, Pallas kernels, prepare_rest(): pl.pallas_call(prepare_rest_kernel, out_shape=(shape(*stack),) * 8, in_sp...  0.76 us
    pallas_call x1, Pallas kernels, write_depth(): pl.pallas_call(depth_kernel, out_shape=shape(*block), in_specs=[VMEM], ou...  0.75 us
  transfers between devices with their start and end apart: 11, of which 3 were waited for; matrix products, arithmetic and copies ran while one was open for 0% of the time, Pallas kernels for 20%

profile of v10, /device:TPU:0, one launch (start us, length us, event | category | flops | bytes accessed | tf_op | source)
XLA Modules:
  0.0 24.8 jit_solution(7794688662300573292)
XLA Ops:
  0.7 1.0 %pack_x.1._ = f32[2,8,512]{2,1,0:T(8,128)S(1)} custom-call(f32[128,512]{1,0:T(8,128)} %h.5, f32[128,512]{1,0:T(8,128)} %p.3, f32[128,512]{1,0:T(8,128)} %q.3, f32[128,512]{1,0:T(8,128)} %b.3, s32[128,512]{1,0:T(8,128)} %m.3), custom_call_target="tpu_custom_call" | custom-call | tf_op jit(solution)/shard_map/pack_x/pallas_call | solution.py:78
  1.7 0.1 copy-done.3
  1.7 0.1 copy-done.2
  1.8 0.1 copy-done.1
  1.9 0.1 copy-done
  2.0 0.2 pack_y.1
  2.2 0.5 %collective-permute-start.2 = (f32[2,8,128]{2,1,0:T(8,128)S(1)}, f32[2,8,128]{2,1,0:T(8,128)S(1)}, u32[]{:S(2)}, u32[]{:S(2)}) collective-permute-start(f32[2,8,128]{2,1,0:T(8,128)S(1)} %pack_y.1), channel_id=1, source_target_pairs={{0,1},{1,0},{2,3},{3,2},{4,5},{5,4},{6,7},{7,6},{8,9},{9,8},{10,11... | collective-permute-start | bytes 24584 | tf_op jit(solution)/shard_map/ppermute | solution.py:741
  2.7 2.6 %collective-permute-start = (f32[2,8,512]{2,1,0:T(8,128)S(1)}, f32[2,8,512]{2,1,0:T(8,128)S(1)}, u32[]{:S(2)}, u32[]{:S(2)}) collective-permute-start(f32[2,8,512]{2,1,0:T(8,128)S(1)} %pack_x.1._), channel_id=1, source_target_pairs={{0,4},{4,0},{8,12},{12,8},{16,20},{20,16},{24,28},{28,24},{1,5},{5... | collective-permute-start | bytes 98312 | tf_op jit(solution)/shard_map/ppermute | solution.py:741
  5.3 1.5 %collective-permute-start.3 = (f32[48,128]{1,0:T(8,128)S(1)}, f32[48,128]{1,0:T(8,128)S(1)}, u32[]{:S(2)}, u32[]{:S(2)}) collective-permute-start(f32[48,128]{1,0:T(8,128)S(1)} %pad.4), channel_id=1, source_target_pairs={{0,2},{1,0},{2,3},{3,1},{4,6},{5,4},{6,7},{7,5},{8,10},{9,8},{10,1... | collective-permute-start | bytes 73736 | tf_op jit(solution)/shard_map/ppermute | solution.py:737
  6.8 0.5 %prepare_depth.1 = (f32[512,128]{1,0:T(8,128)S(1)}, f32[512,128]{1,0:T(8,128)S(1)}, f32[512,128]{1,0:T(8,128)S(1)}, f32[512,128]{1,0:T(8,128)S(1)}, f32[3,32,128...) custom-call(f32[128,512]{1,0:T(8,128)S(1)} %copy-done), custom_call_target="tpu_custom_call" | custom-call | flops 2000000 | bytes 4000000 | tf_op jit(solution)/shard_map/prepare_depth/pallas_call | solution.py:243
  7.4 1.9 %collective-permute-start.1 = (f32[8,512]{1,0:T(8,128)S(1)}, f32[8,512]{1,0:T(8,128)S(1)}, u32[]{:S(2)}, u32[]{:S(2)}) collective-permute-start(f32[8,512]{1,0:T(8,128)S(1)} %second_of.1), channel_id=1, source_target_pairs={{0,8},{4,0},{8,16},{12,4},{16,24},{20,12},{24,28},{28,20},{1,9},{5... | collective-permute-start | bytes 49160 | tf_op jit(solution)/shard_map/ppermute | solution.py:737
  9.3 0.8 %prepare_rest.1 = (f32[512,128]{1,0:T(8,128)S(1)}, f32[512,128]{1,0:T(8,128)S(1)}, f32[512,128]{1,0:T(8,128)S(1)}, f32[512,128]{1,0:T(8,128)S(1)}, f32[512,128]{...) custom-call(f32[128,512]{1,0:T(8,128)S(1)} %copy-done.1, ...), custom_call_target="tpu_custom_call" | custom-call | flops 2000000 | bytes 6000000 | tf_op jit(solution)/shard_map/prepare_rest/pallas_call | solution.py:263
  10.0 0.6 %fluxes_x_inner.1 = (f32[512,128]{1,0:T(8,128)S(1)}, f32[512,128]{1,0:T(8,128)S(1)}, f32[512,128]{1,0:T(8,128)S(1)}) custom-call(f32[512,128]{1,0:T(8,128)S(1)} %get-tuple-element.39.hx, f32[512,128]{1,0:T(8,128)S(1)} %get-tuple-element.40.px, f32[512,128]{1,0:T(8,128)S(1)} %get-tuple-element.41.qx, f32[512,128]{1,0:T(8,128)S(1)} %get-tuple-element.42.bx, ...), custom_call_target="tpu_custom_call" | custom-call | flops 4000000 | bytes 4000000 | tf_op jit(solution)/shard_map/fluxes_x_inner/pallas_call | solution.py:424
  10.6 0.0 collective-permute-done.3.far
  10.6 1.0 %fluxes_y.1 = (f32[512,128]{1,0:T(8,128)S(1)}, f32[512,128]{1,0:T(8,128)S(1)}, f32[512,128]{1,0:T(8,128)S(1)}) custom-call(f32[2,8,128]{2,1,0:T(8,128)S(1)} %collective-permute-done.2.near, f32[48,128]{1,0:T(8,128)S(1)} %collective-permute-done.3.far, f32[512,128]{1,0:T(8,128)S(1)} %get-tuple-element.48.hy, f32[512,128]{1,0:T(8,128)S(1)} %get-tuple-element.49.py, ...), custom_call_target="tpu_custom_call" | custom-call | flops 4000000 | bytes 4000000 | tf_op jit(solution)/shard_map/fluxes_y/pallas_call | solution.py:382
  11.6 0.5 %fluxes_x.1 = (f32[512,128]{1,0:T(8,128)S(1)}, f32[512,128]{1,0:T(8,128)S(1)}, f32[512,128]{1,0:T(8,128)S(1)}, f32[4,32,128]{2,1,0:T(8,128)S(1)}, f32[1,2560]{1,0:T(1,128)S(1)}) custom-call(f32[2,8,512]{2,1,0:T(8,128)S(1)} %collective-permute-done.both.near, f32[8,512]{1,0:T(8,128)S(1)} %collective-permute-done.1.far, f32[512,128]{1,0:T(8,128)S(1)} %get-tuple-element.39.hx, ...), custom_call_target="tpu_custom_call" | custom-call | tf_op jit(solution)/shard_map/fluxes_x/pallas_call | solution.py:479
  12.1 1.3 %collective-permute-start.4 = (f32[1,2560]{1,0:T(1,128)S(1)}, f32[1,2560]{1,0:T(1,128)S(1)}, u32[]{:S(2)}, u32[]{:S(2)}) collective-permute-start(f32[1,2560]{1,0:T(1,128)S(1)} %get-tuple-element.70.mine.refs_0_), channel_id=1, source_target_pairs={{0,4},{4,0},{8,12},{12,8},{16,20},{20,16},{24,28},{28,24},{1,5},{5... | collective-permute-start | bytes 30728 | tf_op jit(solution)/shard_map/ppermute | solution.py:741
  13.4 0.3 %join_y.1 = (f32[512,128]{1,0:T(8,128)S(1)}, f32[512,128]{1,0:T(8,128)S(1)}, f32[6,32,128]{2,1,0:T(8,128)S(1)}, f32[1,640]{1,0:T(1,128)S(1)}, f32[1,2048]{1,0:T(1,128)S(1)}) custom-call(f32[512,128]{1,0:T(8,128)S(1)} %get-tuple-element.44.depth_inner, f32[512,128]{1,0:T(8,128)S(1)} %get-tuple-element.45.across_inner, ...), custom_call_target="tpu_custom_call" | custom-call | flops 2000000 | bytes 2000000 | tf_op jit(solution)/shard_map/join_y/pallas_call | solution.py:528
  13.8 0.1 collective-permute-start.5
  13.8 1.6 %collective-permute-start.9 = (f32[1,2048]{1,0:T(1,128)S(1)}, f32[1,2048]{1,0:T(1,128)S(1)}, u32[]{:S(2)}, u32[]{:S(2)}) collective-permute-start(f32[1,2048]{1,0:T(1,128)S(1)} %get-tuple-element.74), channel_id=1, source_target_pairs={{0,2},{1,3},{2,0},{3,1},{4,6},{5,7},{6,4},{7,5},{8,10},{9,11},{10,... | collective-permute-start | bytes 24584 | tf_op jit(solution)/shard_map/ppermute | solution.py:741
  15.4 0.4 %collective-permute-done.4.theirs.refs_1_ = f32[1,2560]{1,0:T(1,128)S(1)} collective-permute-done((f32[1,2560]{1,0:T(1,128)S(1)}, f32[1,2560]{1,0:T(1,128)S(1)}, u32[]{:S(2)}, u32[]{:S(2)}) %collective-permute-start.4) | collective-permute-done | bytes 10272 | tf_op jit(solution)/shard_map/ppermute | solution.py:741
  15.8 3.6 %collective-permute-start.8 = (f32[1,2560]{1,0:T(1,128)S(1)}, f32[1,2560]{1,0:T(1,128)S(1)}, u32[]{:S(2)}, u32[]{:S(2)}) collective-permute-start(f32[1,2560]{1,0:T(1,128)S(1)} %merge.1.refs_2_), channel_id=1, source_target_pairs={{0,24},{4,28},{8,16},{12,20},{16,8},{20,12},{24,0},{28,4},{1,25},{... | collective-permute-start | bytes 30728 | tf_op jit(solution)/shard_map/ppermute | solution.py:741
  19.4 0.9 %collective-permute-start.6 = (f32[1,2560]{1,0:T(1,128)S(1)}, f32[1,2560]{1,0:T(1,128)S(1)}, u32[]{:S(2)}, u32[]{:S(2)}) collective-permute-start(f32[1,2560]{1,0:T(1,128)S(1)} %merge.1.refs_2_), channel_id=1, source_target_pairs={{0,8},{4,12},{8,0},{12,4},{16,24},{20,28},{24,16},{28,20},{1,9},{5... | collective-permute-start | bytes 30728 | tf_op jit(solution)/shard_map/ppermute | solution.py:741
  20.3 0.0 collective-permute-done.9.refs_2_
  20.3 0.0 collective-permute-start.10
  20.3 0.7 %write_depth.1 = f32[128,512]{1,0:T(8,128)} custom-call(f32[512,128]{1,0:T(8,128)S(1)} %get-tuple-element.65.depth), custom_call_target="tpu_custom_call" | custom-call | flops 100000 | bytes 2000000 | tf_op jit(solution)/shard_map/write_depth/pallas_call | solution.py:563
  21.1 0.1 rest_x.1.rest
  21.2 0.3 %collective-permute-done.10.refs_3_ = f32[1,640]{1,0:T(1,128)S(1)} collective-permute-done((f32[1,640]{1,0:T(1,128)S(1)}, f32[1,640]{1,0:T(1,128)S(1)}, u32[]{:S(2)}, u32[]{:S(2)}) %collective-permute-start.10) | collective-permute-done | bytes 2592 | tf_op jit(solution)/shard_map/ppermute | solution.py:741
  21.5 1.0 %solve_y.1 = f32[128,512]{1,0:T(8,128)} custom-call(f32[512,128]{1,0:T(8,128)S(1)} %get-tuple-element.61.iy.inv_ref, f32[512,128]{1,0:T(8,128)S(1)} %get-tuple-element.72.r_ref, f32[3,32,128]{2,1,0:T(8,128)S(1)} %get-tuple-element.62.ty.t_ref, f32[15,32,128]{2,1,0:T(8,128)S(1)} %get-tuple-element.63.wy.w_ref, f32[6,32,128]{2,1,0:T(8,128)S(1)} %get-tuple-element.73.s_ref, ...), custom_call_target="tpu_custom_call" | custom-call | flops 1000000 | bytes 4000000 | tf_op jit(solution)/shard_map/solve_y/pallas_call | solution.py:722
  22.5 1.5 %collective-permute-done.7.refs_4_ = f32[1,2560]{1,0:T(1,128)S(1)} collective-permute-done((f32[1,2560]{1,0:T(1,128)S(1)}, f32[1,2560]{1,0:T(1,128)S(1)}, u32[]{:S(2)}, u32[]{:S(2)}) %collective-permute-start.7) | collective-permute-done | bytes 10272 | tf_op jit(solution)/shard_map/ppermute | solution.py:741
  24.0 0.0 collective-permute-done.6.refs_3_
  24.0 0.8 %solve_x.1 = f32[128,512]{1,0:T(8,128)} custom-call(f32[512,128]{1,0:T(8,128)S(1)} %get-tuple-element.66.from_left, f32[512,128]{1,0:T(8,128)S(1)} %get-tuple-element.67.from_right, f32[512,128]{1,0:T(8,128)S(1)} %rest_x.1.rest, f32[1,2560]{1,0:T(1,128)S(1)} %get-tuple-element.70.mine.refs_0_, f32[1,2560]{1,0:T(1,128)S(1)} %collective-permute-done.4.theirs.refs_1_, ...), custom_call_target="tpu_custom_call" | custom-call | flops 1000000 | bytes 4000000 | tf_op jit(solution)/shard_map/solve_x/pallas_call | solution.py:722
  (17 shorter events, 0.1 us)
Async XLA Ops:
  0.6 1.1 %copy-start.4 = (s32[128,512]{1,0:T(8,128)S(1)}, s32[128,512]{1,0:T(8,128)}, u32[]{:S(2)}) copy-start(s32[128,512]{1,0:T(8,128)} %m.3) | copy-start | bytes 786436
  0.6 1.1 %copy-start.3 = (f32[128,512]{1,0:T(8,128)S(1)}, f32[128,512]{1,0:T(8,128)}, u32[]{:S(2)}) copy-start(f32[128,512]{1,0:T(8,128)} %b.3) | copy-start | bytes 786436
  0.7 1.2 %copy-start.2 = (f32[128,512]{1,0:T(8,128)S(1)}, f32[128,512]{1,0:T(8,128)}, u32[]{:S(2)}) copy-start(f32[128,512]{1,0:T(8,128)} %q.3) | copy-start | bytes 786436
  0.7 1.2 %copy-start.1 = (f32[128,512]{1,0:T(8,128)S(1)}, f32[128,512]{1,0:T(8,128)}, u32[]{:S(2)}) copy-start(f32[128,512]{1,0:T(8,128)} %p.3) | copy-start | bytes 786436
  0.7 1.3 %copy-start = (f32[128,512]{1,0:T(8,128)S(1)}, f32[128,512]{1,0:T(8,128)}, u32[]{:S(2)}) copy-start(f32[128,512]{1,0:T(8,128)} %h.5) | copy-start | bytes 786436
  2.2 3.1 %collective-permute-start.2 = (f32[2,8,128]{2,1,0:T(8,128)S(1)}, f32[2,8,128]{2,1,0:T(8,128)S(1)}, u32[]{:S(2)}, u32[]{:S(2)}) collective-permute-start(f32[2,8,128]{2,1,0:T(8,128)S(1)} %pack_y.1), channel_id=1, source_target_pairs={{0,1},{1,0},{2,3},{3,2},{4,5},{5,4},{6,7},{7,6},{8,9},{9,8},{10,11... | collective-permute-start | bytes 24584 | tf_op jit(solution)/shard_map/ppermute | solution.py:741
  2.7 4.7 %collective-permute-start = (f32[2,8,512]{2,1,0:T(8,128)S(1)}, f32[2,8,512]{2,1,0:T(8,128)S(1)}, u32[]{:S(2)}, u32[]{:S(2)}) collective-permute-start(f32[2,8,512]{2,1,0:T(8,128)S(1)} %pack_x.1._), channel_id=1, source_target_pairs={{0,4},{4,0},{8,12},{12,8},{16,20},{20,16},{24,28},{28,24},{1,5},{5... | collective-permute-start | bytes 98312 | tf_op jit(solution)/shard_map/ppermute | solution.py:741
  5.3 5.4 %collective-permute-start.3 = (f32[48,128]{1,0:T(8,128)S(1)}, f32[48,128]{1,0:T(8,128)S(1)}, u32[]{:S(2)}, u32[]{:S(2)}) collective-permute-start(f32[48,128]{1,0:T(8,128)S(1)} %pad.4), channel_id=1, source_target_pairs={{0,2},{1,0},{2,3},{3,1},{4,6},{5,4},{6,7},{7,5},{8,10},{9,8},{10,1... | collective-permute-start | bytes 73736 | tf_op jit(solution)/shard_map/ppermute | solution.py:737
  7.4 4.2 %collective-permute-start.1 = (f32[8,512]{1,0:T(8,128)S(1)}, f32[8,512]{1,0:T(8,128)S(1)}, u32[]{:S(2)}, u32[]{:S(2)}) collective-permute-start(f32[8,512]{1,0:T(8,128)S(1)} %second_of.1), channel_id=1, source_target_pairs={{0,8},{4,0},{8,16},{12,4},{16,24},{20,12},{24,28},{28,20},{1,9},{5... | collective-permute-start | bytes 49160 | tf_op jit(solution)/shard_map/ppermute | solution.py:737
  12.1 3.7 %collective-permute-start.4 = (f32[1,2560]{1,0:T(1,128)S(1)}, f32[1,2560]{1,0:T(1,128)S(1)}, u32[]{:S(2)}, u32[]{:S(2)}) collective-permute-start(f32[1,2560]{1,0:T(1,128)S(1)} %get-tuple-element.70.mine.refs_0_), channel_id=1, source_target_pairs={{0,4},{4,0},{8,12},{12,8},{16,20},{20,16},{24,28},{28,24},{1,5},{5... | collective-permute-start | bytes 30728 | tf_op jit(solution)/shard_map/ppermute | solution.py:741
  13.8 1.7 %collective-permute-start.5 = (f32[1,640]{1,0:T(1,128)S(1)}, f32[1,640]{1,0:T(1,128)S(1)}, u32[]{:S(2)}, u32[]{:S(2)}) collective-permute-start(f32[1,640]{1,0:T(1,128)S(1)} %get-tuple-element.71.refs_0_), channel_id=1, source_target_pairs={{0,1},{1,0},{2,3},{3,2},{4,5},{5,4},{6,7},{7,6},{8,9},{9,8},{10,11... | collective-permute-start | bytes 7688 | tf_op jit(solution)/shard_map/ppermute | solution.py:741
  13.8 6.5 %collective-permute-start.9 = (f32[1,2048]{1,0:T(1,128)S(1)}, f32[1,2048]{1,0:T(1,128)S(1)}, u32[]{:S(2)}, u32[]{:S(2)}) collective-permute-start(f32[1,2048]{1,0:T(1,128)S(1)} %get-tuple-element.74), channel_id=1, source_target_pairs={{0,2},{1,3},{2,0},{3,1},{4,6},{5,7},{6,4},{7,5},{8,10},{9,11},{10,... | collective-permute-start | bytes 24584 | tf_op jit(solution)/shard_map/ppermute | solution.py:741
  15.8 6.6 %collective-permute-start.8 = (f32[1,2560]{1,0:T(1,128)S(1)}, f32[1,2560]{1,0:T(1,128)S(1)}, u32[]{:S(2)}, u32[]{:S(2)}) collective-permute-start(f32[1,2560]{1,0:T(1,128)S(1)} %merge.1.refs_2_), channel_id=1, source_target_pairs={{0,24},{4,28},{8,16},{12,20},{16,8},{20,12},{24,0},{28,4},{1,25},{... | collective-permute-start | bytes 30728 | tf_op jit(solution)/shard_map/ppermute | solution.py:741
  19.4 4.6 %collective-permute-start.7 = (f32[1,2560]{1,0:T(1,128)S(1)}, f32[1,2560]{1,0:T(1,128)S(1)}, u32[]{:S(2)}, u32[]{:S(2)}) collective-permute-start(f32[1,2560]{1,0:T(1,128)S(1)} %merge.1.refs_2_), channel_id=1, source_target_pairs={{0,16},{4,20},{8,24},{12,28},{16,0},{20,4},{24,8},{28,12},{1,17},{... | collective-permute-start | bytes 30728 | tf_op jit(solution)/shard_map/ppermute | solution.py:741
  19.4 4.6 %collective-permute-start.6 = (f32[1,2560]{1,0:T(1,128)S(1)}, f32[1,2560]{1,0:T(1,128)S(1)}, u32[]{:S(2)}, u32[]{:S(2)}) collective-permute-start(f32[1,2560]{1,0:T(1,128)S(1)} %merge.1.refs_2_), channel_id=1, source_target_pairs={{0,8},{4,12},{8,0},{12,4},{16,24},{20,28},{24,16},{28,20},{1,9},{5... | collective-permute-start | bytes 30728 | tf_op jit(solution)/shard_map/ppermute | solution.py:741
  20.3 1.2 %collective-permute-start.10 = (f32[1,640]{1,0:T(1,128)S(1)}, f32[1,640]{1,0:T(1,128)S(1)}, u32[]{:S(2)}, u32[]{:S(2)}) collective-permute-start(f32[1,640]{1,0:T(1,128)S(1)} %slice.9), channel_id=1, source_target_pairs={{0,1},{1,0},{2,3},{3,2},{4,5},{5,4},{6,7},{7,6},{8,9},{9,8},{10,11... | collective-permute-start | bytes 7688 | tf_op jit(solution)/shard_map/ppermute | solution.py:741

commit v11 on v10

--- a/solution.py
+++ b/solution.py
@@ -44,7 +44,7 @@
     return jax.ShapeDtypeStruct(dims, F32)
 
 
-def pack_x_kernel(h, p, q, b, m, slabs, top, bottom, itop, ibottom, sems):
+def pack_x_kernel(h, p, q, b, m, near, outer, top, bottom, itop, ibottom, sems):
     rows = h.shape[0]
     copies = []
     for f, src in enumerate((h, p, q, b, m)):
@@ -69,17 +69,17 @@
         ]
     )
     even = lax.axis_index("gx") % 2 == 0
-    slabs[0] = jnp.where(even, last, first)
-    slabs[1] = jnp.where(even, first, last)
+    near[...] = jnp.where(even, last, first)
+    outer[...] = jnp.where(even, first, last)
 
 
 def pack_x(*fields):
     cols = fields[0].shape[1]
     return pl.pallas_call(
         pack_x_kernel,
-        out_shape=shape(2, SUB, cols),
+        out_shape=(shape(SUB, cols), shape(SUB, cols)),
         in_specs=[HBM] * 5,
-        out_specs=VMEM,
+        out_specs=(VMEM, VMEM),
         scratch_shapes=[
             pltpu.VMEM((4, SUB, cols), F32),
             pltpu.VMEM((4, SUB, cols), F32),
@@ -123,19 +123,19 @@
     )(*fields, after)
 
 
-def tie_kernel(both, _, out):
-    out[...] = both[1]
-
-
-def second_of(both, after):
+def tie_kernel(value, _, out):
+    out[...] = value[...]
+
+
+def once(value, after):
     return pl.pallas_call(
         tie_kernel,
-        out_shape=shape(*both.shape[1:]),
+        out_shape=shape(*value.shape),
         in_specs=[VMEM, VMEM],
         out_specs=VMEM,
         compiler_params=PARAMS,
-        name="second_of",
-    )(both, after)
+        name="once",
+    )(value, after)
 
 
 def merge_coefficients(one, two):
@@ -439,7 +439,7 @@
     *, inv_cx,
 ):
     tiles = hx.shape[0] // LANES
-    low, high = low_high("gx", near[0], far[...])
+    low, high = low_high("gx", near[...], far[...])
     store = x_store(hx, px, mx, depth, push, across)
     for tile in range(tiles):
         span = tile_span(tile)
@@ -762,12 +762,12 @@
     rows, cols = block
     inv_cx = 3.0 / (rows * lax.axis_size("gx") / 4.0) ** 2
     inv_cy = 3.0 / (cols * lax.axis_size("gy") / 4.0) ** 2
-    slabs_x = pack_x(h, p, q, b, m)
-    near_x = cross(slabs_x, "gx", 1)
-    near_y = cross(pack_y(h, p, q, b, m, after=slabs_x), "gy", 1)
+    near_x, outer_x = pack_x(h, p, q, b, m)
+    near_y = cross(pack_y(h, p, q, b, m, after=outer_x), "gy", 1)
+    outer_x, near_x = cross(outer_x, "gx", 1), cross(near_x, "gx", 1)
     far_y = hand_on(jnp.pad(near_y[1], ((0, 5 * SUB), (0, 0))), "gy")
     hx, hy, ix, iy, tx, wx, ty, wy, coef_x, coef_y, left_x, right_x = prepare_depth(h, inv_cx, inv_cy)
-    far_x = hand_on(second_of(near_x, coef_x), "gx")
+    far_x = hand_on(once(outer_x, coef_x), "gx")
     px, py, qx, qy, bx, by, mx, my = prepare_rest(p, q, b, m)
     depth_inner, push_inner, across_inner = fluxes_x_inner(hx, px, qx, bx, mx)
     mass_y, shear_y, normal_y = fluxes_y(near_y, far_y, hy, py, qy, by, my)

time: 25 us -> 25.7 us (1.028)
  waiting for transfers between devices: 2.22 us -> 3.09 us
    ppermute x9 -> x10, waiting for transfers between devices: 2.21 us -> 3.08 us  [cross(): lax.ppermute(value, axis, [(i, i ^ mask) for i in range(lax.axis_size(axi...]
    ppermute x9 -> x10, starting transfers between devices: 10.5 us -> 10.6 us  [cross(): lax.ppermute(value, axis, [(i, i ^ mask) for i in range(lax.axis_size(axi...]
  transfers between devices with their start and end apart: 11 -> 12, of which waited for: 3 -> 3; matrix products, arithmetic and copies ran while one was open for 0% -> 0% of each run, Pallas kernels for 20% -> 20%
where the time goes in v11:
time: 25.7 us; the launch traced here: 25.5 us
  starting transfers between devices  13.7 us (53%)
  Pallas kernels  7.56 us (29%)
  waiting for transfers between devices  3.09 us (12%)
  between operations  0.82 us (3%)
  local copies, waits for them, and re-layouts  0.31 us (1%)
    ppermute x10, starting transfers between devices, cross(): lax.ppermute(value, axis, [(i, i ^ mask) for i in range(lax.axis_size(axi...  10.6 us
    ppermute x2, starting transfers between devices, hand_on(): lax.ppermute(value, axis, [(i, t if 0 <= t < count else i ^ 1) for i, t i...  3.16 us
    ppermute x10, waiting for transfers between devices, cross(): lax.ppermute(value, axis, [(i, i ^ mask) for i in range(lax.axis_size(axi...  3.08 us
    pallas_call x2, Pallas kernels, solve(): pl.pallas_call(kernel, out_shape=shape(*block), in_specs=[VMEM] * (len(pi...  1.83 us
    pallas_call x1, Pallas kernels, pack_x(): pl.pallas_call(pack_x_kernel, out_shape=(shape(SUB, cols), shape(SUB, col...  0.99 us
    pallas_call x1, Pallas kernels, fluxes_y(): pl.pallas_call(flux_y_kernel, out_shape=(shape(*stack),) * 3, in_specs=[V...  0.97 us
    pallas_call x1, Pallas kernels, prepare_rest(): pl.pallas_call(prepare_rest_kernel, out_shape=(shape(*stack),) * 8, in_sp...  0.76 us
    pallas_call x1, Pallas kernels, write_depth(): pl.pallas_call(depth_kernel, out_shape=shape(*block), in_specs=[VMEM], ou...  0.75 us
  transfers between devices with their start and end apart: 12, of which 3 were waited for; matrix products, arithmetic and copies ran while one was open for 0% of the time, Pallas kernels for 20%

profile of v11, /device:TPU:0, one launch (start us, length us, event | category | flops | bytes accessed | tf_op | source)
XLA Modules:
  0.0 25.5 jit_solution(4522567212556993877)
XLA Ops:
  0.7 1.0 %pack_x.1 = (f32[8,512]{1,0:T(8,128)S(1)}, f32[8,512]{1,0:T(8,128)S(1)}) custom-call(f32[128,512]{1,0:T(8,128)} %h.5, f32[128,512]{1,0:T(8,128)} %p.3, f32[128,512]{1,0:T(8,128)} %q.3, f32[128,512]{1,0:T(8,128)} %b.3, s32[128,512]{1,0:T(8,128)} %m.3), custom_call_target="tpu_custom_call" | custom-call | tf_op jit(solution)/shard_map/pack_x/pallas_call | solution.py:78
  1.7 0.1 copy-done.3
  1.7 0.1 copy-done.2
  1.8 0.1 copy-done.1
  1.9 0.1 copy-done
  2.0 0.2 pack_y.1
  2.2 0.5 %collective-permute-start.3 = (f32[2,8,128]{2,1,0:T(8,128)S(1)}, f32[2,8,128]{2,1,0:T(8,128)S(1)}, u32[]{:S(2)}, u32[]{:S(2)}) collective-permute-start(f32[2,8,128]{2,1,0:T(8,128)S(1)} %pack_y.1), channel_id=1, source_target_pairs={{0,1},{1,0},{2,3},{3,2},{4,5},{5,4},{6,7},{7,6},{8,9},{9,8},{10,11... | collective-permute-start | bytes 24584 | tf_op jit(solution)/shard_map/ppermute | solution.py:741
  2.7 2.6 %collective-permute-start.1 = (f32[8,512]{1,0:T(8,128)S(1)}, f32[8,512]{1,0:T(8,128)S(1)}, u32[]{:S(2)}, u32[]{:S(2)}) collective-permute-start(f32[8,512]{1,0:T(8,128)S(1)} %get-tuple-element.49._), channel_id=1, source_target_pairs={{0,4},{4,0},{8,12},{12,8},{16,20},{20,16},{24,28},{28,24},{1,5},{5... | collective-permute-start | bytes 49160 | tf_op jit(solution)/shard_map/ppermute | solution.py:741
  5.3 1.5 %collective-permute-start.4 = (f32[48,128]{1,0:T(8,128)S(1)}, f32[48,128]{1,0:T(8,128)S(1)}, u32[]{:S(2)}, u32[]{:S(2)}) collective-permute-start(f32[48,128]{1,0:T(8,128)S(1)} %pad.4), channel_id=1, source_target_pairs={{0,2},{1,0},{2,3},{3,1},{4,6},{5,4},{6,7},{7,5},{8,10},{9,8},{10,1... | collective-permute-start | bytes 73736 | tf_op jit(solution)/shard_map/ppermute | solution.py:737
  6.8 1.1 %collective-permute-start = (f32[8,512]{1,0:T(8,128)S(1)}, f32[8,512]{1,0:T(8,128)S(1)}, u32[]{:S(2)}, u32[]{:S(2)}) collective-permute-start(f32[8,512]{1,0:T(8,128)S(1)} %get-tuple-element.48), channel_id=1, source_target_pairs={{0,4},{4,0},{8,12},{12,8},{16,20},{20,16},{24,28},{28,24},{1,5},{5... | collective-permute-start | bytes 49160 | tf_op jit(solution)/shard_map/ppermute | solution.py:741
  7.9 0.5 %prepare_depth.1 = (f32[512,128]{1,0:T(8,128)S(1)}, f32[512,128]{1,0:T(8,128)S(1)}, f32[512,128]{1,0:T(8,128)S(1)}, f32[512,128]{1,0:T(8,128)S(1)}, f32[3,32,128...) custom-call(f32[128,512]{1,0:T(8,128)S(1)} %copy-done), custom_call_target="tpu_custom_call" | custom-call | flops 2000000 | bytes 4000000 | tf_op jit(solution)/shard_map/prepare_depth/pallas_call | solution.py:243
  8.4 1.6 %collective-permute-start.2 = (f32[8,512]{1,0:T(8,128)S(1)}, f32[8,512]{1,0:T(8,128)S(1)}, u32[]{:S(2)}, u32[]{:S(2)}) collective-permute-start(f32[8,512]{1,0:T(8,128)S(1)} %once.1), channel_id=1, source_target_pairs={{0,8},{4,0},{8,16},{12,4},{16,24},{20,12},{24,28},{28,20},{1,9},{5... | collective-permute-start | bytes 49160 | tf_op jit(solution)/shard_map/ppermute | solution.py:737
  10.1 0.8 %prepare_rest.1 = (f32[512,128]{1,0:T(8,128)S(1)}, f32[512,128]{1,0:T(8,128)S(1)}, f32[512,128]{1,0:T(8,128)S(1)}, f32[512,128]{1,0:T(8,128)S(1)}, f32[512,128]{...) custom-call(f32[128,512]{1,0:T(8,128)S(1)} %copy-done.1, ...), custom_call_target="tpu_custom_call" | custom-call | flops 2000000 | bytes 6000000 | tf_op jit(solution)/shard_map/prepare_rest/pallas_call | solution.py:263
  10.8 0.6 %fluxes_x_inner.1 = (f32[512,128]{1,0:T(8,128)S(1)}, f32[512,128]{1,0:T(8,128)S(1)}, f32[512,128]{1,0:T(8,128)S(1)}) custom-call(f32[512,128]{1,0:T(8,128)S(1)} %get-tuple-element.41.hx, f32[512,128]{1,0:T(8,128)S(1)} %get-tuple-element.42.px, f32[512,128]{1,0:T(8,128)S(1)} %get-tuple-element.43.qx, f32[512,128]{1,0:T(8,128)S(1)} %get-tuple-element.44.bx, ...), custom_call_target="tpu_custom_call" | custom-call | flops 4000000 | bytes 4000000 | tf_op jit(solution)/shard_map/fluxes_x_inner/pallas_call | solution.py:424
  11.5 1.0 %fluxes_y.1 = (f32[512,128]{1,0:T(8,128)S(1)}, f32[512,128]{1,0:T(8,128)S(1)}, f32[512,128]{1,0:T(8,128)S(1)}) custom-call(f32[2,8,128]{2,1,0:T(8,128)S(1)} %collective-permute-done.3.near, f32[48,128]{1,0:T(8,128)S(1)} %collective-permute-done.4.far, f32[512,128]{1,0:T(8,128)S(1)} %get-tuple-element.52.hy, f32[512,128]{1,0:T(8,128)S(1)} %get-tuple-element.53.py, ...), custom_call_target="tpu_custom_call" | custom-call | flops 4000000 | bytes 4000000 | tf_op jit(solution)/shard_map/fluxes_y/pallas_call | solution.py:382
  12.4 0.0 collective-permute-done.near
  12.4 0.0 collective-permute-done.2.far
  12.5 0.5 %fluxes_x.1 = (f32[512,128]{1,0:T(8,128)S(1)}, f32[512,128]{1,0:T(8,128)S(1)}, f32[512,128]{1,0:T(8,128)S(1)}, f32[4,32,128]{2,1,0:T(8,128)S(1)}, f32[1,2560]{1,0:T(1,128)S(1)}) custom-call(f32[8,512]{1,0:T(8,128)S(1)} %collective-permute-done.near, f32[8,512]{1,0:T(8,128)S(1)} %collective-permute-done.2.far, f32[512,128]{1,0:T(8,128)S(1)} %get-tuple-element.41.hx, ...), custom_call_target="tpu_custom_call" | custom-call | tf_op jit(solution)/shard_map/fluxes_x/pallas_call | solution.py:479
  12.9 0.8 %collective-permute-start.5 = (f32[1,2560]{1,0:T(1,128)S(1)}, f32[1,2560]{1,0:T(1,128)S(1)}, u32[]{:S(2)}, u32[]{:S(2)}) collective-permute-start(f32[1,2560]{1,0:T(1,128)S(1)} %get-tuple-element.74.mine.refs_0_), channel_id=1, source_target_pairs={{0,4},{4,0},{8,12},{12,8},{16,20},{20,16},{24,28},{28,24},{1,5},{5... | collective-permute-start | bytes 30728 | tf_op jit(solution)/shard_map/ppermute | solution.py:741
  13.7 0.3 %join_y.1 = (f32[512,128]{1,0:T(8,128)S(1)}, f32[512,128]{1,0:T(8,128)S(1)}, f32[6,32,128]{2,1,0:T(8,128)S(1)}, f32[1,640]{1,0:T(1,128)S(1)}, f32[1,2048]{1,0:T(1,128)S(1)}) custom-call(f32[512,128]{1,0:T(8,128)S(1)} %get-tuple-element.46.depth_inner, f32[512,128]{1,0:T(8,128)S(1)} %get-tuple-element.47.across_inner, ...), custom_call_target="tpu_custom_call" | custom-call | flops 2000000 | bytes 2000000 | tf_op jit(solution)/shard_map/join_y/pallas_call | solution.py:528
  14.0 0.1 collective-permute-start.6
  14.1 1.1 %collective-permute-start.10 = (f32[1,2048]{1,0:T(1,128)S(1)}, f32[1,2048]{1,0:T(1,128)S(1)}, u32[]{:S(2)}, u32[]{:S(2)}) collective-permute-start(f32[1,2048]{1,0:T(1,128)S(1)} %get-tuple-element.78), channel_id=1, source_target_pairs={{0,2},{1,3},{2,0},{3,1},{4,6},{5,7},{6,4},{7,5},{8,10},{9,11},{10,... | collective-permute-start | bytes 24584 | tf_op jit(solution)/shard_map/ppermute | solution.py:741
  15.2 0.0 collective-permute-done.6.refs_0_.refs_1_
  15.3 1.4 %collective-permute-done.5.theirs.refs_1_ = f32[1,2560]{1,0:T(1,128)S(1)} collective-permute-done((f32[1,2560]{1,0:T(1,128)S(1)}, f32[1,2560]{1,0:T(1,128)S(1)}, u32[]{:S(2)}, u32[]{:S(2)}) %collective-permute-start.5) | collective-permute-done | bytes 10272 | tf_op jit(solution)/shard_map/ppermute | solution.py:741
  16.7 3.4 %collective-permute-start.9 = (f32[1,2560]{1,0:T(1,128)S(1)}, f32[1,2560]{1,0:T(1,128)S(1)}, u32[]{:S(2)}, u32[]{:S(2)}) collective-permute-start(f32[1,2560]{1,0:T(1,128)S(1)} %merge.1.refs_2_), channel_id=1, source_target_pairs={{0,24},{4,28},{8,16},{12,20},{16,8},{20,12},{24,0},{28,4},{1,25},{... | collective-permute-start | bytes 30728 | tf_op jit(solution)/shard_map/ppermute | solution.py:741
  20.1 1.0 %collective-permute-start.7 = (f32[1,2560]{1,0:T(1,128)S(1)}, f32[1,2560]{1,0:T(1,128)S(1)}, u32[]{:S(2)}, u32[]{:S(2)}) collective-permute-start(f32[1,2560]{1,0:T(1,128)S(1)} %merge.1.refs_2_), channel_id=1, source_target_pairs={{0,8},{4,12},{8,0},{12,4},{16,24},{20,28},{24,16},{28,20},{1,9},{5... | collective-permute-start | bytes 30728 | tf_op jit(solution)/shard_map/ppermute | solution.py:741
  21.1 0.7 %write_depth.1 = f32[128,512]{1,0:T(8,128)} custom-call(f32[512,128]{1,0:T(8,128)S(1)} %get-tuple-element.69.depth), custom_call_target="tpu_custom_call" | custom-call | flops 100000 | bytes 2000000 | tf_op jit(solution)/shard_map/write_depth/pallas_call | solution.py:563
  21.9 0.1 rest_x.1.rest
  22.0 0.3 %collective-permute-done.11.refs_3_ = f32[1,640]{1,0:T(1,128)S(1)} collective-permute-done((f32[1,640]{1,0:T(1,128)S(1)}, f32[1,640]{1,0:T(1,128)S(1)}, u32[]{:S(2)}, u32[]{:S(2)}) %collective-permute-start.11) | collective-permute-done | bytes 2592 | tf_op jit(solution)/shard_map/ppermute | solution.py:741
  22.3 1.0 %solve_y.1 = f32[128,512]{1,0:T(8,128)} custom-call(f32[512,128]{1,0:T(8,128)S(1)} %get-tuple-element.65.iy.inv_ref, f32[512,128]{1,0:T(8,128)S(1)} %get-tuple-element.76.r_ref, f32[3,32,128]{2,1,0:T(8,128)S(1)} %get-tuple-element.66.ty.t_ref, f32[15,32,128]{2,1,0:T(8,128)S(1)} %get-tuple-element.67.wy.w_ref, f32[6,32,128]{2,1,0:T(8,128)S(1)} %get-tuple-element.77.s_ref, ...), custom_call_target="tpu_custom_call" | custom-call | flops 1000000 | bytes 4000000 | tf_op jit(solution)/shard_map/solve_y/pallas_call | solution.py:722
  23.3 1.4 %collective-permute-done.8.refs_4_ = f32[1,2560]{1,0:T(1,128)S(1)} collective-permute-done((f32[1,2560]{1,0:T(1,128)S(1)}, f32[1,2560]{1,0:T(1,128)S(1)}, u32[]{:S(2)}, u32[]{:S(2)}) %collective-permute-start.8) | collective-permute-done | bytes 10272 | tf_op jit(solution)/shard_map/ppermute | solution.py:741
  24.7 0.8 %solve_x.1 = f32[128,512]{1,0:T(8,128)} custom-call(f32[512,128]{1,0:T(8,128)S(1)} %get-tuple-element.70.from_left, f32[512,128]{1,0:T(8,128)S(1)} %get-tuple-element.71.from_right, f32[512,128]{1,0:T(8,128)S(1)} %rest_x.1.rest, f32[1,2560]{1,0:T(1,128)S(1)} %get-tuple-element.74.mine.refs_0_, f32[1,2560]{1,0:T(1,128)S(1)} %collective-permute-done.5.theirs.refs_1_, ...), custom_call_target="tpu_custom_call" | custom-call | flops 1000000 | bytes 4000000 | tf_op jit(solution)/shard_map/solve_x/pallas_call | solution.py:722
  (19 shorter events, 0.1 us)
Async XLA Ops:
  0.6 1.1 %copy-start.4 = (s32[128,512]{1,0:T(8,128)S(1)}, s32[128,512]{1,0:T(8,128)}, u32[]{:S(2)}) copy-start(s32[128,512]{1,0:T(8,128)} %m.3) | copy-start | bytes 786436
  0.6 1.1 %copy-start.3 = (f32[128,512]{1,0:T(8,128)S(1)}, f32[128,512]{1,0:T(8,128)}, u32[]{:S(2)}) copy-start(f32[128,512]{1,0:T(8,128)} %b.3) | copy-start | bytes 786436
  0.7 1.2 %copy-start.2 = (f32[128,512]{1,0:T(8,128)S(1)}, f32[128,512]{1,0:T(8,128)}, u32[]{:S(2)}) copy-start(f32[128,512]{1,0:T(8,128)} %q.3) | copy-start | bytes 786436
  0.7 1.2 %copy-start.1 = (f32[128,512]{1,0:T(8,128)S(1)}, f32[128,512]{1,0:T(8,128)}, u32[]{:S(2)}) copy-start(f32[128,512]{1,0:T(8,128)} %p.3) | copy-start | bytes 786436
  0.7 1.3 %copy-start = (f32[128,512]{1,0:T(8,128)S(1)}, f32[128,512]{1,0:T(8,128)}, u32[]{:S(2)}) copy-start(f32[128,512]{1,0:T(8,128)} %h.5) | copy-start | bytes 786436
  2.2 3.1 %collective-permute-start.3 = (f32[2,8,128]{2,1,0:T(8,128)S(1)}, f32[2,8,128]{2,1,0:T(8,128)S(1)}, u32[]{:S(2)}, u32[]{:S(2)}) collective-permute-start(f32[2,8,128]{2,1,0:T(8,128)S(1)} %pack_y.1), channel_id=1, source_target_pairs={{0,1},{1,0},{2,3},{3,2},{4,5},{5,4},{6,7},{7,6},{8,9},{9,8},{10,11... | collective-permute-start | bytes 24584 | tf_op jit(solution)/shard_map/ppermute | solution.py:741
  2.7 5.7 %collective-permute-start.1 = (f32[8,512]{1,0:T(8,128)S(1)}, f32[8,512]{1,0:T(8,128)S(1)}, u32[]{:S(2)}, u32[]{:S(2)}) collective-permute-start(f32[8,512]{1,0:T(8,128)S(1)} %get-tuple-element.49._), channel_id=1, source_target_pairs={{0,4},{4,0},{8,12},{12,8},{16,20},{20,16},{24,28},{28,24},{1,5},{5... | collective-permute-start | bytes 49160 | tf_op jit(solution)/shard_map/ppermute | solution.py:741
  5.3 6.2 %collective-permute-start.4 = (f32[48,128]{1,0:T(8,128)S(1)}, f32[48,128]{1,0:T(8,128)S(1)}, u32[]{:S(2)}, u32[]{:S(2)}) collective-permute-start(f32[48,128]{1,0:T(8,128)S(1)} %pad.4), channel_id=1, source_target_pairs={{0,2},{1,0},{2,3},{3,1},{4,6},{5,4},{6,7},{7,5},{8,10},{9,8},{10,1... | collective-permute-start | bytes 73736 | tf_op jit(solution)/shard_map/ppermute | solution.py:737
  6.8 5.6 %collective-permute-start = (f32[8,512]{1,0:T(8,128)S(1)}, f32[8,512]{1,0:T(8,128)S(1)}, u32[]{:S(2)}, u32[]{:S(2)}) collective-permute-start(f32[8,512]{1,0:T(8,128)S(1)} %get-tuple-element.48), channel_id=1, source_target_pairs={{0,4},{4,0},{8,12},{12,8},{16,20},{20,16},{24,28},{28,24},{1,5},{5... | collective-permute-start | bytes 49160 | tf_op jit(solution)/shard_map/ppermute | solution.py:741
  8.4 4.0 %collective-permute-start.2 = (f32[8,512]{1,0:T(8,128)S(1)}, f32[8,512]{1,0:T(8,128)S(1)}, u32[]{:S(2)}, u32[]{:S(2)}) collective-permute-start(f32[8,512]{1,0:T(8,128)S(1)} %once.1), channel_id=1, source_target_pairs={{0,8},{4,0},{8,16},{12,4},{16,24},{20,12},{24,28},{28,20},{1,9},{5... | collective-permute-start | bytes 49160 | tf_op jit(solution)/shard_map/ppermute | solution.py:737
  12.9 3.7 %collective-permute-start.5 = (f32[1,2560]{1,0:T(1,128)S(1)}, f32[1,2560]{1,0:T(1,128)S(1)}, u32[]{:S(2)}, u32[]{:S(2)}) collective-permute-start(f32[1,2560]{1,0:T(1,128)S(1)} %get-tuple-element.74.mine.refs_0_), channel_id=1, source_target_pairs={{0,4},{4,0},{8,12},{12,8},{16,20},{20,16},{24,28},{28,24},{1,5},{5... | collective-permute-start | bytes 30728 | tf_op jit(solution)/shard_map/ppermute | solution.py:741
  14.0 1.2 %collective-permute-start.6 = (f32[1,640]{1,0:T(1,128)S(1)}, f32[1,640]{1,0:T(1,128)S(1)}, u32[]{:S(2)}, u32[]{:S(2)}) collective-permute-start(f32[1,640]{1,0:T(1,128)S(1)} %get-tuple-element.75.refs_0_), channel_id=1, source_target_pairs={{0,1},{1,0},{2,3},{3,2},{4,5},{5,4},{6,7},{7,6},{8,9},{9,8},{10,11... | collective-permute-start | bytes 7688 | tf_op jit(solution)/shard_map/ppermute | solution.py:741
  14.1 7.0 %collective-permute-start.10 = (f32[1,2048]{1,0:T(1,128)S(1)}, f32[1,2048]{1,0:T(1,128)S(1)}, u32[]{:S(2)}, u32[]{:S(2)}) collective-permute-start(f32[1,2048]{1,0:T(1,128)S(1)} %get-tuple-element.78), channel_id=1, source_target_pairs={{0,2},{1,3},{2,0},{3,1},{4,6},{5,7},{6,4},{7,5},{8,10},{9,11},{10,... | collective-permute-start | bytes 24584 | tf_op jit(solution)/shard_map/ppermute | solution.py:741
  16.7 6.6 %collective-permute-start.9 = (f32[1,2560]{1,0:T(1,128)S(1)}, f32[1,2560]{1,0:T(1,128)S(1)}, u32[]{:S(2)}, u32[]{:S(2)}) collective-permute-start(f32[1,2560]{1,0:T(1,128)S(1)} %merge.1.refs_2_), channel_id=1, source_target_pairs={{0,24},{4,28},{8,16},{12,20},{16,8},{20,12},{24,0},{28,4},{1,25},{... | collective-permute-start | bytes 30728 | tf_op jit(solution)/shard_map/ppermute | solution.py:741
  20.1 4.6 %collective-permute-start.8 = (f32[1,2560]{1,0:T(1,128)S(1)}, f32[1,2560]{1,0:T(1,128)S(1)}, u32[]{:S(2)}, u32[]{:S(2)}) collective-permute-start(f32[1,2560]{1,0:T(1,128)S(1)} %merge.1.refs_2_), channel_id=1, source_target_pairs={{0,16},{4,20},{8,24},{12,28},{16,0},{20,4},{24,8},{28,12},{1,17},{... | collective-permute-start | bytes 30728 | tf_op jit(solution)/shard_map/ppermute | solution.py:741
  20.1 4.6 %collective-permute-start.7 = (f32[1,2560]{1,0:T(1,128)S(1)}, f32[1,2560]{1,0:T(1,128)S(1)}, u32[]{:S(2)}, u32[]{:S(2)}) collective-permute-start(f32[1,2560]{1,0:T(1,128)S(1)} %merge.1.refs_2_), channel_id=1, source_target_pairs={{0,8},{4,12},{8,0},{12,4},{16,24},{20,28},{24,16},{28,20},{1,9},{5... | collective-permute-start | bytes 30728 | tf_op jit(solution)/shard_map/ppermute | solution.py:741
  21.1 1.2 %collective-permute-start.11 = (f32[1,640]{1,0:T(1,128)S(1)}, f32[1,640]{1,0:T(1,128)S(1)}, u32[]{:S(2)}, u32[]{:S(2)}) collective-permute-start(f32[1,640]{1,0:T(1,128)S(1)} %slice.9), channel_id=1, source_target_pairs={{0,1},{1,0},{2,3},{3,2},{4,5},{5,4},{6,7},{7,6},{8,9},{9,8},{10,11... | collective-permute-start | bytes 7688 | tf_op jit(solution)/shard_map/ppermute | solution.py:741

commit v12 on v10

--- a/solution.py
+++ b/solution.py
@@ -602,7 +602,7 @@
     )(mine, theirs, *beside)
 
 
-def line_ends(axis, refs):
+def line_ends(axis, refs, is_crossed=False):
     steps = []
     parts = [rows_of(ref, refs[0].shape[1] // 5) for ref in refs]
     stage = 0
@@ -611,6 +611,11 @@
         steps.append((is_low, weights))
         parts = parts[2:]
         stage += 1
+    if is_crossed:
+        lower = (lax.axis_index(axis) >> (stage + 1)) % 2 == 0
+        both = list(zip(*parts[2:]))
+        parts[2] = tuple(jnp.where(lower, a, b) for a, b in both)
+        parts[3] = tuple(jnp.where(lower, b, a) for a, b in both)
     is_low, (own, weights) = ordered(axis, stage, *parts[:2])
     steps.append((is_low, weights))
     _, (other, _) = ordered(axis, stage, *parts[2:])
@@ -680,7 +685,7 @@
 
 def solve_x_kernel(from_left, from_right, rest, *refs):
     parts, (out, natural, sems) = refs[:-3], refs[-3:]
-    left, right = line_ends("gx", parts)
+    left, right = line_ends("gx", parts, True)
     writes = []
     for tile in range(out.shape[1] // LANES):
         span = tile_span(tile)
@@ -741,6 +746,14 @@
     return lax.ppermute(value, axis, [(i, i ^ mask) for i in range(lax.axis_size(axis))])
 
 
+def crossed(value, axis, stage, half):
+    pairs = []
+    for i in range(lax.axis_size(axis)):
+        upper = (i >> (stage + 1)) & 1
+        pairs.append((i, i ^ ((2 if upper == half else 3) << stage)))
+    return lax.ppermute(value, axis, pairs)
+
+
 def parts_of_line(axis, mine, relay, beside=(), tall=None):
     parts = []
     last = log2(lax.axis_size(axis)) - 2
@@ -753,7 +766,8 @@
         second = cross(mine if tall is None else tall, axis, 2 << last)
         both = cross(second[:, 0 : mine.shape[1]], axis, 1 << last)
     else:
-        first, second, both = (cross(mine, axis, n << last) for n in (1, 2, 3))
+        first = cross(mine, axis, 1 << last)
+        second, both = (crossed(mine, axis, last, n) for n in (1, 0))
     return parts + [mine, first, second, both]
 
 

time: 25 us -> 24.4 us (0.976)
  starting transfers between devices: 13.9 us -> 13.6 us
  waiting for transfers between devices: 2.22 us -> 1.93 us
    ppermute x9 -> x7, starting transfers between devices: 10.5 us -> 6.31 us  [cross(): lax.ppermute(value, axis, [(i, i ^ mask) for i in range(lax.axis_size(axi...]
    ppermute x0 -> x2, starting transfers between devices: none -> 3.88 us  [crossed(): return lax.ppermute(value, axis, pairs)]
    ppermute x9 -> x7, waiting for transfers between devices: 2.21 us -> 1.04 us  [cross(): lax.ppermute(value, axis, [(i, i ^ mask) for i in range(lax.axis_size(axi...]
    ppermute x0 -> x2, waiting for transfers between devices: none -> 0.88 us  [crossed(): return lax.ppermute(value, axis, pairs)]
  transfers between devices with their start and end apart: 11 -> 11, of which waited for: 3 -> 4; matrix products, arithmetic and copies ran while one was open for 0% -> 0% of each run, Pallas kernels for 20% -> 21%
where the time goes in v12:
time: 24.4 us; the launch traced here: 24.2 us
  starting transfers between devices  13.6 us (56%)
  Pallas kernels  7.55 us (31%)
  waiting for transfers between devices  1.93 us (8%)
  between operations  0.81 us (3%)
  local copies, waits for them, and re-layouts  0.31 us (1%)
    ppermute x7, starting transfers between devices, cross(): lax.ppermute(value, axis, [(i, i ^ mask) for i in range(lax.axis_size(axi...  6.31 us
    ppermute x2, starting transfers between devices, crossed(): return lax.ppermute(value, axis, pairs)  3.88 us
    ppermute x2, starting transfers between devices, hand_on(): lax.ppermute(value, axis, [(i, t if 0 <= t < count else i ^ 1) for i, t i...  3.42 us
    pallas_call x2, Pallas kernels, solve(): pl.pallas_call(kernel, out_shape=shape(*block), in_specs=[VMEM] * (len(pi...  1.82 us
    ppermute x7, waiting for transfers between devices, cross(): lax.ppermute(value, axis, [(i, i ^ mask) for i in range(lax.axis_size(axi...  1.04 us
    pallas_call x1, Pallas kernels, pack_x(): pl.pallas_call(pack_x_kernel, out_shape=shape(2, SUB, cols), in_specs=[HB...  0.99 us
    pallas_call x1, Pallas kernels, fluxes_y(): pl.pallas_call(flux_y_kernel, out_shape=(shape(*stack),) * 3, in_specs=[V...  0.97 us
    ppermute x2, waiting for transfers between devices, crossed(): return lax.ppermute(value, axis, pairs)  0.88 us
  transfers between devices with their start and end apart: 11, of which 4 were waited for; matrix products, arithmetic and copies ran while one was open for 0% of the time, Pallas kernels for 21%

profile of v12, /device:TPU:0, one launch (start us, length us, event | category | flops | bytes accessed | tf_op | source)
XLA Modules:
  0.0 24.2 jit_solution(9141609342225674151)
XLA Ops:
  0.7 1.0 %pack_x.1._ = f32[2,8,512]{2,1,0:T(8,128)S(1)} custom-call(f32[128,512]{1,0:T(8,128)} %h.5, f32[128,512]{1,0:T(8,128)} %p.3, f32[128,512]{1,0:T(8,128)} %q.3, f32[128,512]{1,0:T(8,128)} %b.3, s32[128,512]{1,0:T(8,128)} %m.3), custom_call_target="tpu_custom_call" | custom-call | tf_op jit(solution)/shard_map/pack_x/pallas_call | solution.py:78
  1.7 0.1 copy-done.3
  1.7 0.1 copy-done.2
  1.8 0.1 copy-done.1
  1.9 0.1 copy-done
  2.0 0.2 pack_y.1
  2.2 0.5 %collective-permute-start.2 = (f32[2,8,128]{2,1,0:T(8,128)S(1)}, f32[2,8,128]{2,1,0:T(8,128)S(1)}, u32[]{:S(2)}, u32[]{:S(2)}) collective-permute-start(f32[2,8,128]{2,1,0:T(8,128)S(1)} %pack_y.1), channel_id=1, source_target_pairs={{0,1},{1,0},{2,3},{3,2},{4,5},{5,4},{6,7},{7,6},{8,9},{9,8},{10,11... | collective-permute-start | bytes 24584 | tf_op jit(solution)/shard_map/ppermute | solution.py:746
  2.7 2.6 %collective-permute-start = (f32[2,8,512]{2,1,0:T(8,128)S(1)}, f32[2,8,512]{2,1,0:T(8,128)S(1)}, u32[]{:S(2)}, u32[]{:S(2)}) collective-permute-start(f32[2,8,512]{2,1,0:T(8,128)S(1)} %pack_x.1._), channel_id=1, source_target_pairs={{0,4},{4,0},{8,12},{12,8},{16,20},{20,16},{24,28},{28,24},{1,5},{5... | collective-permute-start | bytes 98312 | tf_op jit(solution)/shard_map/ppermute | solution.py:746
  5.3 0.0 collective-permute-done.2.near
  5.3 1.5 %collective-permute-start.3 = (f32[48,128]{1,0:T(8,128)S(1)}, f32[48,128]{1,0:T(8,128)S(1)}, u32[]{:S(2)}, u32[]{:S(2)}) collective-permute-start(f32[48,128]{1,0:T(8,128)S(1)} %pad.4), channel_id=1, source_target_pairs={{0,2},{1,0},{2,3},{3,1},{4,6},{5,4},{6,7},{7,5},{8,10},{9,8},{10,1... | collective-permute-start | bytes 73736 | tf_op jit(solution)/shard_map/ppermute | solution.py:742
  6.8 0.5 %prepare_depth.1 = (f32[512,128]{1,0:T(8,128)S(1)}, f32[512,128]{1,0:T(8,128)S(1)}, f32[512,128]{1,0:T(8,128)S(1)}, f32[512,128]{1,0:T(8,128)S(1)}, f32[3,32,128...) custom-call(f32[128,512]{1,0:T(8,128)S(1)} %copy-done), custom_call_target="tpu_custom_call" | custom-call | flops 2000000 | bytes 4000000 | tf_op jit(solution)/shard_map/prepare_depth/pallas_call | solution.py:243
  7.4 1.9 %collective-permute-start.1 = (f32[8,512]{1,0:T(8,128)S(1)}, f32[8,512]{1,0:T(8,128)S(1)}, u32[]{:S(2)}, u32[]{:S(2)}) collective-permute-start(f32[8,512]{1,0:T(8,128)S(1)} %second_of.1), channel_id=1, source_target_pairs={{0,8},{4,0},{8,16},{12,4},{16,24},{20,12},{24,28},{28,20},{1,9},{5... | collective-permute-start | bytes 49160 | tf_op jit(solution)/shard_map/ppermute | solution.py:742
  9.3 0.8 %prepare_rest.1 = (f32[512,128]{1,0:T(8,128)S(1)}, f32[512,128]{1,0:T(8,128)S(1)}, f32[512,128]{1,0:T(8,128)S(1)}, f32[512,128]{1,0:T(8,128)S(1)}, f32[512,128]{...) custom-call(f32[128,512]{1,0:T(8,128)S(1)} %copy-done.1, ...), custom_call_target="tpu_custom_call" | custom-call | flops 2000000 | bytes 6000000 | tf_op jit(solution)/shard_map/prepare_rest/pallas_call | solution.py:263
  10.0 0.6 %fluxes_x_inner.1 = (f32[512,128]{1,0:T(8,128)S(1)}, f32[512,128]{1,0:T(8,128)S(1)}, f32[512,128]{1,0:T(8,128)S(1)}) custom-call(f32[512,128]{1,0:T(8,128)S(1)} %get-tuple-element.39.hx, f32[512,128]{1,0:T(8,128)S(1)} %get-tuple-element.40.px, f32[512,128]{1,0:T(8,128)S(1)} %get-tuple-element.41.qx, f32[512,128]{1,0:T(8,128)S(1)} %get-tuple-element.42.bx, ...), custom_call_target="tpu_custom_call" | custom-call | flops 4000000 | bytes 4000000 | tf_op jit(solution)/shard_map/fluxes_x_inner/pallas_call | solution.py:424
  10.6 1.0 %fluxes_y.1 = (f32[512,128]{1,0:T(8,128)S(1)}, f32[512,128]{1,0:T(8,128)S(1)}, f32[512,128]{1,0:T(8,128)S(1)}) custom-call(f32[2,8,128]{2,1,0:T(8,128)S(1)} %collective-permute-done.2.near, f32[48,128]{1,0:T(8,128)S(1)} %collective-permute-done.3.far, f32[512,128]{1,0:T(8,128)S(1)} %get-tuple-element.48.hy, f32[512,128]{1,0:T(8,128)S(1)} %get-tuple-element.49.py, ...), custom_call_target="tpu_custom_call" | custom-call | flops 4000000 | bytes 4000000 | tf_op jit(solution)/shard_map/fluxes_y/pallas_call | solution.py:382
  11.6 0.0 collective-permute-done.1.far
  11.6 0.5 %fluxes_x.1 = (f32[512,128]{1,0:T(8,128)S(1)}, f32[512,128]{1,0:T(8,128)S(1)}, f32[512,128]{1,0:T(8,128)S(1)}, f32[4,32,128]{2,1,0:T(8,128)S(1)}, f32[1,2560]{1,0:T(1,128)S(1)}) custom-call(f32[2,8,512]{2,1,0:T(8,128)S(1)} %collective-permute-done.both.near, f32[8,512]{1,0:T(8,128)S(1)} %collective-permute-done.1.far, f32[512,128]{1,0:T(8,128)S(1)} %get-tuple-element.39.hx, ...), custom_call_target="tpu_custom_call" | custom-call | tf_op jit(solution)/shard_map/fluxes_x/pallas_call | solution.py:479
  12.1 1.3 %collective-permute-start.4 = (f32[1,2560]{1,0:T(1,128)S(1)}, f32[1,2560]{1,0:T(1,128)S(1)}, u32[]{:S(2)}, u32[]{:S(2)}) collective-permute-start(f32[1,2560]{1,0:T(1,128)S(1)} %get-tuple-element.70.mine.refs_0_), channel_id=1, source_target_pairs={{0,4},{4,0},{8,12},{12,8},{16,20},{20,16},{24,28},{28,24},{1,5},{5... | collective-permute-start | bytes 30728 | tf_op jit(solution)/shard_map/ppermute | solution.py:746
  13.4 0.3 %join_y.1 = (f32[512,128]{1,0:T(8,128)S(1)}, f32[512,128]{1,0:T(8,128)S(1)}, f32[6,32,128]{2,1,0:T(8,128)S(1)}, f32[1,640]{1,0:T(1,128)S(1)}, f32[1,2048]{1,0:T(1,128)S(1)}) custom-call(f32[512,128]{1,0:T(8,128)S(1)} %get-tuple-element.44.depth_inner, f32[512,128]{1,0:T(8,128)S(1)} %get-tuple-element.45.across_inner, ...), custom_call_target="tpu_custom_call" | custom-call | flops 2000000 | bytes 2000000 | tf_op jit(solution)/shard_map/join_y/pallas_call | solution.py:528
  13.8 0.1 collective-permute-start.5
  13.8 1.6 %collective-permute-start.9 = (f32[1,2048]{1,0:T(1,128)S(1)}, f32[1,2048]{1,0:T(1,128)S(1)}, u32[]{:S(2)}, u32[]{:S(2)}) collective-permute-start(f32[1,2048]{1,0:T(1,128)S(1)} %get-tuple-element.74), channel_id=1, source_target_pairs={{0,2},{1,3},{2,0},{3,1},{4,6},{5,7},{6,4},{7,5},{8,10},{9,11},{10,... | collective-permute-start | bytes 24584 | tf_op jit(solution)/shard_map/ppermute | solution.py:746
  15.4 0.4 %collective-permute-done.4.theirs.refs_1_ = f32[1,2560]{1,0:T(1,128)S(1)} collective-permute-done((f32[1,2560]{1,0:T(1,128)S(1)}, f32[1,2560]{1,0:T(1,128)S(1)}, u32[]{:S(2)}, u32[]{:S(2)}) %collective-permute-start.4) | collective-permute-done | bytes 10272 | tf_op jit(solution)/shard_map/ppermute | solution.py:746
  15.8 2.6 %collective-permute-start.8 = (f32[1,2560]{1,0:T(1,128)S(1)}, f32[1,2560]{1,0:T(1,128)S(1)}, u32[]{:S(2)}, u32[]{:S(2)}) collective-permute-start(f32[1,2560]{1,0:T(1,128)S(1)} %merge.1.refs_2_), channel_id=1, source_target_pairs={{0,16},{4,20},{8,24},{12,28},{16,8},{20,12},{24,0},{28,4},{1,17},{... | collective-permute-start | bytes 30728 | tf_op jit(solution)/shard_map/ppermute | solution.py:754
  18.5 1.2 %collective-permute-start.7 = (f32[1,2560]{1,0:T(1,128)S(1)}, f32[1,2560]{1,0:T(1,128)S(1)}, u32[]{:S(2)}, u32[]{:S(2)}) collective-permute-start(f32[1,2560]{1,0:T(1,128)S(1)} %merge.1.refs_2_), channel_id=1, source_target_pairs={{0,24},{4,28},{8,16},{12,20},{16,0},{20,4},{24,8},{28,12},{1,25},{... | collective-permute-start | bytes 30728 | tf_op jit(solution)/shard_map/ppermute | solution.py:754
  19.7 0.3 %collective-permute-start.6 = (f32[1,2560]{1,0:T(1,128)S(1)}, f32[1,2560]{1,0:T(1,128)S(1)}, u32[]{:S(2)}, u32[]{:S(2)}) collective-permute-start(f32[1,2560]{1,0:T(1,128)S(1)} %merge.1.refs_2_), channel_id=1, source_target_pairs={{0,8},{4,12},{8,0},{12,4},{16,24},{20,28},{24,16},{28,20},{1,9},{5... | collective-permute-start | bytes 30728 | tf_op jit(solution)/shard_map/ppermute | solution.py:746
  20.0 0.7 %write_depth.1 = f32[128,512]{1,0:T(8,128)} custom-call(f32[512,128]{1,0:T(8,128)S(1)} %get-tuple-element.65.depth), custom_call_target="tpu_custom_call" | custom-call | flops 100000 | bytes 2000000 | tf_op jit(solution)/shard_map/write_depth/pallas_call | solution.py:563
  20.8 0.1 rest_x.1.rest
  20.9 0.3 %collective-permute-done.10.refs_3_ = f32[1,640]{1,0:T(1,128)S(1)} collective-permute-done((f32[1,640]{1,0:T(1,128)S(1)}, f32[1,640]{1,0:T(1,128)S(1)}, u32[]{:S(2)}, u32[]{:S(2)}) %collective-permute-start.10) | collective-permute-done | bytes 2592 | tf_op jit(solution)/shard_map/ppermute | solution.py:746
  21.2 1.0 %solve_y.1 = f32[128,512]{1,0:T(8,128)} custom-call(f32[512,128]{1,0:T(8,128)S(1)} %get-tuple-element.61.iy.inv_ref, f32[512,128]{1,0:T(8,128)S(1)} %get-tuple-element.72.r_ref, f32[3,32,128]{2,1,0:T(8,128)S(1)} %get-tuple-element.62.ty.t_ref, f32[15,32,128]{2,1,0:T(8,128)S(1)} %get-tuple-element.63.wy.w_ref, f32[6,32,128]{2,1,0:T(8,128)S(1)} %get-tuple-element.73.s_ref, ...), custom_call_target="tpu_custom_call" | custom-call | flops 1000000 | bytes 4000000 | tf_op jit(solution)/shard_map/solve_y/pallas_call | solution.py:727
  22.2 0.9 %collective-permute-done.7.refs_4_ = f32[1,2560]{1,0:T(1,128)S(1)} collective-permute-done((f32[1,2560]{1,0:T(1,128)S(1)}, f32[1,2560]{1,0:T(1,128)S(1)}, u32[]{:S(2)}, u32[]{:S(2)}) %collective-permute-start.7) | collective-permute-done | bytes 10272 | tf_op jit(solution)/shard_map/ppermute | solution.py:754
  23.1 0.3 %collective-permute-done.6.refs_3_ = f32[1,2560]{1,0:T(1,128)S(1)} collective-permute-done((f32[1,2560]{1,0:T(1,128)S(1)}, f32[1,2560]{1,0:T(1,128)S(1)}, u32[]{:S(2)}, u32[]{:S(2)}) %collective-permute-start.6) | collective-permute-done | bytes 10272 | tf_op jit(solution)/shard_map/ppermute | solution.py:746
  23.4 0.8 %solve_x.1 = f32[128,512]{1,0:T(8,128)} custom-call(f32[512,128]{1,0:T(8,128)S(1)} %get-tuple-element.66.from_left, f32[512,128]{1,0:T(8,128)S(1)} %get-tuple-element.67.from_right, f32[512,128]{1,0:T(8,128)S(1)} %rest_x.1.rest, f32[1,2560]{1,0:T(1,128)S(1)} %get-tuple-element.70.mine.refs_0_, f32[1,2560]{1,0:T(1,128)S(1)} %collective-permute-done.4.theirs.refs_1_, ...), custom_call_target="tpu_custom_call" | custom-call | flops 1000000 | bytes 4000000 | tf_op jit(solution)/shard_map/solve_x/pallas_call | solution.py:727
  (17 shorter events, 0.1 us)
Async XLA Ops:
  0.6 1.1 %copy-start.4 = (s32[128,512]{1,0:T(8,128)S(1)}, s32[128,512]{1,0:T(8,128)}, u32[]{:S(2)}) copy-start(s32[128,512]{1,0:T(8,128)} %m.3) | copy-start | bytes 786436
  0.6 1.1 %copy-start.3 = (f32[128,512]{1,0:T(8,128)S(1)}, f32[128,512]{1,0:T(8,128)}, u32[]{:S(2)}) copy-start(f32[128,512]{1,0:T(8,128)} %b.3) | copy-start | bytes 786436
  0.7 1.2 %copy-start.2 = (f32[128,512]{1,0:T(8,128)S(1)}, f32[128,512]{1,0:T(8,128)}, u32[]{:S(2)}) copy-start(f32[128,512]{1,0:T(8,128)} %q.3) | copy-start | bytes 786436
  0.7 1.2 %copy-start.1 = (f32[128,512]{1,0:T(8,128)S(1)}, f32[128,512]{1,0:T(8,128)}, u32[]{:S(2)}) copy-start(f32[128,512]{1,0:T(8,128)} %p.3) | copy-start | bytes 786436
  0.7 1.3 %copy-start = (f32[128,512]{1,0:T(8,128)S(1)}, f32[128,512]{1,0:T(8,128)}, u32[]{:S(2)}) copy-start(f32[128,512]{1,0:T(8,128)} %h.5) | copy-start | bytes 786436
  2.2 3.1 %collective-permute-start.2 = (f32[2,8,128]{2,1,0:T(8,128)S(1)}, f32[2,8,128]{2,1,0:T(8,128)S(1)}, u32[]{:S(2)}, u32[]{:S(2)}) collective-permute-start(f32[2,8,128]{2,1,0:T(8,128)S(1)} %pack_y.1), channel_id=1, source_target_pairs={{0,1},{1,0},{2,3},{3,2},{4,5},{5,4},{6,7},{7,6},{8,9},{9,8},{10,11... | collective-permute-start | bytes 24584 | tf_op jit(solution)/shard_map/ppermute | solution.py:746
  2.7 4.7 %collective-permute-start = (f32[2,8,512]{2,1,0:T(8,128)S(1)}, f32[2,8,512]{2,1,0:T(8,128)S(1)}, u32[]{:S(2)}, u32[]{:S(2)}) collective-permute-start(f32[2,8,512]{2,1,0:T(8,128)S(1)} %pack_x.1._), channel_id=1, source_target_pairs={{0,4},{4,0},{8,12},{12,8},{16,20},{20,16},{24,28},{28,24},{1,5},{5... | collective-permute-start | bytes 98312 | tf_op jit(solution)/shard_map/ppermute | solution.py:746
  5.3 5.4 %collective-permute-start.3 = (f32[48,128]{1,0:T(8,128)S(1)}, f32[48,128]{1,0:T(8,128)S(1)}, u32[]{:S(2)}, u32[]{:S(2)}) collective-permute-start(f32[48,128]{1,0:T(8,128)S(1)} %pad.4), channel_id=1, source_target_pairs={{0,2},{1,0},{2,3},{3,1},{4,6},{5,4},{6,7},{7,5},{8,10},{9,8},{10,1... | collective-permute-start | bytes 73736 | tf_op jit(solution)/shard_map/ppermute | solution.py:742
  7.4 4.2 %collective-permute-start.1 = (f32[8,512]{1,0:T(8,128)S(1)}, f32[8,512]{1,0:T(8,128)S(1)}, u32[]{:S(2)}, u32[]{:S(2)}) collective-permute-start(f32[8,512]{1,0:T(8,128)S(1)} %second_of.1), channel_id=1, source_target_pairs={{0,8},{4,0},{8,16},{12,4},{16,24},{20,12},{24,28},{28,20},{1,9},{5... | collective-permute-start | bytes 49160 | tf_op jit(solution)/shard_map/ppermute | solution.py:742
  12.1 3.7 %collective-permute-start.4 = (f32[1,2560]{1,0:T(1,128)S(1)}, f32[1,2560]{1,0:T(1,128)S(1)}, u32[]{:S(2)}, u32[]{:S(2)}) collective-permute-start(f32[1,2560]{1,0:T(1,128)S(1)} %get-tuple-element.70.mine.refs_0_), channel_id=1, source_target_pairs={{0,4},{4,0},{8,12},{12,8},{16,20},{20,16},{24,28},{28,24},{1,5},{5... | collective-permute-start | bytes 30728 | tf_op jit(solution)/shard_map/ppermute | solution.py:746
  13.8 1.7 %collective-permute-start.5 = (f32[1,640]{1,0:T(1,128)S(1)}, f32[1,640]{1,0:T(1,128)S(1)}, u32[]{:S(2)}, u32[]{:S(2)}) collective-permute-start(f32[1,640]{1,0:T(1,128)S(1)} %get-tuple-element.71.refs_0_), channel_id=1, source_target_pairs={{0,1},{1,0},{2,3},{3,2},{4,5},{5,4},{6,7},{7,6},{8,9},{9,8},{10,11... | collective-permute-start | bytes 7688 | tf_op jit(solution)/shard_map/ppermute | solution.py:746
  13.8 6.2 %collective-permute-start.9 = (f32[1,2048]{1,0:T(1,128)S(1)}, f32[1,2048]{1,0:T(1,128)S(1)}, u32[]{:S(2)}, u32[]{:S(2)}) collective-permute-start(f32[1,2048]{1,0:T(1,128)S(1)} %get-tuple-element.74), channel_id=1, source_target_pairs={{0,2},{1,3},{2,0},{3,1},{4,6},{5,7},{6,4},{7,5},{8,10},{9,11},{10,... | collective-permute-start | bytes 24584 | tf_op jit(solution)/shard_map/ppermute | solution.py:746
  15.8 6.3 %collective-permute-start.8 = (f32[1,2560]{1,0:T(1,128)S(1)}, f32[1,2560]{1,0:T(1,128)S(1)}, u32[]{:S(2)}, u32[]{:S(2)}) collective-permute-start(f32[1,2560]{1,0:T(1,128)S(1)} %merge.1.refs_2_), channel_id=1, source_target_pairs={{0,16},{4,20},{8,24},{12,28},{16,8},{20,12},{24,0},{28,4},{1,17},{... | collective-permute-start | bytes 30728 | tf_op jit(solution)/shard_map/ppermute | solution.py:754
  18.5 4.6 %collective-permute-start.7 = (f32[1,2560]{1,0:T(1,128)S(1)}, f32[1,2560]{1,0:T(1,128)S(1)}, u32[]{:S(2)}, u32[]{:S(2)}) collective-permute-start(f32[1,2560]{1,0:T(1,128)S(1)} %merge.1.refs_2_), channel_id=1, source_target_pairs={{0,24},{4,28},{8,16},{12,20},{16,0},{20,4},{24,8},{28,12},{1,25},{... | collective-permute-start | bytes 30728 | tf_op jit(solution)/shard_map/ppermute | solution.py:754
  19.7 3.7 %collective-permute-start.6 = (f32[1,2560]{1,0:T(1,128)S(1)}, f32[1,2560]{1,0:T(1,128)S(1)}, u32[]{:S(2)}, u32[]{:S(2)}) collective-permute-start(f32[1,2560]{1,0:T(1,128)S(1)} %merge.1.refs_2_), channel_id=1, source_target_pairs={{0,8},{4,12},{8,0},{12,4},{16,24},{20,28},{24,16},{28,20},{1,9},{5... | collective-permute-start | bytes 30728 | tf_op jit(solution)/shard_map/ppermute | solution.py:746
  20.0 1.2 %collective-permute-start.10 = (f32[1,640]{1,0:T(1,128)S(1)}, f32[1,640]{1,0:T(1,128)S(1)}, u32[]{:S(2)}, u32[]{:S(2)}) collective-permute-start(f32[1,640]{1,0:T(1,128)S(1)} %slice.9), channel_id=1, source_target_pairs={{0,1},{1,0},{2,3},{3,2},{4,5},{5,4},{6,7},{7,6},{8,9},{9,8},{10,11... | collective-permute-start | bytes 7688 | tf_op jit(solution)/shard_map/ppermute | solution.py:746

commit v13 on v12

--- a/solution.py
+++ b/solution.py
@@ -92,7 +92,7 @@
     )(*[pltpu.with_memory_space_constraint(v, pltpu.HBM) for v in fields])
 
 
-def pack_y_kernel(h, p, q, b, m, _, slabs, natural):
+def pack_y_kernel(h, p, q, b, m, _, near, far, natural):
     rows, cols = h.shape
     lane = lane_index((rows, LANES))
     out = None
@@ -105,17 +105,18 @@
     last = jnp.concatenate([turned[0:2], turned[4:6], turned[8:10], turned[13:14], turned[17:18]])
     first = jnp.concatenate([turned[2:4], turned[6:8], turned[10:12], turned[14:15], turned[18:19]])
     even = lax.axis_index("gy") % 2 == 0
-    slabs[0] = jnp.where(even, last, first)
-    slabs[1] = jnp.where(even, first, last)
+    for slab, value in ((near, jnp.where(even, last, first)), (far, jnp.where(even, first, last))):
+        slab[...] = jnp.zeros_like(slab)
+        slab[0:SUB, :] = value
 
 
 def pack_y(*fields, after):
     rows = fields[0].shape[0]
     return pl.pallas_call(
         pack_y_kernel,
-        out_shape=shape(2, SUB, rows),
+        out_shape=(shape(1 * SUB, rows), shape(4 * SUB, rows)),
         in_specs=[VMEM] * 6,
-        out_specs=VMEM,
+        out_specs=(VMEM, VMEM),
         scratch_shapes=[pltpu.VMEM((rows, LANES), F32)],
         compiler_params=PARAMS,
         cost_estimate=pl.CostEstimate(flops=500_000, bytes_accessed=1_000_000, transcendentals=0),
@@ -123,19 +124,19 @@
     )(*fields, after)
 
 
-def tie_kernel(both, _, out):
-    out[...] = both[1]
-
-
-def second_of(both, after):
+def tie_kernel(both, *refs):
+    refs[-1][...] = both[1]
+
+
+def second_of(both, *after):
     return pl.pallas_call(
         tie_kernel,
         out_shape=shape(*both.shape[1:]),
-        in_specs=[VMEM, VMEM],
+        in_specs=[VMEM] * (1 + len(after)),
         out_specs=VMEM,
         compiler_params=PARAMS,
         name="second_of",
-    )(both, after)
+    )(both, *after)
 
 
 def merge_coefficients(one, two):
@@ -352,7 +353,7 @@
 
 def flux_y_kernel(near, far, hy, py, qy, by, my, mass, shear, normal, across, along):
     tiles = hy.shape[0] // LANES
-    low, high = low_high("gy", near[0], far[0:SUB, :])
+    low, high = low_high("gy", near[0:SUB, :], far[0:SUB, :])
     for tile in range(tiles):
 
         def extend(ref, row, layers):
@@ -742,6 +743,12 @@
     return lax.ppermute(value, axis, [(i, t if 0 <= t < count else i ^ 1) for i, t in enumerate(far)])
 
 
+def shift_pair(value, axis):
+    count = lax.axis_size(axis)
+    other = [((i - 1) ^ 1) + 1 for i in range(count)]
+    return lax.ppermute(value, axis, [(i, o if 0 <= o < count else i) for i, o in enumerate(other)])
+
+
 def cross(value, axis, mask):
     return lax.ppermute(value, axis, [(i, i ^ mask) for i in range(lax.axis_size(axis))])
 
@@ -778,10 +785,10 @@
     inv_cy = 3.0 / (cols * lax.axis_size("gy") / 4.0) ** 2
     slabs_x = pack_x(h, p, q, b, m)
     near_x = cross(slabs_x, "gx", 1)
-    near_y = cross(pack_y(h, p, q, b, m, after=slabs_x), "gy", 1)
-    far_y = hand_on(jnp.pad(near_y[1], ((0, 5 * SUB), (0, 0))), "gy")
+    near_y, far_y = pack_y(h, p, q, b, m, after=slabs_x)
+    near_y, far_y = cross(near_y, "gy", 1), shift_pair(far_y, "gy")
     hx, hy, ix, iy, tx, wx, ty, wy, coef_x, coef_y, left_x, right_x = prepare_depth(h, inv_cx, inv_cy)
-    far_x = hand_on(second_of(near_x, coef_x), "gx")
+    far_x = hand_on(second_of(near_x, coef_x, near_y), "gx")
     px, py, qx, qy, bx, by, mx, my = prepare_rest(p, q, b, m)
     depth_inner, push_inner, across_inner = fluxes_x_inner(hx, px, qx, bx, mx)
     mass_y, shear_y, normal_y = fluxes_y(near_y, far_y, hy, py, qy, by, my)

time: 24.4 us -> 23.9 us (0.980)
  starting transfers between devices: 13.6 us -> 13.1 us
  local copies, waits for them, and re-layouts: 0.31 us -> 0.02 us
    ppermute x2 -> x1, starting transfers between devices: 3.42 us -> 2.11 us  [hand_on(): lax.ppermute(value, axis, [(i, t if 0 <= t < count else i ^ 1) for i, t i...]
    ppermute x0 -> x1, starting transfers between devices: none -> 0.66 us  [shift_pair(): lax.ppermute(value, axis, [(i, o if 0 <= o < count else i) for i, o in en...]
    unnamed x10, local copies, waits for them, and re-layouts: 0.3 us -> 0.02 us
  transfers between devices with their start and end apart: 11 -> 11, of which waited for: 4 -> 5; matrix products, arithmetic and copies ran while one was open for 0% -> 0% of each run, Pallas kernels for 21% -> 23%
where the time goes in v13:
time: 23.9 us; the launch traced here: 23.6 us
  starting transfers between devices  13.1 us (55%)
  Pallas kernels  7.58 us (32%)
  waiting for transfers between devices  2.09 us (9%)
  between operations  0.81 us (3%)
    ppermute x7, starting transfers between devices, cross(): lax.ppermute(value, axis, [(i, i ^ mask) for i in range(lax.axis_size(axi...  6.5 us
    ppermute x2, starting transfers between devices, crossed(): return lax.ppermute(value, axis, pairs)  3.88 us
    ppermute x1, starting transfers between devices, hand_on(): lax.ppermute(value, axis, [(i, t if 0 <= t < count else i ^ 1) for i, t i...  2.11 us
    pallas_call x2, Pallas kernels, solve(): pl.pallas_call(kernel, out_shape=shape(*block), in_specs=[VMEM] * (len(pi...  1.82 us
    ppermute x7, waiting for transfers between devices, cross(): lax.ppermute(value, axis, [(i, i ^ mask) for i in range(lax.axis_size(axi...  1.2 us
    pallas_call x1, Pallas kernels, pack_x(): pl.pallas_call(pack_x_kernel, out_shape=shape(2, SUB, cols), in_specs=[HB...  0.99 us
    pallas_call x1, Pallas kernels, fluxes_y(): pl.pallas_call(flux_y_kernel, out_shape=(shape(*stack),) * 3, in_specs=[V...  0.97 us
    ppermute x2, waiting for transfers between devices, crossed(): return lax.ppermute(value, axis, pairs)  0.88 us
  transfers between devices with their start and end apart: 11, of which 5 were waited for; matrix products, arithmetic and copies ran while one was open for 0% of the time, Pallas kernels for 23%

profile of v13, /device:TPU:0, one launch (start us, length us, event | category | flops | bytes accessed | tf_op | source)
XLA Modules:
  0.0 23.6 jit_solution(5135983293448736558)
XLA Ops:
  0.7 1.0 %pack_x.1._ = f32[2,8,512]{2,1,0:T(8,128)S(1)} custom-call(f32[128,512]{1,0:T(8,128)} %h.5, f32[128,512]{1,0:T(8,128)} %p.3, f32[128,512]{1,0:T(8,128)} %q.3, f32[128,512]{1,0:T(8,128)} %b.3, s32[128,512]{1,0:T(8,128)} %m.3), custom_call_target="tpu_custom_call" | custom-call | tf_op jit(solution)/shard_map/pack_x/pallas_call | solution.py:78
  1.7 3.0 %collective-permute-start = (f32[2,8,512]{2,1,0:T(8,128)S(1)}, f32[2,8,512]{2,1,0:T(8,128)S(1)}, u32[]{:S(2)}, u32[]{:S(2)}) collective-permute-start(f32[2,8,512]{2,1,0:T(8,128)S(1)} %pack_x.1._), channel_id=1, source_target_pairs={{0,4},{4,0},{8,12},{12,8},{16,20},{20,16},{24,28},{28,24},{1,5},{5... | collective-permute-start | bytes 98312 | tf_op jit(solution)/shard_map/ppermute | solution.py:753
  4.7 0.2 pack_y.1
  4.9 0.0 collective-permute-start.1
  5.0 0.7 %collective-permute-start.3 = (f32[32,128]{1,0:T(8,128)S(1)}, f32[32,128]{1,0:T(8,128)S(1)}, u32[]{:S(2)}, u32[]{:S(2)}) collective-permute-start(f32[32,128]{1,0:T(8,128)S(1)} %get-tuple-element.51), channel_id=1, source_target_pairs={{0,0},{1,2},{2,1},{3,3},{4,4},{5,6},{6,5},{7,7},{8,8},{9,10},{10,9... | collective-permute-start | bytes 49160 | tf_op jit(solution)/shard_map/ppermute | solution.py:749
  5.6 0.5 %prepare_depth.1 = (f32[512,128]{1,0:T(8,128)S(1)}, f32[512,128]{1,0:T(8,128)S(1)}, f32[512,128]{1,0:T(8,128)S(1)}, f32[512,128]{1,0:T(8,128)S(1)}, f32[3,32,128...) custom-call(f32[128,512]{1,0:T(8,128)S(1)} %copy-done), custom_call_target="tpu_custom_call" | custom-call | flops 2000000 | bytes 4000000 | tf_op jit(solution)/shard_map/prepare_depth/pallas_call | solution.py:244
  6.2 0.4 %collective-permute-done.both.near = f32[2,8,512]{2,1,0:T(8,128)S(1)} collective-permute-done((f32[2,8,512]{2,1,0:T(8,128)S(1)}, f32[2,8,512]{2,1,0:T(8,128)S(1)}, u32[]{:S(2)}, u32[]{:S(2)}) %collective-permute-start) | collective-permute-done | bytes 32800 | tf_op jit(solution)/shard_map/ppermute | solution.py:753
  6.6 2.1 %collective-permute-start.2 = (f32[8,512]{1,0:T(8,128)S(1)}, f32[8,512]{1,0:T(8,128)S(1)}, u32[]{:S(2)}, u32[]{:S(2)}) collective-permute-start(f32[8,512]{1,0:T(8,128)S(1)} %second_of.1), channel_id=1, source_target_pairs={{0,8},{4,0},{8,16},{12,4},{16,24},{20,12},{24,28},{28,20},{1,9},{5... | collective-permute-start | bytes 49160 | tf_op jit(solution)/shard_map/ppermute | solution.py:743
  8.7 0.8 %prepare_rest.1 = (f32[512,128]{1,0:T(8,128)S(1)}, f32[512,128]{1,0:T(8,128)S(1)}, f32[512,128]{1,0:T(8,128)S(1)}, f32[512,128]{1,0:T(8,128)S(1)}, f32[512,128]{...) custom-call(f32[128,512]{1,0:T(8,128)S(1)} %copy-done.1, ...), custom_call_target="tpu_custom_call" | custom-call | flops 2000000 | bytes 6000000 | tf_op jit(solution)/shard_map/prepare_rest/pallas_call | solution.py:264
  9.5 0.6 %fluxes_x_inner.1 = (f32[512,128]{1,0:T(8,128)S(1)}, f32[512,128]{1,0:T(8,128)S(1)}, f32[512,128]{1,0:T(8,128)S(1)}) custom-call(f32[512,128]{1,0:T(8,128)S(1)} %get-tuple-element.41.hx, f32[512,128]{1,0:T(8,128)S(1)} %get-tuple-element.42.px, f32[512,128]{1,0:T(8,128)S(1)} %get-tuple-element.43.qx, f32[512,128]{1,0:T(8,128)S(1)} %get-tuple-element.44.bx, ...), custom_call_target="tpu_custom_call" | custom-call | flops 4000000 | bytes 4000000 | tf_op jit(solution)/shard_map/fluxes_x_inner/pallas_call | solution.py:425
  10.1 0.0 collective-permute-done.3.far
  10.1 1.0 %fluxes_y.1 = (f32[512,128]{1,0:T(8,128)S(1)}, f32[512,128]{1,0:T(8,128)S(1)}, f32[512,128]{1,0:T(8,128)S(1)}) custom-call(f32[8,128]{1,0:T(8,128)S(1)} %collective-permute-done.1.refs_1_.near, f32[32,128]{1,0:T(8,128)S(1)} %collective-permute-done.3.far, f32[512,128]{1,0:T(8,128)S(1)} %get-tuple-element.52.hy, f32[512,128]{1,0:T(8,128)S(1)} %get-tuple-element.53.py, ...), custom_call_target="tpu_custom_call" | custom-call | flops 4000000 | bytes 4000000 | tf_op jit(solution)/shard_map/fluxes_y/pallas_call | solution.py:383
  11.1 0.0 collective-permute-done.2.far
  11.1 0.5 %fluxes_x.1 = (f32[512,128]{1,0:T(8,128)S(1)}, f32[512,128]{1,0:T(8,128)S(1)}, f32[512,128]{1,0:T(8,128)S(1)}, f32[4,32,128]{2,1,0:T(8,128)S(1)}, f32[1,2560]{1,0:T(1,128)S(1)}) custom-call(f32[2,8,512]{2,1,0:T(8,128)S(1)} %collective-permute-done.both.near, f32[8,512]{1,0:T(8,128)S(1)} %collective-permute-done.2.far, f32[512,128]{1,0:T(8,128)S(1)} %get-tuple-element.41.hx, ...), custom_call_target="tpu_custom_call" | custom-call | tf_op jit(solution)/shard_map/fluxes_x/pallas_call | solution.py:480
  11.5 1.4 %collective-permute-start.4 = (f32[1,2560]{1,0:T(1,128)S(1)}, f32[1,2560]{1,0:T(1,128)S(1)}, u32[]{:S(2)}, u32[]{:S(2)}) collective-permute-start(f32[1,2560]{1,0:T(1,128)S(1)} %get-tuple-element.74.mine.refs_0_), channel_id=1, source_target_pairs={{0,4},{4,0},{8,12},{12,8},{16,20},{20,16},{24,28},{28,24},{1,5},{5... | collective-permute-start | bytes 30728 | tf_op jit(solution)/shard_map/ppermute | solution.py:753
  12.9 0.3 %join_y.1 = (f32[512,128]{1,0:T(8,128)S(1)}, f32[512,128]{1,0:T(8,128)S(1)}, f32[6,32,128]{2,1,0:T(8,128)S(1)}, f32[1,640]{1,0:T(1,128)S(1)}, f32[1,2048]{1,0:T(1,128)S(1)}) custom-call(f32[512,128]{1,0:T(8,128)S(1)} %get-tuple-element.46.depth_inner, f32[512,128]{1,0:T(8,128)S(1)} %get-tuple-element.47.across_inner, ...), custom_call_target="tpu_custom_call" | custom-call | flops 2000000 | bytes 2000000 | tf_op jit(solution)/shard_map/join_y/pallas_call | solution.py:529
  13.3 0.7 %collective-permute-start.5 = (f32[1,640]{1,0:T(1,128)S(1)}, f32[1,640]{1,0:T(1,128)S(1)}, u32[]{:S(2)}, u32[]{:S(2)}) collective-permute-start(f32[1,640]{1,0:T(1,128)S(1)} %get-tuple-element.75.refs_0_), channel_id=1, source_target_pairs={{0,1},{1,0},{2,3},{3,2},{4,5},{5,4},{6,7},{7,6},{8,9},{9,8},{10,11... | collective-permute-start | bytes 7688 | tf_op jit(solution)/shard_map/ppermute | solution.py:753
  13.9 1.1 %collective-permute-start.9 = (f32[1,2048]{1,0:T(1,128)S(1)}, f32[1,2048]{1,0:T(1,128)S(1)}, u32[]{:S(2)}, u32[]{:S(2)}) collective-permute-start(f32[1,2048]{1,0:T(1,128)S(1)} %get-tuple-element.78), channel_id=1, source_target_pairs={{0,2},{1,3},{2,0},{3,1},{4,6},{5,7},{6,4},{7,5},{8,10},{9,11},{10,... | collective-permute-start | bytes 24584 | tf_op jit(solution)/shard_map/ppermute | solution.py:753
  15.1 0.0 collective-permute-done.5.refs_0_.refs_1_
  15.1 0.2 collective-permute-done.4.theirs.refs_1_
  15.3 2.6 %collective-permute-start.8 = (f32[1,2560]{1,0:T(1,128)S(1)}, f32[1,2560]{1,0:T(1,128)S(1)}, u32[]{:S(2)}, u32[]{:S(2)}) collective-permute-start(f32[1,2560]{1,0:T(1,128)S(1)} %merge.1.refs_2_), channel_id=1, source_target_pairs={{0,16},{4,20},{8,24},{12,28},{16,8},{20,12},{24,0},{28,4},{1,17},{... | collective-permute-start | bytes 30728 | tf_op jit(solution)/shard_map/ppermute | solution.py:761
  17.9 1.2 %collective-permute-start.7 = (f32[1,2560]{1,0:T(1,128)S(1)}, f32[1,2560]{1,0:T(1,128)S(1)}, u32[]{:S(2)}, u32[]{:S(2)}) collective-permute-start(f32[1,2560]{1,0:T(1,128)S(1)} %merge.1.refs_2_), channel_id=1, source_target_pairs={{0,24},{4,28},{8,16},{12,20},{16,0},{20,4},{24,8},{28,12},{1,25},{... | collective-permute-start | bytes 30728 | tf_op jit(solution)/shard_map/ppermute | solution.py:761
  19.2 0.3 %collective-permute-start.6 = (f32[1,2560]{1,0:T(1,128)S(1)}, f32[1,2560]{1,0:T(1,128)S(1)}, u32[]{:S(2)}, u32[]{:S(2)}) collective-permute-start(f32[1,2560]{1,0:T(1,128)S(1)} %merge.1.refs_2_), channel_id=1, source_target_pairs={{0,8},{4,12},{8,0},{12,4},{16,24},{20,28},{24,16},{28,20},{1,9},{5... | collective-permute-start | bytes 30728 | tf_op jit(solution)/shard_map/ppermute | solution.py:753
  19.4 0.0 collective-permute-done.9.refs_2_
  19.4 0.0 collective-permute-start.10
  19.4 0.7 %write_depth.1 = f32[128,512]{1,0:T(8,128)} custom-call(f32[512,128]{1,0:T(8,128)S(1)} %get-tuple-element.69.depth), custom_call_target="tpu_custom_call" | custom-call | flops 100000 | bytes 2000000 | tf_op jit(solution)/shard_map/write_depth/pallas_call | solution.py:564
  20.2 0.1 rest_x.1.rest
  20.3 0.3 %collective-permute-done.10.refs_3_ = f32[1,640]{1,0:T(1,128)S(1)} collective-permute-done((f32[1,640]{1,0:T(1,128)S(1)}, f32[1,640]{1,0:T(1,128)S(1)}, u32[]{:S(2)}, u32[]{:S(2)}) %collective-permute-start.10) | collective-permute-done | bytes 2592 | tf_op jit(solution)/shard_map/ppermute | solution.py:753
  20.6 1.0 %solve_y.1 = f32[128,512]{1,0:T(8,128)} custom-call(f32[512,128]{1,0:T(8,128)S(1)} %get-tuple-element.65.iy.inv_ref, f32[512,128]{1,0:T(8,128)S(1)} %get-tuple-element.76.r_ref, f32[3,32,128]{2,1,0:T(8,128)S(1)} %get-tuple-element.66.ty.t_ref, f32[15,32,128]{2,1,0:T(8,128)S(1)} %get-tuple-element.67.wy.w_ref, f32[6,32,128]{2,1,0:T(8,128)S(1)} %get-tuple-element.77.s_ref, ...), custom_call_target="tpu_custom_call" | custom-call | flops 1000000 | bytes 4000000 | tf_op jit(solution)/shard_map/solve_y/pallas_call | solution.py:728
  21.6 0.9 %collective-permute-done.7.refs_4_ = f32[1,2560]{1,0:T(1,128)S(1)} collective-permute-done((f32[1,2560]{1,0:T(1,128)S(1)}, f32[1,2560]{1,0:T(1,128)S(1)}, u32[]{:S(2)}, u32[]{:S(2)}) %collective-permute-start.7) | collective-permute-done | bytes 10272 | tf_op jit(solution)/shard_map/ppermute | solution.py:761
  22.5 0.3 %collective-permute-done.6.refs_3_ = f32[1,2560]{1,0:T(1,128)S(1)} collective-permute-done((f32[1,2560]{1,0:T(1,128)S(1)}, f32[1,2560]{1,0:T(1,128)S(1)}, u32[]{:S(2)}, u32[]{:S(2)}) %collective-permute-start.6) | collective-permute-done | bytes 10272 | tf_op jit(solution)/shard_map/ppermute | solution.py:753
  22.8 0.8 %solve_x.1 = f32[128,512]{1,0:T(8,128)} custom-call(f32[512,128]{1,0:T(8,128)S(1)} %get-tuple-element.70.from_left, f32[512,128]{1,0:T(8,128)S(1)} %get-tuple-element.71.from_right, f32[512,128]{1,0:T(8,128)S(1)} %rest_x.1.rest, f32[1,2560]{1,0:T(1,128)S(1)} %get-tuple-element.74.mine.refs_0_, f32[1,2560]{1,0:T(1,128)S(1)} %collective-permute-done.4.theirs.refs_1_, ...), custom_call_target="tpu_custom_call" | custom-call | flops 1000000 | bytes 4000000 | tf_op jit(solution)/shard_map/solve_x/pallas_call | solution.py:728
  (15 shorter events, 0.0 us)
Async XLA Ops:
  0.6 4.1 %copy-start.4 = (s32[128,512]{1,0:T(8,128)S(1)}, s32[128,512]{1,0:T(8,128)}, u32[]{:S(2)}) copy-start(s32[128,512]{1,0:T(8,128)} %m.3) | copy-start | bytes 786436
  0.6 4.1 %copy-start.3 = (f32[128,512]{1,0:T(8,128)S(1)}, f32[128,512]{1,0:T(8,128)}, u32[]{:S(2)}) copy-start(f32[128,512]{1,0:T(8,128)} %b.3) | copy-start | bytes 786436
  0.7 4.0 %copy-start.2 = (f32[128,512]{1,0:T(8,128)S(1)}, f32[128,512]{1,0:T(8,128)}, u32[]{:S(2)}) copy-start(f32[128,512]{1,0:T(8,128)} %q.3) | copy-start | bytes 786436
  0.7 4.0 %copy-start.1 = (f32[128,512]{1,0:T(8,128)S(1)}, f32[128,512]{1,0:T(8,128)}, u32[]{:S(2)}) copy-start(f32[128,512]{1,0:T(8,128)} %p.3) | copy-start | bytes 786436
  0.7 4.0 %copy-start = (f32[128,512]{1,0:T(8,128)S(1)}, f32[128,512]{1,0:T(8,128)}, u32[]{:S(2)}) copy-start(f32[128,512]{1,0:T(8,128)} %h.5) | copy-start | bytes 786436
  1.7 4.9 %collective-permute-start = (f32[2,8,512]{2,1,0:T(8,128)S(1)}, f32[2,8,512]{2,1,0:T(8,128)S(1)}, u32[]{:S(2)}, u32[]{:S(2)}) collective-permute-start(f32[2,8,512]{2,1,0:T(8,128)S(1)} %pack_x.1._), channel_id=1, source_target_pairs={{0,4},{4,0},{8,12},{12,8},{16,20},{20,16},{24,28},{28,24},{1,5},{5... | collective-permute-start | bytes 98312 | tf_op jit(solution)/shard_map/ppermute | solution.py:753
  4.9 1.3 %collective-permute-start.1 = (f32[8,128]{1,0:T(8,128)S(1)}, f32[8,128]{1,0:T(8,128)S(1)}, u32[]{:S(2)}, u32[]{:S(2)}) collective-permute-start(f32[8,128]{1,0:T(8,128)S(1)} %get-tuple-element.49), channel_id=1, source_target_pairs={{0,1},{1,0},{2,3},{3,2},{4,5},{5,4},{6,7},{7,6},{8,9},{9,8},{10,11... | collective-permute-start | bytes 12296 | tf_op jit(solution)/shard_map/ppermute | solution.py:753
  5.0 5.1 %collective-permute-start.3 = (f32[32,128]{1,0:T(8,128)S(1)}, f32[32,128]{1,0:T(8,128)S(1)}, u32[]{:S(2)}, u32[]{:S(2)}) collective-permute-start(f32[32,128]{1,0:T(8,128)S(1)} %get-tuple-element.51), channel_id=1, source_target_pairs={{0,0},{1,2},{2,1},{3,3},{4,4},{5,6},{6,5},{7,7},{8,8},{9,10},{10,9... | collective-permute-start | bytes 49160 | tf_op jit(solution)/shard_map/ppermute | solution.py:749
  6.6 4.5 %collective-permute-start.2 = (f32[8,512]{1,0:T(8,128)S(1)}, f32[8,512]{1,0:T(8,128)S(1)}, u32[]{:S(2)}, u32[]{:S(2)}) collective-permute-start(f32[8,512]{1,0:T(8,128)S(1)} %second_of.1), channel_id=1, source_target_pairs={{0,8},{4,0},{8,16},{12,4},{16,24},{20,12},{24,28},{28,20},{1,9},{5... | collective-permute-start | bytes 49160 | tf_op jit(solution)/shard_map/ppermute | solution.py:743
  11.5 3.7 %collective-permute-start.4 = (f32[1,2560]{1,0:T(1,128)S(1)}, f32[1,2560]{1,0:T(1,128)S(1)}, u32[]{:S(2)}, u32[]{:S(2)}) collective-permute-start(f32[1,2560]{1,0:T(1,128)S(1)} %get-tuple-element.74.mine.refs_0_), channel_id=1, source_target_pairs={{0,4},{4,0},{8,12},{12,8},{16,20},{20,16},{24,28},{28,24},{1,5},{5... | collective-permute-start | bytes 30728 | tf_op jit(solution)/shard_map/ppermute | solution.py:753
  13.3 1.8 %collective-permute-start.5 = (f32[1,640]{1,0:T(1,128)S(1)}, f32[1,640]{1,0:T(1,128)S(1)}, u32[]{:S(2)}, u32[]{:S(2)}) collective-permute-start(f32[1,640]{1,0:T(1,128)S(1)} %get-tuple-element.75.refs_0_), channel_id=1, source_target_pairs={{0,1},{1,0},{2,3},{3,2},{4,5},{5,4},{6,7},{7,6},{8,9},{9,8},{10,11... | collective-permute-start | bytes 7688 | tf_op jit(solution)/shard_map/ppermute | solution.py:753
  13.9 5.5 %collective-permute-start.9 = (f32[1,2048]{1,0:T(1,128)S(1)}, f32[1,2048]{1,0:T(1,128)S(1)}, u32[]{:S(2)}, u32[]{:S(2)}) collective-permute-start(f32[1,2048]{1,0:T(1,128)S(1)} %get-tuple-element.78), channel_id=1, source_target_pairs={{0,2},{1,3},{2,0},{3,1},{4,6},{5,7},{6,4},{7,5},{8,10},{9,11},{10,... | collective-permute-start | bytes 24584 | tf_op jit(solution)/shard_map/ppermute | solution.py:753
  15.3 6.3 %collective-permute-start.8 = (f32[1,2560]{1,0:T(1,128)S(1)}, f32[1,2560]{1,0:T(1,128)S(1)}, u32[]{:S(2)}, u32[]{:S(2)}) collective-permute-start(f32[1,2560]{1,0:T(1,128)S(1)} %merge.1.refs_2_), channel_id=1, source_target_pairs={{0,16},{4,20},{8,24},{12,28},{16,8},{20,12},{24,0},{28,4},{1,17},{... | collective-permute-start | bytes 30728 | tf_op jit(solution)/shard_map/ppermute | solution.py:761
  17.9 4.6 %collective-permute-start.7 = (f32[1,2560]{1,0:T(1,128)S(1)}, f32[1,2560]{1,0:T(1,128)S(1)}, u32[]{:S(2)}, u32[]{:S(2)}) collective-permute-start(f32[1,2560]{1,0:T(1,128)S(1)} %merge.1.refs_2_), channel_id=1, source_target_pairs={{0,24},{4,28},{8,16},{12,20},{16,0},{20,4},{24,8},{28,12},{1,25},{... | collective-permute-start | bytes 30728 | tf_op jit(solution)/shard_map/ppermute | solution.py:761
  19.2 3.7 %collective-permute-start.6 = (f32[1,2560]{1,0:T(1,128)S(1)}, f32[1,2560]{1,0:T(1,128)S(1)}, u32[]{:S(2)}, u32[]{:S(2)}) collective-permute-start(f32[1,2560]{1,0:T(1,128)S(1)} %merge.1.refs_2_), channel_id=1, source_target_pairs={{0,8},{4,12},{8,0},{12,4},{16,24},{20,28},{24,16},{28,20},{1,9},{5... | collective-permute-start | bytes 30728 | tf_op jit(solution)/shard_map/ppermute | solution.py:753
  19.4 1.2 %collective-permute-start.10 = (f32[1,640]{1,0:T(1,128)S(1)}, f32[1,640]{1,0:T(1,128)S(1)}, u32[]{:S(2)}, u32[]{:S(2)}) collective-permute-start(f32[1,640]{1,0:T(1,128)S(1)} %slice.4), channel_id=1, source_target_pairs={{0,1},{1,0},{2,3},{3,2},{4,5},{5,4},{6,7},{7,6},{8,9},{9,8},{10,11... | collective-permute-start | bytes 7688 | tf_op jit(solution)/shard_map/ppermute | solution.py:753

commit v14 on v13

--- a/solution.py
+++ b/solution.py
@@ -314,7 +314,7 @@
     return lambda k: out[k] if k in out else ref[at(tile, k), :]
 
 
-def tile_fluxes(fields, bed, wet, store, start=0, stop=STEPS):
+def tile_fluxes(fields, bed, wet, store, start=0, stop=STEPS, low_face=None, high_face=None):
     def states(k):
         both = []
         for w in fields:
@@ -322,15 +322,23 @@
             both.append((here, half_slope(here - w(k - 1), w(k + 1) - here)))
         return [w + s for w, s in both], [w - s for w, s in both]
 
-    left, _ = states(start - 1)
-    before = None
+    left, before, first = None, None, None
     for k in range(start - 1, stop):
-        left_next, right = states(k + 1)
-        face = face_flux(left, right, wet(k) * wet(k + 1))
-        left = left_next
+        if k == start - 1 and low_face is not None:
+            face = low_face
+        elif k == stop - 1 and high_face is not None:
+            face = high_face
+        else:
+            if left is None:
+                left, _ = states(k)
+            left_next, right = states(k + 1)
+            face = face_flux(left, right, wet(k) * wet(k + 1))
+            left = left_next
         if k >= start:
             store(k, [a - c for a, c in zip(face, before)], bed(k + 1) - bed(k - 1))
+        first = face if first is None else first
         before = face
+    return first, before
 
 
 def march_source(inv_ref, scale, r_ref, t_ref, w_ref, s_ref, levels):
@@ -410,11 +418,13 @@
     return of_tile
 
 
-def flux_x_inner_kernel(hx, px, qx, bx, mx, depth, push, across):
+def flux_x_inner_kernel(hx, px, qx, bx, mx, depth, push, across, faces):
     store = x_store(hx, px, mx, depth, push, across)
     for tile in range(hx.shape[0] // LANES):
         fields = [extended(v, tile, (), ()) for v in (hx, px, qx, bx, mx)]
-        tile_fluxes(fields[:3], fields[3], fields[4], store(tile), *INNER)
+        ends = tile_fluxes(fields[:3], fields[3], fields[4], store(tile), *INNER)
+        for n, v in enumerate(ends[0] + ends[1]):
+            faces[n, tile * SUB : (tile + 1) * SUB, :] = v
         for k in (*range(INNER[0]), *range(INNER[1], STEPS)):
             for ref in (depth, push, across):
                 ref[at(tile, k), :] = jnp.zeros((SUB, LANES), F32)
@@ -424,9 +434,9 @@
     stack = arrays[0].shape
     return pl.pallas_call(
         flux_x_inner_kernel,
-        out_shape=(shape(*stack),) * 3,
+        out_shape=(shape(*stack),) * 3 + (shape(6, stack[0] // STEPS, LANES),),
         in_specs=[VMEM] * len(arrays),
-        out_specs=(VMEM,) * 3,
+        out_specs=(VMEM,) * 4,
         compiler_params=PARAMS,
         cost_estimate=pl.CostEstimate(flops=4_000_000, bytes_accessed=4_000_000, transcendentals=0),
         name="fluxes_x_inner",
@@ -434,7 +444,7 @@
 
 
 def flux_x_kernel(
-    near, far, hx, px, qx, bx, mx, ix, shear_y, push_in, tx, wx, coef,
+    near, far, hx, px, qx, bx, mx, ix, shear_y, push_in, faces, tx, wx, coef,
     depth, across, rx, sx, ends,
     push,
     *, inv_cx,
@@ -451,8 +461,9 @@
             return extended(ref, tile, lows, highs)
 
         fields, bed, wet = [extend(hx, 0, 2), extend(px, 2, 2), extend(qx, 4, 2)], extend(bx, 6, 1), extend(mx, 7, 1)
-        tile_fluxes(fields, bed, wet, store(tile), 0, INNER[0])
-        tile_fluxes(fields, bed, wet, store(tile), INNER[1], STEPS)
+        known = [faces[n, tile * SUB : (tile + 1) * SUB, :] for n in range(6)]
+        tile_fluxes(fields, bed, wet, store(tile), 0, INNER[0], high_face=known[:3])
+        tile_fluxes(fields, bed, wet, store(tile), INNER[1], STEPS, low_face=known[3:])
         for k in range(STEPS):
             here = at(tile, k)
             inverse = ix[here, :]
@@ -538,15 +549,26 @@
     )(*arrays)
 
 
-def tile_write(tiled, whole, tile, sems):
+PARTS = 2
+
+
+def tile_writes(tiled, whole, tile, sems):
     rows = whole.shape[0]
-    return pltpu.make_async_copy(
-        tiled.at[pl.ds(tile * rows, rows), :], whole.at[:, pl.ds(tile * LANES, LANES)], sems.at[tile]
-    )
+    part = rows // PARTS
+    copies = []
+    for n in range(PARTS):
+        copy = pltpu.make_async_copy(
+            tiled.at[pl.ds(tile * rows + n * part, part), :],
+            whole.at[pl.ds(n * part, part), pl.ds(tile * LANES, LANES)],
+            sems.at[tile, n],
+        )
+        copy.start()
+        copies.append(copy)
+    return copies
 
 
 def write_scratch(cols):
-    return [pltpu.VMEM((cols, LANES), F32), pltpu.SemaphoreType.DMA((cols // LANES,))]
+    return [pltpu.VMEM((cols, LANES), F32), pltpu.SemaphoreType.DMA((cols // LANES, PARTS))]
 
 
 def depth_kernel(depth, out, natural, sems):
@@ -554,8 +576,7 @@
     for tile in range(depth.shape[0] // LANES):
         for k in range(STEPS):
             natural[spread_rows(tile, k), :] = depth[at(tile, k), :]
-        writes.append(tile_write(natural, out, tile, sems))
-        writes[-1].start()
+        writes += tile_writes(natural, out, tile, sems)
     for write in writes:
         write.wait()
 
@@ -695,8 +716,7 @@
             natural[spread_rows(tile, k), :] = (
                 from_left[here, :] * left[:, span] + from_right[here, :] * right[:, span] + rest[here, :]
             )
-        writes.append(tile_write(natural, out, tile, sems))
-        writes[-1].start()
+        writes += tile_writes(natural, out, tile, sems)
     for write in writes:
         write.wait()
 
@@ -718,8 +738,7 @@
         block = turned[tile_span(tile), :].T
         for k in range(STEPS):
             natural[spread_rows(tile, k), :] = block[k * SUB : (k + 1) * SUB, :]
-        writes.append(tile_write(natural, out, tile, sems))
-        writes[-1].start()
+        writes += tile_writes(natural, out, tile, sems)
     for write in writes:
         write.wait()
 
@@ -790,10 +809,10 @@
     hx, hy, ix, iy, tx, wx, ty, wy, coef_x, coef_y, left_x, right_x = prepare_depth(h, inv_cx, inv_cy)
     far_x = hand_on(second_of(near_x, coef_x, near_y), "gx")
     px, py, qx, qy, bx, by, mx, my = prepare_rest(p, q, b, m)
-    depth_inner, push_inner, across_inner = fluxes_x_inner(hx, px, qx, bx, mx)
+    depth_inner, push_inner, across_inner, faces = fluxes_x_inner(hx, px, qx, bx, mx)
     mass_y, shear_y, normal_y = fluxes_y(near_y, far_y, hy, py, qy, by, my)
     depth_outer, across_outer, rx, sx, end_x = fluxes_x(
-        near_x, far_x, hx, px, qx, bx, mx, ix, shear_y, push_inner, tx, wx, coef_x, inv_cx=inv_cx
+        near_x, far_x, hx, px, qx, bx, mx, ix, shear_y, push_inner, faces, tx, wx, coef_x, inv_cx=inv_cx
     )
     depth, ry, sy, end_y, tall_y = join_y(
         depth_inner, across_inner, depth_outer, across_outer, mass_y, mx, normal_y, iy, my, ty, wy, coef_y, inv_cy=inv_cy

time: 23.9 us -> 23.9 us (level)
  no operation moved by 1% of the time
where the time goes in v14:
time: 23.9 us; the launch traced here: 23.6 us
  starting transfers between devices  13.1 us (55%)
  Pallas kernels  7.63 us (32%)
  waiting for transfers between devices  2.01 us (8%)
  between operations  0.81 us (3%)
    ppermute x7, starting transfers between devices, cross(): lax.ppermute(value, axis, [(i, i ^ mask) for i in range(lax.axis_size(axi...  6.5 us
    ppermute x2, starting transfers between devices, crossed(): return lax.ppermute(value, axis, pairs)  3.88 us
    ppermute x1, starting transfers between devices, hand_on(): lax.ppermute(value, axis, [(i, t if 0 <= t < count else i ^ 1) for i, t i...  2.11 us
    pallas_call x2, Pallas kernels, solve(): pl.pallas_call(kernel, out_shape=shape(*block), in_specs=[VMEM] * (len(pi...  1.89 us
    ppermute x7, waiting for transfers between devices, cross(): lax.ppermute(value, axis, [(i, i ^ mask) for i in range(lax.axis_size(axi...  1.15 us
    pallas_call x1, Pallas kernels, pack_x(): pl.pallas_call(pack_x_kernel, out_shape=shape(2, SUB, cols), in_specs=[HB...  0.99 us
    pallas_call x1, Pallas kernels, fluxes_y(): pl.pallas_call(flux_y_kernel, out_shape=(shape(*stack),) * 3, in_specs=[V...  0.97 us
    ppermute x2, waiting for transfers between devices, crossed(): return lax.ppermute(value, axis, pairs)  0.85 us
  transfers between devices with their start and end apart: 11, of which 5 were waited for; matrix products, arithmetic and copies ran while one was open for 0% of the time, Pallas kernels for 23%

profile of v14, /device:TPU:0, one launch (start us, length us, event | category | flops | bytes accessed | tf_op | source)
XLA Modules:
  0.0 23.6 jit_solution(4844796934014228494)
XLA Ops:
  0.7 1.0 %pack_x.1._ = f32[2,8,512]{2,1,0:T(8,128)S(1)} custom-call(f32[128,512]{1,0:T(8,128)} %h.5, f32[128,512]{1,0:T(8,128)} %p.3, f32[128,512]{1,0:T(8,128)} %q.3, f32[128,512]{1,0:T(8,128)} %b.3, s32[128,512]{1,0:T(8,128)} %m.3), custom_call_target="tpu_custom_call" | custom-call | tf_op jit(solution)/shard_map/pack_x/pallas_call | solution.py:78
  1.7 3.0 %collective-permute-start = (f32[2,8,512]{2,1,0:T(8,128)S(1)}, f32[2,8,512]{2,1,0:T(8,128)S(1)}, u32[]{:S(2)}, u32[]{:S(2)}) collective-permute-start(f32[2,8,512]{2,1,0:T(8,128)S(1)} %pack_x.1._), channel_id=1, source_target_pairs={{0,4},{4,0},{8,12},{12,8},{16,20},{20,16},{24,28},{28,24},{1,5},{5... | collective-permute-start | bytes 98312 | tf_op jit(solution)/shard_map/ppermute | solution.py:772
  4.7 0.2 pack_y.1
  4.9 0.0 collective-permute-start.1
  5.0 0.7 %collective-permute-start.3 = (f32[32,128]{1,0:T(8,128)S(1)}, f32[32,128]{1,0:T(8,128)S(1)}, u32[]{:S(2)}, u32[]{:S(2)}) collective-permute-start(f32[32,128]{1,0:T(8,128)S(1)} %get-tuple-element.52), channel_id=1, source_target_pairs={{0,0},{1,2},{2,1},{3,3},{4,4},{5,6},{6,5},{7,7},{8,8},{9,10},{10,9... | collective-permute-start | bytes 49160 | tf_op jit(solution)/shard_map/ppermute | solution.py:768
  5.6 0.5 %prepare_depth.1 = (f32[512,128]{1,0:T(8,128)S(1)}, f32[512,128]{1,0:T(8,128)S(1)}, f32[512,128]{1,0:T(8,128)S(1)}, f32[512,128]{1,0:T(8,128)S(1)}, f32[3,32,128...) custom-call(f32[128,512]{1,0:T(8,128)S(1)} %copy-done), custom_call_target="tpu_custom_call" | custom-call | flops 2000000 | bytes 4000000 | tf_op jit(solution)/shard_map/prepare_depth/pallas_call | solution.py:244
  6.2 0.0 collective-permute-done.1.refs_1_.near
  6.2 0.4 %collective-permute-done.both.near = f32[2,8,512]{2,1,0:T(8,128)S(1)} collective-permute-done((f32[2,8,512]{2,1,0:T(8,128)S(1)}, f32[2,8,512]{2,1,0:T(8,128)S(1)}, u32[]{:S(2)}, u32[]{:S(2)}) %collective-permute-start) | collective-permute-done | bytes 32800 | tf_op jit(solution)/shard_map/ppermute | solution.py:772
  6.6 2.1 %collective-permute-start.2 = (f32[8,512]{1,0:T(8,128)S(1)}, f32[8,512]{1,0:T(8,128)S(1)}, u32[]{:S(2)}, u32[]{:S(2)}) collective-permute-start(f32[8,512]{1,0:T(8,128)S(1)} %second_of.1), channel_id=1, source_target_pairs={{0,8},{4,0},{8,16},{12,4},{16,24},{20,12},{24,28},{28,20},{1,9},{5... | collective-permute-start | bytes 49160 | tf_op jit(solution)/shard_map/ppermute | solution.py:762
  8.7 0.8 %prepare_rest.1 = (f32[512,128]{1,0:T(8,128)S(1)}, f32[512,128]{1,0:T(8,128)S(1)}, f32[512,128]{1,0:T(8,128)S(1)}, f32[512,128]{1,0:T(8,128)S(1)}, f32[512,128]{...) custom-call(f32[128,512]{1,0:T(8,128)S(1)} %copy-done.1, ...), custom_call_target="tpu_custom_call" | custom-call | flops 2000000 | bytes 6000000 | tf_op jit(solution)/shard_map/prepare_rest/pallas_call | solution.py:264
  9.5 0.6 %fluxes_x_inner.1 = (f32[512,128]{1,0:T(8,128)S(1)}, f32[512,128]{1,0:T(8,128)S(1)}, f32[512,128]{1,0:T(8,128)S(1)}, f32[6,32,128]{2,1,0:T(8,128)S(1)}) custom-call(f32[512,128]{1,0:T(8,128)S(1)} %get-tuple-element.42.hx, f32[512,128]{1,0:T(8,128)S(1)} %get-tuple-element.43.px, f32[512,128]{1,0:T(8,128)S(1)} %get-tuple-element.44.qx, ...), custom_call_target="tpu_custom_call" | custom-call | flops 4000000 | bytes 4000000 | tf_op jit(solution)/shard_map/fluxes_x_inner/pallas_call | solution.py:435
  10.1 0.0 collective-permute-done.3.far
  10.1 1.0 %fluxes_y.1 = (f32[512,128]{1,0:T(8,128)S(1)}, f32[512,128]{1,0:T(8,128)S(1)}, f32[512,128]{1,0:T(8,128)S(1)}) custom-call(f32[8,128]{1,0:T(8,128)S(1)} %collective-permute-done.1.refs_1_.near, f32[32,128]{1,0:T(8,128)S(1)} %collective-permute-done.3.far, f32[512,128]{1,0:T(8,128)S(1)} %get-tuple-element.53.hy, f32[512,128]{1,0:T(8,128)S(1)} %get-tuple-element.54.py, ...), custom_call_target="tpu_custom_call" | custom-call | flops 4000000 | bytes 4000000 | tf_op jit(solution)/shard_map/fluxes_y/pallas_call | solution.py:391
  11.1 0.0 collective-permute-done.2.far
  11.1 0.4 %fluxes_x.1 = (f32[512,128]{1,0:T(8,128)S(1)}, f32[512,128]{1,0:T(8,128)S(1)}, f32[512,128]{1,0:T(8,128)S(1)}, f32[4,32,128]{2,1,0:T(8,128)S(1)}, f32[1,2560]{1,0:T(1,128)S(1)}) custom-call(f32[2,8,512]{2,1,0:T(8,128)S(1)} %collective-permute-done.both.near, f32[8,512]{1,0:T(8,128)S(1)} %collective-permute-done.2.far, f32[512,128]{1,0:T(8,128)S(1)} %get-tuple-element.42.hx, ...), custom_call_target="tpu_custom_call" | custom-call | tf_op jit(solution)/shard_map/fluxes_x/pallas_call | solution.py:491
  11.5 1.4 %collective-permute-start.4 = (f32[1,2560]{1,0:T(1,128)S(1)}, f32[1,2560]{1,0:T(1,128)S(1)}, u32[]{:S(2)}, u32[]{:S(2)}) collective-permute-start(f32[1,2560]{1,0:T(1,128)S(1)} %get-tuple-element.76.mine.refs_0_), channel_id=1, source_target_pairs={{0,4},{4,0},{8,12},{12,8},{16,20},{20,16},{24,28},{28,24},{1,5},{5... | collective-permute-start | bytes 30728 | tf_op jit(solution)/shard_map/ppermute | solution.py:772
  12.9 0.4 %join_y.1 = (f32[512,128]{1,0:T(8,128)S(1)}, f32[512,128]{1,0:T(8,128)S(1)}, f32[6,32,128]{2,1,0:T(8,128)S(1)}, f32[1,640]{1,0:T(1,128)S(1)}, f32[1,2048]{1,0:T(1,128)S(1)}) custom-call(f32[512,128]{1,0:T(8,128)S(1)} %get-tuple-element.47.depth_inner, f32[512,128]{1,0:T(8,128)S(1)} %get-tuple-element.48.across_inner, ...), custom_call_target="tpu_custom_call" | custom-call | flops 2000000 | bytes 2000000 | tf_op jit(solution)/shard_map/join_y/pallas_call | solution.py:540
  13.2 0.7 %collective-permute-start.5 = (f32[1,640]{1,0:T(1,128)S(1)}, f32[1,640]{1,0:T(1,128)S(1)}, u32[]{:S(2)}, u32[]{:S(2)}) collective-permute-start(f32[1,640]{1,0:T(1,128)S(1)} %get-tuple-element.77.refs_0_), channel_id=1, source_target_pairs={{0,1},{1,0},{2,3},{3,2},{4,5},{5,4},{6,7},{7,6},{8,9},{9,8},{10,11... | collective-permute-start | bytes 7688 | tf_op jit(solution)/shard_map/ppermute | solution.py:772
  13.9 1.1 %collective-permute-start.9 = (f32[1,2048]{1,0:T(1,128)S(1)}, f32[1,2048]{1,0:T(1,128)S(1)}, u32[]{:S(2)}, u32[]{:S(2)}) collective-permute-start(f32[1,2048]{1,0:T(1,128)S(1)} %get-tuple-element.80), channel_id=1, source_target_pairs={{0,2},{1,3},{2,0},{3,1},{4,6},{5,7},{6,4},{7,5},{8,10},{9,11},{10,... | collective-permute-start | bytes 24584 | tf_op jit(solution)/shard_map/ppermute | solution.py:772
  15.0 0.0 collective-permute-done.5.refs_0_.refs_1_
  15.0 0.2 collective-permute-done.4.theirs.refs_1_
  15.2 2.6 %collective-permute-start.8 = (f32[1,2560]{1,0:T(1,128)S(1)}, f32[1,2560]{1,0:T(1,128)S(1)}, u32[]{:S(2)}, u32[]{:S(2)}) collective-permute-start(f32[1,2560]{1,0:T(1,128)S(1)} %merge.1.refs_2_), channel_id=1, source_target_pairs={{0,16},{4,20},{8,24},{12,28},{16,8},{20,12},{24,0},{28,4},{1,17},{... | collective-permute-start | bytes 30728 | tf_op jit(solution)/shard_map/ppermute | solution.py:780
  17.9 1.2 %collective-permute-start.7 = (f32[1,2560]{1,0:T(1,128)S(1)}, f32[1,2560]{1,0:T(1,128)S(1)}, u32[]{:S(2)}, u32[]{:S(2)}) collective-permute-start(f32[1,2560]{1,0:T(1,128)S(1)} %merge.1.refs_2_), channel_id=1, source_target_pairs={{0,24},{4,28},{8,16},{12,20},{16,0},{20,4},{24,8},{28,12},{1,25},{... | collective-permute-start | bytes 30728 | tf_op jit(solution)/shard_map/ppermute | solution.py:780
  19.1 0.3 %collective-permute-start.6 = (f32[1,2560]{1,0:T(1,128)S(1)}, f32[1,2560]{1,0:T(1,128)S(1)}, u32[]{:S(2)}, u32[]{:S(2)}) collective-permute-start(f32[1,2560]{1,0:T(1,128)S(1)} %merge.1.refs_2_), channel_id=1, source_target_pairs={{0,8},{4,12},{8,0},{12,4},{16,24},{20,28},{24,16},{28,20},{1,9},{5... | collective-permute-start | bytes 30728 | tf_op jit(solution)/shard_map/ppermute | solution.py:772
  19.4 0.8 %write_depth.1 = f32[128,512]{1,0:T(8,128)} custom-call(f32[512,128]{1,0:T(8,128)S(1)} %get-tuple-element.71.depth), custom_call_target="tpu_custom_call" | custom-call | flops 100000 | bytes 2000000 | tf_op jit(solution)/shard_map/write_depth/pallas_call | solution.py:585
  20.2 0.1 rest_x.1.rest
  20.3 0.2 %collective-permute-done.10.refs_3_ = f32[1,640]{1,0:T(1,128)S(1)} collective-permute-done((f32[1,640]{1,0:T(1,128)S(1)}, f32[1,640]{1,0:T(1,128)S(1)}, u32[]{:S(2)}, u32[]{:S(2)}) %collective-permute-start.10) | collective-permute-done | bytes 2592 | tf_op jit(solution)/shard_map/ppermute | solution.py:772
  20.5 1.0 %solve_y.1 = f32[128,512]{1,0:T(8,128)} custom-call(f32[512,128]{1,0:T(8,128)S(1)} %get-tuple-element.67.iy.inv_ref, f32[512,128]{1,0:T(8,128)S(1)} %get-tuple-element.78.r_ref, f32[3,32,128]{2,1,0:T(8,128)S(1)} %get-tuple-element.68.ty.t_ref, f32[15,32,128]{2,1,0:T(8,128)S(1)} %get-tuple-element.69.wy.w_ref, f32[6,32,128]{2,1,0:T(8,128)S(1)} %get-tuple-element.79.s_ref, ...), custom_call_target="tpu_custom_call" | custom-call | flops 1000000 | bytes 4000000 | tf_op jit(solution)/shard_map/solve_y/pallas_call | solution.py:747
  21.6 0.0 collective-permute-done.8.refs_5_
  21.6 0.8 %collective-permute-done.7.refs_4_ = f32[1,2560]{1,0:T(1,128)S(1)} collective-permute-done((f32[1,2560]{1,0:T(1,128)S(1)}, f32[1,2560]{1,0:T(1,128)S(1)}, u32[]{:S(2)}, u32[]{:S(2)}) %collective-permute-start.7) | collective-permute-done | bytes 10272 | tf_op jit(solution)/shard_map/ppermute | solution.py:780
  22.4 0.3 %collective-permute-done.6.refs_3_ = f32[1,2560]{1,0:T(1,128)S(1)} collective-permute-done((f32[1,2560]{1,0:T(1,128)S(1)}, f32[1,2560]{1,0:T(1,128)S(1)}, u32[]{:S(2)}, u32[]{:S(2)}) %collective-permute-start.6) | collective-permute-done | bytes 10272 | tf_op jit(solution)/shard_map/ppermute | solution.py:772
  22.8 0.8 %solve_x.1 = f32[128,512]{1,0:T(8,128)} custom-call(f32[512,128]{1,0:T(8,128)S(1)} %get-tuple-element.72.from_left, f32[512,128]{1,0:T(8,128)S(1)} %get-tuple-element.73.from_right, f32[512,128]{1,0:T(8,128)S(1)} %rest_x.1.rest, f32[1,2560]{1,0:T(1,128)S(1)} %get-tuple-element.76.mine.refs_0_, f32[1,2560]{1,0:T(1,128)S(1)} %collective-permute-done.4.theirs.refs_1_, ...), custom_call_target="tpu_custom_call" | custom-call | flops 1000000 | bytes 4000000 | tf_op jit(solution)/shard_map/solve_x/pallas_call | solution.py:747
  (15 shorter events, 0.0 us)
Async XLA Ops:
  0.6 4.1 %copy-start.4 = (s32[128,512]{1,0:T(8,128)S(1)}, s32[128,512]{1,0:T(8,128)}, u32[]{:S(2)}) copy-start(s32[128,512]{1,0:T(8,128)} %m.3) | copy-start | bytes 786436
  0.6 4.1 %copy-start.3 = (f32[128,512]{1,0:T(8,128)S(1)}, f32[128,512]{1,0:T(8,128)}, u32[]{:S(2)}) copy-start(f32[128,512]{1,0:T(8,128)} %b.3) | copy-start | bytes 786436
  0.7 4.0 %copy-start.2 = (f32[128,512]{1,0:T(8,128)S(1)}, f32[128,512]{1,0:T(8,128)}, u32[]{:S(2)}) copy-start(f32[128,512]{1,0:T(8,128)} %q.3) | copy-start | bytes 786436
  0.7 4.0 %copy-start.1 = (f32[128,512]{1,0:T(8,128)S(1)}, f32[128,512]{1,0:T(8,128)}, u32[]{:S(2)}) copy-start(f32[128,512]{1,0:T(8,128)} %p.3) | copy-start | bytes 786436
  0.7 4.0 %copy-start = (f32[128,512]{1,0:T(8,128)S(1)}, f32[128,512]{1,0:T(8,128)}, u32[]{:S(2)}) copy-start(f32[128,512]{1,0:T(8,128)} %h.5) | copy-start | bytes 786436
  1.7 4.9 %collective-permute-start = (f32[2,8,512]{2,1,0:T(8,128)S(1)}, f32[2,8,512]{2,1,0:T(8,128)S(1)}, u32[]{:S(2)}, u32[]{:S(2)}) collective-permute-start(f32[2,8,512]{2,1,0:T(8,128)S(1)} %pack_x.1._), channel_id=1, source_target_pairs={{0,4},{4,0},{8,12},{12,8},{16,20},{20,16},{24,28},{28,24},{1,5},{5... | collective-permute-start | bytes 98312 | tf_op jit(solution)/shard_map/ppermute | solution.py:772
  4.9 1.3 %collective-permute-start.1 = (f32[8,128]{1,0:T(8,128)S(1)}, f32[8,128]{1,0:T(8,128)S(1)}, u32[]{:S(2)}, u32[]{:S(2)}) collective-permute-start(f32[8,128]{1,0:T(8,128)S(1)} %get-tuple-element.50), channel_id=1, source_target_pairs={{0,1},{1,0},{2,3},{3,2},{4,5},{5,4},{6,7},{7,6},{8,9},{9,8},{10,11... | collective-permute-start | bytes 12296 | tf_op jit(solution)/shard_map/ppermute | solution.py:772
  5.0 5.1 %collective-permute-start.3 = (f32[32,128]{1,0:T(8,128)S(1)}, f32[32,128]{1,0:T(8,128)S(1)}, u32[]{:S(2)}, u32[]{:S(2)}) collective-permute-start(f32[32,128]{1,0:T(8,128)S(1)} %get-tuple-element.52), channel_id=1, source_target_pairs={{0,0},{1,2},{2,1},{3,3},{4,4},{5,6},{6,5},{7,7},{8,8},{9,10},{10,9... | collective-permute-start | bytes 49160 | tf_op jit(solution)/shard_map/ppermute | solution.py:768
  6.6 4.5 %collective-permute-start.2 = (f32[8,512]{1,0:T(8,128)S(1)}, f32[8,512]{1,0:T(8,128)S(1)}, u32[]{:S(2)}, u32[]{:S(2)}) collective-permute-start(f32[8,512]{1,0:T(8,128)S(1)} %second_of.1), channel_id=1, source_target_pairs={{0,8},{4,0},{8,16},{12,4},{16,24},{20,12},{24,28},{28,20},{1,9},{5... | collective-permute-start | bytes 49160 | tf_op jit(solution)/shard_map/ppermute | solution.py:762
  11.5 3.7 %collective-permute-start.4 = (f32[1,2560]{1,0:T(1,128)S(1)}, f32[1,2560]{1,0:T(1,128)S(1)}, u32[]{:S(2)}, u32[]{:S(2)}) collective-permute-start(f32[1,2560]{1,0:T(1,128)S(1)} %get-tuple-element.76.mine.refs_0_), channel_id=1, source_target_pairs={{0,4},{4,0},{8,12},{12,8},{16,20},{20,16},{24,28},{28,24},{1,5},{5... | collective-permute-start | bytes 30728 | tf_op jit(solution)/shard_map/ppermute | solution.py:772
  13.2 1.8 %collective-permute-start.5 = (f32[1,640]{1,0:T(1,128)S(1)}, f32[1,640]{1,0:T(1,128)S(1)}, u32[]{:S(2)}, u32[]{:S(2)}) collective-permute-start(f32[1,640]{1,0:T(1,128)S(1)} %get-tuple-element.77.refs_0_), channel_id=1, source_target_pairs={{0,1},{1,0},{2,3},{3,2},{4,5},{5,4},{6,7},{7,6},{8,9},{9,8},{10,11... | collective-permute-start | bytes 7688 | tf_op jit(solution)/shard_map/ppermute | solution.py:772
  13.9 5.5 %collective-permute-start.9 = (f32[1,2048]{1,0:T(1,128)S(1)}, f32[1,2048]{1,0:T(1,128)S(1)}, u32[]{:S(2)}, u32[]{:S(2)}) collective-permute-start(f32[1,2048]{1,0:T(1,128)S(1)} %get-tuple-element.80), channel_id=1, source_target_pairs={{0,2},{1,3},{2,0},{3,1},{4,6},{5,7},{6,4},{7,5},{8,10},{9,11},{10,... | collective-permute-start | bytes 24584 | tf_op jit(solution)/shard_map/ppermute | solution.py:772
  15.2 6.4 %collective-permute-start.8 = (f32[1,2560]{1,0:T(1,128)S(1)}, f32[1,2560]{1,0:T(1,128)S(1)}, u32[]{:S(2)}, u32[]{:S(2)}) collective-permute-start(f32[1,2560]{1,0:T(1,128)S(1)} %merge.1.refs_2_), channel_id=1, source_target_pairs={{0,16},{4,20},{8,24},{12,28},{16,8},{20,12},{24,0},{28,4},{1,17},{... | collective-permute-start | bytes 30728 | tf_op jit(solution)/shard_map/ppermute | solution.py:780
  17.9 4.6 %collective-permute-start.7 = (f32[1,2560]{1,0:T(1,128)S(1)}, f32[1,2560]{1,0:T(1,128)S(1)}, u32[]{:S(2)}, u32[]{:S(2)}) collective-permute-start(f32[1,2560]{1,0:T(1,128)S(1)} %merge.1.refs_2_), channel_id=1, source_target_pairs={{0,24},{4,28},{8,16},{12,20},{16,0},{20,4},{24,8},{28,12},{1,25},{... | collective-permute-start | bytes 30728 | tf_op jit(solution)/shard_map/ppermute | solution.py:780
  19.1 3.7 %collective-permute-start.6 = (f32[1,2560]{1,0:T(1,128)S(1)}, f32[1,2560]{1,0:T(1,128)S(1)}, u32[]{:S(2)}, u32[]{:S(2)}) collective-permute-start(f32[1,2560]{1,0:T(1,128)S(1)} %merge.1.refs_2_), channel_id=1, source_target_pairs={{0,8},{4,12},{8,0},{12,4},{16,24},{20,28},{24,16},{28,20},{1,9},{5... | collective-permute-start | bytes 30728 | tf_op jit(solution)/shard_map/ppermute | solution.py:772
  19.4 1.2 %collective-permute-start.10 = (f32[1,640]{1,0:T(1,128)S(1)}, f32[1,640]{1,0:T(1,128)S(1)}, u32[]{:S(2)}, u32[]{:S(2)}) collective-permute-start(f32[1,640]{1,0:T(1,128)S(1)} %slice.4), channel_id=1, source_target_pairs={{0,1},{1,0},{2,3},{3,2},{4,5},{5,4},{6,7},{7,6},{8,9},{9,8},{10,11... | collective-permute-start | bytes 7688 | tf_op jit(solution)/shard_map/ppermute | solution.py:772

commit v15 on v14

--- a/solution.py
+++ b/solution.py
@@ -549,7 +549,7 @@
     )(*arrays)
 
 
-PARTS = 2
+PARTS = 1
 
 
 def tile_writes(tiled, whole, tile, sems):
@@ -624,20 +624,33 @@
     )(mine, theirs, *beside)
 
 
-def line_ends(axis, refs, is_crossed=False):
+ROUTES = ((1, 3, 0, 2), (2, 1, 3, 0), (3, 0, 2, 1), (0, 2, 1, 3))
+
+
+def by_distance(place, received):
+    chosen = []
+    for mask in (1, 2, 3):
+        came = [next(n for n, route in enumerate(ROUTES) if route[at_place ^ mask] == at_place) for at_place in range(4)]
+        value = received[came[0]]
+        for at_place in range(1, 4):
+            other = received[came[at_place]]
+            value = tuple(jnp.where(place == at_place, b, a) for a, b in zip(value, other))
+        chosen.append(value)
+    return chosen
+
+
+def line_ends(axis, refs, is_routed=False):
     steps = []
     parts = [rows_of(ref, refs[0].shape[1] // 5) for ref in refs]
+    if is_routed:
+        place = (lax.axis_index(axis) >> (len(parts) - 5) // 2) & 3
+        parts = parts[:-4] + by_distance(place, parts[:-5:-1])
     stage = 0
     while len(parts) > 4:
         is_low, (_, weights) = ordered(axis, stage, *parts[:2])
         steps.append((is_low, weights))
         parts = parts[2:]
         stage += 1
-    if is_crossed:
-        lower = (lax.axis_index(axis) >> (stage + 1)) % 2 == 0
-        both = list(zip(*parts[2:]))
-        parts[2] = tuple(jnp.where(lower, a, b) for a, b in both)
-        parts[3] = tuple(jnp.where(lower, b, a) for a, b in both)
     is_low, (own, weights) = ordered(axis, stage, *parts[:2])
     steps.append((is_low, weights))
     _, (other, _) = ordered(axis, stage, *parts[2:])
@@ -772,11 +785,11 @@
     return lax.ppermute(value, axis, [(i, i ^ mask) for i in range(lax.axis_size(axis))])
 
 
-def crossed(value, axis, stage, half):
+def routed(value, axis, stage, route):
     pairs = []
     for i in range(lax.axis_size(axis)):
-        upper = (i >> (stage + 1)) & 1
-        pairs.append((i, i ^ ((2 if upper == half else 3) << stage)))
+        place = (i >> stage) & 3
+        pairs.append((i, i + ((route[place] - place) << stage)))
     return lax.ppermute(value, axis, pairs)
 
 
@@ -792,8 +805,7 @@
         second = cross(mine if tall is None else tall, axis, 2 << last)
         both = cross(second[:, 0 : mine.shape[1]], axis, 1 << last)
     else:
-        first = cross(mine, axis, 1 << last)
-        second, both = (crossed(mine, axis, last, n) for n in (1, 0))
+        return parts + [mine] + [routed(mine, axis, last, route) for route in reversed(ROUTES)]
     return parts + [mine, first, second, both]
 
 

time: 23.9 us -> 28.7 us (1.20)
  starting transfers between devices: 13.1 us -> 19 us
  waiting for transfers between devices: 2.01 us -> 0.86 us
    ppermute x2 -> x4, starting transfers between devices: 3.88 us -> 9.92 us  [routed(): return lax.ppermute(value, axis, pairs)]
    ppermute x2 -> x4, waiting for transfers between devices: 0.85 us -> 0.01 us  [routed(): return lax.ppermute(value, axis, pairs)]
    ppermute x7 -> x6, waiting for transfers between devices: 1.15 us -> 0.84 us  [cross(): lax.ppermute(value, axis, [(i, i ^ mask) for i in range(lax.axis_size(axi...]
    ppermute x7 -> x6, starting transfers between devices: 6.5 us -> 6.31 us  [cross(): lax.ppermute(value, axis, [(i, i ^ mask) for i in range(lax.axis_size(axi...]
  transfers between devices with their start and end apart: 11 -> 12, of which waited for: 5 -> 3; matrix products, arithmetic and copies ran while one was open for 0% -> 0% of each run, Pallas kernels for 23% -> 19%
where the time goes in v15:
time: 28.7 us; the launch traced here: 28.3 us
  starting transfers between devices  19 us (66%)
  Pallas kernels  7.54 us (26%)
  between operations  0.87 us (3%)
  waiting for transfers between devices  0.86 us (3%)
    ppermute x4, starting transfers between devices, routed(): return lax.ppermute(value, axis, pairs)  9.92 us
    ppermute x6, starting transfers between devices, cross(): lax.ppermute(value, axis, [(i, i ^ mask) for i in range(lax.axis_size(axi...  6.31 us
    ppermute x1, starting transfers between devices, hand_on(): lax.ppermute(value, axis, [(i, t if 0 <= t < count else i ^ 1) for i, t i...  2.11 us
    pallas_call x2, Pallas kernels, solve(): pl.pallas_call(kernel, out_shape=shape(*block), in_specs=[VMEM] * (len(pi...  1.84 us
    pallas_call x1, Pallas kernels, pack_x(): pl.pallas_call(pack_x_kernel, out_shape=shape(2, SUB, cols), in_specs=[HB...  0.99 us
    pallas_call x1, Pallas kernels, fluxes_y(): pl.pallas_call(flux_y_kernel, out_shape=(shape(*stack),) * 3, in_specs=[V...  0.97 us
    ppermute x6, waiting for transfers between devices, cross(): lax.ppermute(value, axis, [(i, i ^ mask) for i in range(lax.axis_size(axi...  0.84 us
    pallas_call x1, Pallas kernels, prepare_rest(): pl.pallas_call(prepare_rest_kernel, out_shape=(shape(*stack),) * 8, in_sp...  0.76 us
  transfers between devices with their start and end apart: 12, of which 3 were waited for; matrix products, arithmetic and copies ran while one was open for 0% of the time, Pallas kernels for 19%

profile of v15, /device:TPU:0, one launch (start us, length us, event | category | flops | bytes accessed | tf_op | source)
XLA Modules:
  0.0 28.3 jit_solution(7807336207553340928)
XLA Ops:
  0.7 1.0 %pack_x.1._ = f32[2,8,512]{2,1,0:T(8,128)S(1)} custom-call(f32[128,512]{1,0:T(8,128)} %h.5, f32[128,512]{1,0:T(8,128)} %p.3, f32[128,512]{1,0:T(8,128)} %q.3, f32[128,512]{1,0:T(8,128)} %b.3, s32[128,512]{1,0:T(8,128)} %m.3), custom_call_target="tpu_custom_call" | custom-call | tf_op jit(solution)/shard_map/pack_x/pallas_call | solution.py:78
  1.7 3.0 %collective-permute-start = (f32[2,8,512]{2,1,0:T(8,128)S(1)}, f32[2,8,512]{2,1,0:T(8,128)S(1)}, u32[]{:S(2)}, u32[]{:S(2)}) collective-permute-start(f32[2,8,512]{2,1,0:T(8,128)S(1)} %pack_x.1._), channel_id=1, source_target_pairs={{0,4},{4,0},{8,12},{12,8},{16,20},{20,16},{24,28},{28,24},{1,5},{5... | collective-permute-start | bytes 98312 | tf_op jit(solution)/shard_map/ppermute | solution.py:785
  4.7 0.2 pack_y.1
  4.9 0.0 collective-permute-start.1
  5.0 0.7 %collective-permute-start.3 = (f32[32,128]{1,0:T(8,128)S(1)}, f32[32,128]{1,0:T(8,128)S(1)}, u32[]{:S(2)}, u32[]{:S(2)}) collective-permute-start(f32[32,128]{1,0:T(8,128)S(1)} %get-tuple-element.52), channel_id=1, source_target_pairs={{0,0},{1,2},{2,1},{3,3},{4,4},{5,6},{6,5},{7,7},{8,8},{9,10},{10,9... | collective-permute-start | bytes 49160 | tf_op jit(solution)/shard_map/ppermute | solution.py:781
  5.6 0.5 %prepare_depth.1 = (f32[512,128]{1,0:T(8,128)S(1)}, f32[512,128]{1,0:T(8,128)S(1)}, f32[512,128]{1,0:T(8,128)S(1)}, f32[512,128]{1,0:T(8,128)S(1)}, f32[3,32,128...) custom-call(f32[128,512]{1,0:T(8,128)S(1)} %copy-done), custom_call_target="tpu_custom_call" | custom-call | flops 2000000 | bytes 4000000 | tf_op jit(solution)/shard_map/prepare_depth/pallas_call | solution.py:244
  6.2 0.0 collective-permute-done.1.refs_1_.near
  6.2 0.4 %collective-permute-done.both.near = f32[2,8,512]{2,1,0:T(8,128)S(1)} collective-permute-done((f32[2,8,512]{2,1,0:T(8,128)S(1)}, f32[2,8,512]{2,1,0:T(8,128)S(1)}, u32[]{:S(2)}, u32[]{:S(2)}) %collective-permute-start) | collective-permute-done | bytes 32800 | tf_op jit(solution)/shard_map/ppermute | solution.py:785
  6.6 2.1 %collective-permute-start.2 = (f32[8,512]{1,0:T(8,128)S(1)}, f32[8,512]{1,0:T(8,128)S(1)}, u32[]{:S(2)}, u32[]{:S(2)}) collective-permute-start(f32[8,512]{1,0:T(8,128)S(1)} %second_of.1), channel_id=1, source_target_pairs={{0,8},{4,0},{8,16},{12,4},{16,24},{20,12},{24,28},{28,20},{1,9},{5... | collective-permute-start | bytes 49160 | tf_op jit(solution)/shard_map/ppermute | solution.py:775
  8.7 0.8 %prepare_rest.1 = (f32[512,128]{1,0:T(8,128)S(1)}, f32[512,128]{1,0:T(8,128)S(1)}, f32[512,128]{1,0:T(8,128)S(1)}, f32[512,128]{1,0:T(8,128)S(1)}, f32[512,128]{...) custom-call(f32[128,512]{1,0:T(8,128)S(1)} %copy-done.1, ...), custom_call_target="tpu_custom_call" | custom-call | flops 2000000 | bytes 6000000 | tf_op jit(solution)/shard_map/prepare_rest/pallas_call | solution.py:264
  9.5 0.6 %fluxes_x_inner.1 = (f32[512,128]{1,0:T(8,128)S(1)}, f32[512,128]{1,0:T(8,128)S(1)}, f32[512,128]{1,0:T(8,128)S(1)}, f32[6,32,128]{2,1,0:T(8,128)S(1)}) custom-call(f32[512,128]{1,0:T(8,128)S(1)} %get-tuple-element.42.hx, f32[512,128]{1,0:T(8,128)S(1)} %get-tuple-element.43.px, f32[512,128]{1,0:T(8,128)S(1)} %get-tuple-element.44.qx, ...), custom_call_target="tpu_custom_call" | custom-call | flops 4000000 | bytes 4000000 | tf_op jit(solution)/shard_map/fluxes_x_inner/pallas_call | solution.py:435
  10.1 0.0 collective-permute-done.3.far
  10.1 1.0 %fluxes_y.1 = (f32[512,128]{1,0:T(8,128)S(1)}, f32[512,128]{1,0:T(8,128)S(1)}, f32[512,128]{1,0:T(8,128)S(1)}) custom-call(f32[8,128]{1,0:T(8,128)S(1)} %collective-permute-done.1.refs_1_.near, f32[32,128]{1,0:T(8,128)S(1)} %collective-permute-done.3.far, f32[512,128]{1,0:T(8,128)S(1)} %get-tuple-element.53.hy, f32[512,128]{1,0:T(8,128)S(1)} %get-tuple-element.54.py, ...), custom_call_target="tpu_custom_call" | custom-call | flops 4000000 | bytes 4000000 | tf_op jit(solution)/shard_map/fluxes_y/pallas_call | solution.py:391
  11.1 0.4 %fluxes_x.1 = (f32[512,128]{1,0:T(8,128)S(1)}, f32[512,128]{1,0:T(8,128)S(1)}, f32[512,128]{1,0:T(8,128)S(1)}, f32[4,32,128]{2,1,0:T(8,128)S(1)}, f32[1,2560]{1,0:T(1,128)S(1)}) custom-call(f32[2,8,512]{2,1,0:T(8,128)S(1)} %collective-permute-done.both.near, f32[8,512]{1,0:T(8,128)S(1)} %collective-permute-done.2.far, f32[512,128]{1,0:T(8,128)S(1)} %get-tuple-element.42.hx, ...), custom_call_target="tpu_custom_call" | custom-call | tf_op jit(solution)/shard_map/fluxes_x/pallas_call | solution.py:491
  11.5 1.4 %collective-permute-start.4 = (f32[1,2560]{1,0:T(1,128)S(1)}, f32[1,2560]{1,0:T(1,128)S(1)}, u32[]{:S(2)}, u32[]{:S(2)}) collective-permute-start(f32[1,2560]{1,0:T(1,128)S(1)} %get-tuple-element.76.mine.refs_0_), channel_id=1, source_target_pairs={{0,4},{4,0},{8,12},{12,8},{16,20},{20,16},{24,28},{28,24},{1,5},{5... | collective-permute-start | bytes 30728 | tf_op jit(solution)/shard_map/ppermute | solution.py:785
  12.9 0.4 %join_y.1 = (f32[512,128]{1,0:T(8,128)S(1)}, f32[512,128]{1,0:T(8,128)S(1)}, f32[6,32,128]{2,1,0:T(8,128)S(1)}, f32[1,640]{1,0:T(1,128)S(1)}, f32[1,2048]{1,0:T(1,128)S(1)}) custom-call(f32[512,128]{1,0:T(8,128)S(1)} %get-tuple-element.47.depth_inner, f32[512,128]{1,0:T(8,128)S(1)} %get-tuple-element.48.across_inner, ...), custom_call_target="tpu_custom_call" | custom-call | flops 2000000 | bytes 2000000 | tf_op jit(solution)/shard_map/join_y/pallas_call | solution.py:540
  13.2 0.7 %collective-permute-start.5 = (f32[1,640]{1,0:T(1,128)S(1)}, f32[1,640]{1,0:T(1,128)S(1)}, u32[]{:S(2)}, u32[]{:S(2)}) collective-permute-start(f32[1,640]{1,0:T(1,128)S(1)} %get-tuple-element.77.refs_0_), channel_id=1, source_target_pairs={{0,1},{1,0},{2,3},{3,2},{4,5},{5,4},{6,7},{7,6},{8,9},{9,8},{10,11... | collective-permute-start | bytes 7688 | tf_op jit(solution)/shard_map/ppermute | solution.py:785
  13.9 1.1 %collective-permute-start.10 = (f32[1,2048]{1,0:T(1,128)S(1)}, f32[1,2048]{1,0:T(1,128)S(1)}, u32[]{:S(2)}, u32[]{:S(2)}) collective-permute-start(f32[1,2048]{1,0:T(1,128)S(1)} %get-tuple-element.80), channel_id=1, source_target_pairs={{0,2},{1,3},{2,0},{3,1},{4,6},{5,7},{6,4},{7,5},{8,10},{9,11},{10,... | collective-permute-start | bytes 24584 | tf_op jit(solution)/shard_map/ppermute | solution.py:785
  15.0 0.2 collective-permute-done.4.theirs.refs_1_
  15.2 1.6 %collective-permute-start.9 = (f32[1,2560]{1,0:T(1,128)S(1)}, f32[1,2560]{1,0:T(1,128)S(1)}, u32[]{:S(2)}, u32[]{:S(2)}) collective-permute-start(f32[1,2560]{1,0:T(1,128)S(1)} %merge.1.refs_2_), channel_id=1, source_target_pairs={{0,8},{4,12},{8,24},{12,28},{16,0},{20,4},{24,16},{28,20},{1,9},{5... | collective-permute-start | bytes 30728 | tf_op jit(solution)/shard_map/ppermute | solution.py:793
  16.8 3.2 %collective-permute-start.8 = (f32[1,2560]{1,0:T(1,128)S(1)}, f32[1,2560]{1,0:T(1,128)S(1)}, u32[]{:S(2)}, u32[]{:S(2)}) collective-permute-start(f32[1,2560]{1,0:T(1,128)S(1)} %merge.1.refs_2_), channel_id=1, source_target_pairs={{0,16},{4,20},{8,8},{12,12},{16,24},{20,28},{24,0},{28,4},{1,17},{... | collective-permute-start | bytes 30728 | tf_op jit(solution)/shard_map/ppermute | solution.py:793
  20.1 4.4 %collective-permute-start.7 = (f32[1,2560]{1,0:T(1,128)S(1)}, f32[1,2560]{1,0:T(1,128)S(1)}, u32[]{:S(2)}, u32[]{:S(2)}) collective-permute-start(f32[1,2560]{1,0:T(1,128)S(1)} %merge.1.refs_2_), channel_id=1, source_target_pairs={{0,24},{4,28},{8,0},{12,4},{16,16},{20,20},{24,8},{28,12},{1,25},{... | collective-permute-start | bytes 30728 | tf_op jit(solution)/shard_map/ppermute | solution.py:793
  24.5 0.7 %collective-permute-start.6 = (f32[1,2560]{1,0:T(1,128)S(1)}, f32[1,2560]{1,0:T(1,128)S(1)}, u32[]{:S(2)}, u32[]{:S(2)}) collective-permute-start(f32[1,2560]{1,0:T(1,128)S(1)} %merge.1.refs_2_), channel_id=1, source_target_pairs={{0,0},{4,4},{8,16},{12,20},{16,8},{20,12},{24,24},{28,28},{1,1},{5... | collective-permute-start | bytes 30728 | tf_op jit(solution)/shard_map/ppermute | solution.py:793
  25.2 0.0 collective-permute-done.10.refs_2_
  25.2 0.1 collective-permute-start.11
  25.3 0.7 %write_depth.1 = f32[128,512]{1,0:T(8,128)} custom-call(f32[512,128]{1,0:T(8,128)S(1)} %get-tuple-element.71.depth), custom_call_target="tpu_custom_call" | custom-call | flops 100000 | bytes 2000000 | tf_op jit(solution)/shard_map/write_depth/pallas_call | solution.py:585
  26.0 0.1 rest_x.1.rest
  26.1 0.3 collective-permute-done.11.refs_3_
  26.4 1.0 %solve_y.1 = f32[128,512]{1,0:T(8,128)} custom-call(f32[512,128]{1,0:T(8,128)S(1)} %get-tuple-element.67.iy.inv_ref, f32[512,128]{1,0:T(8,128)S(1)} %get-tuple-element.78.r_ref, f32[3,32,128]{2,1,0:T(8,128)S(1)} %get-tuple-element.68.ty.t_ref, f32[15,32,128]{2,1,0:T(8,128)S(1)} %get-tuple-element.69.wy.w_ref, f32[6,32,128]{2,1,0:T(8,128)S(1)} %get-tuple-element.79.s_ref, ...), custom_call_target="tpu_custom_call" | custom-call | flops 1000000 | bytes 4000000 | tf_op jit(solution)/shard_map/solve_y/pallas_call | solution.py:760
  27.4 0.0 collective-permute-done.9.refs_6_
  27.4 0.0 collective-permute-done.8.refs_5_
  27.5 0.8 %solve_x.1 = f32[128,512]{1,0:T(8,128)} custom-call(f32[512,128]{1,0:T(8,128)S(1)} %get-tuple-element.72.from_left, f32[512,128]{1,0:T(8,128)S(1)} %get-tuple-element.73.from_right, f32[512,128]{1,0:T(8,128)S(1)} %rest_x.1.rest, f32[1,2560]{1,0:T(1,128)S(1)} %get-tuple-element.76.mine.refs_0_, f32[1,2560]{1,0:T(1,128)S(1)} %collective-permute-done.4.theirs.refs_1_, ...), custom_call_target="tpu_custom_call" | custom-call | flops 1000000 | bytes 4000000 | tf_op jit(solution)/shard_map/solve_x/pallas_call | solution.py:760
  (17 shorter events, 0.0 us)
Async XLA Ops:
  0.6 4.1 %copy-start.4 = (s32[128,512]{1,0:T(8,128)S(1)}, s32[128,512]{1,0:T(8,128)}, u32[]{:S(2)}) copy-start(s32[128,512]{1,0:T(8,128)} %m.3) | copy-start | bytes 786436
  0.6 4.1 %copy-start.3 = (f32[128,512]{1,0:T(8,128)S(1)}, f32[128,512]{1,0:T(8,128)}, u32[]{:S(2)}) copy-start(f32[128,512]{1,0:T(8,128)} %b.3) | copy-start | bytes 786436
  0.7 4.0 %copy-start.2 = (f32[128,512]{1,0:T(8,128)S(1)}, f32[128,512]{1,0:T(8,128)}, u32[]{:S(2)}) copy-start(f32[128,512]{1,0:T(8,128)} %q.3) | copy-start | bytes 786436
  0.7 4.0 %copy-start.1 = (f32[128,512]{1,0:T(8,128)S(1)}, f32[128,512]{1,0:T(8,128)}, u32[]{:S(2)}) copy-start(f32[128,512]{1,0:T(8,128)} %p.3) | copy-start | bytes 786436
  0.7 4.0 %copy-start = (f32[128,512]{1,0:T(8,128)S(1)}, f32[128,512]{1,0:T(8,128)}, u32[]{:S(2)}) copy-start(f32[128,512]{1,0:T(8,128)} %h.5) | copy-start | bytes 786436
  1.7 4.9 %collective-permute-start = (f32[2,8,512]{2,1,0:T(8,128)S(1)}, f32[2,8,512]{2,1,0:T(8,128)S(1)}, u32[]{:S(2)}, u32[]{:S(2)}) collective-permute-start(f32[2,8,512]{2,1,0:T(8,128)S(1)} %pack_x.1._), channel_id=1, source_target_pairs={{0,4},{4,0},{8,12},{12,8},{16,20},{20,16},{24,28},{28,24},{1,5},{5... | collective-permute-start | bytes 98312 | tf_op jit(solution)/shard_map/ppermute | solution.py:785
  4.9 1.3 %collective-permute-start.1 = (f32[8,128]{1,0:T(8,128)S(1)}, f32[8,128]{1,0:T(8,128)S(1)}, u32[]{:S(2)}, u32[]{:S(2)}) collective-permute-start(f32[8,128]{1,0:T(8,128)S(1)} %get-tuple-element.50), channel_id=1, source_target_pairs={{0,1},{1,0},{2,3},{3,2},{4,5},{5,4},{6,7},{7,6},{8,9},{9,8},{10,11... | collective-permute-start | bytes 12296 | tf_op jit(solution)/shard_map/ppermute | solution.py:785
  5.0 5.1 %collective-permute-start.3 = (f32[32,128]{1,0:T(8,128)S(1)}, f32[32,128]{1,0:T(8,128)S(1)}, u32[]{:S(2)}, u32[]{:S(2)}) collective-permute-start(f32[32,128]{1,0:T(8,128)S(1)} %get-tuple-element.52), channel_id=1, source_target_pairs={{0,0},{1,2},{2,1},{3,3},{4,4},{5,6},{6,5},{7,7},{8,8},{9,10},{10,9... | collective-permute-start | bytes 49160 | tf_op jit(solution)/shard_map/ppermute | solution.py:781
  6.6 4.5 %collective-permute-start.2 = (f32[8,512]{1,0:T(8,128)S(1)}, f32[8,512]{1,0:T(8,128)S(1)}, u32[]{:S(2)}, u32[]{:S(2)}) collective-permute-start(f32[8,512]{1,0:T(8,128)S(1)} %second_of.1), channel_id=1, source_target_pairs={{0,8},{4,0},{8,16},{12,4},{16,24},{20,12},{24,28},{28,20},{1,9},{5... | collective-permute-start | bytes 49160 | tf_op jit(solution)/shard_map/ppermute | solution.py:775
  11.5 3.7 %collective-permute-start.4 = (f32[1,2560]{1,0:T(1,128)S(1)}, f32[1,2560]{1,0:T(1,128)S(1)}, u32[]{:S(2)}, u32[]{:S(2)}) collective-permute-start(f32[1,2560]{1,0:T(1,128)S(1)} %get-tuple-element.76.mine.refs_0_), channel_id=1, source_target_pairs={{0,4},{4,0},{8,12},{12,8},{16,20},{20,16},{24,28},{28,24},{1,5},{5... | collective-permute-start | bytes 30728 | tf_op jit(solution)/shard_map/ppermute | solution.py:785
  13.2 1.8 %collective-permute-start.5 = (f32[1,640]{1,0:T(1,128)S(1)}, f32[1,640]{1,0:T(1,128)S(1)}, u32[]{:S(2)}, u32[]{:S(2)}) collective-permute-start(f32[1,640]{1,0:T(1,128)S(1)} %get-tuple-element.77.refs_0_), channel_id=1, source_target_pairs={{0,1},{1,0},{2,3},{3,2},{4,5},{5,4},{6,7},{7,6},{8,9},{9,8},{10,11... | collective-permute-start | bytes 7688 | tf_op jit(solution)/shard_map/ppermute | solution.py:785
  13.9 11.3 %collective-permute-start.10 = (f32[1,2048]{1,0:T(1,128)S(1)}, f32[1,2048]{1,0:T(1,128)S(1)}, u32[]{:S(2)}, u32[]{:S(2)}) collective-permute-start(f32[1,2048]{1,0:T(1,128)S(1)} %get-tuple-element.80), channel_id=1, source_target_pairs={{0,2},{1,3},{2,0},{3,1},{4,6},{5,7},{6,4},{7,5},{8,10},{9,11},{10,... | collective-permute-start | bytes 24584 | tf_op jit(solution)/shard_map/ppermute | solution.py:785
  15.2 12.2 %collective-permute-start.9 = (f32[1,2560]{1,0:T(1,128)S(1)}, f32[1,2560]{1,0:T(1,128)S(1)}, u32[]{:S(2)}, u32[]{:S(2)}) collective-permute-start(f32[1,2560]{1,0:T(1,128)S(1)} %merge.1.refs_2_), channel_id=1, source_target_pairs={{0,8},{4,12},{8,24},{12,28},{16,0},{20,4},{24,16},{28,20},{1,9},{5... | collective-permute-start | bytes 30728 | tf_op jit(solution)/shard_map/ppermute | solution.py:793
  16.8 10.6 %collective-permute-start.8 = (f32[1,2560]{1,0:T(1,128)S(1)}, f32[1,2560]{1,0:T(1,128)S(1)}, u32[]{:S(2)}, u32[]{:S(2)}) collective-permute-start(f32[1,2560]{1,0:T(1,128)S(1)} %merge.1.refs_2_), channel_id=1, source_target_pairs={{0,16},{4,20},{8,8},{12,12},{16,24},{20,28},{24,0},{28,4},{1,17},{... | collective-permute-start | bytes 30728 | tf_op jit(solution)/shard_map/ppermute | solution.py:793
  20.1 7.4 %collective-permute-start.7 = (f32[1,2560]{1,0:T(1,128)S(1)}, f32[1,2560]{1,0:T(1,128)S(1)}, u32[]{:S(2)}, u32[]{:S(2)}) collective-permute-start(f32[1,2560]{1,0:T(1,128)S(1)} %merge.1.refs_2_), channel_id=1, source_target_pairs={{0,24},{4,28},{8,0},{12,4},{16,16},{20,20},{24,8},{28,12},{1,25},{... | collective-permute-start | bytes 30728 | tf_op jit(solution)/shard_map/ppermute | solution.py:793
  24.5 3.0 %collective-permute-start.6 = (f32[1,2560]{1,0:T(1,128)S(1)}, f32[1,2560]{1,0:T(1,128)S(1)}, u32[]{:S(2)}, u32[]{:S(2)}) collective-permute-start(f32[1,2560]{1,0:T(1,128)S(1)} %merge.1.refs_2_), channel_id=1, source_target_pairs={{0,0},{4,4},{8,16},{12,20},{16,8},{20,12},{24,24},{28,28},{1,1},{5... | collective-permute-start | bytes 30728 | tf_op jit(solution)/shard_map/ppermute | solution.py:793
  25.2 1.2 %collective-permute-start.11 = (f32[1,640]{1,0:T(1,128)S(1)}, f32[1,640]{1,0:T(1,128)S(1)}, u32[]{:S(2)}, u32[]{:S(2)}) collective-permute-start(f32[1,640]{1,0:T(1,128)S(1)} %slice.4), channel_id=1, source_target_pairs={{0,1},{1,0},{2,3},{3,2},{4,5},{5,4},{6,7},{7,6},{8,9},{9,8},{10,11... | collective-permute-start | bytes 7688 | tf_op jit(solution)/shard_map/ppermute | solution.py:785

commit v16 on v14

--- a/solution.py
+++ b/solution.py
@@ -549,7 +549,7 @@
     )(*arrays)
 
 
-PARTS = 2
+PARTS = 1
 
 
 def tile_writes(tiled, whole, tile, sems):

time: 23.9 us -> 23.8 us (level)
  no operation moved by 1% of the time
where the time goes in v16:
time: 23.8 us; the launch traced here: 23.6 us
  starting transfers between devices  13.1 us (55%)
  Pallas kernels  7.53 us (32%)
  waiting for transfers between devices  2.07 us (9%)
  between operations  0.81 us (3%)
    ppermute x7, starting transfers between devices, cross(): lax.ppermute(value, axis, [(i, i ^ mask) for i in range(lax.axis_size(axi...  6.5 us
    ppermute x2, starting transfers between devices, crossed(): return lax.ppermute(value, axis, pairs)  3.88 us
    ppermute x1, starting transfers between devices, hand_on(): lax.ppermute(value, axis, [(i, t if 0 <= t < count else i ^ 1) for i, t i...  2.11 us
    pallas_call x2, Pallas kernels, solve(): pl.pallas_call(kernel, out_shape=shape(*block), in_specs=[VMEM] * (len(pi...  1.82 us
    ppermute x7, waiting for transfers between devices, cross(): lax.ppermute(value, axis, [(i, i ^ mask) for i in range(lax.axis_size(axi...  1.19 us
    pallas_call x1, Pallas kernels, pack_x(): pl.pallas_call(pack_x_kernel, out_shape=shape(2, SUB, cols), in_specs=[HB...  0.99 us
    pallas_call x1, Pallas kernels, fluxes_y(): pl.pallas_call(flux_y_kernel, out_shape=(shape(*stack),) * 3, in_specs=[V...  0.97 us
    ppermute x2, waiting for transfers between devices, crossed(): return lax.ppermute(value, axis, pairs)  0.88 us
  transfers between devices with their start and end apart: 11, of which 5 were waited for; matrix products, arithmetic and copies ran while one was open for 0% of the time, Pallas kernels for 23%

profile of v16, /device:TPU:0, one launch (start us, length us, event | category | flops | bytes accessed | tf_op | source)
XLA Modules:
  0.0 23.6 jit_solution(11628078528802569902)
XLA Ops:
  0.7 1.0 %pack_x.1._ = f32[2,8,512]{2,1,0:T(8,128)S(1)} custom-call(f32[128,512]{1,0:T(8,128)} %h.5, f32[128,512]{1,0:T(8,128)} %p.3, f32[128,512]{1,0:T(8,128)} %q.3, f32[128,512]{1,0:T(8,128)} %b.3, s32[128,512]{1,0:T(8,128)} %m.3), custom_call_target="tpu_custom_call" | custom-call | tf_op jit(solution)/shard_map/pack_x/pallas_call | solution.py:78
  1.7 3.0 %collective-permute-start = (f32[2,8,512]{2,1,0:T(8,128)S(1)}, f32[2,8,512]{2,1,0:T(8,128)S(1)}, u32[]{:S(2)}, u32[]{:S(2)}) collective-permute-start(f32[2,8,512]{2,1,0:T(8,128)S(1)} %pack_x.1._), channel_id=1, source_target_pairs={{0,4},{4,0},{8,12},{12,8},{16,20},{20,16},{24,28},{28,24},{1,5},{5... | collective-permute-start | bytes 98312 | tf_op jit(solution)/shard_map/ppermute | solution.py:772
  4.7 0.2 pack_y.1
  4.9 0.0 collective-permute-start.1
  5.0 0.7 %collective-permute-start.3 = (f32[32,128]{1,0:T(8,128)S(1)}, f32[32,128]{1,0:T(8,128)S(1)}, u32[]{:S(2)}, u32[]{:S(2)}) collective-permute-start(f32[32,128]{1,0:T(8,128)S(1)} %get-tuple-element.52), channel_id=1, source_target_pairs={{0,0},{1,2},{2,1},{3,3},{4,4},{5,6},{6,5},{7,7},{8,8},{9,10},{10,9... | collective-permute-start | bytes 49160 | tf_op jit(solution)/shard_map/ppermute | solution.py:768
  5.6 0.5 %prepare_depth.1 = (f32[512,128]{1,0:T(8,128)S(1)}, f32[512,128]{1,0:T(8,128)S(1)}, f32[512,128]{1,0:T(8,128)S(1)}, f32[512,128]{1,0:T(8,128)S(1)}, f32[3,32,128...) custom-call(f32[128,512]{1,0:T(8,128)S(1)} %copy-done), custom_call_target="tpu_custom_call" | custom-call | flops 2000000 | bytes 4000000 | tf_op jit(solution)/shard_map/prepare_depth/pallas_call | solution.py:244
  6.2 0.0 collective-permute-done.1.refs_1_.near
  6.2 0.4 %collective-permute-done.both.near = f32[2,8,512]{2,1,0:T(8,128)S(1)} collective-permute-done((f32[2,8,512]{2,1,0:T(8,128)S(1)}, f32[2,8,512]{2,1,0:T(8,128)S(1)}, u32[]{:S(2)}, u32[]{:S(2)}) %collective-permute-start) | collective-permute-done | bytes 32800 | tf_op jit(solution)/shard_map/ppermute | solution.py:772
  6.6 2.1 %collective-permute-start.2 = (f32[8,512]{1,0:T(8,128)S(1)}, f32[8,512]{1,0:T(8,128)S(1)}, u32[]{:S(2)}, u32[]{:S(2)}) collective-permute-start(f32[8,512]{1,0:T(8,128)S(1)} %second_of.1), channel_id=1, source_target_pairs={{0,8},{4,0},{8,16},{12,4},{16,24},{20,12},{24,28},{28,20},{1,9},{5... | collective-permute-start | bytes 49160 | tf_op jit(solution)/shard_map/ppermute | solution.py:762
  8.7 0.8 %prepare_rest.1 = (f32[512,128]{1,0:T(8,128)S(1)}, f32[512,128]{1,0:T(8,128)S(1)}, f32[512,128]{1,0:T(8,128)S(1)}, f32[512,128]{1,0:T(8,128)S(1)}, f32[512,128]{...) custom-call(f32[128,512]{1,0:T(8,128)S(1)} %copy-done.1, ...), custom_call_target="tpu_custom_call" | custom-call | flops 2000000 | bytes 6000000 | tf_op jit(solution)/shard_map/prepare_rest/pallas_call | solution.py:264
  9.5 0.6 %fluxes_x_inner.1 = (f32[512,128]{1,0:T(8,128)S(1)}, f32[512,128]{1,0:T(8,128)S(1)}, f32[512,128]{1,0:T(8,128)S(1)}, f32[6,32,128]{2,1,0:T(8,128)S(1)}) custom-call(f32[512,128]{1,0:T(8,128)S(1)} %get-tuple-element.42.hx, f32[512,128]{1,0:T(8,128)S(1)} %get-tuple-element.43.px, f32[512,128]{1,0:T(8,128)S(1)} %get-tuple-element.44.qx, ...), custom_call_target="tpu_custom_call" | custom-call | flops 4000000 | bytes 4000000 | tf_op jit(solution)/shard_map/fluxes_x_inner/pallas_call | solution.py:435
  10.1 0.0 collective-permute-done.3.far
  10.1 1.0 %fluxes_y.1 = (f32[512,128]{1,0:T(8,128)S(1)}, f32[512,128]{1,0:T(8,128)S(1)}, f32[512,128]{1,0:T(8,128)S(1)}) custom-call(f32[8,128]{1,0:T(8,128)S(1)} %collective-permute-done.1.refs_1_.near, f32[32,128]{1,0:T(8,128)S(1)} %collective-permute-done.3.far, f32[512,128]{1,0:T(8,128)S(1)} %get-tuple-element.53.hy, f32[512,128]{1,0:T(8,128)S(1)} %get-tuple-element.54.py, ...), custom_call_target="tpu_custom_call" | custom-call | flops 4000000 | bytes 4000000 | tf_op jit(solution)/shard_map/fluxes_y/pallas_call | solution.py:391
  11.1 0.0 collective-permute-done.2.far
  11.1 0.4 %fluxes_x.1 = (f32[512,128]{1,0:T(8,128)S(1)}, f32[512,128]{1,0:T(8,128)S(1)}, f32[512,128]{1,0:T(8,128)S(1)}, f32[4,32,128]{2,1,0:T(8,128)S(1)}, f32[1,2560]{1,0:T(1,128)S(1)}) custom-call(f32[2,8,512]{2,1,0:T(8,128)S(1)} %collective-permute-done.both.near, f32[8,512]{1,0:T(8,128)S(1)} %collective-permute-done.2.far, f32[512,128]{1,0:T(8,128)S(1)} %get-tuple-element.42.hx, ...), custom_call_target="tpu_custom_call" | custom-call | tf_op jit(solution)/shard_map/fluxes_x/pallas_call | solution.py:491
  11.5 1.4 %collective-permute-start.4 = (f32[1,2560]{1,0:T(1,128)S(1)}, f32[1,2560]{1,0:T(1,128)S(1)}, u32[]{:S(2)}, u32[]{:S(2)}) collective-permute-start(f32[1,2560]{1,0:T(1,128)S(1)} %get-tuple-element.76.mine.refs_0_), channel_id=1, source_target_pairs={{0,4},{4,0},{8,12},{12,8},{16,20},{20,16},{24,28},{28,24},{1,5},{5... | collective-permute-start | bytes 30728 | tf_op jit(solution)/shard_map/ppermute | solution.py:772
  12.9 0.4 %join_y.1 = (f32[512,128]{1,0:T(8,128)S(1)}, f32[512,128]{1,0:T(8,128)S(1)}, f32[6,32,128]{2,1,0:T(8,128)S(1)}, f32[1,640]{1,0:T(1,128)S(1)}, f32[1,2048]{1,0:T(1,128)S(1)}) custom-call(f32[512,128]{1,0:T(8,128)S(1)} %get-tuple-element.47.depth_inner, f32[512,128]{1,0:T(8,128)S(1)} %get-tuple-element.48.across_inner, ...), custom_call_target="tpu_custom_call" | custom-call | flops 2000000 | bytes 2000000 | tf_op jit(solution)/shard_map/join_y/pallas_call | solution.py:540
  13.2 0.7 %collective-permute-start.5 = (f32[1,640]{1,0:T(1,128)S(1)}, f32[1,640]{1,0:T(1,128)S(1)}, u32[]{:S(2)}, u32[]{:S(2)}) collective-permute-start(f32[1,640]{1,0:T(1,128)S(1)} %get-tuple-element.77.refs_0_), channel_id=1, source_target_pairs={{0,1},{1,0},{2,3},{3,2},{4,5},{5,4},{6,7},{7,6},{8,9},{9,8},{10,11... | collective-permute-start | bytes 7688 | tf_op jit(solution)/shard_map/ppermute | solution.py:772
  13.9 1.1 %collective-permute-start.9 = (f32[1,2048]{1,0:T(1,128)S(1)}, f32[1,2048]{1,0:T(1,128)S(1)}, u32[]{:S(2)}, u32[]{:S(2)}) collective-permute-start(f32[1,2048]{1,0:T(1,128)S(1)} %get-tuple-element.80), channel_id=1, source_target_pairs={{0,2},{1,3},{2,0},{3,1},{4,6},{5,7},{6,4},{7,5},{8,10},{9,11},{10,... | collective-permute-start | bytes 24584 | tf_op jit(solution)/shard_map/ppermute | solution.py:772
  15.0 0.0 collective-permute-done.5.refs_0_.refs_1_
  15.0 0.2 collective-permute-done.4.theirs.refs_1_
  15.2 2.6 %collective-permute-start.8 = (f32[1,2560]{1,0:T(1,128)S(1)}, f32[1,2560]{1,0:T(1,128)S(1)}, u32[]{:S(2)}, u32[]{:S(2)}) collective-permute-start(f32[1,2560]{1,0:T(1,128)S(1)} %merge.1.refs_2_), channel_id=1, source_target_pairs={{0,16},{4,20},{8,24},{12,28},{16,8},{20,12},{24,0},{28,4},{1,17},{... | collective-permute-start | bytes 30728 | tf_op jit(solution)/shard_map/ppermute | solution.py:780
  17.9 1.2 %collective-permute-start.7 = (f32[1,2560]{1,0:T(1,128)S(1)}, f32[1,2560]{1,0:T(1,128)S(1)}, u32[]{:S(2)}, u32[]{:S(2)}) collective-permute-start(f32[1,2560]{1,0:T(1,128)S(1)} %merge.1.refs_2_), channel_id=1, source_target_pairs={{0,24},{4,28},{8,16},{12,20},{16,0},{20,4},{24,8},{28,12},{1,25},{... | collective-permute-start | bytes 30728 | tf_op jit(solution)/shard_map/ppermute | solution.py:780
  19.1 0.3 %collective-permute-start.6 = (f32[1,2560]{1,0:T(1,128)S(1)}, f32[1,2560]{1,0:T(1,128)S(1)}, u32[]{:S(2)}, u32[]{:S(2)}) collective-permute-start(f32[1,2560]{1,0:T(1,128)S(1)} %merge.1.refs_2_), channel_id=1, source_target_pairs={{0,8},{4,12},{8,0},{12,4},{16,24},{20,28},{24,16},{28,20},{1,9},{5... | collective-permute-start | bytes 30728 | tf_op jit(solution)/shard_map/ppermute | solution.py:772
  19.4 0.7 %write_depth.1 = f32[128,512]{1,0:T(8,128)} custom-call(f32[512,128]{1,0:T(8,128)S(1)} %get-tuple-element.71.depth), custom_call_target="tpu_custom_call" | custom-call | flops 100000 | bytes 2000000 | tf_op jit(solution)/shard_map/write_depth/pallas_call | solution.py:585
  20.1 0.1 rest_x.1.rest
  20.2 0.3 %collective-permute-done.10.refs_3_ = f32[1,640]{1,0:T(1,128)S(1)} collective-permute-done((f32[1,640]{1,0:T(1,128)S(1)}, f32[1,640]{1,0:T(1,128)S(1)}, u32[]{:S(2)}, u32[]{:S(2)}) %collective-permute-start.10) | collective-permute-done | bytes 2592 | tf_op jit(solution)/shard_map/ppermute | solution.py:772
  20.5 1.0 %solve_y.1 = f32[128,512]{1,0:T(8,128)} custom-call(f32[512,128]{1,0:T(8,128)S(1)} %get-tuple-element.67.iy.inv_ref, f32[512,128]{1,0:T(8,128)S(1)} %get-tuple-element.78.r_ref, f32[3,32,128]{2,1,0:T(8,128)S(1)} %get-tuple-element.68.ty.t_ref, f32[15,32,128]{2,1,0:T(8,128)S(1)} %get-tuple-element.69.wy.w_ref, f32[6,32,128]{2,1,0:T(8,128)S(1)} %get-tuple-element.79.s_ref, ...), custom_call_target="tpu_custom_call" | custom-call | flops 1000000 | bytes 4000000 | tf_op jit(solution)/shard_map/solve_y/pallas_call | solution.py:747
  21.5 0.0 collective-permute-done.8.refs_5_
  21.5 0.9 %collective-permute-done.7.refs_4_ = f32[1,2560]{1,0:T(1,128)S(1)} collective-permute-done((f32[1,2560]{1,0:T(1,128)S(1)}, f32[1,2560]{1,0:T(1,128)S(1)}, u32[]{:S(2)}, u32[]{:S(2)}) %collective-permute-start.7) | collective-permute-done | bytes 10272 | tf_op jit(solution)/shard_map/ppermute | solution.py:780
  22.4 0.3 %collective-permute-done.6.refs_3_ = f32[1,2560]{1,0:T(1,128)S(1)} collective-permute-done((f32[1,2560]{1,0:T(1,128)S(1)}, f32[1,2560]{1,0:T(1,128)S(1)}, u32[]{:S(2)}, u32[]{:S(2)}) %collective-permute-start.6) | collective-permute-done | bytes 10272 | tf_op jit(solution)/shard_map/ppermute | solution.py:772
  22.8 0.8 %solve_x.1 = f32[128,512]{1,0:T(8,128)} custom-call(f32[512,128]{1,0:T(8,128)S(1)} %get-tuple-element.72.from_left, f32[512,128]{1,0:T(8,128)S(1)} %get-tuple-element.73.from_right, f32[512,128]{1,0:T(8,128)S(1)} %rest_x.1.rest, f32[1,2560]{1,0:T(1,128)S(1)} %get-tuple-element.76.mine.refs_0_, f32[1,2560]{1,0:T(1,128)S(1)} %collective-permute-done.4.theirs.refs_1_, ...), custom_call_target="tpu_custom_call" | custom-call | flops 1000000 | bytes 4000000 | tf_op jit(solution)/shard_map/solve_x/pallas_call | solution.py:747
  (15 shorter events, 0.0 us)
Async XLA Ops:
  0.6 4.1 %copy-start.4 = (s32[128,512]{1,0:T(8,128)S(1)}, s32[128,512]{1,0:T(8,128)}, u32[]{:S(2)}) copy-start(s32[128,512]{1,0:T(8,128)} %m.3) | copy-start | bytes 786436
  0.6 4.1 %copy-start.3 = (f32[128,512]{1,0:T(8,128)S(1)}, f32[128,512]{1,0:T(8,128)}, u32[]{:S(2)}) copy-start(f32[128,512]{1,0:T(8,128)} %b.3) | copy-start | bytes 786436
  0.7 4.0 %copy-start.2 = (f32[128,512]{1,0:T(8,128)S(1)}, f32[128,512]{1,0:T(8,128)}, u32[]{:S(2)}) copy-start(f32[128,512]{1,0:T(8,128)} %q.3) | copy-start | bytes 786436
  0.7 4.0 %copy-start.1 = (f32[128,512]{1,0:T(8,128)S(1)}, f32[128,512]{1,0:T(8,128)}, u32[]{:S(2)}) copy-start(f32[128,512]{1,0:T(8,128)} %p.3) | copy-start | bytes 786436
  0.7 4.0 %copy-start = (f32[128,512]{1,0:T(8,128)S(1)}, f32[128,512]{1,0:T(8,128)}, u32[]{:S(2)}) copy-start(f32[128,512]{1,0:T(8,128)} %h.5) | copy-start | bytes 786436
  1.7 4.9 %collective-permute-start = (f32[2,8,512]{2,1,0:T(8,128)S(1)}, f32[2,8,512]{2,1,0:T(8,128)S(1)}, u32[]{:S(2)}, u32[]{:S(2)}) collective-permute-start(f32[2,8,512]{2,1,0:T(8,128)S(1)} %pack_x.1._), channel_id=1, source_target_pairs={{0,4},{4,0},{8,12},{12,8},{16,20},{20,16},{24,28},{28,24},{1,5},{5... | collective-permute-start | bytes 98312 | tf_op jit(solution)/shard_map/ppermute | solution.py:772
  4.9 1.3 %collective-permute-start.1 = (f32[8,128]{1,0:T(8,128)S(1)}, f32[8,128]{1,0:T(8,128)S(1)}, u32[]{:S(2)}, u32[]{:S(2)}) collective-permute-start(f32[8,128]{1,0:T(8,128)S(1)} %get-tuple-element.50), channel_id=1, source_target_pairs={{0,1},{1,0},{2,3},{3,2},{4,5},{5,4},{6,7},{7,6},{8,9},{9,8},{10,11... | collective-permute-start | bytes 12296 | tf_op jit(solution)/shard_map/ppermute | solution.py:772
  5.0 5.1 %collective-permute-start.3 = (f32[32,128]{1,0:T(8,128)S(1)}, f32[32,128]{1,0:T(8,128)S(1)}, u32[]{:S(2)}, u32[]{:S(2)}) collective-permute-start(f32[32,128]{1,0:T(8,128)S(1)} %get-tuple-element.52), channel_id=1, source_target_pairs={{0,0},{1,2},{2,1},{3,3},{4,4},{5,6},{6,5},{7,7},{8,8},{9,10},{10,9... | collective-permute-start | bytes 49160 | tf_op jit(solution)/shard_map/ppermute | solution.py:768
  6.6 4.5 %collective-permute-start.2 = (f32[8,512]{1,0:T(8,128)S(1)}, f32[8,512]{1,0:T(8,128)S(1)}, u32[]{:S(2)}, u32[]{:S(2)}) collective-permute-start(f32[8,512]{1,0:T(8,128)S(1)} %second_of.1), channel_id=1, source_target_pairs={{0,8},{4,0},{8,16},{12,4},{16,24},{20,12},{24,28},{28,20},{1,9},{5... | collective-permute-start | bytes 49160 | tf_op jit(solution)/shard_map/ppermute | solution.py:762
  11.5 3.7 %collective-permute-start.4 = (f32[1,2560]{1,0:T(1,128)S(1)}, f32[1,2560]{1,0:T(1,128)S(1)}, u32[]{:S(2)}, u32[]{:S(2)}) collective-permute-start(f32[1,2560]{1,0:T(1,128)S(1)} %get-tuple-element.76.mine.refs_0_), channel_id=1, source_target_pairs={{0,4},{4,0},{8,12},{12,8},{16,20},{20,16},{24,28},{28,24},{1,5},{5... | collective-permute-start | bytes 30728 | tf_op jit(solution)/shard_map/ppermute | solution.py:772
  13.2 1.8 %collective-permute-start.5 = (f32[1,640]{1,0:T(1,128)S(1)}, f32[1,640]{1,0:T(1,128)S(1)}, u32[]{:S(2)}, u32[]{:S(2)}) collective-permute-start(f32[1,640]{1,0:T(1,128)S(1)} %get-tuple-element.77.refs_0_), channel_id=1, source_target_pairs={{0,1},{1,0},{2,3},{3,2},{4,5},{5,4},{6,7},{7,6},{8,9},{9,8},{10,11... | collective-permute-start | bytes 7688 | tf_op jit(solution)/shard_map/ppermute | solution.py:772
  13.9 5.5 %collective-permute-start.9 = (f32[1,2048]{1,0:T(1,128)S(1)}, f32[1,2048]{1,0:T(1,128)S(1)}, u32[]{:S(2)}, u32[]{:S(2)}) collective-permute-start(f32[1,2048]{1,0:T(1,128)S(1)} %get-tuple-element.80), channel_id=1, source_target_pairs={{0,2},{1,3},{2,0},{3,1},{4,6},{5,7},{6,4},{7,5},{8,10},{9,11},{10,... | collective-permute-start | bytes 24584 | tf_op jit(solution)/shard_map/ppermute | solution.py:772
  15.2 6.3 %collective-permute-start.8 = (f32[1,2560]{1,0:T(1,128)S(1)}, f32[1,2560]{1,0:T(1,128)S(1)}, u32[]{:S(2)}, u32[]{:S(2)}) collective-permute-start(f32[1,2560]{1,0:T(1,128)S(1)} %merge.1.refs_2_), channel_id=1, source_target_pairs={{0,16},{4,20},{8,24},{12,28},{16,8},{20,12},{24,0},{28,4},{1,17},{... | collective-permute-start | bytes 30728 | tf_op jit(solution)/shard_map/ppermute | solution.py:780
  17.9 4.6 %collective-permute-start.7 = (f32[1,2560]{1,0:T(1,128)S(1)}, f32[1,2560]{1,0:T(1,128)S(1)}, u32[]{:S(2)}, u32[]{:S(2)}) collective-permute-start(f32[1,2560]{1,0:T(1,128)S(1)} %merge.1.refs_2_), channel_id=1, source_target_pairs={{0,24},{4,28},{8,16},{12,20},{16,0},{20,4},{24,8},{28,12},{1,25},{... | collective-permute-start | bytes 30728 | tf_op jit(solution)/shard_map/ppermute | solution.py:780
  19.1 3.7 %collective-permute-start.6 = (f32[1,2560]{1,0:T(1,128)S(1)}, f32[1,2560]{1,0:T(1,128)S(1)}, u32[]{:S(2)}, u32[]{:S(2)}) collective-permute-start(f32[1,2560]{1,0:T(1,128)S(1)} %merge.1.refs_2_), channel_id=1, source_target_pairs={{0,8},{4,12},{8,0},{12,4},{16,24},{20,28},{24,16},{28,20},{1,9},{5... | collective-permute-start | bytes 30728 | tf_op jit(solution)/shard_map/ppermute | solution.py:772
  19.4 1.2 %collective-permute-start.10 = (f32[1,640]{1,0:T(1,128)S(1)}, f32[1,640]{1,0:T(1,128)S(1)}, u32[]{:S(2)}, u32[]{:S(2)}) collective-permute-start(f32[1,640]{1,0:T(1,128)S(1)} %slice.4), channel_id=1, source_target_pairs={{0,1},{1,0},{2,3},{3,2},{4,5},{5,4},{6,7},{7,6},{8,9},{9,8},{10,11... | collective-permute-start | bytes 7688 | tf_op jit(solution)/shard_map/ppermute | solution.py:772

commit v17 on v16

--- a/solution.py
+++ b/solution.py
@@ -758,8 +758,8 @@
 
 def hand_on(value, axis):
     count = lax.axis_size(axis)
-    far = [i + 2 if i % 2 == 0 else i - 2 for i in range(count)]
-    return lax.ppermute(value, axis, [(i, t if 0 <= t < count else i ^ 1) for i, t in enumerate(far)])
+    far = [(i, i + 2 if i % 2 == 0 else i - 2) for i in range(count)]
+    return lax.ppermute(value, axis, [(i, t) for i, t in far if 0 <= t < count])
 
 
 def shift_pair(value, axis):

time: 23.8 us -> 25.8 us (1.084)
  starting transfers between devices: 13.1 us -> 14.7 us
  waiting for transfers between devices: 2.07 us -> 2.43 us
    ppermute x1, starting transfers between devices: 2.11 us -> 4 us  [hand_on(): return lax.ppermute(value, axis, [(i, t) for i, t in far if 0 <= t < count])]
    ppermute x7, starting transfers between devices: 6.5 us -> 6.14 us  [cross(): lax.ppermute(value, axis, [(i, i ^ mask) for i in range(lax.axis_size(axi...]
  transfers between devices with their start and end apart: 11 -> 11, of which waited for: 5 -> 5; matrix products, arithmetic and copies ran while one was open for 0% -> 0% of each run, Pallas kernels for 23% -> 21%
where the time goes in v17:
time: 25.8 us; the launch traced here: 25.5 us
  starting transfers between devices  14.7 us (57%)
  Pallas kernels  7.53 us (29%)
  waiting for transfers between devices  2.43 us (9%)
  between operations  0.82 us (3%)
    ppermute x7, starting transfers between devices, cross(): lax.ppermute(value, axis, [(i, i ^ mask) for i in range(lax.axis_size(axi...  6.14 us
    ppermute x1, starting transfers between devices, hand_on(): return lax.ppermute(value, axis, [(i, t) for i, t in far if 0 <= t < count])  4 us
    ppermute x2, starting transfers between devices, crossed(): return lax.ppermute(value, axis, pairs)  3.88 us
    pallas_call x2, Pallas kernels, solve(): pl.pallas_call(kernel, out_shape=shape(*block), in_specs=[VMEM] * (len(pi...  1.82 us
    ppermute x7, waiting for transfers between devices, cross(): lax.ppermute(value, axis, [(i, i ^ mask) for i in range(lax.axis_size(axi...  1.39 us
    ppermute x2, waiting for transfers between devices, crossed(): return lax.ppermute(value, axis, pairs)  1.04 us
    pallas_call x1, Pallas kernels, pack_x(): pl.pallas_call(pack_x_kernel, out_shape=shape(2, SUB, cols), in_specs=[HB...  0.99 us
    pallas_call x1, Pallas kernels, fluxes_y(): pl.pallas_call(flux_y_kernel, out_shape=(shape(*stack),) * 3, in_specs=[V...  0.97 us
  transfers between devices with their start and end apart: 11, of which 5 were waited for; matrix products, arithmetic and copies ran while one was open for 0% of the time, Pallas kernels for 21%

profile of v17, /device:TPU:0, one launch (start us, length us, event | category | flops | bytes accessed | tf_op | source)
XLA Modules:
  0.0 25.5 jit_solution(2978838117722097424)
XLA Ops:
  0.7 1.0 %pack_x.1._ = f32[2,8,512]{2,1,0:T(8,128)S(1)} custom-call(f32[128,512]{1,0:T(8,128)} %h.5, f32[128,512]{1,0:T(8,128)} %p.3, f32[128,512]{1,0:T(8,128)} %q.3, f32[128,512]{1,0:T(8,128)} %b.3, s32[128,512]{1,0:T(8,128)} %m.3), custom_call_target="tpu_custom_call" | custom-call | tf_op jit(solution)/shard_map/pack_x/pallas_call | solution.py:78
  1.7 3.0 %collective-permute-start = (f32[2,8,512]{2,1,0:T(8,128)S(1)}, f32[2,8,512]{2,1,0:T(8,128)S(1)}, u32[]{:S(2)}, u32[]{:S(2)}) collective-permute-start(f32[2,8,512]{2,1,0:T(8,128)S(1)} %pack_x.1._), channel_id=1, source_target_pairs={{0,4},{4,0},{8,12},{12,8},{16,20},{20,16},{24,28},{28,24},{1,5},{5... | collective-permute-start | bytes 98312 | tf_op jit(solution)/shard_map/ppermute | solution.py:772
  4.7 0.2 pack_y.1
  4.9 0.0 collective-permute-start.1
  5.0 0.7 %collective-permute-start.3 = (f32[32,128]{1,0:T(8,128)S(1)}, f32[32,128]{1,0:T(8,128)S(1)}, u32[]{:S(2)}, u32[]{:S(2)}) collective-permute-start(f32[32,128]{1,0:T(8,128)S(1)} %get-tuple-element.52), channel_id=1, source_target_pairs={{0,0},{1,2},{2,1},{3,3},{4,4},{5,6},{6,5},{7,7},{8,8},{9,10},{10,9... | collective-permute-start | bytes 49160 | tf_op jit(solution)/shard_map/ppermute | solution.py:768
  5.6 0.5 %prepare_depth.1 = (f32[512,128]{1,0:T(8,128)S(1)}, f32[512,128]{1,0:T(8,128)S(1)}, f32[512,128]{1,0:T(8,128)S(1)}, f32[512,128]{1,0:T(8,128)S(1)}, f32[3,32,128...) custom-call(f32[128,512]{1,0:T(8,128)S(1)} %copy-done), custom_call_target="tpu_custom_call" | custom-call | flops 2000000 | bytes 4000000 | tf_op jit(solution)/shard_map/prepare_depth/pallas_call | solution.py:244
  6.2 0.0 collective-permute-done.1.refs_1_.near
  6.2 0.4 %collective-permute-done.both.near = f32[2,8,512]{2,1,0:T(8,128)S(1)} collective-permute-done((f32[2,8,512]{2,1,0:T(8,128)S(1)}, f32[2,8,512]{2,1,0:T(8,128)S(1)}, u32[]{:S(2)}, u32[]{:S(2)}) %collective-permute-start) | collective-permute-done | bytes 32800 | tf_op jit(solution)/shard_map/ppermute | solution.py:772
  6.6 4.0 %collective-permute-start.2 = (f32[8,512]{1,0:T(8,128)S(1)}, f32[8,512]{1,0:T(8,128)S(1)}, u32[]{:S(2)}, u32[]{:S(2)}) collective-permute-start(f32[8,512]{1,0:T(8,128)S(1)} %second_of.1), channel_id=1, source_target_pairs={{0,8},{8,16},{12,4},{16,24},{20,12},{28,20},{1,9},{9,17},{13,5},{1... | collective-permute-start | bytes 49160 | tf_op jit(solution)/shard_map/ppermute | solution.py:762
  10.6 0.8 %prepare_rest.1 = (f32[512,128]{1,0:T(8,128)S(1)}, f32[512,128]{1,0:T(8,128)S(1)}, f32[512,128]{1,0:T(8,128)S(1)}, f32[512,128]{1,0:T(8,128)S(1)}, f32[512,128]{...) custom-call(f32[128,512]{1,0:T(8,128)S(1)} %copy-done.1, ...), custom_call_target="tpu_custom_call" | custom-call | flops 2000000 | bytes 6000000 | tf_op jit(solution)/shard_map/prepare_rest/pallas_call | solution.py:264
  11.4 0.6 %fluxes_x_inner.1 = (f32[512,128]{1,0:T(8,128)S(1)}, f32[512,128]{1,0:T(8,128)S(1)}, f32[512,128]{1,0:T(8,128)S(1)}, f32[6,32,128]{2,1,0:T(8,128)S(1)}) custom-call(f32[512,128]{1,0:T(8,128)S(1)} %get-tuple-element.42.hx, f32[512,128]{1,0:T(8,128)S(1)} %get-tuple-element.43.px, f32[512,128]{1,0:T(8,128)S(1)} %get-tuple-element.44.qx, ...), custom_call_target="tpu_custom_call" | custom-call | flops 4000000 | bytes 4000000 | tf_op jit(solution)/shard_map/fluxes_x_inner/pallas_call | solution.py:435
  12.0 0.0 collective-permute-done.3.far
  12.0 1.0 %fluxes_y.1 = (f32[512,128]{1,0:T(8,128)S(1)}, f32[512,128]{1,0:T(8,128)S(1)}, f32[512,128]{1,0:T(8,128)S(1)}) custom-call(f32[8,128]{1,0:T(8,128)S(1)} %collective-permute-done.1.refs_1_.near, f32[32,128]{1,0:T(8,128)S(1)} %collective-permute-done.3.far, f32[512,128]{1,0:T(8,128)S(1)} %get-tuple-element.53.hy, f32[512,128]{1,0:T(8,128)S(1)} %get-tuple-element.54.py, ...), custom_call_target="tpu_custom_call" | custom-call | flops 4000000 | bytes 4000000 | tf_op jit(solution)/shard_map/fluxes_y/pallas_call | solution.py:391
  13.0 0.0 collective-permute-done.2.far
  13.0 0.4 %fluxes_x.1 = (f32[512,128]{1,0:T(8,128)S(1)}, f32[512,128]{1,0:T(8,128)S(1)}, f32[512,128]{1,0:T(8,128)S(1)}, f32[4,32,128]{2,1,0:T(8,128)S(1)}, f32[1,2560]{1,0:T(1,128)S(1)}) custom-call(f32[2,8,512]{2,1,0:T(8,128)S(1)} %collective-permute-done.both.near, f32[8,512]{1,0:T(8,128)S(1)} %collective-permute-done.2.far, f32[512,128]{1,0:T(8,128)S(1)} %get-tuple-element.42.hx, ...), custom_call_target="tpu_custom_call" | custom-call | tf_op jit(solution)/shard_map/fluxes_x/pallas_call | solution.py:491
  13.4 1.4 %collective-permute-start.4 = (f32[1,2560]{1,0:T(1,128)S(1)}, f32[1,2560]{1,0:T(1,128)S(1)}, u32[]{:S(2)}, u32[]{:S(2)}) collective-permute-start(f32[1,2560]{1,0:T(1,128)S(1)} %get-tuple-element.76.mine.refs_0_), channel_id=1, source_target_pairs={{0,4},{4,0},{8,12},{12,8},{16,20},{20,16},{24,28},{28,24},{1,5},{5... | collective-permute-start | bytes 30728 | tf_op jit(solution)/shard_map/ppermute | solution.py:772
  14.8 0.4 %join_y.1 = (f32[512,128]{1,0:T(8,128)S(1)}, f32[512,128]{1,0:T(8,128)S(1)}, f32[6,32,128]{2,1,0:T(8,128)S(1)}, f32[1,640]{1,0:T(1,128)S(1)}, f32[1,2048]{1,0:T(1,128)S(1)}) custom-call(f32[512,128]{1,0:T(8,128)S(1)} %get-tuple-element.47.depth_inner, f32[512,128]{1,0:T(8,128)S(1)} %get-tuple-element.48.across_inner, ...), custom_call_target="tpu_custom_call" | custom-call | flops 2000000 | bytes 2000000 | tf_op jit(solution)/shard_map/join_y/pallas_call | solution.py:540
  15.1 0.5 %collective-permute-start.5 = (f32[1,640]{1,0:T(1,128)S(1)}, f32[1,640]{1,0:T(1,128)S(1)}, u32[]{:S(2)}, u32[]{:S(2)}) collective-permute-start(f32[1,640]{1,0:T(1,128)S(1)} %get-tuple-element.77.refs_0_), channel_id=1, source_target_pairs={{0,1},{1,0},{2,3},{3,2},{4,5},{5,4},{6,7},{7,6},{8,9},{9,8},{10,11... | collective-permute-start | bytes 7688 | tf_op jit(solution)/shard_map/ppermute | solution.py:772
  15.6 1.1 %collective-permute-start.9 = (f32[1,2048]{1,0:T(1,128)S(1)}, f32[1,2048]{1,0:T(1,128)S(1)}, u32[]{:S(2)}, u32[]{:S(2)}) collective-permute-start(f32[1,2048]{1,0:T(1,128)S(1)} %get-tuple-element.80), channel_id=1, source_target_pairs={{0,2},{1,3},{2,0},{3,1},{4,6},{5,7},{6,4},{7,5},{8,10},{9,11},{10,... | collective-permute-start | bytes 24584 | tf_op jit(solution)/shard_map/ppermute | solution.py:772
  16.7 0.0 collective-permute-done.5.refs_0_.refs_1_
  16.7 0.4 %collective-permute-done.4.theirs.refs_1_ = f32[1,2560]{1,0:T(1,128)S(1)} collective-permute-done((f32[1,2560]{1,0:T(1,128)S(1)}, f32[1,2560]{1,0:T(1,128)S(1)}, u32[]{:S(2)}, u32[]{:S(2)}) %collective-permute-start.4) | collective-permute-done | bytes 10272 | tf_op jit(solution)/shard_map/ppermute | solution.py:772
  17.1 2.6 %collective-permute-start.8 = (f32[1,2560]{1,0:T(1,128)S(1)}, f32[1,2560]{1,0:T(1,128)S(1)}, u32[]{:S(2)}, u32[]{:S(2)}) collective-permute-start(f32[1,2560]{1,0:T(1,128)S(1)} %merge.1.refs_2_), channel_id=1, source_target_pairs={{0,16},{4,20},{8,24},{12,28},{16,8},{20,12},{24,0},{28,4},{1,17},{... | collective-permute-start | bytes 30728 | tf_op jit(solution)/shard_map/ppermute | solution.py:780
  19.8 1.2 %collective-permute-start.7 = (f32[1,2560]{1,0:T(1,128)S(1)}, f32[1,2560]{1,0:T(1,128)S(1)}, u32[]{:S(2)}, u32[]{:S(2)}) collective-permute-start(f32[1,2560]{1,0:T(1,128)S(1)} %merge.1.refs_2_), channel_id=1, source_target_pairs={{0,24},{4,28},{8,16},{12,20},{16,0},{20,4},{24,8},{28,12},{1,25},{... | collective-permute-start | bytes 30728 | tf_op jit(solution)/shard_map/ppermute | solution.py:780
  21.0 0.1 collective-permute-start.6
  21.1 0.0 collective-permute-done.9.refs_2_
  21.1 0.7 %write_depth.1 = f32[128,512]{1,0:T(8,128)} custom-call(f32[512,128]{1,0:T(8,128)S(1)} %get-tuple-element.71.depth), custom_call_target="tpu_custom_call" | custom-call | flops 100000 | bytes 2000000 | tf_op jit(solution)/shard_map/write_depth/pallas_call | solution.py:585
  21.9 0.1 rest_x.1.rest
  22.0 0.3 %collective-permute-done.10.refs_3_ = f32[1,640]{1,0:T(1,128)S(1)} collective-permute-done((f32[1,640]{1,0:T(1,128)S(1)}, f32[1,640]{1,0:T(1,128)S(1)}, u32[]{:S(2)}, u32[]{:S(2)}) %collective-permute-start.10) | collective-permute-done | bytes 2592 | tf_op jit(solution)/shard_map/ppermute | solution.py:772
  22.3 1.0 %solve_y.1 = f32[128,512]{1,0:T(8,128)} custom-call(f32[512,128]{1,0:T(8,128)S(1)} %get-tuple-element.67.iy.inv_ref, f32[512,128]{1,0:T(8,128)S(1)} %get-tuple-element.78.r_ref, f32[3,32,128]{2,1,0:T(8,128)S(1)} %get-tuple-element.68.ty.t_ref, f32[15,32,128]{2,1,0:T(8,128)S(1)} %get-tuple-element.69.wy.w_ref, f32[6,32,128]{2,1,0:T(8,128)S(1)} %get-tuple-element.79.s_ref, ...), custom_call_target="tpu_custom_call" | custom-call | flops 1000000 | bytes 4000000 | tf_op jit(solution)/shard_map/solve_y/pallas_call | solution.py:747
  23.3 1.0 %collective-permute-done.7.refs_4_ = f32[1,2560]{1,0:T(1,128)S(1)} collective-permute-done((f32[1,2560]{1,0:T(1,128)S(1)}, f32[1,2560]{1,0:T(1,128)S(1)}, u32[]{:S(2)}, u32[]{:S(2)}) %collective-permute-start.7) | collective-permute-done | bytes 10272 | tf_op jit(solution)/shard_map/ppermute | solution.py:780
  24.3 0.3 %collective-permute-done.6.refs_3_ = f32[1,2560]{1,0:T(1,128)S(1)} collective-permute-done((f32[1,2560]{1,0:T(1,128)S(1)}, f32[1,2560]{1,0:T(1,128)S(1)}, u32[]{:S(2)}, u32[]{:S(2)}) %collective-permute-start.6) | collective-permute-done | bytes 10272 | tf_op jit(solution)/shard_map/ppermute | solution.py:772
  24.7 0.8 %solve_x.1 = f32[128,512]{1,0:T(8,128)} custom-call(f32[512,128]{1,0:T(8,128)S(1)} %get-tuple-element.72.from_left, f32[512,128]{1,0:T(8,128)S(1)} %get-tuple-element.73.from_right, f32[512,128]{1,0:T(8,128)S(1)} %rest_x.1.rest, f32[1,2560]{1,0:T(1,128)S(1)} %get-tuple-element.76.mine.refs_0_, f32[1,2560]{1,0:T(1,128)S(1)} %collective-permute-done.4.theirs.refs_1_, ...), custom_call_target="tpu_custom_call" | custom-call | flops 1000000 | bytes 4000000 | tf_op jit(solution)/shard_map/solve_x/pallas_call | solution.py:747
  (15 shorter events, 0.0 us)
Async XLA Ops:
  0.6 4.1 %copy-start.4 = (s32[128,512]{1,0:T(8,128)S(1)}, s32[128,512]{1,0:T(8,128)}, u32[]{:S(2)}) copy-start(s32[128,512]{1,0:T(8,128)} %m.3) | copy-start | bytes 786436
  0.6 4.1 %copy-start.3 = (f32[128,512]{1,0:T(8,128)S(1)}, f32[128,512]{1,0:T(8,128)}, u32[]{:S(2)}) copy-start(f32[128,512]{1,0:T(8,128)} %b.3) | copy-start | bytes 786436
  0.7 4.0 %copy-start.2 = (f32[128,512]{1,0:T(8,128)S(1)}, f32[128,512]{1,0:T(8,128)}, u32[]{:S(2)}) copy-start(f32[128,512]{1,0:T(8,128)} %q.3) | copy-start | bytes 786436
  0.7 4.0 %copy-start.1 = (f32[128,512]{1,0:T(8,128)S(1)}, f32[128,512]{1,0:T(8,128)}, u32[]{:S(2)}) copy-start(f32[128,512]{1,0:T(8,128)} %p.3) | copy-start | bytes 786436
  0.7 4.0 %copy-start = (f32[128,512]{1,0:T(8,128)S(1)}, f32[128,512]{1,0:T(8,128)}, u32[]{:S(2)}) copy-start(f32[128,512]{1,0:T(8,128)} %h.5) | copy-start | bytes 786436
  1.7 4.9 %collective-permute-start = (f32[2,8,512]{2,1,0:T(8,128)S(1)}, f32[2,8,512]{2,1,0:T(8,128)S(1)}, u32[]{:S(2)}, u32[]{:S(2)}) collective-permute-start(f32[2,8,512]{2,1,0:T(8,128)S(1)} %pack_x.1._), channel_id=1, source_target_pairs={{0,4},{4,0},{8,12},{12,8},{16,20},{20,16},{24,28},{28,24},{1,5},{5... | collective-permute-start | bytes 98312 | tf_op jit(solution)/shard_map/ppermute | solution.py:772
  4.9 1.3 %collective-permute-start.1 = (f32[8,128]{1,0:T(8,128)S(1)}, f32[8,128]{1,0:T(8,128)S(1)}, u32[]{:S(2)}, u32[]{:S(2)}) collective-permute-start(f32[8,128]{1,0:T(8,128)S(1)} %get-tuple-element.50), channel_id=1, source_target_pairs={{0,1},{1,0},{2,3},{3,2},{4,5},{5,4},{6,7},{7,6},{8,9},{9,8},{10,11... | collective-permute-start | bytes 12296 | tf_op jit(solution)/shard_map/ppermute | solution.py:772
  5.0 7.0 %collective-permute-start.3 = (f32[32,128]{1,0:T(8,128)S(1)}, f32[32,128]{1,0:T(8,128)S(1)}, u32[]{:S(2)}, u32[]{:S(2)}) collective-permute-start(f32[32,128]{1,0:T(8,128)S(1)} %get-tuple-element.52), channel_id=1, source_target_pairs={{0,0},{1,2},{2,1},{3,3},{4,4},{5,6},{6,5},{7,7},{8,8},{9,10},{10,9... | collective-permute-start | bytes 49160 | tf_op jit(solution)/shard_map/ppermute | solution.py:768
  6.6 6.4 %collective-permute-start.2 = (f32[8,512]{1,0:T(8,128)S(1)}, f32[8,512]{1,0:T(8,128)S(1)}, u32[]{:S(2)}, u32[]{:S(2)}) collective-permute-start(f32[8,512]{1,0:T(8,128)S(1)} %second_of.1), channel_id=1, source_target_pairs={{0,8},{8,16},{12,4},{16,24},{20,12},{28,20},{1,9},{9,17},{13,5},{1... | collective-permute-start | bytes 49160 | tf_op jit(solution)/shard_map/ppermute | solution.py:762
  13.4 3.7 %collective-permute-start.4 = (f32[1,2560]{1,0:T(1,128)S(1)}, f32[1,2560]{1,0:T(1,128)S(1)}, u32[]{:S(2)}, u32[]{:S(2)}) collective-permute-start(f32[1,2560]{1,0:T(1,128)S(1)} %get-tuple-element.76.mine.refs_0_), channel_id=1, source_target_pairs={{0,4},{4,0},{8,12},{12,8},{16,20},{20,16},{24,28},{28,24},{1,5},{5... | collective-permute-start | bytes 30728 | tf_op jit(solution)/shard_map/ppermute | solution.py:772
  15.1 1.6 %collective-permute-start.5 = (f32[1,640]{1,0:T(1,128)S(1)}, f32[1,640]{1,0:T(1,128)S(1)}, u32[]{:S(2)}, u32[]{:S(2)}) collective-permute-start(f32[1,640]{1,0:T(1,128)S(1)} %get-tuple-element.77.refs_0_), channel_id=1, source_target_pairs={{0,1},{1,0},{2,3},{3,2},{4,5},{5,4},{6,7},{7,6},{8,9},{9,8},{10,11... | collective-permute-start | bytes 7688 | tf_op jit(solution)/shard_map/ppermute | solution.py:772
  15.6 5.5 %collective-permute-start.9 = (f32[1,2048]{1,0:T(1,128)S(1)}, f32[1,2048]{1,0:T(1,128)S(1)}, u32[]{:S(2)}, u32[]{:S(2)}) collective-permute-start(f32[1,2048]{1,0:T(1,128)S(1)} %get-tuple-element.80), channel_id=1, source_target_pairs={{0,2},{1,3},{2,0},{3,1},{4,6},{5,7},{6,4},{7,5},{8,10},{9,11},{10,... | collective-permute-start | bytes 24584 | tf_op jit(solution)/shard_map/ppermute | solution.py:772
  17.1 6.2 %collective-permute-start.8 = (f32[1,2560]{1,0:T(1,128)S(1)}, f32[1,2560]{1,0:T(1,128)S(1)}, u32[]{:S(2)}, u32[]{:S(2)}) collective-permute-start(f32[1,2560]{1,0:T(1,128)S(1)} %merge.1.refs_2_), channel_id=1, source_target_pairs={{0,16},{4,20},{8,24},{12,28},{16,8},{20,12},{24,0},{28,4},{1,17},{... | collective-permute-start | bytes 30728 | tf_op jit(solution)/shard_map/ppermute | solution.py:780
  19.8 4.6 %collective-permute-start.7 = (f32[1,2560]{1,0:T(1,128)S(1)}, f32[1,2560]{1,0:T(1,128)S(1)}, u32[]{:S(2)}, u32[]{:S(2)}) collective-permute-start(f32[1,2560]{1,0:T(1,128)S(1)} %merge.1.refs_2_), channel_id=1, source_target_pairs={{0,24},{4,28},{8,16},{12,20},{16,0},{20,4},{24,8},{28,12},{1,25},{... | collective-permute-start | bytes 30728 | tf_op jit(solution)/shard_map/ppermute | solution.py:780
  21.0 3.7 %collective-permute-start.6 = (f32[1,2560]{1,0:T(1,128)S(1)}, f32[1,2560]{1,0:T(1,128)S(1)}, u32[]{:S(2)}, u32[]{:S(2)}) collective-permute-start(f32[1,2560]{1,0:T(1,128)S(1)} %merge.1.refs_2_), channel_id=1, source_target_pairs={{0,8},{4,12},{8,0},{12,4},{16,24},{20,28},{24,16},{28,20},{1,9},{5... | collective-permute-start | bytes 30728 | tf_op jit(solution)/shard_map/ppermute | solution.py:772
  21.1 1.2 %collective-permute-start.10 = (f32[1,640]{1,0:T(1,128)S(1)}, f32[1,640]{1,0:T(1,128)S(1)}, u32[]{:S(2)}, u32[]{:S(2)}) collective-permute-start(f32[1,640]{1,0:T(1,128)S(1)} %slice.4), channel_id=1, source_target_pairs={{0,1},{1,0},{2,3},{3,2},{4,5},{5,4},{6,7},{7,6},{8,9},{9,8},{10,11... | collective-permute-start | bytes 7688 | tf_op jit(solution)/shard_map/ppermute | solution.py:772

commit v18 on v16

--- a/solution.py
+++ b/solution.py
@@ -203,7 +203,7 @@
 
 
 def prepare_depth_kernel(
-    h, hx, hy, ix, iy, tx, wx, ty, wy, endx, endy, from_left, from_right, natural, turned, *, inv_cx, inv_cy
+    h, hx, hy, ix, iy, tx, wx, ty, wy, endx, endy, natural, turned, *, inv_cx, inv_cy
 ):
     tiles = hx.shape[0] // LANES
     lay_out(h, hx, hy, natural, turned)
@@ -216,16 +216,6 @@
             first = (i * tiles + tile) * LANES
             endx[0:1, first : first + LANES] = ends_x[i][tile * SUB : tile * SUB + 1, :]
         endy[0:1, i * LANES : (i + 1) * LANES] = ends_y[i][0:1, :]
-    one = jnp.ones((tiles * SUB, LANES), F32)
-    zero = jnp.zeros_like(one)
-    for out, left, right in ((from_left, one, zero), (from_right, zero, one)):
-
-        def store(k, speed):
-            for tile in range(tiles):
-                out[at(tile, k), :] = speed[tile * SUB : (tile + 1) * SUB, :]
-
-        left, right = segment_ends(left, right, wx, None, log2(SUB))
-        march_values(left, right, tx, None, ix, inv_cx, None, store)
 
 
 def prepare_depth(h, inv_cx, inv_cy):
@@ -238,8 +228,6 @@
         shape(3 * log2(count), count, LANES),
         shape(1, 3 * stack[0]),
         shape(1, 3 * LANES),
-        shape(*stack),
-        shape(*stack),
     ]
     return pl.pallas_call(
         functools.partial(prepare_depth_kernel, inv_cx=inv_cx, inv_cy=inv_cy),
@@ -681,24 +669,30 @@
         store(k, value * inverse)
 
 
-def rest_x_kernel(inv_ref, r_ref, t_ref, w_ref, s_ref, out, *, scale):
-    tiles = out.shape[0] // LANES
+def rest_x_kernel(inv_ref, r_ref, t_ref, w_ref, s_ref, from_left, from_right, rest, *, scale):
+    tiles = rest.shape[0] // LANES
     zero = jnp.zeros((tiles * SUB, LANES), F32)
-
-    def store(k, speed):
-        for tile in range(tiles):
-            out[at(tile, k), :] = speed[tile * SUB : (tile + 1) * SUB, :]
-
-    left, right = segment_ends(zero, zero, w_ref, s_ref, log2(SUB))
-    march_values(left, right, t_ref, s_ref, inv_ref, scale, r_ref, store)
+    one = jnp.ones_like(zero)
+    for out, left, right, sources, pushes in (
+        (from_left, one, zero, None, None),
+        (from_right, zero, one, None, None),
+        (rest, zero, zero, s_ref, r_ref),
+    ):
+
+        def store(k, speed):
+            for tile in range(tiles):
+                out[at(tile, k), :] = speed[tile * SUB : (tile + 1) * SUB, :]
+
+        left, right = segment_ends(left, right, w_ref, sources, log2(SUB))
+        march_values(left, right, t_ref, sources, inv_ref, scale, pushes, store)
 
 
 def rest_x(*pieces, scale):
     return pl.pallas_call(
         functools.partial(rest_x_kernel, scale=scale),
-        out_shape=shape(*pieces[0].shape),
+        out_shape=(shape(*pieces[0].shape),) * 3,
         in_specs=[VMEM] * len(pieces),
-        out_specs=VMEM,
+        out_specs=(VMEM,) * 3,
         compiler_params=PARAMS,
         cost_estimate=pl.CostEstimate(flops=1_000_000, bytes_accessed=2_000_000, transcendentals=0),
         name="rest_x",
@@ -806,7 +800,7 @@
     near_x = cross(slabs_x, "gx", 1)
     near_y, far_y = pack_y(h, p, q, b, m, after=slabs_x)
     near_y, far_y = cross(near_y, "gy", 1), shift_pair(far_y, "gy")
-    hx, hy, ix, iy, tx, wx, ty, wy, coef_x, coef_y, left_x, right_x = prepare_depth(h, inv_cx, inv_cy)
+    hx, hy, ix, iy, tx, wx, ty, wy, coef_x, coef_y = prepare_depth(h, inv_cx, inv_cy)
     far_x = hand_on(second_of(near_x, coef_x, near_y), "gx")
     px, py, qx, qy, bx, by, mx, my = prepare_rest(p, q, b, m)
     depth_inner, push_inner, across_inner, faces = fluxes_x_inner(hx, px, qx, bx, mx)
@@ -823,8 +817,8 @@
     turned = [pltpu.VMEM((cols, LANES), F32)]
     solve_y_scaled = functools.partial(solve_y_kernel, scale=inv_cy)
     vy = solve(solve_y_scaled, "solve_y", (iy, ry, ty, wy, sy), parts_y, block, turned)
-    own_x = rest_x(ix, rx, tx, wx, sx, scale=inv_cx)
-    vx = solve(solve_x_kernel, "solve_x", (left_x, right_x, own_x), parts_x, block)
+    map_x = rest_x(ix, rx, tx, wx, sx, scale=inv_cx)
+    vx = solve(solve_x_kernel, "solve_x", map_x, parts_x, block)
     return new_depth, vx, vy
 
 

time: 23.8 us -> 23.8 us (level)
  transfers between devices with their start and end apart: 11 -> 11, of which waited for: 5 -> 6; matrix products, arithmetic and copies ran while one was open for 0% -> 0% of each run, Pallas kernels for 23% -> 23%
where the time goes in v18:
time: 23.8 us; the launch traced here: 23.6 us
  starting transfers between devices  13 us (55%)
  Pallas kernels  7.54 us (32%)
  waiting for transfers between devices  2.22 us (9%)
  between operations  0.8 us (3%)
    ppermute x7, starting transfers between devices, cross(): lax.ppermute(value, axis, [(i, i ^ mask) for i in range(lax.axis_size(axi...  6.37 us
    ppermute x2, starting transfers between devices, crossed(): return lax.ppermute(value, axis, pairs)  3.88 us
    ppermute x1, starting transfers between devices, hand_on(): lax.ppermute(value, axis, [(i, t if 0 <= t < count else i ^ 1) for i, t i...  2.11 us
    pallas_call x2, Pallas kernels, solve(): pl.pallas_call(kernel, out_shape=shape(*block), in_specs=[VMEM] * (len(pi...  1.83 us
    ppermute x7, waiting for transfers between devices, cross(): lax.ppermute(value, axis, [(i, i ^ mask) for i in range(lax.axis_size(axi...  1.33 us
    pallas_call x1, Pallas kernels, pack_x(): pl.pallas_call(pack_x_kernel, out_shape=shape(2, SUB, cols), in_specs=[HB...  0.99 us
    pallas_call x1, Pallas kernels, fluxes_y(): pl.pallas_call(flux_y_kernel, out_shape=(shape(*stack),) * 3, in_specs=[V...  0.97 us
    ppermute x2, waiting for transfers between devices, crossed(): return lax.ppermute(value, axis, pairs)  0.88 us
  transfers between devices with their start and end apart: 11, of which 6 were waited for; matrix products, arithmetic and copies ran while one was open for 0% of the time, Pallas kernels for 23%

profile of v18, /device:TPU:0, one launch (start us, length us, event | category | flops | bytes accessed | tf_op | source)
XLA Modules:
  0.0 23.6 jit_solution(6528896105765396443)
XLA Ops:
  0.7 1.0 %pack_x.1._ = f32[2,8,512]{2,1,0:T(8,128)S(1)} custom-call(f32[128,512]{1,0:T(8,128)} %h.5, f32[128,512]{1,0:T(8,128)} %p.3, f32[128,512]{1,0:T(8,128)} %q.3, f32[128,512]{1,0:T(8,128)} %b.3, s32[128,512]{1,0:T(8,128)} %m.3), custom_call_target="tpu_custom_call" | custom-call | tf_op jit(solution)/shard_map/pack_x/pallas_call | solution.py:78
  1.7 3.0 %collective-permute-start = (f32[2,8,512]{2,1,0:T(8,128)S(1)}, f32[2,8,512]{2,1,0:T(8,128)S(1)}, u32[]{:S(2)}, u32[]{:S(2)}) collective-permute-start(f32[2,8,512]{2,1,0:T(8,128)S(1)} %pack_x.1._), channel_id=1, source_target_pairs={{0,4},{4,0},{8,12},{12,8},{16,20},{20,16},{24,28},{28,24},{1,5},{5... | collective-permute-start | bytes 98312 | tf_op jit(solution)/shard_map/ppermute | solution.py:766
  4.7 0.2 pack_y.1
  4.9 0.0 collective-permute-start.1
  5.0 0.7 %collective-permute-start.3 = (f32[32,128]{1,0:T(8,128)S(1)}, f32[32,128]{1,0:T(8,128)S(1)}, u32[]{:S(2)}, u32[]{:S(2)}) collective-permute-start(f32[32,128]{1,0:T(8,128)S(1)} %get-tuple-element.53), channel_id=1, source_target_pairs={{0,0},{1,2},{2,1},{3,3},{4,4},{5,6},{6,5},{7,7},{8,8},{9,10},{10,9... | collective-permute-start | bytes 49160 | tf_op jit(solution)/shard_map/ppermute | solution.py:762
  5.6 0.4 %prepare_depth.1 = (f32[512,128]{1,0:T(8,128)S(1)}, f32[512,128]{1,0:T(8,128)S(1)}, f32[512,128]{1,0:T(8,128)S(1)}, f32[512,128]{1,0:T(8,128)S(1)}, f32[3,32,128...) custom-call(f32[128,512]{1,0:T(8,128)S(1)} %copy-done), custom_call_target="tpu_custom_call" | custom-call | flops 2000000 | bytes 4000000 | tf_op jit(solution)/shard_map/prepare_depth/pallas_call | solution.py:232
  6.1 0.1 collective-permute-done.1.refs_1_.near
  6.1 0.5 %collective-permute-done.both.near = f32[2,8,512]{2,1,0:T(8,128)S(1)} collective-permute-done((f32[2,8,512]{2,1,0:T(8,128)S(1)}, f32[2,8,512]{2,1,0:T(8,128)S(1)}, u32[]{:S(2)}, u32[]{:S(2)}) %collective-permute-start) | collective-permute-done | bytes 32800 | tf_op jit(solution)/shard_map/ppermute | solution.py:766
  6.6 2.1 %collective-permute-start.2 = (f32[8,512]{1,0:T(8,128)S(1)}, f32[8,512]{1,0:T(8,128)S(1)}, u32[]{:S(2)}, u32[]{:S(2)}) collective-permute-start(f32[8,512]{1,0:T(8,128)S(1)} %second_of.1), channel_id=1, source_target_pairs={{0,8},{4,0},{8,16},{12,4},{16,24},{20,12},{24,28},{28,20},{1,9},{5... | collective-permute-start | bytes 49160 | tf_op jit(solution)/shard_map/ppermute | solution.py:756
  8.7 0.8 %prepare_rest.1 = (f32[512,128]{1,0:T(8,128)S(1)}, f32[512,128]{1,0:T(8,128)S(1)}, f32[512,128]{1,0:T(8,128)S(1)}, f32[512,128]{1,0:T(8,128)S(1)}, f32[512,128]{...) custom-call(f32[128,512]{1,0:T(8,128)S(1)} %copy-done.1, ...), custom_call_target="tpu_custom_call" | custom-call | flops 2000000 | bytes 6000000 | tf_op jit(solution)/shard_map/prepare_rest/pallas_call | solution.py:252
  9.5 0.6 %fluxes_x_inner.1 = (f32[512,128]{1,0:T(8,128)S(1)}, f32[512,128]{1,0:T(8,128)S(1)}, f32[512,128]{1,0:T(8,128)S(1)}, f32[6,32,128]{2,1,0:T(8,128)S(1)}) custom-call(f32[512,128]{1,0:T(8,128)S(1)} %get-tuple-element.43.hx, f32[512,128]{1,0:T(8,128)S(1)} %get-tuple-element.44.px, f32[512,128]{1,0:T(8,128)S(1)} %get-tuple-element.45.qx, ...), custom_call_target="tpu_custom_call" | custom-call | flops 4000000 | bytes 4000000 | tf_op jit(solution)/shard_map/fluxes_x_inner/pallas_call | solution.py:423
  10.1 0.0 collective-permute-done.3.far
  10.1 1.0 %fluxes_y.1 = (f32[512,128]{1,0:T(8,128)S(1)}, f32[512,128]{1,0:T(8,128)S(1)}, f32[512,128]{1,0:T(8,128)S(1)}) custom-call(f32[8,128]{1,0:T(8,128)S(1)} %collective-permute-done.1.refs_1_.near, f32[32,128]{1,0:T(8,128)S(1)} %collective-permute-done.3.far, f32[512,128]{1,0:T(8,128)S(1)} %get-tuple-element.54.hy, f32[512,128]{1,0:T(8,128)S(1)} %get-tuple-element.55.py, ...), custom_call_target="tpu_custom_call" | custom-call | flops 4000000 | bytes 4000000 | tf_op jit(solution)/shard_map/fluxes_y/pallas_call | solution.py:379
  11.1 0.0 collective-permute-done.2.far
  11.1 0.4 %fluxes_x.1 = (f32[512,128]{1,0:T(8,128)S(1)}, f32[512,128]{1,0:T(8,128)S(1)}, f32[512,128]{1,0:T(8,128)S(1)}, f32[4,32,128]{2,1,0:T(8,128)S(1)}, f32[1,2560]{1,0:T(1,128)S(1)}) custom-call(f32[2,8,512]{2,1,0:T(8,128)S(1)} %collective-permute-done.both.near, f32[8,512]{1,0:T(8,128)S(1)} %collective-permute-done.2.far, f32[512,128]{1,0:T(8,128)S(1)} %get-tuple-element.43.hx, ...), custom_call_target="tpu_custom_call" | custom-call | tf_op jit(solution)/shard_map/fluxes_x/pallas_call | solution.py:479
  11.5 1.5 %collective-permute-start.4 = (f32[1,2560]{1,0:T(1,128)S(1)}, f32[1,2560]{1,0:T(1,128)S(1)}, u32[]{:S(2)}, u32[]{:S(2)}) collective-permute-start(f32[1,2560]{1,0:T(1,128)S(1)} %get-tuple-element.78.mine.refs_0_), channel_id=1, source_target_pairs={{0,4},{4,0},{8,12},{12,8},{16,20},{20,16},{24,28},{28,24},{1,5},{5... | collective-permute-start | bytes 30728 | tf_op jit(solution)/shard_map/ppermute | solution.py:766
  13.0 0.3 %join_y.1 = (f32[512,128]{1,0:T(8,128)S(1)}, f32[512,128]{1,0:T(8,128)S(1)}, f32[6,32,128]{2,1,0:T(8,128)S(1)}, f32[1,640]{1,0:T(1,128)S(1)}, f32[1,2048]{1,0:T(1,128)S(1)}) custom-call(f32[512,128]{1,0:T(8,128)S(1)} %get-tuple-element.48.depth_inner, f32[512,128]{1,0:T(8,128)S(1)} %get-tuple-element.49.across_inner, ...), custom_call_target="tpu_custom_call" | custom-call | flops 2000000 | bytes 2000000 | tf_op jit(solution)/shard_map/join_y/pallas_call | solution.py:528
  13.3 0.4 %collective-permute-start.5 = (f32[1,640]{1,0:T(1,128)S(1)}, f32[1,640]{1,0:T(1,128)S(1)}, u32[]{:S(2)}, u32[]{:S(2)}) collective-permute-start(f32[1,640]{1,0:T(1,128)S(1)} %get-tuple-element.79.refs_0_), channel_id=1, source_target_pairs={{0,1},{1,0},{2,3},{3,2},{4,5},{5,4},{6,7},{7,6},{8,9},{9,8},{10,11... | collective-permute-start | bytes 7688 | tf_op jit(solution)/shard_map/ppermute | solution.py:766
  13.8 1.1 %collective-permute-start.9 = (f32[1,2048]{1,0:T(1,128)S(1)}, f32[1,2048]{1,0:T(1,128)S(1)}, u32[]{:S(2)}, u32[]{:S(2)}) collective-permute-start(f32[1,2048]{1,0:T(1,128)S(1)} %get-tuple-element.82), channel_id=1, source_target_pairs={{0,2},{1,3},{2,0},{3,1},{4,6},{5,7},{6,4},{7,5},{8,10},{9,11},{10,... | collective-permute-start | bytes 24584 | tf_op jit(solution)/shard_map/ppermute | solution.py:766
  14.9 0.0 collective-permute-done.5.refs_0_.refs_1_
  14.9 0.3 %collective-permute-done.4.theirs.refs_1_ = f32[1,2560]{1,0:T(1,128)S(1)} collective-permute-done((f32[1,2560]{1,0:T(1,128)S(1)}, f32[1,2560]{1,0:T(1,128)S(1)}, u32[]{:S(2)}, u32[]{:S(2)}) %collective-permute-start.4) | collective-permute-done | bytes 10272 | tf_op jit(solution)/shard_map/ppermute | solution.py:766
  15.2 2.6 %collective-permute-start.8 = (f32[1,2560]{1,0:T(1,128)S(1)}, f32[1,2560]{1,0:T(1,128)S(1)}, u32[]{:S(2)}, u32[]{:S(2)}) collective-permute-start(f32[1,2560]{1,0:T(1,128)S(1)} %merge.1.refs_2_), channel_id=1, source_target_pairs={{0,16},{4,20},{8,24},{12,28},{16,8},{20,12},{24,0},{28,4},{1,17},{... | collective-permute-start | bytes 30728 | tf_op jit(solution)/shard_map/ppermute | solution.py:774
  17.9 1.2 %collective-permute-start.7 = (f32[1,2560]{1,0:T(1,128)S(1)}, f32[1,2560]{1,0:T(1,128)S(1)}, u32[]{:S(2)}, u32[]{:S(2)}) collective-permute-start(f32[1,2560]{1,0:T(1,128)S(1)} %merge.1.refs_2_), channel_id=1, source_target_pairs={{0,24},{4,28},{8,16},{12,20},{16,0},{20,4},{24,8},{28,12},{1,25},{... | collective-permute-start | bytes 30728 | tf_op jit(solution)/shard_map/ppermute | solution.py:774
  19.1 0.3 %collective-permute-start.6 = (f32[1,2560]{1,0:T(1,128)S(1)}, f32[1,2560]{1,0:T(1,128)S(1)}, u32[]{:S(2)}, u32[]{:S(2)}) collective-permute-start(f32[1,2560]{1,0:T(1,128)S(1)} %merge.1.refs_2_), channel_id=1, source_target_pairs={{0,8},{4,12},{8,0},{12,4},{16,24},{20,28},{24,16},{28,20},{1,9},{5... | collective-permute-start | bytes 30728 | tf_op jit(solution)/shard_map/ppermute | solution.py:766
  19.4 0.0 collective-permute-done.9.refs_2_
  19.4 0.7 %write_depth.1 = f32[128,512]{1,0:T(8,128)} custom-call(f32[512,128]{1,0:T(8,128)S(1)} %get-tuple-element.72.depth), custom_call_target="tpu_custom_call" | custom-call | flops 100000 | bytes 2000000 | tf_op jit(solution)/shard_map/write_depth/pallas_call | solution.py:573
  20.1 0.3 %rest_x.1 = (f32[512,128]{1,0:T(8,128)S(1)}, f32[512,128]{1,0:T(8,128)S(1)}, f32[512,128]{1,0:T(8,128)S(1)}) custom-call(f32[512,128]{1,0:T(8,128)S(1)} %get-tuple-element.52.ix.inv_ref, f32[512,128]{1,0:T(8,128)S(1)} %get-tuple-element.73.r_ref, f32[3,32,128]{2,1,0:T(8,128)S(1)} %get-tuple-element.62.tx.t_ref, ...), custom_call_target="tpu_custom_call" | custom-call | flops 1000000 | bytes 2000000 | tf_op jit(solution)/shard_map/rest_x/pallas_call | solution.py:691
  20.4 0.1 collective-permute-done.10.refs_3_
  20.5 1.0 %solve_y.1 = f32[128,512]{1,0:T(8,128)} custom-call(f32[512,128]{1,0:T(8,128)S(1)} %get-tuple-element.68.iy.inv_ref, f32[512,128]{1,0:T(8,128)S(1)} %get-tuple-element.80.r_ref, f32[3,32,128]{2,1,0:T(8,128)S(1)} %get-tuple-element.69.ty.t_ref, f32[15,32,128]{2,1,0:T(8,128)S(1)} %get-tuple-element.70.wy.w_ref, f32[6,32,128]{2,1,0:T(8,128)S(1)} %get-tuple-element.81.s_ref, ...), custom_call_target="tpu_custom_call" | custom-call | flops 1000000 | bytes 4000000 | tf_op jit(solution)/shard_map/solve_y/pallas_call | solution.py:741
  21.5 0.9 %collective-permute-done.7.refs_4_ = f32[1,2560]{1,0:T(1,128)S(1)} collective-permute-done((f32[1,2560]{1,0:T(1,128)S(1)}, f32[1,2560]{1,0:T(1,128)S(1)}, u32[]{:S(2)}, u32[]{:S(2)}) %collective-permute-start.7) | collective-permute-done | bytes 10272 | tf_op jit(solution)/shard_map/ppermute | solution.py:774
  22.4 0.3 %collective-permute-done.6.refs_3_ = f32[1,2560]{1,0:T(1,128)S(1)} collective-permute-done((f32[1,2560]{1,0:T(1,128)S(1)}, f32[1,2560]{1,0:T(1,128)S(1)}, u32[]{:S(2)}, u32[]{:S(2)}) %collective-permute-start.6) | collective-permute-done | bytes 10272 | tf_op jit(solution)/shard_map/ppermute | solution.py:766
  22.8 0.8 %solve_x.1 = f32[128,512]{1,0:T(8,128)} custom-call(f32[512,128]{1,0:T(8,128)S(1)} %get-tuple-element.75.from_left, f32[512,128]{1,0:T(8,128)S(1)} %get-tuple-element.76.from_right, f32[512,128]{1,0:T(8,128)S(1)} %get-tuple-element.77.rest, f32[1,2560]{1,0:T(1,128)S(1)} %get-tuple-element.78.mine.refs_0_, ...), custom_call_target="tpu_custom_call" | custom-call | flops 1000000 | bytes 4000000 | tf_op jit(solution)/shard_map/solve_x/pallas_call | solution.py:741
  (15 shorter events, 0.0 us)
Async XLA Ops:
  0.6 4.1 %copy-start.4 = (s32[128,512]{1,0:T(8,128)S(1)}, s32[128,512]{1,0:T(8,128)}, u32[]{:S(2)}) copy-start(s32[128,512]{1,0:T(8,128)} %m.3) | copy-start | bytes 786436
  0.6 4.1 %copy-start.3 = (f32[128,512]{1,0:T(8,128)S(1)}, f32[128,512]{1,0:T(8,128)}, u32[]{:S(2)}) copy-start(f32[128,512]{1,0:T(8,128)} %b.3) | copy-start | bytes 786436
  0.7 4.0 %copy-start.2 = (f32[128,512]{1,0:T(8,128)S(1)}, f32[128,512]{1,0:T(8,128)}, u32[]{:S(2)}) copy-start(f32[128,512]{1,0:T(8,128)} %q.3) | copy-start | bytes 786436
  0.7 4.0 %copy-start.1 = (f32[128,512]{1,0:T(8,128)S(1)}, f32[128,512]{1,0:T(8,128)}, u32[]{:S(2)}) copy-start(f32[128,512]{1,0:T(8,128)} %p.3) | copy-start | bytes 786436
  0.7 4.0 %copy-start = (f32[128,512]{1,0:T(8,128)S(1)}, f32[128,512]{1,0:T(8,128)}, u32[]{:S(2)}) copy-start(f32[128,512]{1,0:T(8,128)} %h.5) | copy-start | bytes 786436
  1.7 4.9 %collective-permute-start = (f32[2,8,512]{2,1,0:T(8,128)S(1)}, f32[2,8,512]{2,1,0:T(8,128)S(1)}, u32[]{:S(2)}, u32[]{:S(2)}) collective-permute-start(f32[2,8,512]{2,1,0:T(8,128)S(1)} %pack_x.1._), channel_id=1, source_target_pairs={{0,4},{4,0},{8,12},{12,8},{16,20},{20,16},{24,28},{28,24},{1,5},{5... | collective-permute-start | bytes 98312 | tf_op jit(solution)/shard_map/ppermute | solution.py:766
  4.9 1.2 %collective-permute-start.1 = (f32[8,128]{1,0:T(8,128)S(1)}, f32[8,128]{1,0:T(8,128)S(1)}, u32[]{:S(2)}, u32[]{:S(2)}) collective-permute-start(f32[8,128]{1,0:T(8,128)S(1)} %get-tuple-element.51), channel_id=1, source_target_pairs={{0,1},{1,0},{2,3},{3,2},{4,5},{5,4},{6,7},{7,6},{8,9},{9,8},{10,11... | collective-permute-start | bytes 12296 | tf_op jit(solution)/shard_map/ppermute | solution.py:766
  5.0 5.1 %collective-permute-start.3 = (f32[32,128]{1,0:T(8,128)S(1)}, f32[32,128]{1,0:T(8,128)S(1)}, u32[]{:S(2)}, u32[]{:S(2)}) collective-permute-start(f32[32,128]{1,0:T(8,128)S(1)} %get-tuple-element.53), channel_id=1, source_target_pairs={{0,0},{1,2},{2,1},{3,3},{4,4},{5,6},{6,5},{7,7},{8,8},{9,10},{10,9... | collective-permute-start | bytes 49160 | tf_op jit(solution)/shard_map/ppermute | solution.py:762
  6.6 4.5 %collective-permute-start.2 = (f32[8,512]{1,0:T(8,128)S(1)}, f32[8,512]{1,0:T(8,128)S(1)}, u32[]{:S(2)}, u32[]{:S(2)}) collective-permute-start(f32[8,512]{1,0:T(8,128)S(1)} %second_of.1), channel_id=1, source_target_pairs={{0,8},{4,0},{8,16},{12,4},{16,24},{20,12},{24,28},{28,20},{1,9},{5... | collective-permute-start | bytes 49160 | tf_op jit(solution)/shard_map/ppermute | solution.py:756
  11.5 3.7 %collective-permute-start.4 = (f32[1,2560]{1,0:T(1,128)S(1)}, f32[1,2560]{1,0:T(1,128)S(1)}, u32[]{:S(2)}, u32[]{:S(2)}) collective-permute-start(f32[1,2560]{1,0:T(1,128)S(1)} %get-tuple-element.78.mine.refs_0_), channel_id=1, source_target_pairs={{0,4},{4,0},{8,12},{12,8},{16,20},{20,16},{24,28},{28,24},{1,5},{5... | collective-permute-start | bytes 30728 | tf_op jit(solution)/shard_map/ppermute | solution.py:766
  13.3 1.6 %collective-permute-start.5 = (f32[1,640]{1,0:T(1,128)S(1)}, f32[1,640]{1,0:T(1,128)S(1)}, u32[]{:S(2)}, u32[]{:S(2)}) collective-permute-start(f32[1,640]{1,0:T(1,128)S(1)} %get-tuple-element.79.refs_0_), channel_id=1, source_target_pairs={{0,1},{1,0},{2,3},{3,2},{4,5},{5,4},{6,7},{7,6},{8,9},{9,8},{10,11... | collective-permute-start | bytes 7688 | tf_op jit(solution)/shard_map/ppermute | solution.py:766
  13.8 5.6 %collective-permute-start.9 = (f32[1,2048]{1,0:T(1,128)S(1)}, f32[1,2048]{1,0:T(1,128)S(1)}, u32[]{:S(2)}, u32[]{:S(2)}) collective-permute-start(f32[1,2048]{1,0:T(1,128)S(1)} %get-tuple-element.82), channel_id=1, source_target_pairs={{0,2},{1,3},{2,0},{3,1},{4,6},{5,7},{6,4},{7,5},{8,10},{9,11},{10,... | collective-permute-start | bytes 24584 | tf_op jit(solution)/shard_map/ppermute | solution.py:766
  15.2 6.3 %collective-permute-start.8 = (f32[1,2560]{1,0:T(1,128)S(1)}, f32[1,2560]{1,0:T(1,128)S(1)}, u32[]{:S(2)}, u32[]{:S(2)}) collective-permute-start(f32[1,2560]{1,0:T(1,128)S(1)} %merge.1.refs_2_), channel_id=1, source_target_pairs={{0,16},{4,20},{8,24},{12,28},{16,8},{20,12},{24,0},{28,4},{1,17},{... | collective-permute-start | bytes 30728 | tf_op jit(solution)/shard_map/ppermute | solution.py:774
  17.9 4.6 %collective-permute-start.7 = (f32[1,2560]{1,0:T(1,128)S(1)}, f32[1,2560]{1,0:T(1,128)S(1)}, u32[]{:S(2)}, u32[]{:S(2)}) collective-permute-start(f32[1,2560]{1,0:T(1,128)S(1)} %merge.1.refs_2_), channel_id=1, source_target_pairs={{0,24},{4,28},{8,16},{12,20},{16,0},{20,4},{24,8},{28,12},{1,25},{... | collective-permute-start | bytes 30728 | tf_op jit(solution)/shard_map/ppermute | solution.py:774
  19.1 3.7 %collective-permute-start.6 = (f32[1,2560]{1,0:T(1,128)S(1)}, f32[1,2560]{1,0:T(1,128)S(1)}, u32[]{:S(2)}, u32[]{:S(2)}) collective-permute-start(f32[1,2560]{1,0:T(1,128)S(1)} %merge.1.refs_2_), channel_id=1, source_target_pairs={{0,8},{4,12},{8,0},{12,4},{16,24},{20,28},{24,16},{28,20},{1,9},{5... | collective-permute-start | bytes 30728 | tf_op jit(solution)/shard_map/ppermute | solution.py:766
  19.4 1.2 %collective-permute-start.10 = (f32[1,640]{1,0:T(1,128)S(1)}, f32[1,640]{1,0:T(1,128)S(1)}, u32[]{:S(2)}, u32[]{:S(2)}) collective-permute-start(f32[1,640]{1,0:T(1,128)S(1)} %slice.4), channel_id=1, source_target_pairs={{0,1},{1,0},{2,3},{3,2},{4,5},{5,4},{6,7},{7,6},{8,9},{9,8},{10,11... | collective-permute-start | bytes 7688 | tf_op jit(solution)/shard_map/ppermute | solution.py:766
